TPU v7x, 32 devices: a whole 2x2x4 slice. The times are simulated.
32 devices in a mesh: dp: 8 (over y, x, core), mp: 4 (over z).
Axes of the slice: x: 2, y: 2, z: 4, core: 2. Of those that a mesh axis runs over, the one named last changes fastest.
Arguments:
- pool: bfloat16 [64, 32, 5120], P('dp', None, 'mp'), may hold values from -20 to 20
- send_table: int32 [8, 8], P('dp'), may hold values from -1 to 7, as said below
- slot_source: int32 [64], P('dp'), may hold values from 0 to 7, as said below
- multiplicity: int32 [64], P('dp'), may hold values from 1 to 4
- slot_weight: float32 [64], P('dp'), may hold values from 0.1 to 1
- cotangent: bfloat16 [64, 32, 4096], P('dp', None, 'mp'), may hold values from -6 to 6
- w_query: bfloat16 [5120, 4096], P(None, 'mp'), may hold values from -0.078125 to 0.078125
- w_key: bfloat16 [5120, 512], P('mp'), may hold values from -0.078125 to 0.078125
- w_value: bfloat16 [5120, 512], P('mp'), may hold values from -0.078125 to 0.078125
- query_gain: float32 [128], replicated, may hold values from 0.5 to 5
- key_gain: float32 [128], replicated, may hold values from 0.5 to 5
Outputs:
- attended: bfloat16 [64, 32, 4096], P('dp', None, 'mp')
- grad_query: float32 [5120, 4096], P('dp', 'mp')
- key_gradient: float32 [5120, 512], P('mp', 'dp')
- grad_value: float32 [5120, 512], P('mp', 'dp')
Inputs may be any that keep to these rules, and one draw needn't show every extreme that they name: Entry [r, d] is the sequence of rank r's pool of 8 that data rank d receives from rank r, or -1 where rank d takes nothing from rank r; send_table[r, d] >= 0 exactly where r is among the sources of rank d's slots. `slot_source`: the 8 slots of data rank d (entries d * 8 to d * 8 + 7) name 8 different source ranks.
All inputs are finite; a program needn't handle non-finite values.
Results may differ from a plain program's by a relative error of at most 0.025.
The roundings to bfloat16 on the way count: a program that leaves them out, or rounds other values in their place, can miss the bound.
Values may be sent and summed in bfloat16 or wider, within the bound.
No kernel may reach another device: no remote copies, remote signals or barrier semaphores. Data moves between devices by JAX's collectives and lax.ppermute only.
A program may use at most 64 MiB of HBM per device.

v0:
```python
import math

import jax
import jax.numpy as jnp
from jax import lax
from jax.sharding import PartitionSpec as P

HEADS = 32
KV_HEADS = 4


def rms_scale(values, gain):
    inverse = lax.rsqrt(jnp.mean(values * values, axis=-1, keepdims=True) + 1e-06)
    return (values * inverse * gain, inverse)


def rms_back(values, inverse, gain, grad_out):
    scaled = grad_out * gain
    inner = jnp.mean(values * scaled, axis=-1, keepdims=True)
    return inverse * scaled - values * (inverse * inverse * inverse) * inner


def forward_core(query, key_sum, value_sum, query_gain, key_gain):
    scale = 1.0 / math.sqrt(query.shape[-1])
    q_norm, q_inverse = rms_scale(query, query_gain)
    k_norm, k_inverse = rms_scale(key_sum, key_gain)
    q_half = q_norm.astype(jnp.bfloat16)
    k_half = k_norm.astype(jnp.bfloat16)
    v_half = value_sum.astype(jnp.bfloat16)
    score_matrix = (
        jnp.einsum("sqgph,skgh->sgpqk", q_half, k_half, preferred_element_type=jnp.float32) * scale
    )
    length = query.shape[1]
    causal = lax.broadcasted_iota(jnp.int32, (length, length), 0) >= lax.broadcasted_iota(
        jnp.int32, (length, length), 1
    )
    score_matrix = jnp.where(causal, score_matrix, -1e30)
    peak = jnp.max(score_matrix, axis=-1, keepdims=True)
    raised = jnp.exp(score_matrix - peak)
    probs = raised / jnp.sum(raised, axis=-1, keepdims=True)
    p_half = probs.astype(jnp.bfloat16)
    attended = jnp.einsum("sgpqk,skgh->sqgph", p_half, v_half, preferred_element_type=jnp.float32)
    return (attended, (q_inverse, k_inverse, q_half, k_half, v_half, probs, p_half))


def backward_core(d_out, query, key_sum, query_gain, key_gain, saved):
    q_inverse, k_inverse, q_half, k_half, v_half, probs, p_half = saved
    scale = 1.0 / math.sqrt(query.shape[-1])
    out_half = d_out.astype(jnp.bfloat16)
    d_probs = jnp.einsum("sqgph,skgh->sgpqk", out_half, v_half, preferred_element_type=jnp.float32)
    d_value = jnp.einsum("sgpqk,sqgph->skgh", p_half, out_half, preferred_element_type=jnp.float32)
    d_scores = probs * (d_probs - jnp.sum(d_probs * probs, axis=-1, keepdims=True)) * scale
    score_half = d_scores.astype(jnp.bfloat16)
    d_qnorm = jnp.einsum(
        "sgpqk,skgh->sqgph", score_half, k_half, preferred_element_type=jnp.float32
    )
    d_knorm = jnp.einsum(
        "sgpqk,sqgph->skgh", score_half, q_half, preferred_element_type=jnp.float32
    )
    d_query = rms_back(query, q_inverse, query_gain, d_qnorm)
    d_key = rms_back(key_sum, k_inverse, key_gain, d_knorm)
    return (d_query, d_key, d_value)


def local(
    pool,
    send_table,
    slot_source,
    multiplicity,
    slot_weight,
    cotangent,
    w_query,
    w_key,
    w_value,
    query_gain,
    key_gain,
):
    slot_count = slot_source.shape[0]
    length = pool.shape[1]
    local_width = pool.shape[2]
    query_cols = w_query.shape[1]
    key_cols = w_key.shape[1]
    head_dim = query_gain.shape[0]
    heads_here = query_cols // head_dim
    group_size = HEADS // KV_HEADS
    token_count = slot_count * length
    outgoing_index = send_table[0]
    outgoing = jnp.take(pool, jnp.maximum(outgoing_index, 0), axis=0)
    outgoing = jnp.where((outgoing_index >= 0)[:, None, None], outgoing, jnp.zeros_like(outgoing))
    arrived = lax.all_to_all(outgoing, "dp", split_axis=0, concat_axis=0, tiled=True)
    chosen = jnp.take(arrived, slot_source, axis=0)
    local_rows = chosen.reshape(token_count, local_width)
    piece = lax.all_gather(local_rows, "mp", axis=1, tiled=True)
    query_total = jnp.dot(piece, w_query, preferred_element_type=jnp.float32)
    key_part = jnp.dot(local_rows, w_key, preferred_element_type=jnp.float32)
    value_part = jnp.dot(local_rows, w_value, preferred_element_type=jnp.float32)
    group_index = lax.axis_index("mp") * heads_here // group_size
    offset = group_index * head_dim
    key_all, value_all = lax.psum((key_part, value_part), "mp")
    key_own = lax.dynamic_slice_in_dim(key_all, offset, head_dim, 1)
    value_own = lax.dynamic_slice_in_dim(value_all, offset, head_dim, 1)
    key_sum = key_own.reshape(slot_count, length, 1, head_dim)
    value_sum = value_own.reshape(slot_count, length, 1, head_dim)
    query = query_total.reshape(slot_count, length, 1, heads_here, head_dim)
    attended, saved = forward_core(query, key_sum, value_sum, query_gain, key_gain)
    attended_out = attended.reshape(slot_count, length, query_cols).astype(jnp.bfloat16)
    factor = multiplicity.astype(jnp.float32) * slot_weight / length
    d_out = (
        cotangent.astype(jnp.float32).reshape(slot_count, length, 1, heads_here, head_dim)
        * factor[:, None, None, None, None]
    )
    d_query, d_key, d_value = backward_core(d_out, query, key_sum, query_gain, key_gain, saved)
    query_rows = d_query.reshape(token_count, query_cols).astype(jnp.bfloat16)
    blank = jnp.zeros((token_count, key_cols), jnp.float32)
    key_place = lax.dynamic_update_slice_in_dim(
        blank, d_key.reshape(token_count, head_dim), offset, 1
    )
    value_place = lax.dynamic_update_slice_in_dim(
        blank, d_value.reshape(token_count, head_dim), offset, 1
    )
    key_grads, value_grads = (
        lax.psum(key_place.astype(jnp.bfloat16), "mp").astype(jnp.float32),
        lax.psum(value_place.astype(jnp.bfloat16), "mp").astype(jnp.float32),
    )
    key_half = key_grads.astype(jnp.bfloat16)
    value_half = value_grads.astype(jnp.bfloat16)
    key_term = jnp.einsum("td,tc->dc", local_rows, key_half, preferred_element_type=jnp.float32)
    value_term = jnp.einsum("td,tc->dc", local_rows, value_half, preferred_element_type=jnp.float32)
    query_whole = jnp.einsum("td,tc->dc", piece, query_rows, preferred_element_type=jnp.float32)
    grad_query, key_gradient, grad_value = (
        lax.psum_scatter(
            query_whole.astype(jnp.bfloat16), "dp", scatter_dimension=0, tiled=True
        ).astype(jnp.float32),
        lax.psum_scatter(
            key_term.astype(jnp.bfloat16), "dp", scatter_dimension=1, tiled=True
        ).astype(jnp.float32),
        lax.psum_scatter(
            value_term.astype(jnp.bfloat16), "dp", scatter_dimension=1, tiled=True
        ).astype(jnp.float32),
    )
    return (attended_out, grad_query, key_gradient, grad_value)


def solution(mesh):
    return jax.shard_map(
        local,
        mesh=mesh,
        in_specs=(
            P("dp", None, "mp"),
            P("dp", None),
            P("dp"),
            P("dp"),
            P("dp"),
            P("dp", None, "mp"),
            P(None, "mp"),
            P("mp", None),
            P("mp", None),
            P(),
            P(),
        ),
        out_specs=(P("dp", None, "mp"), P("dp", "mp"), P("mp", "dp"), P("mp", "dp")),
        check_vma=False,
    )
```

profile of v0, /device:TPU:7, one launch (start us, length us, event | category | flops | bytes accessed | tf_op | source)
XLA Modules:
  0.0 358.6 jit_solution(3323450831312931513)
XLA Ops:
  8.6 1.7 gather_fusion
  11.3 4.5 %all-to-all-start = ((bf16[8,32,1280]{2,1,0:T(8,128)(2,1)}), bf16[8,32,1280]{2,1,0:T(8,128)(2,1)S(1)}, u32[]{:S(2)}, u32[]{:S(2)}) async-start(bf16[8,32,1280]{2,1,0:T(8,128)(2,1)} %select_select_fusion), calls=%async_computation | async-start | bytes 1310720 | tf_op jit(solution)/shard_map/all_to_all | solution.py:90
  15.9 8.5 %all-to-all-done = bf16[8,32,1280]{2,1,0:T(8,128)(2,1)S(1)} async-done(((bf16[8,32,1280]{2,1,0:T(8,128)(2,1)}), bf16[8,32,1280]{2,1,0:T(8,128)(2,1)S(1)}, u32[]{:S(2)}, u32[]{:S(2)}) %all-to-all-start) | async-done | bytes 655392 | tf_op jit(solution)/shard_map/all_to_all | solution.py:90
  25.1 1.3 fusion.31
  27.3 1.6 fusion.30
  28.9 31.4 %all-reduce.8 = bf16[256,512]{1,0:T(8,128)(2,1)S(1)} all-reduce(f32[256,512]{1,0:T(8,128)S(1)} %fusion.30), channel_id=1, replica_groups=mesh['dp'=8,'mp'=4] {'mp'}, use_global_device_ids=true, to_apply=%region_0.0 | all-reduce | flops 131072 | bytes 786432 | tf_op jit(solution)/shard_map/psum | solution.py:99
  60.3 11.0 %all-reduce.5.cloned.1.call-done = f32[256,512]{1,0:T(8,128)} async-done(((f32[256,512]{1,0:T(8,128)}), f32[256,512]{1,0:T(8,128)}) %all-reduce.5.cloned.1.call-update) | async-done | bytes 524304 | tf_op jit(solution)/shard_map/psum | solution.py:99
  72.5 56.6 %all-gather.2.cloned.1.call-done = bf16[256,5120]{1,0:T(8,128)(2,1)} async-done(((bf16[256,1280]{1,0:T(8,128)(2,1)}), bf16[256,5120]{1,0:T(8,128)(2,1)}) %all-gather.2.cloned.1.call-update) | async-done | bytes 2621456 | tf_op jit(solution)/shard_map/all_gather | solution.py:93
  129.0 6.4 %convolution_bitcast_fusion.2 = f32[32,8,8,128]{3,1,2,0:T(8,128)S(1)} fusion(bf16[256,5120]{1,0:T(8,128)(2,1)} %all-gather.2.cloned.1.call-done, bf16[5120,1024]{1,0:T(8,128)(2,1)} %param.19), kind=kOutput, calls=%fused_computation.7 | convolution fusion | flops 2684354560 | bytes 14155776 | tf_op jit(solution)/shard_map/dot_general | solution.py:94
  136.7 1.0 fusion.29
  138.1 1.5 fusion.15
  141.6 1.0 multiply_reduce_fusion.1
  145.8 36.4 %all-reduce.7.cloned.1.call-done = (bf16[256,512]{1,0:T(8,128)(2,1)}, bf16[256,512]{1,0:T(8,128)(2,1)}) async-done(((bf16[256,512]{1,0:T(8,128)(2,1)}, bf16[256,512]{1,0:T(8,128)(2,1)}), (bf16[256,512]{1,0:T(8,128)(2,1)}, bf16[256,512]{1,0:T(8,128)(2,1)})) %all-reduce.7.cloned.1.call-update) | async-done | bytes 524304 | tf_op jit(solution)/shard_map/psum | solution.py:122
  182.2 2.6 convolution_convert_fusion.2
  184.9 2.6 convolution_convert_fusion.1
  187.7 1.8 multiply_reduce_fusion
  190.7 5.7 %convolution_convert_fusion = bf16[5120,1024]{1,0:T(8,128)(2,1)} fusion(bf16[256,5120]{1,0:T(8,128)(2,1)S(1)} %copy-done.5, bf16[32,8,8,128]{3,2,1,0:T(8,128)(2,1)S(1)} %bitcast.131), kind=kOutput, calls=%fused_computation.2 | convolution fusion | flops 2689597440 | bytes 13631488 | tf_op jit(solution)/shard_map/td,tc->dc/dot_general | solution.py:129
  196.4 1.2 copy-done.4
  199.3 23.9 %reduce-scatter.6.cloned.1.call-done = bf16[1280,64]{0,1:T(8,128)(2,1)} async-done(((bf16[1280,512]{0,1:T(8,128)(2,1)}), bf16[1280,64]{0,1:T(8,128)(2,1)}) %reduce-scatter.6.cloned.1.call-update) | async-done | bytes 163856 | tf_op jit(solution)/shard_map/reduce_scatter | solution.py:134
  223.2 1.7 convert_element_type.105
  224.8 38.8 %reduce-scatter.8.cloned.1.call-done = bf16[1280,64]{0,1:T(8,128)(2,1)} async-done(((bf16[1280,512]{0,1:T(8,128)(2,1)}), bf16[1280,64]{0,1:T(8,128)(2,1)}) %reduce-scatter.8.cloned.1.call-update) | async-done | bytes 163856 | tf_op jit(solution)/shard_map/reduce_scatter | solution.py:137
  263.6 1.7 convert_element_type.108
  265.3 83.4 %reduce-scatter.4.cloned.1.call-done = bf16[640,1024]{1,0:T(8,128)(2,1)} async-done(((bf16[5120,1024]{1,0:T(8,128)(2,1)}), bf16[640,1024]{1,0:T(8,128)(2,1)}) %reduce-scatter.4.cloned.1.call-update) | async-done | bytes 1310736 | tf_op jit(solution)/shard_map/reduce_scatter | solution.py:131
  348.7 3.1 convert_element_type.102
  (93 shorter events, 14.9 us)
Async XLA Ops:
  7.2 17.9 %copy-start = (bf16[1280,512]{1,0:T(8,128)(2,1)S(1)}, bf16[1280,512]{1,0:T(8,128)(2,1)}, u32[]{:S(2)}) copy-start(bf16[1280,512]{1,0:T(8,128)(2,1)} %param.20) | copy-start | bytes 3932164
  7.2 8.7 %copy-start.21 = (s32[8]{0:T(128)S(1)}, s32[8]{0:T(128)}, u32[]{:S(2)}) copy-start(s32[8]{0:T(128)} %param.15) | copy-start | bytes 100
  11.3 13.0 %all-to-all-start = ((bf16[8,32,1280]{2,1,0:T(8,128)(2,1)}), bf16[8,32,1280]{2,1,0:T(8,128)(2,1)S(1)}, u32[]{:S(2)}, u32[]{:S(2)}) async-start(bf16[8,32,1280]{2,1,0:T(8,128)(2,1)} %select_select_fusion), calls=%async_computation | async-start | bytes 1310720 | tf_op jit(solution)/shard_map/all_to_all | solution.py:90
  15.8 55.5 %all-reduce.5.cloned.1.call-start = ((), (), s32[]{:S(2)}) async-start(), calls=%async_computation.4 | async-start | bytes 1048576 | tf_op jit(solution)/shard_map/psum | solution.py:99
  24.9 2.3 copy-start.22
  24.9 2.3 copy-start.23
  25.1 1.4 copy-start.1
  25.1 2.2 copy-start.8
  26.4 102.6 %all-gather.2.cloned.1.call-start = ((), (), s32[]{:S(2)}) async-start(), calls=%async_computation.5 | async-start | bytes 3276800 | tf_op jit(solution)/shard_map/all_gather | solution.py:93
  27.2 155.0 %all-reduce.7.cloned.1.call-start = ((), (), s32[]{:S(2)}) async-start(), calls=%async_computation.9 | async-start | bytes 1048576 | tf_op jit(solution)/shard_map/psum | solution.py:122
  72.3 64.4 %copy-start.6 = (f32[256,128]{1,0:T(8,128)}, f32[256,128]{1,0:T(8,128)S(1)}, u32[]{:S(2)}) copy-start(f32[256,128]{1,0:T(8,128)S(1)} %get-tuple-element.8) | copy-start | bytes 393220
  135.4 1.3 copy-start.18
  136.7 6.4 %copy-start.9 = (f32[8,32,8]{1,2,0:T(8,128)}, f32[8,32,8]{1,2,0:T(8,128)S(1)}, u32[]{:S(2)}) copy-start(f32[8,32,8]{1,2,0:T(8,128)S(1)} %get-tuple-element.12) | copy-start | bytes 24580
  137.7 4.9 %copy-start.3 = (f32[8,1,8,32,32]{3,4,2,0,1:T(8,128)}, f32[8,1,8,32,32]{3,4,2,0,1:T(8,128)S(1)}, u32[]{:S(2)}) copy-start(f32[8,1,8,32,32]{3,4,2,0,1:T(8,128)S(1)} %get-tuple-element.14) | copy-start | bytes 786436
  137.8 4.9 %copy-start.11 = (f32[8,8,32]{2,1,0:T(8,128)}, f32[8,8,32]{2,1,0:T(8,128)S(1)}, u32[]{:S(2)}) copy-start(f32[8,8,32]{2,1,0:T(8,128)S(1)} %get-tuple-element.13) | copy-start | bytes 24580
  138.1 4.6 %copy-start.13 = (f32[8,8,32]{2,1,0:T(8,128)}, f32[8,8,32]{2,1,0:T(8,128)S(1)}, u32[]{:S(2)}) copy-start(f32[8,8,32]{2,1,0:T(8,128)S(1)} %fusion.11) | copy-start | bytes 24580
  138.1 3.5 copy-start.20
  142.7 39.5 %copy-start.2 = (bf16[8,32,1280]{2,1,0:T(8,128)(2,1)S(1)}, bf16[8,32,1280]{2,1,0:T(8,128)(2,1)}, u32[]{:S(2)}) copy-start(bf16[8,32,1280]{2,1,0:T(8,128)(2,1)} %copy-done.1) | copy-start | bytes 1966084
  145.8 77.4 %reduce-scatter.6.cloned.1.call-start = ((), (), s32[]{:S(2)}) async-start(), calls=%async_computation.7 | async-start | bytes 1474560 | tf_op jit(solution)/shard_map/reduce_scatter | solution.py:134
  184.8 78.8 %reduce-scatter.8.cloned.1.call-start = ((), (), s32[]{:S(2)}) async-start(), calls=%async_computation.8 | async-start | bytes 1474560 | tf_op jit(solution)/shard_map/reduce_scatter | solution.py:137
  187.4 2.1 copy-start.10
  187.4 2.1 copy-start.15
  187.5 161.2 %reduce-scatter.4.cloned.1.call-start = ((), (), s32[]{:S(2)}) async-start(), calls=%async_computation.6 | async-start | bytes 11796480 | tf_op jit(solution)/shard_map/reduce_scatter | solution.py:131
  187.7 3.0 copy-start.5
  (7 other events, 7.8 us)
Sparse Core Ops, SparseCore 0:
  26.6 44.7 all-reduce.4
  73.5 55.5 all-gather.1
  145.9 36.2 all-reduce.6
  185.9 37.2 reduce-scatter.5
  226.3 37.2 reduce-scatter.7
  267.0 81.6 reduce-scatter.3
where the time goes:
time: 362 us; the launch traced here: 359 us
  waiting for transfers between devices  259 us (72%)
  blocking collectives  31.4 us (9%)
  matrix products  26.4 us (7%)
  between operations  14.6 us (4%)
  other arithmetic  12.8 us (4%)
  local copies, waits for them, and re-layouts  9.21 us (3%)
  starting transfers between devices  4.9 us (1%)
    reduce_scatter x1, waiting for transfers between devices, local(): lax.psum_scatter(query_whole.astype(jnp.bfloat16), 'dp', scatter_dimensio...  83.4 us
    all_gather x1, waiting for transfers between devices, local(): piece = lax.all_gather(local_rows, 'mp', axis=1, tiled=True)  56.6 us
    reduce_scatter x1, waiting for transfers between devices, local(): lax.psum_scatter(value_term.astype(jnp.bfloat16), 'dp', scatter_dimension...  38.8 us
    psum x1, waiting for transfers between devices, local(): lax.psum(key_place.astype(jnp.bfloat16), 'mp').astype(jnp.float32)  36.4 us
    psum x1, blocking collectives, local(): key_all, value_all = lax.psum((key_part, value_part), 'mp')  31.4 us
    reduce_scatter x1, waiting for transfers between devices, local(): lax.psum_scatter(key_term.astype(jnp.bfloat16), 'dp', scatter_dimension=1...  23.9 us
    psum x1, waiting for transfers between devices, local(): key_all, value_all = lax.psum((key_part, value_part), 'mp')  11 us
    all_to_all x1, waiting for transfers between devices, local(): lax.all_to_all(outgoing, 'dp', split_axis=0, concat_axis=0, tiled=True)  8.45 us
  transfers between devices with their start and end apart: 7, of which 7 were waited for; matrix products, arithmetic and copies ran while one was open for 5% of the time, Pallas kernels for 0%

commit v1 on v0

v1 whole, which is shorter than its diff:
```python
import functools
import math

import jax
import jax.numpy as jnp
from jax import lax
from jax.sharding import PartitionSpec as P

HEADS = 32
KV_HEADS = 4
F32 = jnp.float32
BF16 = jnp.bfloat16


def rms_scale(values, gain):
    inverse = lax.rsqrt(jnp.mean(values * values, axis=-1, keepdims=True) + 1e-06)
    return (values * inverse * gain, inverse)


def rms_back(values, inverse, gain, grad_out):
    scaled = grad_out * gain
    inner = jnp.mean(values * scaled, axis=-1, keepdims=True)
    return inverse * scaled - values * (inverse * inverse * inverse) * inner


def forward_core(query, key_sum, value_sum, query_gain, key_gain):
    scale = 1.0 / math.sqrt(query.shape[-1])
    q_norm, q_inverse = rms_scale(query, query_gain)
    k_norm, k_inverse = rms_scale(key_sum, key_gain)
    q_half = q_norm.astype(jnp.bfloat16)
    k_half = k_norm.astype(jnp.bfloat16)
    v_half = value_sum.astype(jnp.bfloat16)
    score_matrix = (
        jnp.einsum("sqgph,skgh->sgpqk", q_half, k_half, preferred_element_type=jnp.float32) * scale
    )
    length = query.shape[1]
    causal = lax.broadcasted_iota(jnp.int32, (length, length), 0) >= lax.broadcasted_iota(
        jnp.int32, (length, length), 1
    )
    score_matrix = jnp.where(causal, score_matrix, -1e30)
    peak = jnp.max(score_matrix, axis=-1, keepdims=True)
    raised = jnp.exp(score_matrix - peak)
    probs = raised / jnp.sum(raised, axis=-1, keepdims=True)
    p_half = probs.astype(jnp.bfloat16)
    attended = jnp.einsum("sgpqk,skgh->sqgph", p_half, v_half, preferred_element_type=jnp.float32)
    return (attended, (q_inverse, k_inverse, q_half, k_half, v_half, probs, p_half))


def backward_core(d_out, query, key_sum, query_gain, key_gain, saved):
    q_inverse, k_inverse, q_half, k_half, v_half, probs, p_half = saved
    scale = 1.0 / math.sqrt(query.shape[-1])
    out_half = d_out.astype(jnp.bfloat16)
    d_probs = jnp.einsum("sqgph,skgh->sgpqk", out_half, v_half, preferred_element_type=jnp.float32)
    d_value = jnp.einsum("sgpqk,sqgph->skgh", p_half, out_half, preferred_element_type=jnp.float32)
    d_scores = probs * (d_probs - jnp.sum(d_probs * probs, axis=-1, keepdims=True)) * scale
    score_half = d_scores.astype(jnp.bfloat16)
    d_qnorm = jnp.einsum(
        "sgpqk,skgh->sqgph", score_half, k_half, preferred_element_type=jnp.float32
    )
    d_knorm = jnp.einsum(
        "sgpqk,sqgph->skgh", score_half, q_half, preferred_element_type=jnp.float32
    )
    d_query = rms_back(query, q_inverse, query_gain, d_qnorm)
    d_key = rms_back(key_sum, k_inverse, key_gain, d_knorm)
    return (d_query, d_key, d_value)


def attend(x, w_query, w_kv, cot, factor, query_gain, key_gain, length, device_cols):
    blocks, tokens, width = x.shape
    dim = query_gain.shape[0]
    slots = tokens // length
    heads = w_query.shape[1] // dim
    x = x.transpose(1, 0, 2).reshape(tokens, blocks * width)
    query = jnp.dot(x, w_query, preferred_element_type=F32)
    kv = jnp.dot(x, w_kv, preferred_element_type=F32)
    query = query.reshape(slots, length, 1, heads, dim)
    key = kv[:, :dim].reshape(slots, length, 1, dim)
    value = kv[:, dim:].reshape(slots, length, 1, dim)
    attended, saved = forward_core(query, key, value, query_gain, key_gain)
    d_out = cot.astype(F32).reshape(slots, length, 1, heads, dim)
    d_out = d_out * factor[:, None, None, None, None]
    d_query, d_key, d_value = backward_core(d_out, query, key, query_gain, key_gain, saved)
    pairs = [d_key.reshape(tokens, -1, device_cols), d_value.reshape(tokens, -1, device_cols)]
    d_kv = jnp.stack(pairs, axis=2).reshape(tokens, 2 * dim)
    return (
        attended.reshape(tokens, -1).astype(BF16),
        d_query.reshape(tokens, -1).astype(BF16),
        d_kv.astype(BF16),
    )


def line_gather(block, axis, count):
    me = lax.axis_index(axis)
    up, down = [block], [block]
    for hop in range(1, count):
        up.append(lax.ppermute(up[-1], axis, [(i, i + 1) for i in range(hop - 1, count - 1)]))
        down.append(
            lax.ppermute(down[-1], axis, [(i, i - 1) for i in range(count - hop, 0, -1)])
        )
    return [block] + [jnp.where(me >= hop, up[hop], down[count - hop]) for hop in range(1, count)]


def pick(array, index):
    return array.at[index].get(mode="promise_in_bounds")


def flip(block, axis, count, bits):
    return lax.ppermute(block, axis, [(i, i ^ bits) for i in range(count)])


def local(
    n_dp,
    n_mp,
    pool,
    send_table,
    slot_source,
    multiplicity,
    slot_weight,
    cotangent,
    w_query,
    w_key,
    w_value,
    query_gain,
    key_gain,
):
    slots = slot_source.shape[0]
    length = pool.shape[1]
    width = pool.shape[2]
    query_cols = w_query.shape[1]
    key_cols = w_key.shape[1]
    dim = query_gain.shape[0]
    tokens = slots * length
    chips = n_dp // 2
    dp = lax.axis_index("dp")
    mp = lax.axis_index("mp")
    chip, core = dp // 2, dp % 2

    share = width // n_dp
    own_key = lax.dynamic_slice_in_dim(w_key, dp * share, share, 0)
    own_value = lax.dynamic_slice_in_dim(w_value, dp * share, share, 0)
    pairs = []
    for i in range(n_mp):
        head = i * KV_HEADS // n_mp
        columns = slice(head * dim, (head + 1) * dim)
        pairs.append(jnp.concatenate([own_key[:, columns], own_value[:, columns]], axis=1))
    both = jnp.stack(pairs)
    both = lax.all_to_all(both, "mp", split_axis=0, concat_axis=0, tiled=True)
    shares = jnp.stack([both] + [flip(both, "dp", n_dp, 2 * k) for k in range(1, chips)])
    shares = jnp.stack([shares, flip(shares, "dp", n_dp, 1)], axis=1)
    shares = shares.reshape(n_dp, n_mp, share, 2 * dim)
    shares = pick(shares, dp ^ jnp.arange(n_dp))
    w_kv = shares.transpose(1, 0, 2, 3).reshape(n_mp * width, 2 * dim)

    outgoing = pick(pool, jnp.maximum(send_table[0], 0))
    arrived = lax.all_to_all(outgoing, "dp", split_axis=0, concat_axis=0, tiled=True)
    rows = pick(arrived, slot_source).reshape(tokens, width)

    if n_mp <= 4:
        near = jnp.stack(line_gather(rows, "mp", n_mp))
        x = pick(near, (mp - jnp.arange(n_mp)) % n_mp)
    else:
        x = lax.all_gather(rows, "mp", axis=0)

    plane_rows = jnp.stack([rows] + [flip(rows, "dp", n_dp, 2 * k) for k in range(1, chips)])
    plane_rows = plane_rows.reshape(chips * tokens, width)

    chip_width = n_mp * width // chips
    if chip_width == width:
        parts = x
    else:
        parts = x.transpose(1, 0, 2).reshape(tokens, chips, chip_width).transpose(1, 0, 2)
    part = lambda k: lax.dynamic_index_in_dim(parts, chip ^ k, 0, keepdims=False)
    chip_rows = jnp.stack([part(0)] + [flip(part(k), "dp", n_dp, 2 * k) for k in range(1, chips)])
    chip_rows = chip_rows.reshape(chips * tokens, chip_width)

    factor = multiplicity.astype(F32) * slot_weight / length
    attended, d_query, d_kv = attend(
        x,
        w_query,
        w_kv,
        cotangent.reshape(tokens, query_cols),
        factor,
        query_gain,
        key_gain,
        length,
        key_cols // n_dp,
    )

    d_all = jnp.stack([d_query] + [flip(d_query, "dp", n_dp, 2 * k) for k in range(1, chips)])
    d_all = d_all.reshape(chips * tokens, query_cols)
    half = chip_width // 2

    def query_half(which):
        mine = lax.dynamic_slice_in_dim(chip_rows, which * half, half, 1)
        return jnp.einsum("td,tc->dc", mine, d_all, preferred_element_type=F32)

    other = flip(query_half(1 - core).astype(BF16), "dp", n_dp, 1)
    grad_query = query_half(core) + other.astype(F32)

    spread = jnp.broadcast_to(d_kv[None], (n_mp,) + d_kv.shape)
    spread = lax.all_to_all(spread, "mp", split_axis=0, concat_axis=0, tiled=True)
    if n_mp > KV_HEADS:
        spread = spread.reshape(KV_HEADS, n_mp // KV_HEADS, tokens, 2 * dim)
        spread = jnp.sum(spread.astype(F32), axis=1).astype(BF16)
    chip_cols = 2 * key_cols // chips
    if chip_cols != 2 * dim:
        spread = spread.reshape(KV_HEADS, tokens, chips // KV_HEADS, chip_cols)
        spread = spread.transpose(0, 2, 1, 3).reshape(chips, tokens, chip_cols)
    kv_part = lambda k: lax.dynamic_index_in_dim(spread, chip ^ k, 0, keepdims=False)
    kv_all = jnp.stack([kv_part(0)] + [flip(kv_part(k), "dp", n_dp, 2 * k) for k in range(1, chips)])
    kv_all = kv_all.reshape(chips * tokens, chip_cols)
    partial = jnp.einsum("td,tc->dc", plane_rows, kv_all, preferred_element_type=F32)
    mine, theirs = partial[:, : chip_cols // 2], partial[:, chip_cols // 2 :]
    mine, theirs = jnp.where(core == 0, mine, theirs), jnp.where(core == 0, theirs, mine)
    grad_kv = mine + flip(theirs.astype(BF16), "dp", n_dp, 1).astype(F32)
    device_cols = chip_cols // 4

    return (
        attended.reshape(slots, length, query_cols),
        grad_query,
        grad_kv[:, :device_cols],
        grad_kv[:, device_cols:],
    )


def solution(mesh):
    return jax.shard_map(
        functools.partial(local, mesh.shape["dp"], mesh.shape["mp"]),
        mesh=mesh,
        in_specs=(
            P("dp", None, "mp"),
            P("dp", None),
            P("dp"),
            P("dp"),
            P("dp"),
            P("dp", None, "mp"),
            P(None, "mp"),
            P("mp", None),
            P("mp", None),
            P(),
            P(),
        ),
        out_specs=(P("dp", None, "mp"), P("dp", "mp"), P("mp", "dp"), P("mp", "dp")),
        check_vma=False,
    )
```

time: 362 us -> 217 us (0.60)
  waiting for transfers between devices: 259 us -> 81.2 us
  starting transfers between devices: 4.9 us -> 66.5 us
  blocking collectives: 31.4 us -> 0 us
  local copies, waits for them, and re-layouts: 9.21 us -> 25.1 us
  between operations: 14.6 us -> 1.32 us
    reduce_scatter x3 -> x0, waiting for transfers between devices: 146 us -> none  [the longest x1 83.4 us: local(): lax.psum_scatter(query_whole.astype(jnp.bfloat16), 'dp', scatter_dimensio...]
    ppermute x0 -> x24, waiting for transfers between devices: none -> 72.6 us  [the longest x18 50.1 us: flip(): return lax.ppermute(block, axis, [(i, i ^ bits) for i in range(count)])]
    all_gather x1 -> x0, waiting for transfers between devices: 56.6 us -> none  [local(): piece = lax.all_gather(local_rows, 'mp', axis=1, tiled=True)]
    ppermute x0 -> x24, starting transfers between devices: none -> 52.4 us  [the longest x18 41.5 us: flip(): return lax.ppermute(block, axis, [(i, i ^ bits) for i in range(count)])]
    psum x2 -> x0, waiting for transfers between devices: 47.4 us -> none  [the longest x1 36.4 us: local(): lax.psum(key_place.astype(jnp.bfloat16), 'mp').astype(jnp.float32)]
    psum x1 -> x0, blocking collectives: 31.4 us -> none  [local(): key_all, value_all = lax.psum((key_part, value_part), 'mp')]
    another operation x1 -> x16, other arithmetic: 0.36 us -> 10.9 us  [the longest x4 5.33 us: local(): near = jnp.stack(line_gather(rows, 'mp', n_mp))]
    all_to_all x0 -> x2, starting transfers between devices: none -> 9.61 us  [the longest x1 5.02 us: local(): lax.all_to_all(spread, 'mp', split_axis=0, concat_axis=0, tiled=True)]
  transfers between devices with their start and end apart: 7 -> 27, of which waited for: 7 -> 11; matrix products, arithmetic and copies ran while one was open for 5% -> 25% of each run, Pallas kernels for 0% -> 0%
where the time goes in v1:
time: 217 us; the launch traced here: 214 us
  waiting for transfers between devices  81.2 us (37%)
  starting transfers between devices  66.5 us (31%)
  matrix products  25.3 us (12%)
  local copies, waits for them, and re-layouts  25.1 us (12%)
  other arithmetic  15.1 us (7%)
    ppermute x18, waiting for transfers between devices, flip(): return lax.ppermute(block, axis, [(i, i ^ bits) for i in range(count)])  50.1 us
    ppermute x18, starting transfers between devices, flip(): return lax.ppermute(block, axis, [(i, i ^ bits) for i in range(count)])  41.5 us
    ppermute x3, waiting for transfers between devices, line_gather(): lax.ppermute(down[-1], axis, [(i, i - 1) for i in range(count - hop, 0, -...  22.5 us
    gather x4, local copies, waits for them, and re-layouts, pick(): return array.at[index].get(mode='promise_in_bounds')  7.53 us
    dot_general x2, matrix products, query_half(): return jnp.einsum('td,tc->dc', mine, d_all, preferred_element_type=F32)  7.07 us
    ppermute x3, starting transfers between devices, line_gather(): lax.ppermute(up[-1], axis, [(i, i + 1) for i in range(hop - 1, count - 1)])  7.06 us
    all_to_all x1, waiting for transfers between devices, local(): lax.all_to_all(outgoing, 'dp', split_axis=0, concat_axis=0, tiled=True)  6.7 us
    dot_general x1, matrix products, attend(): query = jnp.dot(x, w_query, preferred_element_type=F32)  5.61 us
  transfers between devices with their start and end apart: 27, of which 11 were waited for; matrix products, arithmetic and copies ran while one was open for 25% of the time, Pallas kernels for 0%

profile of v1, /device:TPU:7, one launch (start us, length us, event | category | flops | bytes accessed | tf_op | source)
XLA Modules:
  0.0 214.5 jit_solution(270159946894625533)
XLA Ops:
  3.2 4.5 %all-to-all-start = ((bf16[8,32,1280]{2,1,0:T(8,128)(2,1)}), bf16[8,32,1280]{2,1,0:T(8,128)(2,1)S(1)}, u32[]{:S(2)}, u32[]{:S(2)}) async-start(bf16[8,32,1280]{2,1,0:T(8,128)(2,1)} %gather_fusion), calls=%async_computation | async-start | bytes 1310720 | tf_op jit(solution)/shard_map/all_to_all | solution.py:155
  9.5 6.7 %all-to-all-done = bf16[8,32,1280]{2,1,0:T(8,128)(2,1)S(1)} async-done(((bf16[8,32,1280]{2,1,0:T(8,128)(2,1)}), bf16[8,32,1280]{2,1,0:T(8,128)(2,1)S(1)}, u32[]{:S(2)}, u32[]{:S(2)}) %all-to-all-start) | async-done | bytes 655392 | tf_op jit(solution)/shard_map/all_to_all | solution.py:155
  16.2 4.6 %all-to-all-start.1 = ((bf16[4,160,256]{2,1,0:T(8,128)(2,1)}), bf16[4,160,256]{2,1,0:T(8,128)(2,1)S(1)}, u32[]{:S(2)}, u32[]{:S(2)}) async-start(bf16[4,160,256]{2,1,0:T(8,128)(2,1)} %pad_maximum_fusion.6), calls=%async_computation.1 | async-start | bytes 655360 | tf_op jit(solution)/shard_map/all_to_all | solution.py:147
  23.6 4.0 %collective-permute-start = (bf16[256,1280]{1,0:T(8,128)(2,1)}, bf16[256,1280]{1,0:T(8,128)(2,1)S(1)}, u32[]{:S(2)}, u32[]{:S(2)}) collective-permute-start(bf16[256,1280]{1,0:T(8,128)(2,1)} %bitcast.2), channel_id=1, source_target_pairs={{0,1},{1,2},{2,3},{4,5},{5,6},{6,7},{8,9},{9,10},{10,11},{12,13},{... | collective-permute-start | bytes 1966088 | tf_op jit(solution)/shard_map/ppermute | solution.py:96
  32.1 3.6 %collective-permute-done.6 = bf16[4,160,256]{2,1,0:T(8,128)(2,1)S(1)} collective-permute-done((bf16[4,160,256]{2,1,0:T(8,128)(2,1)S(1)}, bf16[4,160,256]{2,1,0:T(8,128)(2,1)S(1)}, u32[]{:S(2)}, u32[]{:S(2)}) %collective-permute-start.6) | collective-permute-done | bytes 327712 | tf_op jit(solution)/shard_map/ppermute | solution.py:108
  35.7 7.2 %collective-permute-done.8 = bf16[4,160,256]{2,1,0:T(8,128)(2,1)S(1)} collective-permute-done((bf16[4,160,256]{2,1,0:T(8,128)(2,1)S(1)}, bf16[4,160,256]{2,1,0:T(8,128)(2,1)S(1)}, u32[]{:S(2)}, u32[]{:S(2)}) %collective-permute-start.8) | collective-permute-done | bytes 327712 | tf_op jit(solution)/shard_map/ppermute | solution.py:108
  43.1 4.9 %collective-permute-start.9 = (bf16[4,4,160,256]{3,2,1,0:T(8,128)(2,1)S(1)}, bf16[4,4,160,256]{3,2,1,0:T(8,128)(2,1)S(1)}, u32[]{:S(2)}, u32[]{:S(2)}) collective-permute-start(bf16[4,4,160,256]{3,2,1,0:T(8,128)(2,1)S(1)} %get-tuple-element.9), channel_id=1, source_target_pairs={{0,4},{4,0},{8,12},{12,8},{16,20},{20,16},{24,28},{28,24},{1,5},{5... | collective-permute-start | bytes 3932168 | tf_op jit(solution)/shard_map/ppermute | solution.py:108
  51.4 14.9 %collective-permute-done.2 = bf16[256,1280]{1,0:T(8,128)(2,1)} collective-permute-done((bf16[256,1280]{1,0:T(8,128)(2,1)S(1)}, bf16[256,1280]{1,0:T(8,128)(2,1)}, u32[]{:S(2)}, u32[]{:S(2)}) %collective-permute-start.2) | collective-permute-done | bytes 655392 | tf_op jit(solution)/shard_map/ppermute | solution.py:98
  72.8 3.5 %copy.71 = bf16[4,8,160,256]{3,2,1,0:T(8,128)(2,1)} copy(bf16[4,8,160,256]{3,2,0,1:T(8,128)(2,1)} %bitcast.196) | data formatting | bytes 5242880 | tf_op jit(solution)/shard_map/transpose | solution.py:152
  76.4 7.6 %collective-permute-done.3 = bf16[256,1280]{1,0:T(8,128)(2,1)} collective-permute-done((bf16[256,1280]{1,0:T(8,128)(2,1)}, bf16[256,1280]{1,0:T(8,128)(2,1)}, u32[]{:S(2)}, u32[]{:S(2)}) %collective-permute-start.3) | collective-permute-done | bytes 655392 | tf_op jit(solution)/shard_map/ppermute | solution.py:98
  85.3 2.9 %fusion.1 = bf16[4,256,1280]{2,1,0:T(8,128)(2,1)} fusion(bf16[1,256,1280]{2,1,0:T(8,128)(2,1)} %bitcast.1, bf16[1,256,1280]{2,1,0:T(8,128)(2,1)S(1)} %select_bitcast_fusion, bf16[1,256,1280]{2,1,0:T(8,128)(2,1)S(1)} %select_bitcast_fusion.1, bf16[1,256,1280]{2,1,0:T(8,128)(2,1)S(1)} %select_bitcast_fusion.2), kind=kLoop, calls=%fused_computation.8 | loop fusion | flops 3932160 | bytes 5242880 | tf_op jit(solution)/shard_map/stack | solution.py:159
  90.7 3.0 %copy.69 = bf16[256,4,1280]{0,2,1:T(8,128)(2,1)} copy(bf16[256,4,1280]{2,0,1:T(8,128)(2,1)S(1)} %bitcast.192) | data formatting | bytes 5242880 | tf_op jit(solution)/shard_map/transpose | solution.py:73
  93.6 3.6 %fusion.54 = f32[256,256]{1,0:T(8,128)S(1)} fusion(bf16[256,5120]{0,1:T(8,128)(2,1)} %bitcast.193, bf16[5120,256]{1,0:T(8,128)(2,1)} %bitcast.202), kind=kOutput, calls=%fused_computation.120 | convolution fusion | flops 671088640 | bytes 5505024 | tf_op jit(solution)/shard_map/dot_general | solution.py:75
  97.4 5.6 %convolution_bitcast_fusion.3 = f32[32,8,8,128]{3,1,2,0:T(8,128)S(1)} fusion(bf16[256,5120]{0,1:T(8,128)(2,1)S(1)} %bitcast.194, bf16[5120,1024]{1,0:T(8,128)(2,1)} %param.17), kind=kOutput, calls=%fused_computation.21 | convolution fusion | flops 2684354560 | bytes 14155776 | tf_op jit(solution)/shard_map/dot_general | solution.py:74
  118.0 5.0 %all-to-all-start.2 = ((bf16[4,256,256]{1,2,0:T(8,128)(2,1)}), bf16[4,256,256]{1,2,0:T(8,128)(2,1)}, u32[]{:S(2)}, u32[]{:S(2)}) async-start(bf16[4,256,256]{1,2,0:T(8,128)(2,1)} %broadcast_in_dim.15), calls=%async_computation.2 | async-start | bytes 1048576 | tf_op jit(solution)/shard_map/all_to_all | solution.py:201
  127.9 6.7 %collective-permute-done.15 = bf16[256,1024]{1,0:T(8,128)(2,1)} collective-permute-done((bf16[256,1024]{1,0:T(8,128)(2,1)}, bf16[256,1024]{1,0:T(8,128)(2,1)}, u32[]{:S(2)}, u32[]{:S(2)}) %collective-permute-start.15) | collective-permute-done | bytes 524320 | tf_op jit(solution)/shard_map/ppermute | solution.py:108
  136.0 3.0 %pad_maximum_fusion.4 = bf16[4,256,1024]{2,1,0:T(8,128)(2,1)} fusion(bf16[1,256,1024]{2,1,0:T(8,128)(2,1)} %bitcast.53, bf16[1,256,1024]{2,1,0:T(8,128)(2,1)} %bitcast.52, bf16[1,256,1024]{2,1,0:T(8,128)(2,1)} %bitcast.51, bf16[1,256,1024]{2,1,0:T(8,128)(2,1)S(1)} %convert_element_type.111), kind=kLoop, calls=%fused_computation.17 | loop fusion | flops 3145728 | bytes 4194304 | tf_op jit(solution)/shard_map/stack | solution.py:189
  140.2 8.4 %collective-permute-done.10 = bf16[256,1280]{1,0:T(8,128)(2,1)S(1)} collective-permute-done((bf16[256,1280]{1,0:T(8,128)(2,1)}, bf16[256,1280]{1,0:T(8,128)(2,1)S(1)}, u32[]{:S(2)}, u32[]{:S(2)}) %collective-permute-start.10) | collective-permute-done | bytes 655392 | tf_op jit(solution)/shard_map/ppermute | solution.py:108
  149.0 4.0 %collective-permute-done.11 = bf16[256,1280]{1,0:T(8,128)(2,1)S(1)} collective-permute-done((bf16[256,1280]{1,0:T(8,128)(2,1)}, bf16[256,1280]{1,0:T(8,128)(2,1)S(1)}, u32[]{:S(2)}, u32[]{:S(2)}) %collective-permute-start.11) | collective-permute-done | bytes 655392 | tf_op jit(solution)/shard_map/ppermute | solution.py:108
  153.1 25.1 %collective-permute-start.21 = (bf16[256,256]{0,1:T(8,128)(2,1)S(1)}, bf16[256,256]{0,1:T(8,128)(2,1)S(1)}, u32[]{:S(2)}, u32[]{:S(2)}) collective-permute-start(bf16[256,256]{0,1:T(8,128)(2,1)S(1)} %get-tuple-element.22), channel_id=1, source_target_pairs={{0,16},{4,20},{8,24},{12,28},{16,0},{20,4},{24,8},{28,12},{1,17},{... | collective-permute-start | bytes 393224 | tf_op jit(solution)/shard_map/ppermute | solution.py:108
  178.5 17.4 %collective-permute-done.18 = bf16[256,1280]{1,0:T(8,128)(2,1)} collective-permute-done((bf16[256,1280]{1,0:T(8,128)(2,1)}, bf16[256,1280]{1,0:T(8,128)(2,1)}, u32[]{:S(2)}, u32[]{:S(2)}) %collective-permute-start.18) | collective-permute-done | bytes 655392 | tf_op jit(solution)/shard_map/ppermute | solution.py:108
  195.9 2.7 %collective-permute-done.21 = bf16[256,256]{0,1:T(8,128)(2,1)S(1)} collective-permute-done((bf16[256,256]{0,1:T(8,128)(2,1)S(1)}, bf16[256,256]{0,1:T(8,128)(2,1)S(1)}, u32[]{:S(2)}, u32[]{:S(2)}) %collective-permute-start.21) | collective-permute-done | bytes 131104 | tf_op jit(solution)/shard_map/ppermute | solution.py:108
  198.6 2.7 %convolution_bitcast_fusion = f32[1280,256]{0,1:T(8,128)S(1)} fusion(bf16[1,256,1280]{2,1,0:T(8,128)(2,1)} %bitcast.1, bf16[1,256,1280]{2,1,0:T(8,128)(2,1)} %bitcast.57, bf16[1,256,1280]{2,1,0:T(8,128)(2,1)} %bitcast.56, bf16[1,256,1280]{2,1,0:T(8,128)(2,1)} %bitcast.55, bf16[1,256,256]{1,2,0:T(8,128)(2,1)S(1)} %bitcast.219, ...), kind=kOutput, calls=%fused_computation.6 | convolution fusion | flops 675807232 | bytes 4456448 | tf_op jit(solution)/shard_map/td,tc->dc/dot_general | solution.py:212
  210.1 4.4 %convert_add_fusion = f32[640,1024]{1,0:T(8,128)} fusion(bf16[640,1024]{1,0:T(8,128)(2,1)} %collective-permute-done.16, bf16[1024,1024]{1,0:T(8,128)(2,1)S(1)} %bitcast.198, bf16[1024,1280]{1,0:T(8,128)(2,1)S(1)} %bitcast.200, s32[]{:T(128)S(6)} %select_n.130), kind=kOutput, calls=%fused_computation.16 | convolution fusion | flops 1343488000 | bytes 7340036 | tf_op jit(solution)/shard_map/td,tc->dc/dot_general | solution.py:195
  (161 shorter events, 57.1 us)
Async XLA Ops:
  3.2 13.0 %all-to-all-start = ((bf16[8,32,1280]{2,1,0:T(8,128)(2,1)}), bf16[8,32,1280]{2,1,0:T(8,128)(2,1)S(1)}, u32[]{:S(2)}, u32[]{:S(2)}) async-start(bf16[8,32,1280]{2,1,0:T(8,128)(2,1)} %gather_fusion), calls=%async_computation | async-start | bytes 1310720 | tf_op jit(solution)/shard_map/all_to_all | solution.py:155
  16.2 13.3 %all-to-all-start.1 = ((bf16[4,160,256]{2,1,0:T(8,128)(2,1)}), bf16[4,160,256]{2,1,0:T(8,128)(2,1)S(1)}, u32[]{:S(2)}, u32[]{:S(2)}) async-start(bf16[4,160,256]{2,1,0:T(8,128)(2,1)} %pad_maximum_fusion.6), calls=%async_computation.1 | async-start | bytes 655360 | tf_op jit(solution)/shard_map/all_to_all | solution.py:147
  22.3 25.7 %collective-permute-start.1 = (bf16[256,1280]{1,0:T(8,128)(2,1)}, bf16[256,1280]{1,0:T(8,128)(2,1)S(1)}, u32[]{:S(2)}, u32[]{:S(2)}) collective-permute-start(bf16[256,1280]{1,0:T(8,128)(2,1)} %bitcast.2), channel_id=1, source_target_pairs={{3,2},{2,1},{1,0},{7,6},{6,5},{5,4},{11,10},{10,9},{9,8},{15,14},{... | collective-permute-start | bytes 1966088 | tf_op jit(solution)/shard_map/ppermute | solution.py:98
  23.6 25.8 %collective-permute-start = (bf16[256,1280]{1,0:T(8,128)(2,1)}, bf16[256,1280]{1,0:T(8,128)(2,1)S(1)}, u32[]{:S(2)}, u32[]{:S(2)}) collective-permute-start(bf16[256,1280]{1,0:T(8,128)(2,1)} %bitcast.2), channel_id=1, source_target_pairs={{0,1},{1,2},{2,3},{4,5},{5,6},{6,7},{8,9},{9,10},{10,11},{12,13},{... | collective-permute-start | bytes 1966088 | tf_op jit(solution)/shard_map/ppermute | solution.py:96
  29.4 6.2 %collective-permute-start.7 = (bf16[4,160,256]{2,1,0:T(8,128)(2,1)S(1)}, bf16[4,160,256]{2,1,0:T(8,128)(2,1)S(1)}, u32[]{:S(2)}, u32[]{:S(2)}) collective-permute-start(bf16[4,160,256]{2,1,0:T(8,128)(2,1)S(1)} %all-to-all-done.1), channel_id=1, source_target_pairs={{0,16},{4,20},{8,24},{12,28},{16,0},{20,4},{24,8},{28,12},{1,17},{... | collective-permute-start | bytes 983048 | tf_op jit(solution)/shard_map/ppermute | solution.py:108
  30.9 12.0 %collective-permute-start.8 = (bf16[4,160,256]{2,1,0:T(8,128)(2,1)S(1)}, bf16[4,160,256]{2,1,0:T(8,128)(2,1)S(1)}, u32[]{:S(2)}, u32[]{:S(2)}) collective-permute-start(bf16[4,160,256]{2,1,0:T(8,128)(2,1)S(1)} %all-to-all-done.1), channel_id=1, source_target_pairs={{0,24},{4,28},{8,16},{12,20},{16,8},{20,12},{24,0},{28,4},{1,25},{... | collective-permute-start | bytes 983048 | tf_op jit(solution)/shard_map/ppermute | solution.py:108
  43.1 27.2 %collective-permute-start.9 = (bf16[4,4,160,256]{3,2,1,0:T(8,128)(2,1)S(1)}, bf16[4,4,160,256]{3,2,1,0:T(8,128)(2,1)S(1)}, u32[]{:S(2)}, u32[]{:S(2)}) collective-permute-start(bf16[4,4,160,256]{3,2,1,0:T(8,128)(2,1)S(1)} %get-tuple-element.9), channel_id=1, source_target_pairs={{0,4},{4,0},{8,12},{12,8},{16,20},{20,16},{24,28},{28,24},{1,5},{5... | collective-permute-start | bytes 3932168 | tf_op jit(solution)/shard_map/ppermute | solution.py:108
  48.0 18.3 %collective-permute-start.2 = (bf16[256,1280]{1,0:T(8,128)(2,1)S(1)}, bf16[256,1280]{1,0:T(8,128)(2,1)}, u32[]{:S(2)}, u32[]{:S(2)}) collective-permute-start(bf16[256,1280]{1,0:T(8,128)(2,1)S(1)} %collective-permute-done.1), channel_id=1, source_target_pairs={{2,1},{1,0},{6,5},{5,4},{10,9},{9,8},{14,13},{13,12},{18,17},{17,1... | collective-permute-start | bytes 1966088 | tf_op jit(solution)/shard_map/ppermute | solution.py:98
  49.3 18.3 %collective-permute-start.4 = (bf16[256,1280]{1,0:T(8,128)(2,1)S(1)}, bf16[256,1280]{1,0:T(8,128)(2,1)}, u32[]{:S(2)}, u32[]{:S(2)}) collective-permute-start(bf16[256,1280]{1,0:T(8,128)(2,1)S(1)} %collective-permute-done), channel_id=1, source_target_pairs={{1,2},{2,3},{5,6},{6,7},{9,10},{10,11},{13,14},{14,15},{17,18},{18... | collective-permute-start | bytes 1966088 | tf_op jit(solution)/shard_map/ppermute | solution.py:96
  50.9 73.8 %collective-permute-start.17 = (bf16[256,1280]{1,0:T(8,128)(2,1)}, bf16[256,1280]{1,0:T(8,128)(2,1)}, u32[]{:S(2)}, u32[]{:S(2)}) collective-permute-start(bf16[256,1280]{1,0:T(8,128)(2,1)} %bitcast.2), channel_id=1, source_target_pairs={{0,8},{4,12},{8,0},{12,4},{16,24},{20,28},{24,16},{28,20},{1,9},{5... | collective-permute-start | bytes 1966088 | tf_op jit(solution)/shard_map/ppermute | solution.py:108
  66.3 17.6 %collective-permute-start.3 = (bf16[256,1280]{1,0:T(8,128)(2,1)}, bf16[256,1280]{1,0:T(8,128)(2,1)}, u32[]{:S(2)}, u32[]{:S(2)}) collective-permute-start(bf16[256,1280]{1,0:T(8,128)(2,1)} %collective-permute-done.2), channel_id=1, source_target_pairs={{1,0},{5,4},{9,8},{13,12},{17,16},{21,20},{25,24},{29,28}} | collective-permute-start | bytes 1966088 | tf_op jit(solution)/shard_map/ppermute | solution.py:98
  67.7 17.5 %collective-permute-start.5 = (bf16[256,1280]{1,0:T(8,128)(2,1)}, bf16[256,1280]{1,0:T(8,128)(2,1)}, u32[]{:S(2)}, u32[]{:S(2)}) collective-permute-start(bf16[256,1280]{1,0:T(8,128)(2,1)} %collective-permute-done.4), channel_id=1, source_target_pairs={{2,3},{6,7},{10,11},{14,15},{18,19},{22,23},{26,27},{30,31}} | collective-permute-start | bytes 1966088 | tf_op jit(solution)/shard_map/ppermute | solution.py:96
  111.3 14.9 %collective-permute-start.13 = (bf16[256,1024]{1,0:T(8,128)(2,1)}, bf16[256,1024]{1,0:T(8,128)(2,1)}, u32[]{:S(2)}, u32[]{:S(2)}) collective-permute-start(bf16[256,1024]{1,0:T(8,128)(2,1)} %bitcast.186), channel_id=1, source_target_pairs={{0,8},{4,12},{8,0},{12,4},{16,24},{20,28},{24,16},{28,20},{1,9},{5... | collective-permute-start | bytes 1572872 | tf_op jit(solution)/shard_map/ppermute | solution.py:108
  111.8 15.7 %collective-permute-start.14 = (bf16[256,1024]{1,0:T(8,128)(2,1)}, bf16[256,1024]{1,0:T(8,128)(2,1)}, u32[]{:S(2)}, u32[]{:S(2)}) collective-permute-start(bf16[256,1024]{1,0:T(8,128)(2,1)} %bitcast.186), channel_id=1, source_target_pairs={{0,16},{4,20},{8,24},{12,28},{16,0},{20,4},{24,8},{28,12},{1,17},{... | collective-permute-start | bytes 1572872 | tf_op jit(solution)/shard_map/ppermute | solution.py:108
  113.1 21.6 %collective-permute-start.15 = (bf16[256,1024]{1,0:T(8,128)(2,1)}, bf16[256,1024]{1,0:T(8,128)(2,1)}, u32[]{:S(2)}, u32[]{:S(2)}) collective-permute-start(bf16[256,1024]{1,0:T(8,128)(2,1)} %bitcast.186), channel_id=1, source_target_pairs={{0,24},{4,28},{8,16},{12,20},{16,8},{20,12},{24,0},{28,4},{1,25},{... | collective-permute-start | bytes 1572872 | tf_op jit(solution)/shard_map/ppermute | solution.py:108
  118.0 21.0 %all-to-all-start.2 = ((bf16[4,256,256]{1,2,0:T(8,128)(2,1)}), bf16[4,256,256]{1,2,0:T(8,128)(2,1)}, u32[]{:S(2)}, u32[]{:S(2)}) async-start(bf16[4,256,256]{1,2,0:T(8,128)(2,1)} %broadcast_in_dim.15), calls=%async_computation.2 | async-start | bytes 1048576 | tf_op jit(solution)/shard_map/all_to_all | solution.py:201
  124.6 24.0 %collective-permute-start.10 = (bf16[256,1280]{1,0:T(8,128)(2,1)}, bf16[256,1280]{1,0:T(8,128)(2,1)S(1)}, u32[]{:S(2)}, u32[]{:S(2)}) collective-permute-start(bf16[256,1280]{1,0:T(8,128)(2,1)} %get-tuple-element.6), channel_id=1, source_target_pairs={{0,8},{4,12},{8,0},{12,4},{16,24},{20,28},{24,16},{28,20},{1,9},{5... | collective-permute-start | bytes 1966088 | tf_op jit(solution)/shard_map/ppermute | solution.py:108
  124.8 28.3 %collective-permute-start.11 = (bf16[256,1280]{1,0:T(8,128)(2,1)}, bf16[256,1280]{1,0:T(8,128)(2,1)S(1)}, u32[]{:S(2)}, u32[]{:S(2)}) collective-permute-start(bf16[256,1280]{1,0:T(8,128)(2,1)} %get-tuple-element.5), channel_id=1, source_target_pairs={{0,16},{4,20},{8,24},{12,28},{16,0},{20,4},{24,8},{28,12},{1,17},{... | collective-permute-start | bytes 1966088 | tf_op jit(solution)/shard_map/ppermute | solution.py:108
  126.2 51.9 %collective-permute-start.12 = (bf16[256,1280]{1,0:T(8,128)(2,1)}, bf16[256,1280]{1,0:T(8,128)(2,1)S(1)}, u32[]{:S(2)}, u32[]{:S(2)}) collective-permute-start(bf16[256,1280]{1,0:T(8,128)(2,1)} %get-tuple-element.7), channel_id=1, source_target_pairs={{0,24},{4,28},{8,16},{12,20},{16,8},{20,12},{24,0},{28,4},{1,25},{... | collective-permute-start | bytes 1966088 | tf_op jit(solution)/shard_map/ppermute | solution.py:108
  127.5 68.4 %collective-permute-start.18 = (bf16[256,1280]{1,0:T(8,128)(2,1)}, bf16[256,1280]{1,0:T(8,128)(2,1)}, u32[]{:S(2)}, u32[]{:S(2)}) collective-permute-start(bf16[256,1280]{1,0:T(8,128)(2,1)} %bitcast.2), channel_id=1, source_target_pairs={{0,16},{4,20},{8,24},{12,28},{16,0},{20,4},{24,8},{28,12},{1,17},{... | collective-permute-start | bytes 1966088 | tf_op jit(solution)/shard_map/ppermute | solution.py:108
  134.7 61.2 %collective-permute-start.19 = (bf16[256,1280]{1,0:T(8,128)(2,1)}, bf16[256,1280]{1,0:T(8,128)(2,1)}, u32[]{:S(2)}, u32[]{:S(2)}) collective-permute-start(bf16[256,1280]{1,0:T(8,128)(2,1)} %bitcast.2), channel_id=1, source_target_pairs={{0,24},{4,28},{8,16},{12,20},{16,8},{20,12},{24,0},{28,4},{1,25},{... | collective-permute-start | bytes 1966088 | tf_op jit(solution)/shard_map/ppermute | solution.py:108
  148.6 47.3 %collective-permute-start.20 = (bf16[256,256]{0,1:T(8,128)(2,1)S(1)}, bf16[256,256]{0,1:T(8,128)(2,1)S(1)}, u32[]{:S(2)}, u32[]{:S(2)}) collective-permute-start(bf16[256,256]{0,1:T(8,128)(2,1)S(1)} %get-tuple-element.23), channel_id=1, source_target_pairs={{0,8},{4,12},{8,0},{12,4},{16,24},{20,28},{24,16},{28,20},{1,9},{5... | collective-permute-start | bytes 393224 | tf_op jit(solution)/shard_map/ppermute | solution.py:108
  153.1 45.5 %collective-permute-start.21 = (bf16[256,256]{0,1:T(8,128)(2,1)S(1)}, bf16[256,256]{0,1:T(8,128)(2,1)S(1)}, u32[]{:S(2)}, u32[]{:S(2)}) collective-permute-start(bf16[256,256]{0,1:T(8,128)(2,1)S(1)} %get-tuple-element.22), channel_id=1, source_target_pairs={{0,16},{4,20},{8,24},{12,28},{16,0},{20,4},{24,8},{28,12},{1,17},{... | collective-permute-start | bytes 393224 | tf_op jit(solution)/shard_map/ppermute | solution.py:108
  178.2 20.4 %collective-permute-start.22 = (bf16[256,256]{0,1:T(8,128)(2,1)S(1)}, bf16[256,256]{0,1:T(8,128)(2,1)S(1)}, u32[]{:S(2)}, u32[]{:S(2)}) collective-permute-start(bf16[256,256]{0,1:T(8,128)(2,1)S(1)} %get-tuple-element.21), channel_id=1, source_target_pairs={{0,24},{4,28},{8,16},{12,20},{16,8},{20,12},{24,0},{28,4},{1,25},{... | collective-permute-start | bytes 393224 | tf_op jit(solution)/shard_map/ppermute | solution.py:108
  (33 other events, 316.4 us)

commit v2 on v1

--- a/solution.py
+++ b/solution.py
@@ -65,14 +65,11 @@
     return (d_query, d_key, d_value)
 
 
-def attend(x, w_query, w_kv, cot, factor, query_gain, key_gain, length, device_cols):
-    blocks, tokens, width = x.shape
+def attend(query, kv, cot, factor, query_gain, key_gain, length, device_cols):
+    tokens = query.shape[0]
     dim = query_gain.shape[0]
     slots = tokens // length
-    heads = w_query.shape[1] // dim
-    x = x.transpose(1, 0, 2).reshape(tokens, blocks * width)
-    query = jnp.dot(x, w_query, preferred_element_type=F32)
-    kv = jnp.dot(x, w_kv, preferred_element_type=F32)
+    heads = query.shape[1] // dim
     query = query.reshape(slots, length, 1, heads, dim)
     key = kv[:, :dim].reshape(slots, length, 1, dim)
     value = kv[:, dim:].reshape(slots, length, 1, dim)
@@ -89,23 +86,12 @@
     )
 
 
-def line_gather(block, axis, count):
-    me = lax.axis_index(axis)
-    up, down = [block], [block]
-    for hop in range(1, count):
-        up.append(lax.ppermute(up[-1], axis, [(i, i + 1) for i in range(hop - 1, count - 1)]))
-        down.append(
-            lax.ppermute(down[-1], axis, [(i, i - 1) for i in range(count - hop, 0, -1)])
-        )
-    return [block] + [jnp.where(me >= hop, up[hop], down[count - hop]) for hop in range(1, count)]
+def together(*values):
+    return lax.optimization_barrier(values)
 
 
 def pick(array, index):
     return array.at[index].get(mode="promise_in_bounds")
-
-
-def flip(block, axis, count, bits):
-    return lax.ppermute(block, axis, [(i, i ^ bits) for i in range(count)])
 
 
 def local(
@@ -135,49 +121,129 @@
     mp = lax.axis_index("mp")
     chip, core = dp // 2, dp % 2
 
+    def flip(block, bits):
+        return lax.ppermute(block, "dp", [(i, i ^ bits) for i in range(n_dp)])
+
+    def other_chips(blocks):
+        return [flip(blocks[k], 2 * k) for k in range(1, chips)]
+
+    def around(blocks):
+        return [blocks[0]] + [
+            lax.ppermute(blocks[k], "mp", [(i, (i + k) % n_mp) for i in range(n_mp)])
+            for k in range(1, n_mp)
+        ]
+
+    def up(block, hop):
+        return lax.ppermute(block, "mp", [(i, i + 1) for i in range(hop - 1, n_mp - 1)])
+
+    def down(block, hop):
+        return lax.ppermute(block, "mp", [(i, i - 1) for i in range(n_mp - hop, 0, -1)])
+
+    outgoing = pick(pool, jnp.maximum(send_table[0], 0))
+    outgoing, w_key, w_value = together(outgoing, w_key, w_value)
+    arrived = lax.all_to_all(outgoing, "dp", split_axis=0, concat_axis=0, tiled=True)
+
     share = width // n_dp
     own_key = lax.dynamic_slice_in_dim(w_key, dp * share, share, 0)
     own_value = lax.dynamic_slice_in_dim(w_value, dp * share, share, 0)
     pairs = []
-    for i in range(n_mp):
-        head = i * KV_HEADS // n_mp
+    for head in range(KV_HEADS):
         columns = slice(head * dim, (head + 1) * dim)
         pairs.append(jnp.concatenate([own_key[:, columns], own_value[:, columns]], axis=1))
-    both = jnp.stack(pairs)
-    both = lax.all_to_all(both, "mp", split_axis=0, concat_axis=0, tiled=True)
-    shares = jnp.stack([both] + [flip(both, "dp", n_dp, 2 * k) for k in range(1, chips)])
-    shares = jnp.stack([shares, flip(shares, "dp", n_dp, 1)], axis=1)
-    shares = shares.reshape(n_dp, n_mp, share, 2 * dim)
+    pairs = jnp.stack(pairs)
+    heads = [(mp + k) % n_mp * KV_HEADS // n_mp for k in range(n_mp)]
+    shares = around([lax.dynamic_index_in_dim(pairs, h, 0, False) for h in heads])
+    arrived, *shares = together(arrived, *shares)
+    shares = jnp.stack(shares)
+    rows = pick(arrived, slot_source).reshape(tokens, width)
+
+    ups, downs = [rows], [rows]
+    steps = n_mp - 1 if n_mp <= 4 else 1
+    near = rows
+    for hop in range(1, steps + 1):
+        if n_mp <= 4:
+            ups.append(up(ups[-1], hop))
+            downs.append(down(downs[-1], hop))
+        else:
+            ups.append(near)
+            downs.append(lax.all_gather(near, "mp", axis=0))
+        if hop == 1:
+            shares = [shares] + other_chips([shares] * chips)
+            near, ups[-1], downs[-1], *shares = together(near, ups[-1], downs[-1], *shares)
+            shares = jnp.stack(shares)
+        elif hop == 2:
+            straight = [flip(near, 2 << b) for b in range(chips.bit_length() - 1)]
+            other_shares = flip(shares, 1)
+            near, ups[-1], downs[-1], other_shares, *straight = together(
+                near, ups[-1], downs[-1], other_shares, *straight
+            )
+    if steps < 2:
+        straight = [flip(near, 2 << b) for b in range(chips.bit_length() - 1)]
+        other_shares = flip(shares, 1)
+    straight = {1 << b: block for b, block in enumerate(straight)}
+    plane_rows = [rows] + [
+        straight[k] if k in straight else flip(near, 2 * k) for k in range(1, chips)
+    ]
+    if n_mp <= 4:
+        ups[-1], downs[-1], *plane_rows = together(ups[-1], downs[-1], *plane_rows)
+    plane_rows = jnp.stack(plane_rows).reshape(chips * tokens, width)
+
+    shares = jnp.stack([shares, other_shares], axis=1).reshape(n_dp, n_mp, share, 2 * dim)
     shares = pick(shares, dp ^ jnp.arange(n_dp))
-    w_kv = shares.transpose(1, 0, 2, 3).reshape(n_mp * width, 2 * dim)
-
-    outgoing = pick(pool, jnp.maximum(send_table[0], 0))
-    arrived = lax.all_to_all(outgoing, "dp", split_axis=0, concat_axis=0, tiled=True)
-    rows = pick(arrived, slot_source).reshape(tokens, width)
+    w_kv = shares.transpose(1, 0, 2, 3)
+    w_kv = w_kv.reshape(n_mp, width, 2 * dim)
+
+    def project(block, index):
+        index = jnp.clip(index, 0, n_mp - 1)
+        rows_of = lax.dynamic_slice_in_dim(w_query, index * width, width, 0)
+        kv_rows = lax.dynamic_index_in_dim(w_kv, (mp - index) % n_mp, 0, False)
+        return (
+            jnp.dot(block, rows_of, preferred_element_type=F32),
+            jnp.dot(block, kv_rows, preferred_element_type=F32),
+        )
 
     if n_mp <= 4:
-        near = jnp.stack(line_gather(rows, "mp", n_mp))
-        x = pick(near, (mp - jnp.arange(n_mp)) % n_mp)
+        terms = [project(rows, mp)]
+        for hop in range(1, n_mp):
+            if 2 * hop < n_mp:
+                terms.append(project(ups[hop], mp - hop))
+                terms.append(project(downs[hop], mp + hop))
+            else:
+                block = jnp.where(mp >= hop, ups[hop], downs[hop])
+                terms.append(project(block, jnp.where(mp >= hop, mp - hop, mp + hop)))
+        query = sum(term[0] for term in terms)
+        kv = sum(term[1] for term in terms)
+        blocks = [rows] + [
+            jnp.where(mp >= hop, ups[hop], downs[n_mp - hop]) for hop in range(1, n_mp)
+        ]
+        blocks = jnp.stack(blocks)
+        part = lambda k: lax.dynamic_index_in_dim(blocks, (mp - (chip ^ k)) % n_mp, 0, False)
     else:
-        x = lax.all_gather(rows, "mp", axis=0)
-
-    plane_rows = jnp.stack([rows] + [flip(rows, "dp", n_dp, 2 * k) for k in range(1, chips)])
-    plane_rows = plane_rows.reshape(chips * tokens, width)
-
-    chip_width = n_mp * width // chips
-    if chip_width == width:
-        parts = x
-    else:
-        parts = x.transpose(1, 0, 2).reshape(tokens, chips, chip_width).transpose(1, 0, 2)
-    part = lambda k: lax.dynamic_index_in_dim(parts, chip ^ k, 0, keepdims=False)
-    chip_rows = jnp.stack([part(0)] + [flip(part(k), "dp", n_dp, 2 * k) for k in range(1, chips)])
-    chip_rows = chip_rows.reshape(chips * tokens, chip_width)
+        x = downs[-1].transpose(1, 0, 2).reshape(tokens, n_mp * width)
+        query = jnp.dot(x, w_query, preferred_element_type=F32)
+        kv = jnp.dot(
+            x,
+            pick(w_kv, (mp - jnp.arange(n_mp)) % n_mp).reshape(n_mp * width, 2 * dim),
+            preferred_element_type=F32,
+        )
+        chip_width = n_mp * width // chips
+        blocks = x.reshape(tokens, chips, chip_width).transpose(1, 0, 2)
+        part = lambda k: lax.dynamic_index_in_dim(blocks, chip ^ k, 0, False)
+
+    chip_rows = [part(k) for k in range(chips)]
+    chip_rows = [
+        flip(block, 2 * k) if k in straight else block for k, block in enumerate(chip_rows)
+    ]
+    query, kv, *chip_rows = together(query, kv, *chip_rows)
+    chip_rows = [
+        block if k in straight or k == 0 else flip(block, 2 * k)
+        for k, block in enumerate(chip_rows)
+    ]
 
     factor = multiplicity.astype(F32) * slot_weight / length
     attended, d_query, d_kv = attend(
-        x,
-        w_query,
-        w_kv,
+        query,
+        kv,
         cotangent.reshape(tokens, query_cols),
         factor,
         query_gain,
@@ -186,33 +252,42 @@
         key_cols // n_dp,
     )
 
-    d_all = jnp.stack([d_query] + [flip(d_query, "dp", n_dp, 2 * k) for k in range(1, chips)])
-    d_all = d_all.reshape(chips * tokens, query_cols)
-    half = chip_width // 2
+    d_query, d_kv, *chip_rows = together(d_query, d_kv, *chip_rows)
+
+    d_all = [flip(d_query, 2 * k) if k in straight else d_query for k in range(chips)]
+    spread = around([d_kv] * n_mp)
+    *d_all, spread = together(*d_all, jnp.stack(spread))
+    d_all = [
+        block if k in straight or k == 0 else flip(block, 2 * k) for k, block in enumerate(d_all)
+    ]
+    d_all = jnp.stack(d_all).reshape(chips * tokens, query_cols)
+    chip_rows = jnp.stack(chip_rows).reshape(chips * tokens, -1)
+    half = chip_rows.shape[1] // 2
 
     def query_half(which):
         mine = lax.dynamic_slice_in_dim(chip_rows, which * half, half, 1)
         return jnp.einsum("td,tc->dc", mine, d_all, preferred_element_type=F32)
 
-    other = flip(query_half(1 - core).astype(BF16), "dp", n_dp, 1)
+    other = flip(query_half(1 - core).astype(BF16), 1)
     grad_query = query_half(core) + other.astype(F32)
 
-    spread = jnp.broadcast_to(d_kv[None], (n_mp,) + d_kv.shape)
-    spread = lax.all_to_all(spread, "mp", split_axis=0, concat_axis=0, tiled=True)
     if n_mp > KV_HEADS:
+        spread = pick(spread, (mp - jnp.arange(n_mp)) % n_mp)
         spread = spread.reshape(KV_HEADS, n_mp // KV_HEADS, tokens, 2 * dim)
         spread = jnp.sum(spread.astype(F32), axis=1).astype(BF16)
+        spread_at = lambda index: index
+    else:
+        spread_at = lambda index: (mp - index) % n_mp
     chip_cols = 2 * key_cols // chips
     if chip_cols != 2 * dim:
         spread = spread.reshape(KV_HEADS, tokens, chips // KV_HEADS, chip_cols)
         spread = spread.transpose(0, 2, 1, 3).reshape(chips, tokens, chip_cols)
-    kv_part = lambda k: lax.dynamic_index_in_dim(spread, chip ^ k, 0, keepdims=False)
-    kv_all = jnp.stack([kv_part(0)] + [flip(kv_part(k), "dp", n_dp, 2 * k) for k in range(1, chips)])
-    kv_all = kv_all.reshape(chips * tokens, chip_cols)
+    kv_all = [lax.dynamic_index_in_dim(spread, spread_at(chip ^ k), 0, False) for k in range(chips)]
+    kv_all = jnp.stack([kv_all[0]] + other_chips(kv_all)).reshape(chips * tokens, chip_cols)
     partial = jnp.einsum("td,tc->dc", plane_rows, kv_all, preferred_element_type=F32)
     mine, theirs = partial[:, : chip_cols // 2], partial[:, chip_cols // 2 :]
     mine, theirs = jnp.where(core == 0, mine, theirs), jnp.where(core == 0, theirs, mine)
-    grad_kv = mine + flip(theirs.astype(BF16), "dp", n_dp, 1).astype(F32)
+    grad_kv = mine + flip(theirs.astype(BF16), 1).astype(F32)
     device_cols = chip_cols // 4
 
     return (

time: 217 us -> 183 us (0.84)
  waiting for transfers between devices: 81.2 us -> 61.3 us
  starting transfers between devices: 66.5 us -> 49.4 us
  matrix products: 25.3 us -> 35.6 us
  local copies, waits for them, and re-layouts: 25.1 us -> 15.3 us
  other arithmetic: 15.1 us -> 17.8 us
    ppermute x24 -> x30, waiting for transfers between devices: 72.6 us -> 61.3 us  [the longest x18 37 us: flip(): return lax.ppermute(block, 'dp', [(i, i ^ bits) for i in range(n_dp)])]
    dot_general x2 -> x10, matrix products: 9.16 us -> 19.7 us  [the longest x5 15.7 us: project(): jnp.dot(block, rows_of, preferred_element_type=F32)]
    all_to_all x2 -> x0, starting transfers between devices: 9.61 us -> none  [the longest x1 5.02 us: local(): lax.all_to_all(spread, 'mp', split_axis=0, concat_axis=0, tiled=True)]
    ppermute x24 -> x30, starting transfers between devices: 52.4 us -> 44.9 us  [the longest x18 27.1 us: flip(): return lax.ppermute(block, 'dp', [(i, i ^ bits) for i in range(n_dp)])]
    all_to_all x1, waiting for transfers between devices: 6.7 us -> 0.01 us  [local(): lax.all_to_all(outgoing, 'dp', split_axis=0, concat_axis=0, tiled=True)]
    transpose x2 -> x1, local copies, waits for them, and re-layouts: 6.52 us -> 1.93 us  [local(): w_kv = shares.transpose(1, 0, 2, 3)]
    dynamic_slice x2 -> x1, local copies, waits for them, and re-layouts: 2.69 us -> 0.04 us  [local(): lax.dynamic_index_in_dim(spread, spread_at(chip ^ k), 0, False)]
    gather x4 -> x3, local copies, waits for them, and re-layouts: 7.53 us -> 5.05 us  [pick(): return array.at[index].get(mode='promise_in_bounds')]
  transfers between devices with their start and end apart: 27 -> 31, of which waited for: 11 -> 15; matrix products, arithmetic and copies ran while one was open for 25% -> 24% of each run, Pallas kernels for 0% -> 0%
where the time goes in v2:
time: 183 us; the launch traced here: 181 us
  waiting for transfers between devices  61.3 us (33%)
  starting transfers between devices  49.4 us (27%)
  matrix products  35.6 us (19%)
  other arithmetic  17.8 us (10%)
  local copies, waits for them, and re-layouts  15.3 us (8%)
    ppermute x18, waiting for transfers between devices, flip(): return lax.ppermute(block, 'dp', [(i, i ^ bits) for i in range(n_dp)])  37 us
    ppermute x18, starting transfers between devices, flip(): return lax.ppermute(block, 'dp', [(i, i ^ bits) for i in range(n_dp)])  27.1 us
    dot_general x5, matrix products, project(): jnp.dot(block, rows_of, preferred_element_type=F32)  15.7 us
    ppermute x3, waiting for transfers between devices, down(): lax.ppermute(block, 'mp', [(i, i - 1) for i in range(n_mp - hop, 0, -1)])  12.3 us
    ppermute x6, waiting for transfers between devices, around(): lax.ppermute(blocks[k], 'mp', [(i, (i + k) % n_mp) for i in range(n_mp)])  12 us
    ppermute x3, starting transfers between devices, up(): lax.ppermute(block, 'mp', [(i, i + 1) for i in range(hop - 1, n_mp - 1)])  7.22 us
    dot_general x2, matrix products, query_half(): return jnp.einsum('td,tc->dc', mine, d_all, preferred_element_type=F32)  7.05 us
    ppermute x6, starting transfers between devices, around(): lax.ppermute(blocks[k], 'mp', [(i, (i + k) % n_mp) for i in range(n_mp)])  6.61 us
  transfers between devices with their start and end apart: 31, of which 15 were waited for; matrix products, arithmetic and copies ran while one was open for 24% of the time, Pallas kernels for 0%

profile of v2, /device:TPU:7, one launch (start us, length us, event | category | flops | bytes accessed | tf_op | source)
XLA Modules:
  0.0 180.8 jit_solution(17197454613363969928)
XLA Ops:
  3.2 4.5 %all-to-all-start = ((bf16[8,32,1280]{2,1,0:T(8,128)(2,1)}), bf16[8,32,1280]{2,1,0:T(8,128)(2,1)S(1)}, u32[]{:S(2)}, u32[]{:S(2)}) async-start(bf16[8,32,1280]{2,1,0:T(8,128)(2,1)} %gather_fusion), calls=%async_computation | async-start | bytes 1310720 | tf_op jit(solution)/shard_map/all_to_all | solution.py:144
  10.2 2.3 %collective-permute-start.1 = (bf16[160,256]{1,0:T(8,128)(2,1)S(1)}, bf16[160,256]{1,0:T(8,128)(2,1)S(1)}, u32[]{:S(2)}, u32[]{:S(2)}) collective-permute-start(bf16[160,256]{1,0:T(8,128)(2,1)S(1)} %get-tuple-element.113), channel_id=1, source_target_pairs={{0,2},{1,3},{2,0},{3,1},{4,6},{5,7},{6,4},{7,5},{8,10},{9,11},{10,... | collective-permute-start | bytes 245768 | tf_op jit(solution)/shard_map/ppermute | solution.py:132
  14.5 4.1 %collective-permute-done.1 = bf16[160,256]{1,0:T(8,128)(2,1)S(1)} collective-permute-done((bf16[160,256]{1,0:T(8,128)(2,1)S(1)}, bf16[160,256]{1,0:T(8,128)(2,1)S(1)}, u32[]{:S(2)}, u32[]{:S(2)}) %collective-permute-start.1) | collective-permute-done | bytes 81952 | tf_op jit(solution)/shard_map/ppermute | solution.py:132
  20.1 4.1 %collective-permute-start.3 = (bf16[256,1280]{1,0:T(8,128)(2,1)}, bf16[256,1280]{1,0:T(8,128)(2,1)S(1)}, u32[]{:S(2)}, u32[]{:S(2)}) collective-permute-start(bf16[256,1280]{1,0:T(8,128)(2,1)} %bitcast.9), channel_id=1, source_target_pairs={{0,1},{1,2},{2,3},{4,5},{5,6},{6,7},{8,9},{9,10},{10,11},{12,13},{... | collective-permute-start | bytes 1966088 | tf_op jit(solution)/shard_map/ppermute | solution.py:137
  26.0 2.3 %collective-permute-start.7 = (bf16[4,160,256]{2,1,0:T(8,128)(2,1)S(1)}, bf16[4,160,256]{2,1,0:T(8,128)(2,1)S(1)}, u32[]{:S(2)}, u32[]{:S(2)}) collective-permute-start(bf16[4,160,256]{2,1,0:T(8,128)(2,1)S(1)} %pad_maximum_fusion.7), channel_id=1, source_target_pairs={{0,24},{4,28},{8,16},{12,20},{16,8},{20,12},{24,0},{28,4},{1,25},{... | collective-permute-start | bytes 983048 | tf_op jit(solution)/shard_map/ppermute | solution.py:125
  28.3 5.8 %collective-permute-done.5 = bf16[4,160,256]{2,1,0:T(8,128)(2,1)S(1)} collective-permute-done((bf16[4,160,256]{2,1,0:T(8,128)(2,1)S(1)}, bf16[4,160,256]{2,1,0:T(8,128)(2,1)S(1)}, u32[]{:S(2)}, u32[]{:S(2)}) %collective-permute-start.5) | collective-permute-done | bytes 327712 | tf_op jit(solution)/shard_map/ppermute | solution.py:125
  34.1 7.1 %collective-permute-done.7 = bf16[4,160,256]{2,1,0:T(8,128)(2,1)S(1)} collective-permute-done((bf16[4,160,256]{2,1,0:T(8,128)(2,1)S(1)}, bf16[4,160,256]{2,1,0:T(8,128)(2,1)S(1)}, u32[]{:S(2)}, u32[]{:S(2)}) %collective-permute-start.7) | collective-permute-done | bytes 327712 | tf_op jit(solution)/shard_map/ppermute | solution.py:125
  49.7 3.8 %fusion.15 = f32[256,1024]{1,0:T(8,128)} fusion(bf16[256,1280]{1,0:T(8,128)(2,1)} %bitcast.9, bf16[5120,1024]{1,0:T(8,128)(2,1)} %param.17, s32[]{:T(128)S(6)} %select_n.231), kind=kOutput, calls=%fused_computation.23 | convolution fusion | flops 671088640 | bytes 4325380 | tf_op jit(solution)/shard_map/dot_general | solution.py:201
  53.4 3.7 %fusion.11 = f32[256,1024]{1,0:T(8,128)} fusion(bf16[256,1280]{1,0:T(8,128)(2,1)S(1)} %collective-permute-done.4, bf16[5120,1024]{1,0:T(8,128)(2,1)} %param.17, s32[]{:T(128)S(6)} %select_n.233), kind=kOutput, calls=%fused_computation.19 | convolution fusion | flops 671088640 | bytes 4325380 | tf_op jit(solution)/shard_map/dot_general | solution.py:201
  57.1 9.9 %collective-permute-done.9 = bf16[256,1280]{1,0:T(8,128)(2,1)} collective-permute-done((bf16[256,1280]{1,0:T(8,128)(2,1)S(1)}, bf16[256,1280]{1,0:T(8,128)(2,1)}, u32[]{:S(2)}, u32[]{:S(2)}) %collective-permute-start.9) | collective-permute-done | bytes 655392 | tf_op jit(solution)/shard_map/ppermute | solution.py:140
  74.9 2.2 %gather_fusion.2 = bf16[8,4,160,256]{3,2,1,0:T(8,128)(2,1)} fusion(bf16[8,4,160,256]{3,2,1,0:T(8,128)(2,1)S(1)} %bitcast.227, s32[1024]{0:T(1024)S(1)} %pad_clamp_fusion), kind=kCustom, calls=%fused_computation.2 | custom fusion | bytes 5242912 | tf_op jit(solution)/shard_map/gather | solution.py:94
  81.7 2.6 %fusion.9 = f32[256,1024]{1,0:T(8,128)S(1)} fusion(bf16[256,1280]{1,0:T(8,128)(2,1)S(1)} %copy-done.4, bf16[5120,1024]{1,0:T(8,128)(2,1)} %param.17, s32[]{:T(128)S(6)} %select_n.237), kind=kOutput, calls=%fused_computation.17 | convolution fusion | flops 671088640 | bytes 4325380 | tf_op jit(solution)/shard_map/dot_general | solution.py:201
  86.1 2.7 %collective-permute-done.15 = bf16[256,1280]{1,0:T(8,128)(2,1)} collective-permute-done((bf16[256,1280]{1,0:T(8,128)(2,1)}, bf16[256,1280]{1,0:T(8,128)(2,1)}, u32[]{:S(2)}, u32[]{:S(2)}) %collective-permute-start.15) | collective-permute-done | bytes 655392 | tf_op jit(solution)/shard_map/ppermute | solution.py:125
  88.9 2.8 %fusion.7 = f32[256,1024]{1,0:T(8,128)S(1)} fusion(bf16[5120,1024]{1,0:T(8,128)(2,1)} %param.17, s32[]{:T(128)S(6)} %select_n.241, bf16[256,1280]{1,0:T(8,128)(2,1)} %collective-permute-done.13, bf16[256,1280]{1,0:T(8,128)(2,1)} %collective-permute-done.14, pred[]{:T(512)S(6)} %ge.17), kind=kOutput, calls=%fused_computation.15 | convolution fusion | flops 671416320 | bytes 4980741 | tf_op jit(solution)/shard_map/dot_general | solution.py:201
  98.3 2.8 %fusion.31 = f32[256,1024]{1,0:T(8,128)S(1)} fusion(f32[256,1024]{1,0:T(8,128)S(1)} %fusion.7, f32[256,1024]{1,0:T(8,128)S(1)} %fusion.9, f32[256,1024]{1,0:T(8,128)S(1)} %copy-done.14, f32[256,1024]{1,0:T(8,128)S(1)} %copy-done.13, bf16[256,1280]{1,0:T(8,128)(2,1)S(1)} %collective-permute-done.3, bf16[5120,1024]{1,0:T(8,128)(2,1)} %param.17, s32[]{:T(128)S(6)} %select_n.232), kind=kOutput, calls=%fused_computation.39 | convolution fusion | flops 672137216 | bytes 8519684 | tf_op jit(solution)/shard_map/dot_general | solution.py:201
  101.1 8.8 %collective-permute-done.16 = bf16[256,1280]{1,0:T(8,128)(2,1)S(1)} collective-permute-done((bf16[256,1280]{1,0:T(8,128)(2,1)S(1)}, bf16[256,1280]{1,0:T(8,128)(2,1)S(1)}, u32[]{:S(2)}, u32[]{:S(2)}) %collective-permute-start.16) | collective-permute-done | bytes 655392 | tf_op jit(solution)/shard_map/ppermute | solution.py:125
  113.6 2.1 %fusion.40 = bf16[8,32,1,128]{3,1,0,2:T(8,128)(2,1)} fusion(f32[8]{0:T(128)S(1)} %copy-done.29, f32[8,1,8,32,32]{3,4,2,0,1:T(8,128)S(1)} %get-tuple-element.121, f32[8,8,32]{2,1,0:T(8,128)S(1)} %fusion.45, f32[8,8,32]{2,1,0:T(8,128)S(1)} %get-tuple-element.120, bf16[8,32,1024]{2,1,0:T(8,128)(2,1)} %param.16), kind=kOutput, calls=%fused_computation.52 | convolution fusion | flops 17793024 | bytes 868384 | tf_op jit(solution)/shard_map/sgpqk,sqgph->skgh/dot_general | solution.py:54
  124.1 9.6 %collective-permute-done.18 = bf16[256,1280]{1,0:T(8,128)(2,1)} collective-permute-done((bf16[256,1280]{1,0:T(8,128)(2,1)}, bf16[256,1280]{1,0:T(8,128)(2,1)}, u32[]{:S(2)}, u32[]{:S(2)}) %collective-permute-start.18) | collective-permute-done | bytes 655392 | tf_op jit(solution)/shard_map/ppermute | solution.py:125
  138.6 5.0 %collective-permute-done.22 = bf16[256,256]{0,1:T(8,128)(2,1)S(1)} collective-permute-done((bf16[256,256]{0,1:T(8,128)(2,1)S(1)}, bf16[256,256]{0,1:T(8,128)(2,1)S(1)}, u32[]{:S(2)}, u32[]{:S(2)}) %collective-permute-start.22) | collective-permute-done | bytes 131104 | tf_op jit(solution)/shard_map/ppermute | solution.py:132
  151.0 2.4 %convolution_bitcast_fusion = f32[1280,256]{0,1:T(8,128)S(1)} fusion(bf16[1,256,1280]{2,1,0:T(8,128)(2,1)} %bitcast.85, bf16[1,256,1280]{2,1,0:T(8,128)(2,1)} %bitcast.84, bf16[1,256,1280]{2,1,0:T(8,128)(2,1)S(1)} %bitcast.265, bf16[1,256,1280]{2,1,0:T(8,128)(2,1)} %bitcast.82, bf16[1,256,256]{1,2,0:T(8,128)(2,1)S(1)} %bitcast.266, ...), kind=kOutput, calls=%fused_computation.3 | convolution fusion | flops 675807232 | bytes 4456448 | tf_op jit(solution)/shard_map/td,tc->dc/dot_general | solution.py:287
  153.5 10.3 %collective-permute-start.29 = (bf16[1280,128]{0,1:T(8,128)(2,1)S(1)}, bf16[1280,128]{0,1:T(8,128)(2,1)S(1)}, u32[]{:S(2)}, u32[]{:S(2)}) collective-permute-start(bf16[1280,128]{0,1:T(8,128)(2,1)S(1)} %select_convert_fusion), channel_id=1, source_target_pairs={{0,4},{4,0},{8,12},{12,8},{16,20},{20,16},{24,28},{28,24},{1,5},{5... | collective-permute-start | bytes 983048 | tf_op jit(solution)/shard_map/ppermute | solution.py:125
  166.6 2.7 %convolution_convert_fusion = bf16[640,1024]{1,0:T(8,128)(2,1)} fusion(bf16[1024,1024]{1,0:T(8,128)(2,1)S(1)} %bitcast.229, bf16[1024,1280]{1,0:T(8,128)(2,1)S(1)} %bitcast.232, s32[]{:T(128)S(6)} %select_n.268), kind=kOutput, calls=%fused_computation.26 | convolution fusion | flops 1342832640 | bytes 4718596 | tf_op jit(solution)/shard_map/td,tc->dc/dot_general | solution.py:269
  169.2 3.1 %collective-permute-start.25 = (bf16[640,1024]{1,0:T(8,128)(2,1)}, bf16[640,1024]{1,0:T(8,128)(2,1)}, u32[]{:S(2)}, u32[]{:S(2)}) collective-permute-start(bf16[640,1024]{1,0:T(8,128)(2,1)} %convolution_convert_fusion), channel_id=1, source_target_pairs={{0,4},{4,0},{8,12},{12,8},{16,20},{20,16},{24,28},{28,24},{1,5},{5... | collective-permute-start | bytes 3932168 | tf_op jit(solution)/shard_map/ppermute | solution.py:125
  176.4 4.4 %convert_add_fusion = f32[640,1024]{1,0:T(8,128)} fusion(bf16[640,1024]{1,0:T(8,128)(2,1)} %collective-permute-done.25, bf16[1024,1024]{1,0:T(8,128)(2,1)S(1)} %bitcast.230, bf16[1024,1280]{1,0:T(8,128)(2,1)S(1)} %bitcast.233, s32[]{:T(128)S(6)} %select_n.267), kind=kOutput, calls=%fused_computation.14 | convolution fusion | flops 1343488000 | bytes 7340036 | tf_op jit(solution)/shard_map/td,tc->dc/dot_general | solution.py:269
  (174 shorter events, 70.4 us)
Async XLA Ops:
  3.2 15.5 %all-to-all-start = ((bf16[8,32,1280]{2,1,0:T(8,128)(2,1)}), bf16[8,32,1280]{2,1,0:T(8,128)(2,1)S(1)}, u32[]{:S(2)}, u32[]{:S(2)}) async-start(bf16[8,32,1280]{2,1,0:T(8,128)(2,1)} %gather_fusion), calls=%async_computation | async-start | bytes 1310720 | tf_op jit(solution)/shard_map/all_to_all | solution.py:144
  10.2 8.4 %collective-permute-start.1 = (bf16[160,256]{1,0:T(8,128)(2,1)S(1)}, bf16[160,256]{1,0:T(8,128)(2,1)S(1)}, u32[]{:S(2)}, u32[]{:S(2)}) collective-permute-start(bf16[160,256]{1,0:T(8,128)(2,1)S(1)} %get-tuple-element.113), channel_id=1, source_target_pairs={{0,2},{1,3},{2,0},{3,1},{4,6},{5,7},{6,4},{7,5},{8,10},{9,11},{10,... | collective-permute-start | bytes 245768 | tf_op jit(solution)/shard_map/ppermute | solution.py:132
  20.1 21.1 %collective-permute-start.3 = (bf16[256,1280]{1,0:T(8,128)(2,1)}, bf16[256,1280]{1,0:T(8,128)(2,1)S(1)}, u32[]{:S(2)}, u32[]{:S(2)}) collective-permute-start(bf16[256,1280]{1,0:T(8,128)(2,1)} %bitcast.9), channel_id=1, source_target_pairs={{0,1},{1,2},{2,3},{4,5},{5,6},{6,7},{8,9},{9,10},{10,11},{12,13},{... | collective-permute-start | bytes 1966088 | tf_op jit(solution)/shard_map/ppermute | solution.py:137
  24.2 17.6 %collective-permute-start.4 = (bf16[256,1280]{1,0:T(8,128)(2,1)}, bf16[256,1280]{1,0:T(8,128)(2,1)S(1)}, u32[]{:S(2)}, u32[]{:S(2)}) collective-permute-start(bf16[256,1280]{1,0:T(8,128)(2,1)} %bitcast.9), channel_id=1, source_target_pairs={{3,2},{2,1},{1,0},{7,6},{6,5},{5,4},{11,10},{10,9},{9,8},{15,14},{... | collective-permute-start | bytes 1966088 | tf_op jit(solution)/shard_map/ppermute | solution.py:140
  25.6 8.5 %collective-permute-start.5 = (bf16[4,160,256]{2,1,0:T(8,128)(2,1)S(1)}, bf16[4,160,256]{2,1,0:T(8,128)(2,1)S(1)}, u32[]{:S(2)}, u32[]{:S(2)}) collective-permute-start(bf16[4,160,256]{2,1,0:T(8,128)(2,1)S(1)} %pad_maximum_fusion.7), channel_id=1, source_target_pairs={{0,8},{4,12},{8,0},{12,4},{16,24},{20,28},{24,16},{28,20},{1,9},{5... | collective-permute-start | bytes 983048 | tf_op jit(solution)/shard_map/ppermute | solution.py:125
  25.9 8.2 %collective-permute-start.6 = (bf16[4,160,256]{2,1,0:T(8,128)(2,1)S(1)}, bf16[4,160,256]{2,1,0:T(8,128)(2,1)S(1)}, u32[]{:S(2)}, u32[]{:S(2)}) collective-permute-start(bf16[4,160,256]{2,1,0:T(8,128)(2,1)S(1)} %pad_maximum_fusion.7), channel_id=1, source_target_pairs={{0,16},{4,20},{8,24},{12,28},{16,0},{20,4},{24,8},{28,12},{1,17},{... | collective-permute-start | bytes 983048 | tf_op jit(solution)/shard_map/ppermute | solution.py:125
  26.0 15.1 %collective-permute-start.7 = (bf16[4,160,256]{2,1,0:T(8,128)(2,1)S(1)}, bf16[4,160,256]{2,1,0:T(8,128)(2,1)S(1)}, u32[]{:S(2)}, u32[]{:S(2)}) collective-permute-start(bf16[4,160,256]{2,1,0:T(8,128)(2,1)S(1)} %pad_maximum_fusion.7), channel_id=1, source_target_pairs={{0,24},{4,28},{8,16},{12,20},{16,8},{20,12},{24,0},{28,4},{1,25},{... | collective-permute-start | bytes 983048 | tf_op jit(solution)/shard_map/ppermute | solution.py:125
  43.5 23.5 %collective-permute-start.10 = (bf16[4,4,160,256]{3,2,1,0:T(8,128)(2,1)}, bf16[4,4,160,256]{3,2,1,0:T(8,128)(2,1)S(1)}, u32[]{:S(2)}, u32[]{:S(2)}) collective-permute-start(bf16[4,4,160,256]{3,2,1,0:T(8,128)(2,1)} %get-tuple-element.97), channel_id=1, source_target_pairs={{0,4},{4,0},{8,12},{12,8},{16,20},{20,16},{24,28},{28,24},{1,5},{5... | collective-permute-start | bytes 3932168 | tf_op jit(solution)/shard_map/ppermute | solution.py:125
  45.7 11.4 %collective-permute-start.8 = (bf16[256,1280]{1,0:T(8,128)(2,1)S(1)}, bf16[256,1280]{1,0:T(8,128)(2,1)}, u32[]{:S(2)}, u32[]{:S(2)}) collective-permute-start(bf16[256,1280]{1,0:T(8,128)(2,1)S(1)} %collective-permute-done.3), channel_id=1, source_target_pairs={{1,2},{2,3},{5,6},{6,7},{9,10},{10,11},{13,14},{14,15},{17,18},{18... | collective-permute-start | bytes 1966088 | tf_op jit(solution)/shard_map/ppermute | solution.py:137
  47.2 19.8 %collective-permute-start.9 = (bf16[256,1280]{1,0:T(8,128)(2,1)S(1)}, bf16[256,1280]{1,0:T(8,128)(2,1)}, u32[]{:S(2)}, u32[]{:S(2)}) collective-permute-start(bf16[256,1280]{1,0:T(8,128)(2,1)S(1)} %collective-permute-done.4), channel_id=1, source_target_pairs={{2,1},{1,0},{6,5},{5,4},{10,9},{9,8},{14,13},{13,12},{18,17},{17,1... | collective-permute-start | bytes 1966088 | tf_op jit(solution)/shard_map/ppermute | solution.py:140
  48.5 18.5 %collective-permute-start.11 = (bf16[256,1280]{1,0:T(8,128)(2,1)}, bf16[256,1280]{1,0:T(8,128)(2,1)S(1)}, u32[]{:S(2)}, u32[]{:S(2)}) collective-permute-start(bf16[256,1280]{1,0:T(8,128)(2,1)} %bitcast.9), channel_id=1, source_target_pairs={{0,8},{4,12},{8,0},{12,4},{16,24},{20,28},{24,16},{28,20},{1,9},{5... | collective-permute-start | bytes 1966088 | tf_op jit(solution)/shard_map/ppermute | solution.py:125
  49.4 17.7 %collective-permute-start.12 = (bf16[256,1280]{1,0:T(8,128)(2,1)}, bf16[256,1280]{1,0:T(8,128)(2,1)}, u32[]{:S(2)}, u32[]{:S(2)}) collective-permute-start(bf16[256,1280]{1,0:T(8,128)(2,1)} %bitcast.9), channel_id=1, source_target_pairs={{0,16},{4,20},{8,24},{12,28},{16,0},{20,4},{24,8},{28,12},{1,17},{... | collective-permute-start | bytes 1966088 | tf_op jit(solution)/shard_map/ppermute | solution.py:125
  67.1 17.2 %collective-permute-start.13 = (bf16[256,1280]{1,0:T(8,128)(2,1)}, bf16[256,1280]{1,0:T(8,128)(2,1)}, u32[]{:S(2)}, u32[]{:S(2)}) collective-permute-start(bf16[256,1280]{1,0:T(8,128)(2,1)} %collective-permute-done.8), channel_id=1, source_target_pairs={{2,3},{6,7},{10,11},{14,15},{18,19},{22,23},{26,27},{30,31}} | collective-permute-start | bytes 1966088 | tf_op jit(solution)/shard_map/ppermute | solution.py:137
  68.6 17.5 %collective-permute-start.14 = (bf16[256,1280]{1,0:T(8,128)(2,1)}, bf16[256,1280]{1,0:T(8,128)(2,1)}, u32[]{:S(2)}, u32[]{:S(2)}) collective-permute-start(bf16[256,1280]{1,0:T(8,128)(2,1)} %collective-permute-done.9), channel_id=1, source_target_pairs={{1,0},{5,4},{9,8},{13,12},{17,16},{21,20},{25,24},{29,28}} | collective-permute-start | bytes 1966088 | tf_op jit(solution)/shard_map/ppermute | solution.py:140
  72.1 16.7 %collective-permute-start.15 = (bf16[256,1280]{1,0:T(8,128)(2,1)}, bf16[256,1280]{1,0:T(8,128)(2,1)}, u32[]{:S(2)}, u32[]{:S(2)}) collective-permute-start(bf16[256,1280]{1,0:T(8,128)(2,1)} %bitcast.9), channel_id=1, source_target_pairs={{0,24},{4,28},{8,16},{12,20},{16,8},{20,12},{24,0},{28,4},{1,25},{... | collective-permute-start | bytes 1966088 | tf_op jit(solution)/shard_map/ppermute | solution.py:125
  95.3 14.5 %collective-permute-start.16 = (bf16[256,1280]{1,0:T(8,128)(2,1)S(1)}, bf16[256,1280]{1,0:T(8,128)(2,1)S(1)}, u32[]{:S(2)}, u32[]{:S(2)}) collective-permute-start(bf16[256,1280]{1,0:T(8,128)(2,1)S(1)} %get-tuple-element.94), channel_id=1, source_target_pairs={{0,8},{4,12},{8,0},{12,4},{16,24},{20,28},{24,16},{28,20},{1,9},{5... | collective-permute-start | bytes 1966088 | tf_op jit(solution)/shard_map/ppermute | solution.py:125
  96.5 14.3 %collective-permute-start.17 = (bf16[256,1280]{1,0:T(8,128)(2,1)S(1)}, bf16[256,1280]{1,0:T(8,128)(2,1)S(1)}, u32[]{:S(2)}, u32[]{:S(2)}) collective-permute-start(bf16[256,1280]{1,0:T(8,128)(2,1)S(1)} %get-tuple-element.93), channel_id=1, source_target_pairs={{0,16},{4,20},{8,24},{12,28},{16,0},{20,4},{24,8},{28,12},{1,17},{... | collective-permute-start | bytes 1966088 | tf_op jit(solution)/shard_map/ppermute | solution.py:125
  119.1 14.6 %collective-permute-start.18 = (bf16[256,1280]{1,0:T(8,128)(2,1)}, bf16[256,1280]{1,0:T(8,128)(2,1)}, u32[]{:S(2)}, u32[]{:S(2)}) collective-permute-start(bf16[256,1280]{1,0:T(8,128)(2,1)} %get-tuple-element.76), channel_id=1, source_target_pairs={{0,24},{4,28},{8,16},{12,20},{16,8},{20,12},{24,0},{28,4},{1,25},{... | collective-permute-start | bytes 1966088 | tf_op jit(solution)/shard_map/ppermute | solution.py:125
  133.6 10.1 %collective-permute-start.19 = (bf16[256,1024]{1,0:T(8,128)(2,1)S(1)}, bf16[256,1024]{1,0:T(8,128)(2,1)}, u32[]{:S(2)}, u32[]{:S(2)}) collective-permute-start(bf16[256,1024]{1,0:T(8,128)(2,1)S(1)} %bitcast.240), channel_id=1, source_target_pairs={{0,8},{4,12},{8,0},{12,4},{16,24},{20,28},{24,16},{28,20},{1,9},{5... | collective-permute-start | bytes 1572872 | tf_op jit(solution)/shard_map/ppermute | solution.py:125
  134.4 9.9 %collective-permute-start.20 = (bf16[256,1024]{1,0:T(8,128)(2,1)S(1)}, bf16[256,1024]{1,0:T(8,128)(2,1)}, u32[]{:S(2)}, u32[]{:S(2)}) collective-permute-start(bf16[256,1024]{1,0:T(8,128)(2,1)S(1)} %bitcast.241), channel_id=1, source_target_pairs={{0,16},{4,20},{8,24},{12,28},{16,0},{20,4},{24,8},{28,12},{1,17},{... | collective-permute-start | bytes 1572872 | tf_op jit(solution)/shard_map/ppermute | solution.py:125
  134.8 8.8 %collective-permute-start.22 = (bf16[256,256]{0,1:T(8,128)(2,1)S(1)}, bf16[256,256]{0,1:T(8,128)(2,1)S(1)}, u32[]{:S(2)}, u32[]{:S(2)}) collective-permute-start(bf16[256,256]{0,1:T(8,128)(2,1)S(1)} %bitcast.249), channel_id=1, source_target_pairs={{0,2},{1,3},{2,0},{3,1},{4,6},{5,7},{6,4},{7,5},{8,10},{9,11},{10,... | collective-permute-start | bytes 393224 | tf_op jit(solution)/shard_map/ppermute | solution.py:132
  148.7 15.0 %collective-permute-start.24 = (bf16[256,1024]{1,0:T(8,128)(2,1)S(1)}, bf16[256,1024]{1,0:T(8,128)(2,1)S(1)}, u32[]{:S(2)}, u32[]{:S(2)}) collective-permute-start(bf16[256,1024]{1,0:T(8,128)(2,1)S(1)} %bitcast.242), channel_id=1, source_target_pairs={{0,24},{4,28},{8,16},{12,20},{16,8},{20,12},{24,0},{28,4},{1,25},{... | collective-permute-start | bytes 1572872 | tf_op jit(solution)/shard_map/ppermute | solution.py:125
  153.5 20.5 %collective-permute-start.29 = (bf16[1280,128]{0,1:T(8,128)(2,1)S(1)}, bf16[1280,128]{0,1:T(8,128)(2,1)S(1)}, u32[]{:S(2)}, u32[]{:S(2)}) collective-permute-start(bf16[1280,128]{0,1:T(8,128)(2,1)S(1)} %select_convert_fusion), channel_id=1, source_target_pairs={{0,4},{4,0},{8,12},{12,8},{16,20},{20,16},{24,28},{28,24},{1,5},{5... | collective-permute-start | bytes 983048 | tf_op jit(solution)/shard_map/ppermute | solution.py:125
  169.2 7.2 %collective-permute-start.25 = (bf16[640,1024]{1,0:T(8,128)(2,1)}, bf16[640,1024]{1,0:T(8,128)(2,1)}, u32[]{:S(2)}, u32[]{:S(2)}) collective-permute-start(bf16[640,1024]{1,0:T(8,128)(2,1)} %convolution_convert_fusion), channel_id=1, source_target_pairs={{0,4},{4,0},{8,12},{12,8},{16,20},{20,16},{24,28},{28,24},{1,5},{5... | collective-permute-start | bytes 3932168 | tf_op jit(solution)/shard_map/ppermute | solution.py:125
  (37 other events, 284.4 us)

commit v3 on v1

--- a/solution.py
+++ b/solution.py
@@ -65,18 +65,18 @@
     return (d_query, d_key, d_value)
 
 
-def attend(x, w_query, w_kv, cot, factor, query_gain, key_gain, length, device_cols):
-    blocks, tokens, width = x.shape
+def attend(query, kv, cot, factor, query_gain, key_gain, length, device_cols, beside):
+    tokens = query.shape[0]
     dim = query_gain.shape[0]
     slots = tokens // length
-    heads = w_query.shape[1] // dim
-    x = x.transpose(1, 0, 2).reshape(tokens, blocks * width)
-    query = jnp.dot(x, w_query, preferred_element_type=F32)
-    kv = jnp.dot(x, w_kv, preferred_element_type=F32)
+    heads = query.shape[1] // dim
     query = query.reshape(slots, length, 1, heads, dim)
     key = kv[:, :dim].reshape(slots, length, 1, dim)
     value = kv[:, dim:].reshape(slots, length, 1, dim)
     attended, saved = forward_core(query, key, value, query_gain, key_gain)
+    *saved, probs, p_half = saved
+    probs, *beside = together(probs, *beside)
+    saved = (*saved, probs, p_half)
     d_out = cot.astype(F32).reshape(slots, length, 1, heads, dim)
     d_out = d_out * factor[:, None, None, None, None]
     d_query, d_key, d_value = backward_core(d_out, query, key, query_gain, key_gain, saved)
@@ -86,26 +86,16 @@
         attended.reshape(tokens, -1).astype(BF16),
         d_query.reshape(tokens, -1).astype(BF16),
         d_kv.astype(BF16),
-    )
-
-
-def line_gather(block, axis, count):
-    me = lax.axis_index(axis)
-    up, down = [block], [block]
-    for hop in range(1, count):
-        up.append(lax.ppermute(up[-1], axis, [(i, i + 1) for i in range(hop - 1, count - 1)]))
-        down.append(
-            lax.ppermute(down[-1], axis, [(i, i - 1) for i in range(count - hop, 0, -1)])
-        )
-    return [block] + [jnp.where(me >= hop, up[hop], down[count - hop]) for hop in range(1, count)]
+        beside,
+    )
+
+
+def together(*values):
+    return lax.optimization_barrier(values)
 
 
 def pick(array, index):
     return array.at[index].get(mode="promise_in_bounds")
-
-
-def flip(block, axis, count, bits):
-    return lax.ppermute(block, axis, [(i, i ^ bits) for i in range(count)])
 
 
 def local(
@@ -135,84 +125,134 @@
     mp = lax.axis_index("mp")
     chip, core = dp // 2, dp % 2
 
+    def flip(block, bits):
+        return lax.ppermute(block, "dp", [(i, i ^ bits) for i in range(n_dp)])
+
+    def other_chips(blocks):
+        return [flip(blocks[k], 2 * k) for k in range(1, chips)]
+
+    def around(blocks):
+        return [blocks[0]] + [
+            lax.ppermute(blocks[k], "mp", [(i, (i + k) % n_mp) for i in range(n_mp)])
+            for k in range(1, n_mp)
+        ]
+
+    near = [1 << b for b in range(chips.bit_length() - 1)]
+
+    def from_near(block):
+        return [flip(block, 2 * k) for k in near]
+
+    def from_far(block, arrived):
+        arrived = dict(zip(near, arrived))
+        middle = block.shape[0] // 2
+        blocks = [block]
+        for k in range(1, chips):
+            bits = [n for n in near if k & n]
+            if len(bits) == 1:
+                blocks.append(arrived[k])
+            elif len(bits) == 2:
+                first = flip(arrived[bits[0]][:middle], 2 * bits[1])
+                second = flip(arrived[bits[1]][middle:], 2 * bits[0])
+                blocks.append(jnp.concatenate([first, second]))
+            else:
+                blocks.append(flip(block, 2 * k))
+        return blocks
+
+    outgoing = pick(pool, jnp.maximum(send_table[0], 0))
+    outgoing, w_key, w_value = together(outgoing, w_key, w_value)
+    arrived = lax.all_to_all(outgoing, "dp", split_axis=0, concat_axis=0, tiled=True)
+
     share = width // n_dp
     own_key = lax.dynamic_slice_in_dim(w_key, dp * share, share, 0)
     own_value = lax.dynamic_slice_in_dim(w_value, dp * share, share, 0)
     pairs = []
-    for i in range(n_mp):
-        head = i * KV_HEADS // n_mp
+    for head in range(KV_HEADS):
         columns = slice(head * dim, (head + 1) * dim)
         pairs.append(jnp.concatenate([own_key[:, columns], own_value[:, columns]], axis=1))
-    both = jnp.stack(pairs)
-    both = lax.all_to_all(both, "mp", split_axis=0, concat_axis=0, tiled=True)
-    shares = jnp.stack([both] + [flip(both, "dp", n_dp, 2 * k) for k in range(1, chips)])
-    shares = jnp.stack([shares, flip(shares, "dp", n_dp, 1)], axis=1)
-    shares = shares.reshape(n_dp, n_mp, share, 2 * dim)
-    shares = pick(shares, dp ^ jnp.arange(n_dp))
-    w_kv = shares.transpose(1, 0, 2, 3).reshape(n_mp * width, 2 * dim)
-
-    outgoing = pick(pool, jnp.maximum(send_table[0], 0))
-    arrived = lax.all_to_all(outgoing, "dp", split_axis=0, concat_axis=0, tiled=True)
+    pairs = jnp.stack(pairs)
+    heads = [(mp + k) % n_mp * KV_HEADS // n_mp for k in range(n_mp)]
+    shares = around([lax.dynamic_index_in_dim(pairs, h, 0, False) for h in heads])
+    arrived, *shares = together(arrived, *shares)
+    shares = jnp.stack(shares)
     rows = pick(arrived, slot_source).reshape(tokens, width)
 
-    if n_mp <= 4:
-        near = jnp.stack(line_gather(rows, "mp", n_mp))
-        x = pick(near, (mp - jnp.arange(n_mp)) % n_mp)
-    else:
-        x = lax.all_gather(rows, "mp", axis=0)
-
-    plane_rows = jnp.stack([rows] + [flip(rows, "dp", n_dp, 2 * k) for k in range(1, chips)])
-    plane_rows = plane_rows.reshape(chips * tokens, width)
+    x = lax.all_gather(rows, "mp", axis=1, tiled=True)
+    shares = jnp.stack([shares] + other_chips([shares] * chips))
+    native, shares = together(rows, shares)
+    other_shares, *plane_rows = together(flip(shares, 1), *from_near(native))
+    plane_rows = jnp.stack(from_far(native, plane_rows)).reshape(chips * tokens, width)
+
+    shares = jnp.stack([shares, other_shares], axis=1).reshape(n_dp * n_mp, share, 2 * dim)
+    order = (dp ^ jnp.arange(n_dp))[None, :] * n_mp + ((mp - jnp.arange(n_mp)) % n_mp)[:, None]
+    w_kv = pick(shares, order.reshape(-1)).reshape(n_mp * width, 2 * dim)
+
+    x, w_kv, plane_rows = together(x, w_kv, plane_rows)
+    query = jnp.dot(x, w_query, preferred_element_type=F32)
+    kv = jnp.dot(x, w_kv, preferred_element_type=F32)
 
     chip_width = n_mp * width // chips
-    if chip_width == width:
-        parts = x
-    else:
-        parts = x.transpose(1, 0, 2).reshape(tokens, chips, chip_width).transpose(1, 0, 2)
-    part = lambda k: lax.dynamic_index_in_dim(parts, chip ^ k, 0, keepdims=False)
-    chip_rows = jnp.stack([part(0)] + [flip(part(k), "dp", n_dp, 2 * k) for k in range(1, chips)])
-    chip_rows = chip_rows.reshape(chips * tokens, chip_width)
+    chip_rows = [
+        lax.dynamic_slice_in_dim(x, (chip ^ k) * chip_width, chip_width, 1) for k in range(chips)
+    ]
+    near_rows = [flip(chip_rows[k], 2 * k) for k in near]
 
     factor = multiplicity.astype(F32) * slot_weight / length
-    attended, d_query, d_kv = attend(
-        x,
-        w_query,
-        w_kv,
+    attended, d_query, d_kv, near_rows = attend(
+        query,
+        kv,
         cotangent.reshape(tokens, query_cols),
         factor,
         query_gain,
         key_gain,
         length,
         key_cols // n_dp,
-    )
-
-    d_all = jnp.stack([d_query] + [flip(d_query, "dp", n_dp, 2 * k) for k in range(1, chips)])
-    d_all = d_all.reshape(chips * tokens, query_cols)
+        near_rows,
+    )
+
+    near_rows = dict(zip(near, near_rows))
+    chip_rows = [
+        chip_rows[0] if k == 0 else near_rows[k] if k in near else flip(chip_rows[k], 2 * k)
+        for k in range(chips)
+    ]
+    d_query, d_kv, *chip_rows = together(d_query, d_kv, *chip_rows)
+
+    d_near = from_near(d_query)
+    spread = around([d_kv] * n_mp)
+    spread, *d_near = together(jnp.stack(spread), *d_near)
+    d_all = from_far(d_query, d_near)
     half = chip_width // 2
+    early = [0] + near
+    late = [k for k in range(chips) if k not in early]
 
     def query_half(which):
-        mine = lax.dynamic_slice_in_dim(chip_rows, which * half, half, 1)
-        return jnp.einsum("td,tc->dc", mine, d_all, preferred_element_type=F32)
-
-    other = flip(query_half(1 - core).astype(BF16), "dp", n_dp, 1)
+        total = 0
+        for some in (early, late):
+            mine = jnp.concatenate([chip_rows[k] for k in some])
+            mine = lax.dynamic_slice_in_dim(mine, which * half, half, 1)
+            theirs = jnp.concatenate([d_all[k] for k in some])
+            total = total + jnp.einsum("td,tc->dc", mine, theirs, preferred_element_type=F32)
+        return total
+
+    other = flip(query_half(1 - core).astype(BF16), 1)
     grad_query = query_half(core) + other.astype(F32)
 
-    spread = jnp.broadcast_to(d_kv[None], (n_mp,) + d_kv.shape)
-    spread = lax.all_to_all(spread, "mp", split_axis=0, concat_axis=0, tiled=True)
     if n_mp > KV_HEADS:
+        spread = pick(spread, (mp - jnp.arange(n_mp)) % n_mp)
         spread = spread.reshape(KV_HEADS, n_mp // KV_HEADS, tokens, 2 * dim)
         spread = jnp.sum(spread.astype(F32), axis=1).astype(BF16)
+        spread_at = lambda index: index
+    else:
+        spread_at = lambda index: (mp - index) % n_mp
     chip_cols = 2 * key_cols // chips
     if chip_cols != 2 * dim:
         spread = spread.reshape(KV_HEADS, tokens, chips // KV_HEADS, chip_cols)
         spread = spread.transpose(0, 2, 1, 3).reshape(chips, tokens, chip_cols)
-    kv_part = lambda k: lax.dynamic_index_in_dim(spread, chip ^ k, 0, keepdims=False)
-    kv_all = jnp.stack([kv_part(0)] + [flip(kv_part(k), "dp", n_dp, 2 * k) for k in range(1, chips)])
-    kv_all = kv_all.reshape(chips * tokens, chip_cols)
+    kv_all = [lax.dynamic_index_in_dim(spread, spread_at(chip ^ k), 0, False) for k in range(chips)]
+    kv_all = jnp.stack([kv_all[0]] + other_chips(kv_all)).reshape(chips * tokens, chip_cols)
     partial = jnp.einsum("td,tc->dc", plane_rows, kv_all, preferred_element_type=F32)
     mine, theirs = partial[:, : chip_cols // 2], partial[:, chip_cols // 2 :]
     mine, theirs = jnp.where(core == 0, mine, theirs), jnp.where(core == 0, theirs, mine)
-    grad_kv = mine + flip(theirs.astype(BF16), "dp", n_dp, 1).astype(F32)
+    grad_kv = mine + flip(theirs.astype(BF16), 1).astype(F32)
     device_cols = chip_cols // 4
 
     return (

time: 217 us -> 191 us (0.88)
  starting transfers between devices: 66.5 us -> 31.2 us
  between operations: 1.32 us -> 14.6 us
  waiting for transfers between devices: 81.2 us -> 77.2 us
  matrix products: 25.3 us -> 27.5 us
    ppermute x24 -> x26, starting transfers between devices: 52.4 us -> 26.6 us  [the longest x20 20.2 us: flip(): return lax.ppermute(block, 'dp', [(i, i ^ bits) for i in range(n_dp)])]
    all_to_all x2 -> x0, starting transfers between devices: 9.61 us -> none  [the longest x1 5.02 us: local(): lax.all_to_all(spread, 'mp', split_axis=0, concat_axis=0, tiled=True)]
    all_to_all x1, waiting for transfers between devices: 6.7 us -> 0.01 us  [local(): lax.all_to_all(outgoing, 'dp', split_axis=0, concat_axis=0, tiled=True)]
    transpose x2 -> x0, local copies, waits for them, and re-layouts: 6.52 us -> none  [the longest x1 3.54 us: local(): w_kv = shares.transpose(1, 0, 2, 3).reshape(n_mp * width, 2 * dim)]
    all_gather x0 -> x1, waiting for transfers between devices: none -> 4.67 us  [local(): x = lax.all_gather(rows, 'mp', axis=1, tiled=True)]
    another operation x15 -> x14, other arithmetic: 10.5 us -> 7.09 us  [the longest x2 4.21 us: local(): jnp.stack(from_far(native, plane_rows)).reshape(chips * tokens, width)]
    slice x0 -> x4, local copies, waits for them, and re-layouts: none -> 3.01 us  [the longest x2 1.55 us: from_far(): first = flip(arrived[bits[0]][:middle], 2 * bits[1])]
    gather x4 -> x3, local copies, waits for them, and re-layouts: 7.53 us -> 5.08 us  [pick(): return array.at[index].get(mode='promise_in_bounds')]
  transfers between devices with their start and end apart: 27 -> 28, of which waited for: 11 -> 12; matrix products, arithmetic and copies ran while one was open for 25% -> 22% of each run, Pallas kernels for 0% -> 0%
where the time goes in v3:
time: 191 us; the launch traced here: 189 us
  waiting for transfers between devices  77.2 us (40%)
  starting transfers between devices  31.2 us (16%)
  matrix products  27.5 us (14%)
  local copies, waits for them, and re-layouts  24.6 us (13%)
  between operations  14.6 us (8%)
  other arithmetic  13.5 us (7%)
    ppermute x20, waiting for transfers between devices, flip(): return lax.ppermute(block, 'dp', [(i, i ^ bits) for i in range(n_dp)])  59.1 us
    ppermute x20, starting transfers between devices, flip(): return lax.ppermute(block, 'dp', [(i, i ^ bits) for i in range(n_dp)])  20.2 us
    ppermute x6, waiting for transfers between devices, around(): lax.ppermute(blocks[k], 'mp', [(i, (i + k) % n_mp) for i in range(n_mp)])  13.4 us
    dot_general x4, matrix products, query_half(): jnp.einsum('td,tc->dc', mine, theirs, preferred_element_type=F32)  9.49 us
    ppermute x6, starting transfers between devices, around(): lax.ppermute(blocks[k], 'mp', [(i, (i + k) % n_mp) for i in range(n_mp)])  6.34 us
    dot_general x1, matrix products, local(): query = jnp.dot(x, w_query, preferred_element_type=F32)  5.59 us
    unnamed x55, local copies, waits for them, and re-layouts  5.55 us
    gather x3, local copies, waits for them, and re-layouts, pick(): return array.at[index].get(mode='promise_in_bounds')  5.08 us
  transfers between devices with their start and end apart: 28, of which 12 were waited for; matrix products, arithmetic and copies ran while one was open for 22% of the time, Pallas kernels for 0%

profile of v3, /device:TPU:7, one launch (start us, length us, event | category | flops | bytes accessed | tf_op | source)
XLA Modules:
  0.0 188.6 jit_solution(15449146378357828483)
XLA Ops:
  9.7 4.6 %all-to-all-start = ((bf16[8,32,1280]{2,1,0:T(8,128)(2,1)}), bf16[8,32,1280]{2,1,0:T(8,128)(2,1)S(1)}, u32[]{:S(2)}, u32[]{:S(2)}) async-start(bf16[8,32,1280]{2,1,0:T(8,128)(2,1)} %gather_fusion), calls=%async_computation | async-start | bytes 1310720 | tf_op jit(solution)/shard_map/all_to_all | solution.py:163
  15.5 3.4 %collective-permute-start.2 = (bf16[160,256]{1,0:T(8,128)(2,1)S(1)}, bf16[160,256]{1,0:T(8,128)(2,1)S(1)}, u32[]{:S(2)}, u32[]{:S(2)}) collective-permute-start(bf16[160,256]{1,0:T(8,128)(2,1)S(1)} %get-tuple-element.80), channel_id=1, source_target_pairs={{0,3},{1,0},{2,1},{3,2},{4,7},{5,4},{6,5},{7,6},{8,11},{9,8},{10,9... | collective-permute-start | bytes 245768 | tf_op jit(solution)/shard_map/ppermute | solution.py:136
  20.3 6.5 %collective-permute-done.1 = bf16[160,256]{1,0:T(8,128)(2,1)S(1)} collective-permute-done((bf16[160,256]{1,0:T(8,128)(2,1)S(1)}, bf16[160,256]{1,0:T(8,128)(2,1)S(1)}, u32[]{:S(2)}, u32[]{:S(2)}) %collective-permute-start.1) | collective-permute-done | bytes 81952 | tf_op jit(solution)/shard_map/ppermute | solution.py:136
  29.0 2.1 %collective-permute-start.5 = (bf16[4,160,256]{2,1,0:T(8,128)(2,1)S(1)}, bf16[4,160,256]{2,1,0:T(8,128)(2,1)S(1)}, u32[]{:S(2)}, u32[]{:S(2)}) collective-permute-start(bf16[4,160,256]{2,1,0:T(8,128)(2,1)S(1)} %get-tuple-element.79), channel_id=1, source_target_pairs={{0,24},{4,28},{8,16},{12,20},{16,8},{20,12},{24,0},{28,4},{1,25},{... | collective-permute-start | bytes 983048 | tf_op jit(solution)/shard_map/ppermute | solution.py:129
  31.1 5.9 %collective-permute-done.4 = bf16[4,160,256]{2,1,0:T(8,128)(2,1)S(1)} collective-permute-done((bf16[4,160,256]{2,1,0:T(8,128)(2,1)S(1)}, bf16[4,160,256]{2,1,0:T(8,128)(2,1)S(1)}, u32[]{:S(2)}, u32[]{:S(2)}) %collective-permute-start.4) | collective-permute-done | bytes 327712 | tf_op jit(solution)/shard_map/ppermute | solution.py:129
  37.0 8.0 %collective-permute-done.5 = bf16[4,160,256]{2,1,0:T(8,128)(2,1)S(1)} collective-permute-done((bf16[4,160,256]{2,1,0:T(8,128)(2,1)S(1)}, bf16[4,160,256]{2,1,0:T(8,128)(2,1)S(1)}, u32[]{:S(2)}, u32[]{:S(2)}) %collective-permute-start.5) | collective-permute-done | bytes 327712 | tf_op jit(solution)/shard_map/ppermute | solution.py:129
  45.2 1.8 collective-permute-start.6
  47.6 15.9 %collective-permute-done.8 = bf16[256,1280]{1,0:T(8,128)(2,1)S(1)} collective-permute-done((bf16[256,1280]{1,0:T(8,128)(2,1)S(1)}, bf16[256,1280]{1,0:T(8,128)(2,1)S(1)}, u32[]{:S(2)}, u32[]{:S(2)}) %collective-permute-start.8) | collective-permute-done | bytes 655392 | tf_op jit(solution)/shard_map/ppermute | solution.py:129
  67.0 2.0 %pad_maximum_fusion = bf16[4,2,4,160,256]{4,3,2,1,0:T(8,128)(2,1)S(1)} fusion(bf16[4,1,4,160,256]{4,3,2,1,0:T(8,128)(2,1)} %bitcast.202, bf16[4,1,4,160,256]{4,3,2,1,0:T(8,128)(2,1)} %bitcast.190), kind=kLoop, calls=%fused_computation.3 | loop fusion | flops 1310720 | bytes 5242880 | tf_op jit(solution)/shard_map/stack | solution.py:185
  68.9 2.2 %gather_fusion.2 = bf16[32,160,256]{2,1,0:T(8,128)(2,1)} fusion(bf16[32,160,256]{2,1,0:T(8,128)(2,1)S(1)} %bitcast.185, s32[1024]{0:T(1024)S(1)} %get-tuple-element.96), kind=kCustom, calls=%fused_computation.2 | custom fusion | bytes 5243008 | tf_op jit(solution)/shard_map/gather | solution.py:98
  71.1 2.7 %collective-permute-done.10 = bf16[128,1280]{1,0:T(8,128)(2,1)} collective-permute-done((bf16[128,1280]{1,0:T(8,128)(2,1)}, bf16[128,1280]{1,0:T(8,128)(2,1)}, u32[]{:S(2)}, u32[]{:S(2)}) %collective-permute-start.10) | collective-permute-done | bytes 327712 | tf_op jit(solution)/shard_map/ppermute | solution.py:129
  75.0 3.1 %pad_maximum_fusion.1 = bf16[4,256,1280]{2,1,0:T(8,128)(2,1)} fusion(bf16[1,256,1280]{2,1,0:T(8,128)(2,1)S(1)} %maximum_bitcast_fusion, bf16[1,256,1280]{2,1,0:T(8,128)(2,1)} %bitcast.200, bf16[1,256,1280]{2,1,0:T(8,128)(2,1)} %bitcast.201, bf16[1,256,1280]{2,1,0:T(8,128)(2,1)S(1)} %bitcast.189), kind=kLoop, calls=%fused_computation.4 | loop fusion | flops 3932160 | bytes 5242880 | tf_op jit(solution)/shard_map/stack | solution.py:183
  78.1 4.7 %all-gather.2.cloned.1.call-done = bf16[256,5120]{1,0:T(8,128)(2,1)} async-done(((bf16[256,1280]{1,0:T(8,128)(2,1)}), bf16[256,5120]{1,0:T(8,128)(2,1)}) %all-gather.2.cloned.1.call-update) | async-done | bytes 2621456 | tf_op jit(solution)/shard_map/all_gather | solution.py:179
  82.7 3.5 %fusion.41 = f32[256,256]{1,0:T(8,128)S(1)} fusion(bf16[256,5120]{1,0:T(8,128)(2,1)} %all-gather.2.cloned.1.call-done, bf16[5120,256]{1,0:T(8,128)(2,1)} %bitcast.191), kind=kOutput, calls=%fused_computation.118 | convolution fusion | flops 671088640 | bytes 5505024 | tf_op jit(solution)/shard_map/dot_general | solution.py:191
  86.5 5.6 %convolution_bitcast_fusion.2 = f32[32,8,8,128]{3,1,2,0:T(8,128)S(1)} fusion(bf16[256,5120]{1,0:T(8,128)(2,1)S(1)} %copy-done.4, bf16[5120,1024]{1,0:T(8,128)(2,1)} %param.17), kind=kOutput, calls=%fused_computation.9 | convolution fusion | flops 2684354560 | bytes 14155776 | tf_op jit(solution)/shard_map/dot_general | solution.py:190
  92.8 3.0 %constant_dynamic-slice_fusion.3 = (bf16[256,1280]{1,0:T(8,128)(2,1)}, bf16[256,1280]{1,0:T(8,128)(2,1)S(1)}, bf16[256,1280]{1,0:T(8,128)(2,1)}, bf16[256,1280]{1,0:T(8,128)(2,1)}) fusion(bf16[256,5120]{1,0:T(8,128)(2,1)} %all-gather.2.cloned.1.call-done, s32[]{:T(128)S(6)} %select_n.166, s32[]{:T(128)S(6)} %select_n.165, s32[]{:T(128)S(6)} %select_n.164, ...), kind=kLoop, calls=%fused_computation.95 | loop fusion | bytes 5242896 | tf_op jit(solution)/shard_map/dynamic_slice | solution.py:195
  103.2 23.3 %collective-permute-done.12 = bf16[256,1280]{1,0:T(8,128)(2,1)} collective-permute-done((bf16[256,1280]{1,0:T(8,128)(2,1)}, bf16[256,1280]{1,0:T(8,128)(2,1)}, u32[]{:S(2)}, u32[]{:S(2)}) %collective-permute-start.12) | collective-permute-done | bytes 655392 | tf_op jit(solution)/shard_map/ppermute | solution.py:129
  127.8 2.2 %multiply_reduce_fusion = (f32[8,32,8]{1,2,0:T(8,128)}, f32[8,32,1,8,128]{4,1,3,0,2:T(8,128)}) fusion(f32[8,32,1,8,128]{4,3,1,0,2:T(8,128)S(1)} %bitcast.181, f32[128]{0:T(128)S(1)} %copy-done.18, bf16[8,8,32,32]{2,3,1,0:T(8,128)(2,1)S(1)} %fusion.16, f32[8,32,128]{2,1,0:T(8,128)S(1)} %bitcast.193, f32[128]{0:T(128)S(1)} %copy-done.19, f32[8,32]{1,0:T(8,128)S(1)} %rsqrt.26), kind=kOutput, calls=%fused_computation.31 | convolution fusion | flops 17659904 | bytes 2369536 | tf_op jit(solution)/shard_map/sgpqk,skgh->sqgph/dot_general | solution.py:57
  132.3 2.0 %subtract_convert_fusion = bf16[8,32,1,8,128]{4,1,3,0,2:T(8,128)(2,1)S(1)} fusion(f32[8,32,1,8,128]{4,1,3,0,2:T(8,128)} %get-tuple-element.93, f32[8,32,1,8,128]{4,3,1,0,2:T(8,128)S(1)} %bitcast.183, f32[8,32,8]{1,2,0:T(8,128)S(1)} %broadcast_multiply_fusion, f32[8,32,8]{1,2,0:T(8,128)S(1)} %get-tuple-element.86, f32[8,32,8]{1,2,0:T(8,128)S(1)} %get-tuple-element.87), kind=kLoop, calls=%fused_computation.30 | loop fusion | flops 1310720 | bytes 2646016 | tf_op jit(solution)/shard_map/convert_element_type | solution.py:87
  141.4 6.0 %collective-permute-done.15 = bf16[256,256]{0,1:T(8,128)(2,1)S(1)} collective-permute-done((bf16[256,256]{0,1:T(8,128)(2,1)S(1)}, bf16[256,256]{0,1:T(8,128)(2,1)S(1)}, u32[]{:S(2)}, u32[]{:S(2)}) %collective-permute-start.15) | collective-permute-done | bytes 131104 | tf_op jit(solution)/shard_map/ppermute | solution.py:136
  157.7 2.6 %fusion.42 = f32[1280,256]{0,1:T(8,128)S(1)} fusion(bf16[1024,1280]{1,0:T(8,128)(2,1)} %bitcast.184, bf16[1024,256]{1,0:T(8,128)(2,1)S(1)} %bitcast.195), kind=kOutput, calls=%fused_computation.119 | convolution fusion | flops 671088640 | bytes 4456448 | tf_op jit(solution)/shard_map/td,tc->dc/dot_general | solution.py:252
  161.1 4.5 %collective-permute-start.25 = (bf16[1280,128]{0,1:T(8,128)(2,1)}, bf16[1280,128]{0,1:T(8,128)(2,1)S(1)}, u32[]{:S(2)}, u32[]{:S(2)}) collective-permute-start(bf16[1280,128]{0,1:T(8,128)(2,1)} %select_convert_fusion), channel_id=1, source_target_pairs={{0,4},{4,0},{8,12},{12,8},{16,20},{20,16},{24,28},{28,24},{1,5},{5... | collective-permute-start | bytes 983048 | tf_op jit(solution)/shard_map/ppermute | solution.py:129
  169.2 2.3 %add_convert_fusion = bf16[640,1024]{1,0:T(8,128)(2,1)} fusion(f32[640,1024]{1,0:T(8,128)S(1)} %fusion.19, bf16[768,1024]{1,0:T(8,128)(2,1)S(1)} %copy-done.16, bf16[768,1280]{1,0:T(8,128)(2,1)S(1)} %copy-done.13, s32[]{:T(128)S(6)} %select_n.169), kind=kOutput, calls=%fused_computation.6 | convolution fusion | flops 1007943680 | bytes 6488068 | tf_op jit(solution)/shard_map/td,tc->dc/dot_general | solution.py:233
  177.6 4.2 %convert_add_fusion = f32[640,1024]{1,0:T(8,128)} fusion(bf16[640,1024]{1,0:T(8,128)(2,1)} %collective-permute-done.21, f32[640,1024]{1,0:T(8,128)S(1)} %fusion.21, bf16[768,1024]{1,0:T(8,128)(2,1)S(1)} %copy-done.17, bf16[768,1280]{1,0:T(8,128)(2,1)S(1)} %copy-done.14, s32[]{:T(128)S(6)} %select_n.168), kind=kOutput, calls=%fused_computation.5 | convolution fusion | flops 1008599040 | bytes 9109508 | tf_op jit(solution)/shard_map/td,tc->dc/dot_general | solution.py:233
  (164 shorter events, 51.9 us)
Async XLA Ops:
  9.7 17.1 %all-to-all-start = ((bf16[8,32,1280]{2,1,0:T(8,128)(2,1)}), bf16[8,32,1280]{2,1,0:T(8,128)(2,1)S(1)}, u32[]{:S(2)}, u32[]{:S(2)}) async-start(bf16[8,32,1280]{2,1,0:T(8,128)(2,1)} %gather_fusion), calls=%async_computation | async-start | bytes 1310720 | tf_op jit(solution)/shard_map/all_to_all | solution.py:163
  14.3 68.4 %all-gather.2.cloned.1.call-start = ((), (), s32[]{:S(2)}) async-start(), calls=%async_computation.1 | async-start | bytes 3276800 | tf_op jit(solution)/shard_map/all_gather | solution.py:179
  18.9 8.0 %collective-permute-start.1 = (bf16[160,256]{1,0:T(8,128)(2,1)S(1)}, bf16[160,256]{1,0:T(8,128)(2,1)S(1)}, u32[]{:S(2)}, u32[]{:S(2)}) collective-permute-start(bf16[160,256]{1,0:T(8,128)(2,1)S(1)} %get-tuple-element.81), channel_id=1, source_target_pairs={{0,2},{1,3},{2,0},{3,1},{4,6},{5,7},{6,4},{7,5},{8,10},{9,11},{10,... | collective-permute-start | bytes 245768 | tf_op jit(solution)/shard_map/ppermute | solution.py:136
  18.9 8.0 %collective-permute-start = (bf16[160,256]{1,0:T(8,128)(2,1)S(1)}, bf16[160,256]{1,0:T(8,128)(2,1)S(1)}, u32[]{:S(2)}, u32[]{:S(2)}) collective-permute-start(bf16[160,256]{1,0:T(8,128)(2,1)S(1)} %get-tuple-element.82), channel_id=1, source_target_pairs={{0,1},{1,2},{2,3},{3,0},{4,5},{5,6},{6,7},{7,4},{8,9},{9,10},{10,1... | collective-permute-start | bytes 245768 | tf_op jit(solution)/shard_map/ppermute | solution.py:136
  28.4 8.6 %collective-permute-start.4 = (bf16[4,160,256]{2,1,0:T(8,128)(2,1)S(1)}, bf16[4,160,256]{2,1,0:T(8,128)(2,1)S(1)}, u32[]{:S(2)}, u32[]{:S(2)}) collective-permute-start(bf16[4,160,256]{2,1,0:T(8,128)(2,1)S(1)} %get-tuple-element.79), channel_id=1, source_target_pairs={{0,16},{4,20},{8,24},{12,28},{16,0},{20,4},{24,8},{28,12},{1,17},{... | collective-permute-start | bytes 983048 | tf_op jit(solution)/shard_map/ppermute | solution.py:129
  28.7 8.3 %collective-permute-start.3 = (bf16[4,160,256]{2,1,0:T(8,128)(2,1)S(1)}, bf16[4,160,256]{2,1,0:T(8,128)(2,1)S(1)}, u32[]{:S(2)}, u32[]{:S(2)}) collective-permute-start(bf16[4,160,256]{2,1,0:T(8,128)(2,1)S(1)} %get-tuple-element.79), channel_id=1, source_target_pairs={{0,8},{4,12},{8,0},{12,4},{16,24},{20,28},{24,16},{28,20},{1,9},{5... | collective-permute-start | bytes 983048 | tf_op jit(solution)/shard_map/ppermute | solution.py:129
  29.0 16.1 %collective-permute-start.5 = (bf16[4,160,256]{2,1,0:T(8,128)(2,1)S(1)}, bf16[4,160,256]{2,1,0:T(8,128)(2,1)S(1)}, u32[]{:S(2)}, u32[]{:S(2)}) collective-permute-start(bf16[4,160,256]{2,1,0:T(8,128)(2,1)S(1)} %get-tuple-element.79), channel_id=1, source_target_pairs={{0,24},{4,28},{8,16},{12,20},{16,8},{20,12},{24,0},{28,4},{1,25},{... | collective-permute-start | bytes 983048 | tf_op jit(solution)/shard_map/ppermute | solution.py:129
  45.2 18.2 %collective-permute-start.6 = (bf16[4,4,160,256]{3,2,1,0:T(8,128)(2,1)S(1)}, bf16[4,4,160,256]{3,2,1,0:T(8,128)(2,1)S(1)}, u32[]{:S(2)}, u32[]{:S(2)}) collective-permute-start(bf16[4,4,160,256]{3,2,1,0:T(8,128)(2,1)S(1)} %pad_maximum_fusion.2), channel_id=1, source_target_pairs={{0,4},{4,0},{8,12},{12,8},{16,20},{20,16},{24,28},{28,24},{1,5},{5... | collective-permute-start | bytes 3932168 | tf_op jit(solution)/shard_map/ppermute | solution.py:129
  47.1 16.4 %collective-permute-start.8 = (bf16[256,1280]{1,0:T(8,128)(2,1)S(1)}, bf16[256,1280]{1,0:T(8,128)(2,1)S(1)}, u32[]{:S(2)}, u32[]{:S(2)}) collective-permute-start(bf16[256,1280]{1,0:T(8,128)(2,1)S(1)} %bitcast.187), channel_id=1, source_target_pairs={{0,16},{4,20},{8,24},{12,28},{16,0},{20,4},{24,8},{28,12},{1,17},{... | collective-permute-start | bytes 1966088 | tf_op jit(solution)/shard_map/ppermute | solution.py:129
  47.3 16.1 %collective-permute-start.7 = (bf16[256,1280]{1,0:T(8,128)(2,1)S(1)}, bf16[256,1280]{1,0:T(8,128)(2,1)S(1)}, u32[]{:S(2)}, u32[]{:S(2)}) collective-permute-start(bf16[256,1280]{1,0:T(8,128)(2,1)S(1)} %bitcast.188), channel_id=1, source_target_pairs={{0,8},{4,12},{8,0},{12,4},{16,24},{20,28},{24,16},{28,20},{1,9},{5... | collective-permute-start | bytes 1966088 | tf_op jit(solution)/shard_map/ppermute | solution.py:129
  65.2 8.7 %collective-permute-start.10 = (bf16[128,1280]{1,0:T(8,128)(2,1)}, bf16[128,1280]{1,0:T(8,128)(2,1)}, u32[]{:S(2)}, u32[]{:S(2)}) collective-permute-start(bf16[128,1280]{1,0:T(8,128)(2,1)} %slice.64), channel_id=1, source_target_pairs={{0,8},{4,12},{8,0},{12,4},{16,24},{20,28},{24,16},{28,20},{1,9},{5... | collective-permute-start | bytes 983048 | tf_op jit(solution)/shard_map/ppermute | solution.py:129
  65.4 8.4 %collective-permute-start.9 = (bf16[128,1280]{1,0:T(8,128)(2,1)}, bf16[128,1280]{1,0:T(8,128)(2,1)}, u32[]{:S(2)}, u32[]{:S(2)}) collective-permute-start(bf16[128,1280]{1,0:T(8,128)(2,1)} %slice.63), channel_id=1, source_target_pairs={{0,16},{4,20},{8,24},{12,28},{16,0},{20,4},{24,8},{28,12},{1,17},{... | collective-permute-start | bytes 983048 | tf_op jit(solution)/shard_map/ppermute | solution.py:129
  95.8 38.8 %collective-permute-start.13 = (bf16[256,1280]{1,0:T(8,128)(2,1)}, bf16[256,1280]{1,0:T(8,128)(2,1)}, u32[]{:S(2)}, u32[]{:S(2)}) collective-permute-start(bf16[256,1280]{1,0:T(8,128)(2,1)} %get-tuple-element.60), channel_id=1, source_target_pairs={{0,24},{4,28},{8,16},{12,20},{16,8},{20,12},{24,0},{28,4},{1,25},{... | collective-permute-start | bytes 1966088 | tf_op jit(solution)/shard_map/ppermute | solution.py:129
  96.1 30.3 %collective-permute-start.12 = (bf16[256,1280]{1,0:T(8,128)(2,1)}, bf16[256,1280]{1,0:T(8,128)(2,1)}, u32[]{:S(2)}, u32[]{:S(2)}) collective-permute-start(bf16[256,1280]{1,0:T(8,128)(2,1)} %get-tuple-element.62), channel_id=1, source_target_pairs={{0,16},{4,20},{8,24},{12,28},{16,0},{20,4},{24,8},{28,12},{1,17},{... | collective-permute-start | bytes 1966088 | tf_op jit(solution)/shard_map/ppermute | solution.py:129
  97.3 29.1 %collective-permute-start.11 = (bf16[256,1280]{1,0:T(8,128)(2,1)}, bf16[256,1280]{1,0:T(8,128)(2,1)}, u32[]{:S(2)}, u32[]{:S(2)}) collective-permute-start(bf16[256,1280]{1,0:T(8,128)(2,1)} %get-tuple-element.63), channel_id=1, source_target_pairs={{0,8},{4,12},{8,0},{12,4},{16,24},{20,28},{24,16},{28,20},{1,9},{5... | collective-permute-start | bytes 1966088 | tf_op jit(solution)/shard_map/ppermute | solution.py:129
  134.7 6.7 %collective-permute-start.16 = (bf16[256,256]{0,1:T(8,128)(2,1)S(1)}, bf16[256,256]{0,1:T(8,128)(2,1)S(1)}, u32[]{:S(2)}, u32[]{:S(2)}) collective-permute-start(bf16[256,256]{0,1:T(8,128)(2,1)S(1)} %bitcast.205), channel_id=1, source_target_pairs={{0,3},{1,0},{2,1},{3,2},{4,7},{5,4},{6,5},{7,6},{8,11},{9,8},{10,9... | collective-permute-start | bytes 393224 | tf_op jit(solution)/shard_map/ppermute | solution.py:136
  135.4 12.0 %collective-permute-start.15 = (bf16[256,256]{0,1:T(8,128)(2,1)S(1)}, bf16[256,256]{0,1:T(8,128)(2,1)S(1)}, u32[]{:S(2)}, u32[]{:S(2)}) collective-permute-start(bf16[256,256]{0,1:T(8,128)(2,1)S(1)} %bitcast.206), channel_id=1, source_target_pairs={{0,2},{1,3},{2,0},{3,1},{4,6},{5,7},{6,4},{7,5},{8,10},{9,11},{10,... | collective-permute-start | bytes 393224 | tf_op jit(solution)/shard_map/ppermute | solution.py:136
  135.8 11.6 %collective-permute-start.14 = (bf16[256,256]{0,1:T(8,128)(2,1)S(1)}, bf16[256,256]{0,1:T(8,128)(2,1)S(1)}, u32[]{:S(2)}, u32[]{:S(2)}) collective-permute-start(bf16[256,256]{0,1:T(8,128)(2,1)S(1)} %bitcast.207), channel_id=1, source_target_pairs={{0,1},{1,2},{2,3},{3,0},{4,5},{5,6},{6,7},{7,4},{8,9},{9,10},{10,1... | collective-permute-start | bytes 393224 | tf_op jit(solution)/shard_map/ppermute | solution.py:136
  137.2 11.5 %collective-permute-start.18 = (bf16[256,1024]{1,0:T(8,128)(2,1)S(1)}, bf16[256,1024]{1,0:T(8,128)(2,1)S(1)}, u32[]{:S(2)}, u32[]{:S(2)}) collective-permute-start(bf16[256,1024]{1,0:T(8,128)(2,1)S(1)} %bitcast.196), channel_id=1, source_target_pairs={{0,16},{4,20},{8,24},{12,28},{16,0},{20,4},{24,8},{28,12},{1,17},{... | collective-permute-start | bytes 1572872 | tf_op jit(solution)/shard_map/ppermute | solution.py:129
  138.7 11.7 %collective-permute-start.17 = (bf16[256,1024]{1,0:T(8,128)(2,1)S(1)}, bf16[256,1024]{1,0:T(8,128)(2,1)S(1)}, u32[]{:S(2)}, u32[]{:S(2)}) collective-permute-start(bf16[256,1024]{1,0:T(8,128)(2,1)S(1)} %bitcast.197), channel_id=1, source_target_pairs={{0,8},{4,12},{8,0},{12,4},{16,24},{20,28},{24,16},{28,20},{1,9},{5... | collective-permute-start | bytes 1572872 | tf_op jit(solution)/shard_map/ppermute | solution.py:129
  150.5 5.8 %collective-permute-start.24 = (bf16[256,256]{0,1:T(8,128)(2,1)S(1)}, bf16[256,256]{0,1:T(8,128)(2,1)S(1)}, u32[]{:S(2)}, u32[]{:S(2)}) collective-permute-start(bf16[256,256]{0,1:T(8,128)(2,1)S(1)} %get-tuple-element.75), channel_id=1, source_target_pairs={{0,24},{4,28},{8,16},{12,20},{16,8},{20,12},{24,0},{28,4},{1,25},{... | collective-permute-start | bytes 393224 | tf_op jit(solution)/shard_map/ppermute | solution.py:129
  154.6 11.9 %collective-permute-start.20 = (bf16[128,1024]{1,0:T(8,128)(2,1)}, bf16[128,1024]{1,0:T(8,128)(2,1)}, u32[]{:S(2)}, u32[]{:S(2)}) collective-permute-start(bf16[128,1024]{1,0:T(8,128)(2,1)} %slice.68), channel_id=1, source_target_pairs={{0,8},{4,12},{8,0},{12,4},{16,24},{20,28},{24,16},{28,20},{1,9},{5... | collective-permute-start | bytes 786440 | tf_op jit(solution)/shard_map/ppermute | solution.py:129
  155.0 10.5 %collective-permute-start.19 = (bf16[128,1024]{1,0:T(8,128)(2,1)}, bf16[128,1024]{1,0:T(8,128)(2,1)}, u32[]{:S(2)}, u32[]{:S(2)}) collective-permute-start(bf16[128,1024]{1,0:T(8,128)(2,1)} %slice.67), channel_id=1, source_target_pairs={{0,16},{4,20},{8,24},{12,28},{16,0},{20,4},{24,8},{28,12},{1,17},{... | collective-permute-start | bytes 786440 | tf_op jit(solution)/shard_map/ppermute | solution.py:129
  161.1 14.2 %collective-permute-start.25 = (bf16[1280,128]{0,1:T(8,128)(2,1)}, bf16[1280,128]{0,1:T(8,128)(2,1)S(1)}, u32[]{:S(2)}, u32[]{:S(2)}) collective-permute-start(bf16[1280,128]{0,1:T(8,128)(2,1)} %select_convert_fusion), channel_id=1, source_target_pairs={{0,4},{4,0},{8,12},{12,8},{16,20},{20,16},{24,28},{28,24},{1,5},{5... | collective-permute-start | bytes 983048 | tf_op jit(solution)/shard_map/ppermute | solution.py:129
  (28 other events, 176.5 us)
Sparse Core Ops, SparseCore 0:
  28.4 54.2 all-gather.1

commit v4 on v3

--- a/solution.py
+++ b/solution.py
@@ -4,6 +4,8 @@
 import jax
 import jax.numpy as jnp
 from jax import lax
+from jax.experimental import pallas as pl
+from jax.experimental.pallas import tpu as pltpu
 from jax.sharding import PartitionSpec as P
 
 HEADS = 32
@@ -12,9 +14,8 @@
 BF16 = jnp.bfloat16
 
 
-def rms_scale(values, gain):
-    inverse = lax.rsqrt(jnp.mean(values * values, axis=-1, keepdims=True) + 1e-06)
-    return (values * inverse * gain, inverse)
+def dot(a, b, contract):
+    return lax.dot_general(a, b, ((contract[0], contract[1]), ((), ())), preferred_element_type=F32)
 
 
 def rms_back(values, inverse, gain, grad_out):
@@ -23,71 +24,141 @@
     return inverse * scaled - values * (inverse * inverse * inverse) * inner
 
 
-def forward_core(query, key_sum, value_sum, query_gain, key_gain):
-    scale = 1.0 / math.sqrt(query.shape[-1])
-    q_norm, q_inverse = rms_scale(query, query_gain)
-    k_norm, k_inverse = rms_scale(key_sum, key_gain)
-    q_half = q_norm.astype(jnp.bfloat16)
-    k_half = k_norm.astype(jnp.bfloat16)
-    v_half = value_sum.astype(jnp.bfloat16)
-    score_matrix = (
-        jnp.einsum("sqgph,skgh->sgpqk", q_half, k_half, preferred_element_type=jnp.float32) * scale
+def attend_tile(query, key, value, d_out, query_gain, key_gain, length):
+    tokens, dim = key.shape
+    heads = query.shape[1] // dim
+    scale = 1.0 / math.sqrt(dim)
+
+    def stack(wide):
+        return jnp.concatenate([wide[:, h * dim : (h + 1) * dim] for h in range(heads)], axis=0)
+
+    def unstack(tall):
+        return jnp.concatenate(
+            [tall[h * tokens : (h + 1) * tokens] for h in range(heads)], axis=1
+        )
+
+    query = stack(query)
+    q_inverse = lax.rsqrt(jnp.mean(query * query, axis=-1, keepdims=True) + 1e-06)
+    q_half = (query * q_inverse * query_gain).astype(BF16)
+    k_inverse = lax.rsqrt(jnp.mean(key * key, axis=-1, keepdims=True) + 1e-06)
+    k_half = (key * k_inverse * key_gain).astype(BF16)
+    v_half = value.astype(BF16)
+    out_half = stack(d_out).astype(BF16)
+
+    shape = (tokens, tokens)
+    row = lax.broadcasted_iota(jnp.int32, shape, 0)
+    col = lax.broadcasted_iota(jnp.int32, shape, 1)
+    size = jnp.full(shape, length, jnp.int32)
+    allowed = (row >= col) & (lax.div(row, size) == lax.div(col, size))
+    allowed = jnp.concatenate([allowed] * heads, axis=0)
+
+    scores = dot(q_half, k_half, ((1,), (1,))) * scale
+    scores = jnp.where(allowed, scores, -1e30)
+    raised = jnp.exp(scores - jnp.max(scores, axis=-1, keepdims=True))
+    probs = raised / jnp.sum(raised, axis=-1, keepdims=True)
+    p_half = probs.astype(BF16)
+    attended = dot(p_half, v_half, ((1,), (0,)))
+    d_probs = dot(out_half, v_half, ((1,), (1,)))
+    d_value = dot(p_half, out_half, ((0,), (0,)))
+    inner = jnp.sum(d_probs * probs, axis=-1, keepdims=True)
+    score_half = (probs * (d_probs - inner) * scale).astype(BF16)
+    d_qnorm = dot(score_half, k_half, ((1,), (0,)))
+    d_knorm = dot(score_half, q_half, ((0,), (0,)))
+    d_query = rms_back(query, q_inverse, query_gain, d_qnorm)
+    d_key = rms_back(key, k_inverse, key_gain, d_knorm)
+    return (
+        unstack(attended),
+        unstack(d_query),
+        d_key,
+        d_value,
     )
-    length = query.shape[1]
-    causal = lax.broadcasted_iota(jnp.int32, (length, length), 0) >= lax.broadcasted_iota(
-        jnp.int32, (length, length), 1
-    )
-    score_matrix = jnp.where(causal, score_matrix, -1e30)
-    peak = jnp.max(score_matrix, axis=-1, keepdims=True)
-    raised = jnp.exp(score_matrix - peak)
-    probs = raised / jnp.sum(raised, axis=-1, keepdims=True)
-    p_half = probs.astype(jnp.bfloat16)
-    attended = jnp.einsum("sgpqk,skgh->sqgph", p_half, v_half, preferred_element_type=jnp.float32)
-    return (attended, (q_inverse, k_inverse, q_half, k_half, v_half, probs, p_half))
-
-
-def backward_core(d_out, query, key_sum, query_gain, key_gain, saved):
-    q_inverse, k_inverse, q_half, k_half, v_half, probs, p_half = saved
-    scale = 1.0 / math.sqrt(query.shape[-1])
-    out_half = d_out.astype(jnp.bfloat16)
-    d_probs = jnp.einsum("sqgph,skgh->sgpqk", out_half, v_half, preferred_element_type=jnp.float32)
-    d_value = jnp.einsum("sgpqk,sqgph->skgh", p_half, out_half, preferred_element_type=jnp.float32)
-    d_scores = probs * (d_probs - jnp.sum(d_probs * probs, axis=-1, keepdims=True)) * scale
-    score_half = d_scores.astype(jnp.bfloat16)
-    d_qnorm = jnp.einsum(
-        "sgpqk,skgh->sqgph", score_half, k_half, preferred_element_type=jnp.float32
-    )
-    d_knorm = jnp.einsum(
-        "sgpqk,sqgph->skgh", score_half, q_half, preferred_element_type=jnp.float32
-    )
-    d_query = rms_back(query, q_inverse, query_gain, d_qnorm)
-    d_key = rms_back(key_sum, k_inverse, key_gain, d_knorm)
-    return (d_query, d_key, d_value)
-
-
-def attend(query, kv, cot, factor, query_gain, key_gain, length, device_cols, beside):
-    tokens = query.shape[0]
-    dim = query_gain.shape[0]
-    slots = tokens // length
-    heads = query.shape[1] // dim
-    query = query.reshape(slots, length, 1, heads, dim)
-    key = kv[:, :dim].reshape(slots, length, 1, dim)
-    value = kv[:, dim:].reshape(slots, length, 1, dim)
-    attended, saved = forward_core(query, key, value, query_gain, key_gain)
-    *saved, probs, p_half = saved
-    probs, *beside = together(probs, *beside)
-    saved = (*saved, probs, p_half)
-    d_out = cot.astype(F32).reshape(slots, length, 1, heads, dim)
-    d_out = d_out * factor[:, None, None, None, None]
-    d_query, d_key, d_value = backward_core(d_out, query, key, query_gain, key_gain, saved)
-    pairs = [d_key.reshape(tokens, -1, device_cols), d_value.reshape(tokens, -1, device_cols)]
-    d_kv = jnp.stack(pairs, axis=2).reshape(tokens, 2 * dim)
-    return (
-        attended.reshape(tokens, -1).astype(BF16),
-        d_query.reshape(tokens, -1).astype(BF16),
-        d_kv.astype(BF16),
-        beside,
-    )
+
+
+def attend_kernel(
+    length,
+    device_cols,
+    x_ref,
+    wq_ref,
+    wkv_ref,
+    d_out_ref,
+    query_gain_ref,
+    key_gain_ref,
+    attended_ref,
+    dq_ref,
+    dkv_ref,
+    query_ref,
+    kv_ref,
+):
+    step = pl.program_id(0)
+    x = x_ref[...]
+    query_part = jnp.dot(x, wq_ref[...], preferred_element_type=F32)
+    kv_part = jnp.dot(x, wkv_ref[...], preferred_element_type=F32)
+
+    @pl.when(step == 0)
+    def _():
+        query_ref[...] = query_part
+        kv_ref[...] = kv_part
+
+    @pl.when(step > 0)
+    def _():
+        query_ref[...] += query_part
+        kv_ref[...] += kv_part
+
+    @pl.when(step == pl.num_programs(0) - 1)
+    def _():
+        tokens = query_ref.shape[0]
+        dim = query_gain_ref.shape[1]
+        tile = min(tokens, max(1, 128 // length) * length)
+        for start in range(0, tokens, tile):
+            rows = slice(start, start + tile)
+            attended, d_query, d_key, d_value = attend_tile(
+                query_ref[rows, :],
+                kv_ref[rows, :dim],
+                kv_ref[rows, dim:],
+                d_out_ref[rows, :],
+                query_gain_ref[...],
+                key_gain_ref[...],
+                length,
+            )
+            attended_ref[rows, :] = attended
+            dq_ref[rows, :] = d_query
+            for first in range(0, dim, device_cols):
+                columns = slice(first, first + device_cols)
+                pair = jnp.concatenate([d_key[:, columns], d_value[:, columns]], axis=1)
+                dkv_ref[rows, 2 * first : 2 * first + 2 * device_cols] = pair
+
+
+def attend(x, w_query, w_kv, d_out, query_gain, key_gain, length, device_cols):
+    tokens, depth = x.shape
+    cols = w_query.shape[1]
+    kv_cols = w_kv.shape[1]
+    block = depth // 4
+    whole = lambda shape: pl.BlockSpec(shape, lambda b: (0, 0))
+    return pl.pallas_call(
+        functools.partial(attend_kernel, length, device_cols),
+        grid=(depth // block,),
+        in_specs=[
+            pl.BlockSpec((tokens, block), lambda b: (0, b)),
+            pl.BlockSpec((block, cols), lambda b: (b, 0)),
+            pl.BlockSpec((block, kv_cols), lambda b: (b, 0)),
+            whole(d_out.shape),
+            whole(query_gain.shape),
+            whole(key_gain.shape),
+        ],
+        out_specs=[whole((tokens, cols)), whole((tokens, cols)), whole((tokens, kv_cols))],
+        out_shape=[
+            jax.ShapeDtypeStruct((tokens, cols), F32),
+            jax.ShapeDtypeStruct((tokens, cols), F32),
+            jax.ShapeDtypeStruct((tokens, kv_cols), F32),
+        ],
+        scratch_shapes=[pltpu.VMEM((tokens, cols), F32), pltpu.VMEM((tokens, kv_cols), F32)],
+        compiler_params=pltpu.CompilerParams(vmem_limit_bytes=40 * 1024 * 1024),
+        cost_estimate=pl.CostEstimate(
+            flops=10 * tokens * depth * (cols + kv_cols),
+            bytes_accessed=8 * w_query.size,
+            transcendentals=tokens * cols,
+        ),
+    )(x, w_query, w_kv, d_out, query_gain, key_gain)
 
 
 def together(*values):
@@ -187,54 +258,43 @@
     w_kv = pick(shares, order.reshape(-1)).reshape(n_mp * width, 2 * dim)
 
     x, w_kv, plane_rows = together(x, w_kv, plane_rows)
-    query = jnp.dot(x, w_query, preferred_element_type=F32)
-    kv = jnp.dot(x, w_kv, preferred_element_type=F32)
 
     chip_width = n_mp * width // chips
     chip_rows = [
         lax.dynamic_slice_in_dim(x, (chip ^ k) * chip_width, chip_width, 1) for k in range(chips)
     ]
-    near_rows = [flip(chip_rows[k], 2 * k) for k in near]
+    x, *chip_rows = together(x, *chip_rows)
+    chip_rows = [chip_rows[0]] + other_chips(chip_rows)
 
     factor = multiplicity.astype(F32) * slot_weight / length
-    attended, d_query, d_kv, near_rows = attend(
-        query,
-        kv,
-        cotangent.reshape(tokens, query_cols),
-        factor,
-        query_gain,
-        key_gain,
+    d_out = (cotangent.astype(F32) * factor[:, None, None]).astype(BF16).astype(F32)
+    attended, d_query, d_kv = attend(
+        x,
+        w_query,
+        w_kv,
+        d_out.reshape(tokens, query_cols),
+        query_gain[None, :],
+        key_gain[None, :],
         length,
         key_cols // n_dp,
-        near_rows,
     )
-
-    near_rows = dict(zip(near, near_rows))
-    chip_rows = [
-        chip_rows[0] if k == 0 else near_rows[k] if k in near else flip(chip_rows[k], 2 * k)
-        for k in range(chips)
-    ]
+    attended, d_query, d_kv = [value.astype(BF16) for value in (attended, d_query, d_kv)]
     d_query, d_kv, *chip_rows = together(d_query, d_kv, *chip_rows)
 
-    d_near = from_near(d_query)
-    spread = around([d_kv] * n_mp)
-    spread, *d_near = together(jnp.stack(spread), *d_near)
-    d_all = from_far(d_query, d_near)
+    d_all = [d_query] + other_chips([d_query] * chips)
+    spread = jnp.stack(around([d_kv] * n_mp))
     half = chip_width // 2
     early = [0] + near
     late = [k for k in range(chips) if k not in early]
 
-    def query_half(which):
-        total = 0
-        for some in (early, late):
-            mine = jnp.concatenate([chip_rows[k] for k in some])
-            mine = lax.dynamic_slice_in_dim(mine, which * half, half, 1)
-            theirs = jnp.concatenate([d_all[k] for k in some])
-            total = total + jnp.einsum("td,tc->dc", mine, theirs, preferred_element_type=F32)
-        return total
-
-    other = flip(query_half(1 - core).astype(BF16), 1)
-    grad_query = query_half(core) + other.astype(F32)
+    def product(some, which):
+        mine = jnp.concatenate([chip_rows[k] for k in some])
+        mine = lax.dynamic_slice_in_dim(mine, which * half, half, 1)
+        theirs = jnp.concatenate([d_all[k] for k in some])
+        return jnp.einsum("td,tc->dc", mine, theirs, preferred_element_type=F32)
+
+    other = flip((product(early, 1 - core) + product(late, 1 - core)).astype(BF16), 1)
+    grad_query = product(late, core) + (product(early, core) + other.astype(F32))
 
     if n_mp > KV_HEADS:
         spread = pick(spread, (mp - jnp.arange(n_mp)) % n_mp)

time: 191 us -> 165 us (0.86)
  matrix products: 27.5 us -> 6.02 us
  local copies, waits for them, and re-layouts: 24.6 us -> 12.7 us
  Pallas kernels: 0 us -> 10.3 us
    dot_general x12 -> x4, matrix products: 24.8 us -> 5.12 us  [product(): return jnp.einsum('td,tc->dc', mine, theirs, preferred_element_type=F32)]
    pallas_call x0 -> x1, Pallas kernels: none -> 10.3 us  [attend(): pl.pallas_call(functools.partial(attend_kernel, length, device_cols), gri...]
    unnamed x55 -> x26, local copies, waits for them, and re-layouts: 5.55 us -> 0.57 us
    ppermute x6, waiting for transfers between devices: 13.4 us -> 16.7 us  [around(): lax.ppermute(blocks[k], 'mp', [(i, (i + k) % n_mp) for i in range(n_mp)])]
    concatenate x3 -> x2, local copies, waits for them, and re-layouts: 2.29 us -> 0.08 us  [the longest x1 0.04 us: product(): mine = jnp.concatenate([chip_rows[k] for k in some])]
    another operation x4 -> x0, local copies, waits for them, and re-layouts: 2.05 us -> none  [the longest x3 1.84 us: attend(): d_kv = jnp.stack(pairs, axis=2).reshape(tokens, 2 * dim)]
    ppermute x20 -> x19, waiting for transfers between devices: 59.1 us -> 57.3 us  [flip(): return lax.ppermute(block, 'dp', [(i, i ^ bits) for i in range(n_dp)])]
    ppermute x20 -> x19, starting transfers between devices: 20.2 us -> 18.8 us  [flip(): return lax.ppermute(block, 'dp', [(i, i ^ bits) for i in range(n_dp)])]
  transfers between devices with their start and end apart: 28 -> 27, of which waited for: 12 -> 14; matrix products, arithmetic and copies ran while one was open for 22% -> 14% of each run, Pallas kernels for 0% -> 6%
where the time goes in v4:
time: 165 us; the launch traced here: 163 us
  waiting for transfers between devices  77.6 us (47%)
  starting transfers between devices  29.6 us (18%)
  between operations  14.3 us (9%)
  local copies, waits for them, and re-layouts  12.7 us (8%)
  other arithmetic  12.2 us (7%)
  Pallas kernels  10.3 us (6%)
  matrix products  6.02 us (4%)
    ppermute x19, waiting for transfers between devices, flip(): return lax.ppermute(block, 'dp', [(i, i ^ bits) for i in range(n_dp)])  57.3 us
    ppermute x19, starting transfers between devices, flip(): return lax.ppermute(block, 'dp', [(i, i ^ bits) for i in range(n_dp)])  18.8 us
    ppermute x6, waiting for transfers between devices, around(): lax.ppermute(blocks[k], 'mp', [(i, (i + k) % n_mp) for i in range(n_mp)])  16.7 us
    pallas_call x1, Pallas kernels, attend(): pl.pallas_call(functools.partial(attend_kernel, length, device_cols), gri...  10.3 us
    ppermute x6, starting transfers between devices, around(): lax.ppermute(blocks[k], 'mp', [(i, (i + k) % n_mp) for i in range(n_mp)])  6.15 us
    gather x3, local copies, waits for them, and re-layouts, pick(): return array.at[index].get(mode='promise_in_bounds')  5.32 us
    dot_general x4, matrix products, product(): return jnp.einsum('td,tc->dc', mine, theirs, preferred_element_type=F32)  5.12 us
    all_to_all x1, starting transfers between devices, local(): lax.all_to_all(outgoing, 'dp', split_axis=0, concat_axis=0, tiled=True)  4.64 us
  transfers between devices with their start and end apart: 27, of which 14 were waited for; matrix products, arithmetic and copies ran while one was open for 14% of the time, Pallas kernels for 6%

profile of v4, /device:TPU:7, one launch (start us, length us, event | category | flops | bytes accessed | tf_op | source)
XLA Modules:
  0.0 162.7 jit_solution(15310345418670924693)
XLA Ops:
  9.7 4.6 %all-to-all-start = ((bf16[8,32,1280]{2,1,0:T(8,128)(2,1)}), bf16[8,32,1280]{2,1,0:T(8,128)(2,1)S(1)}, u32[]{:S(2)}, u32[]{:S(2)}) async-start(bf16[8,32,1280]{2,1,0:T(8,128)(2,1)} %gather_fusion), calls=%async_computation | async-start | bytes 1310720 | tf_op jit(solution)/shard_map/all_to_all | solution.py:234
  15.5 3.4 %collective-permute-start.2 = (bf16[160,256]{1,0:T(8,128)(2,1)S(1)}, bf16[160,256]{1,0:T(8,128)(2,1)S(1)}, u32[]{:S(2)}, u32[]{:S(2)}) collective-permute-start(bf16[160,256]{1,0:T(8,128)(2,1)S(1)} %get-tuple-element.84), channel_id=1, source_target_pairs={{0,3},{1,0},{2,1},{3,2},{4,7},{5,4},{6,5},{7,6},{8,11},{9,8},{10,9... | collective-permute-start | bytes 245768 | tf_op jit(solution)/shard_map/ppermute | solution.py:207
  20.3 6.5 %collective-permute-done.1 = bf16[160,256]{1,0:T(8,128)(2,1)S(1)} collective-permute-done((bf16[160,256]{1,0:T(8,128)(2,1)S(1)}, bf16[160,256]{1,0:T(8,128)(2,1)S(1)}, u32[]{:S(2)}, u32[]{:S(2)}) %collective-permute-start.1) | collective-permute-done | bytes 81952 | tf_op jit(solution)/shard_map/ppermute | solution.py:207
  29.0 2.1 %collective-permute-start.5 = (bf16[4,160,256]{2,1,0:T(8,128)(2,1)S(1)}, bf16[4,160,256]{2,1,0:T(8,128)(2,1)S(1)}, u32[]{:S(2)}, u32[]{:S(2)}) collective-permute-start(bf16[4,160,256]{2,1,0:T(8,128)(2,1)S(1)} %get-tuple-element.83), channel_id=1, source_target_pairs={{0,24},{4,28},{8,16},{12,20},{16,8},{20,12},{24,0},{28,4},{1,25},{... | collective-permute-start | bytes 983048 | tf_op jit(solution)/shard_map/ppermute | solution.py:200
  31.1 5.9 %collective-permute-done.4 = bf16[4,160,256]{2,1,0:T(8,128)(2,1)S(1)} collective-permute-done((bf16[4,160,256]{2,1,0:T(8,128)(2,1)S(1)}, bf16[4,160,256]{2,1,0:T(8,128)(2,1)S(1)}, u32[]{:S(2)}, u32[]{:S(2)}) %collective-permute-start.4) | collective-permute-done | bytes 327712 | tf_op jit(solution)/shard_map/ppermute | solution.py:200
  37.1 8.0 %collective-permute-done.5 = bf16[4,160,256]{2,1,0:T(8,128)(2,1)S(1)} collective-permute-done((bf16[4,160,256]{2,1,0:T(8,128)(2,1)S(1)}, bf16[4,160,256]{2,1,0:T(8,128)(2,1)S(1)}, u32[]{:S(2)}, u32[]{:S(2)}) %collective-permute-start.5) | collective-permute-done | bytes 327712 | tf_op jit(solution)/shard_map/ppermute | solution.py:200
  45.2 1.8 %collective-permute-start.6 = (bf16[4,4,160,256]{3,2,1,0:T(8,128)(2,1)S(1)}, bf16[4,4,160,256]{3,2,1,0:T(8,128)(2,1)}, u32[]{:S(2)}, u32[]{:S(2)}) collective-permute-start(bf16[4,4,160,256]{3,2,1,0:T(8,128)(2,1)S(1)} %pad_maximum_fusion.2), channel_id=1, source_target_pairs={{0,4},{4,0},{8,12},{12,8},{16,20},{20,16},{24,28},{28,24},{1,5},{5... | collective-permute-start | bytes 3932168 | tf_op jit(solution)/shard_map/ppermute | solution.py:200
  48.8 14.6 %collective-permute-done.8 = bf16[256,1280]{1,0:T(8,128)(2,1)S(1)} collective-permute-done((bf16[256,1280]{1,0:T(8,128)(2,1)S(1)}, bf16[256,1280]{1,0:T(8,128)(2,1)S(1)}, u32[]{:S(2)}, u32[]{:S(2)}) %collective-permute-start.8) | collective-permute-done | bytes 655392 | tf_op jit(solution)/shard_map/ppermute | solution.py:200
  63.5 2.0 %slice.50 = bf16[128,1280]{1,0:T(8,128)(2,1)} slice(bf16[256,1280]{1,0:T(8,128)(2,1)} %collective-permute-done.7), slice={[0:128], [0:1280]} | slice | bytes 655360 | tf_op jit(solution)/shard_map/slice | solution.py:225
  68.5 3.1 %pad_maximum_fusion = bf16[4,2,4,160,256]{4,3,2,1,0:T(8,128)(2,1)} fusion(bf16[4,1,4,160,256]{4,3,2,1,0:T(8,128)(2,1)} %bitcast.20, bf16[4,1,4,160,256]{4,3,2,1,0:T(8,128)(2,1)S(1)} %bitcast.77), kind=kLoop, calls=%fused_computation.3 | loop fusion | flops 1310720 | bytes 5242880 | tf_op jit(solution)/shard_map/stack | solution.py:256
  71.6 2.5 %gather_fusion.2 = bf16[32,160,256]{2,1,0:T(8,128)(2,1)S(1)} fusion(bf16[32,160,256]{2,1,0:T(8,128)(2,1)} %bitcast.72, s32[1024]{0:T(1024)S(1)} %get-tuple-element.88), kind=kCustom, calls=%fused_computation.2 | custom fusion | bytes 5243008 | tf_op jit(solution)/shard_map/gather | solution.py:169
  75.9 3.3 %pad_maximum_fusion.1 = bf16[4,256,1280]{2,1,0:T(8,128)(2,1)} fusion(bf16[1,256,1280]{2,1,0:T(8,128)(2,1)S(1)} %maximum_bitcast_fusion, bf16[1,256,1280]{2,1,0:T(8,128)(2,1)} %bitcast.79, bf16[1,256,1280]{2,1,0:T(8,128)(2,1)} %bitcast.25, bf16[1,256,1280]{2,1,0:T(8,128)(2,1)} %bitcast.74), kind=kLoop, calls=%fused_computation.4 | loop fusion | flops 3932160 | bytes 5242880 | tf_op jit(solution)/shard_map/stack | solution.py:254
  79.2 3.5 %all-gather.2.cloned.1.call-done.x_ref = bf16[256,5120]{1,0:T(8,128)(2,1)} async-done(((bf16[256,1280]{1,0:T(8,128)(2,1)}), bf16[256,5120]{1,0:T(8,128)(2,1)}) %all-gather.2.cloned.1.call-update) | async-done | bytes 2621456 | tf_op jit(solution)/shard_map/all_gather | solution.py:250
  82.7 2.0 %constant_dynamic-slice_fusion.3 = (bf16[256,1280]{1,0:T(8,128)(2,1)S(1)}, bf16[256,1280]{1,0:T(8,128)(2,1)S(1)}, bf16[256,1280]{1,0:T(8,128)(2,1)S(1)}, bf16[256,1280]{1,0:T(8,128)(2,1)S(1)}) fusion(bf16[256,5120]{1,0:T(8,128)(2,1)} %all-gather.2.cloned.1.call-done.x_ref, s32[]{:T(128)S(6)} %select_n.161, s32[]{:T(128)S(6)} %select_n.160, ...), kind=kLoop, calls=%fused_computation.47 | loop fusion | bytes 5242896 | tf_op jit(solution)/shard_map/dynamic_slice | solution.py:264
  85.4 2.1 %collective-permute-start.13 = (bf16[256,1280]{1,0:T(8,128)(2,1)S(1)}, bf16[256,1280]{1,0:T(8,128)(2,1)S(1)}, u32[]{:S(2)}, u32[]{:S(2)}) collective-permute-start(bf16[256,1280]{1,0:T(8,128)(2,1)S(1)} %get-tuple-element.56), channel_id=1, source_target_pairs={{0,24},{4,28},{8,16},{12,20},{16,8},{20,12},{24,0},{28,4},{1,25},{... | collective-permute-start | bytes 1966088 | tf_op jit(solution)/shard_map/ppermute | solution.py:200
  87.5 10.3 %shard_map.138 = (f32[256,1024]{1,0:T(8,128)S(1)}, f32[256,1024]{1,0:T(8,128)S(1)}, f32[256,256]{1,0:T(8,128)S(1)}) custom-call(bf16[256,5120]{1,0:T(8,128)(2,1)S(1)} %copy-done.1, bf16[5120,1024]{1,0:T(8,128)(2,1)} %wq_ref.1, bf16[5120,256]{1,0:T(8,128)(2,1)S(1)} %bitcast.68, f32[256,1024]{1,0:T(8,128)S(1)} %copy-done.2, f32[1,128]{1,0:T(1,128)S(1)} %bitcast.69, ...), custom_call_target="tpu_custom_call" | custom-call | flops 16777216000 | bytes 41943040 | tf_op jit(solution)/shard_map/pallas_call | solution.py:137
  98.7 1.7 %collective-permute-done.11 = bf16[256,1280]{1,0:T(8,128)(2,1)S(1)} collective-permute-done((bf16[256,1280]{1,0:T(8,128)(2,1)S(1)}, bf16[256,1280]{1,0:T(8,128)(2,1)S(1)}, u32[]{:S(2)}, u32[]{:S(2)}) %collective-permute-start.11) | collective-permute-done | bytes 655392 | tf_op jit(solution)/shard_map/ppermute | solution.py:200
  100.4 14.1 %collective-permute-done.13 = bf16[256,1280]{1,0:T(8,128)(2,1)S(1)} collective-permute-done((bf16[256,1280]{1,0:T(8,128)(2,1)S(1)}, bf16[256,1280]{1,0:T(8,128)(2,1)S(1)}, u32[]{:S(2)}, u32[]{:S(2)}) %collective-permute-start.13) | collective-permute-done | bytes 655392 | tf_op jit(solution)/shard_map/ppermute | solution.py:200
  118.4 9.4 %collective-permute-done.19 = bf16[256,256]{1,0:T(8,128)(2,1)S(1)} collective-permute-done((bf16[256,256]{1,0:T(8,128)(2,1)S(1)}, bf16[256,256]{1,0:T(8,128)(2,1)S(1)}, u32[]{:S(2)}, u32[]{:S(2)}) %collective-permute-start.19) | collective-permute-done | bytes 131104 | tf_op jit(solution)/shard_map/ppermute | solution.py:207
  130.7 2.8 %collective-permute-done.23 = bf16[256,256]{1,0:T(8,128)(2,1)S(1)} collective-permute-done((bf16[256,256]{1,0:T(8,128)(2,1)S(1)}, bf16[256,256]{1,0:T(8,128)(2,1)S(1)}, u32[]{:S(2)}, u32[]{:S(2)}) %collective-permute-start.23) | collective-permute-done | bytes 131104 | tf_op jit(solution)/shard_map/ppermute | solution.py:200
  134.8 2.3 %collective-permute-done.22 = bf16[256,256]{1,0:T(8,128)(2,1)S(1)} collective-permute-done((bf16[256,256]{1,0:T(8,128)(2,1)S(1)}, bf16[256,256]{1,0:T(8,128)(2,1)S(1)}, u32[]{:S(2)}, u32[]{:S(2)}) %collective-permute-start.22) | collective-permute-done | bytes 131104 | tf_op jit(solution)/shard_map/ppermute | solution.py:200
  139.3 6.6 %collective-permute-done.14 = bf16[256,1024]{1,0:T(8,128)(2,1)S(1)} collective-permute-done((bf16[256,1024]{1,0:T(8,128)(2,1)S(1)}, bf16[256,1024]{1,0:T(8,128)(2,1)S(1)}, u32[]{:S(2)}, u32[]{:S(2)}) %collective-permute-start.14) | collective-permute-done | bytes 524320 | tf_op jit(solution)/shard_map/ppermute | solution.py:200
  147.7 3.4 %collective-permute-start.17 = (bf16[640,1024]{1,0:T(8,128)(2,1)S(1)}, bf16[640,1024]{1,0:T(8,128)(2,1)S(1)}, u32[]{:S(2)}, u32[]{:S(2)}) collective-permute-start(bf16[640,1024]{1,0:T(8,128)(2,1)S(1)} %add_convert_fusion), channel_id=1, source_target_pairs={{0,4},{4,0},{8,12},{12,8},{16,20},{20,16},{24,28},{28,24},{1,5},{5... | collective-permute-start | bytes 3932168 | tf_op jit(solution)/shard_map/ppermute | solution.py:200
  153.8 2.1 %add_add_fusion = f32[640,1024]{1,0:T(8,128)} fusion(f32[640,1024]{1,0:T(8,128)S(1)} %fusion.1, bf16[640,1024]{1,0:T(8,128)(2,1)S(1)} %collective-permute-done.17, bf16[256,1024]{1,0:T(8,128)(2,1)S(1)} %collective-permute-done.14, bf16[256,1280]{1,0:T(8,128)(2,1)S(1)} %collective-permute-done.13, s32[]{:T(128)S(6)} %select_n.163), kind=kOutput, calls=%fused_computation.5 | convolution fusion | flops 337510400 | bytes 7405572 | tf_op jit(solution)/shard_map/td,tc->dc/dot_general | solution.py:294
  (104 shorter events, 30.3 us)
Async XLA Ops:
  9.7 17.1 %all-to-all-start = ((bf16[8,32,1280]{2,1,0:T(8,128)(2,1)}), bf16[8,32,1280]{2,1,0:T(8,128)(2,1)S(1)}, u32[]{:S(2)}, u32[]{:S(2)}) async-start(bf16[8,32,1280]{2,1,0:T(8,128)(2,1)} %gather_fusion), calls=%async_computation | async-start | bytes 1310720 | tf_op jit(solution)/shard_map/all_to_all | solution.py:234
  14.3 68.4 %all-gather.2.cloned.1.call-start = ((), (), s32[]{:S(2)}) async-start(), calls=%async_computation.1 | async-start | bytes 3276800 | tf_op jit(solution)/shard_map/all_gather | solution.py:250
  18.9 8.0 %collective-permute-start.1 = (bf16[160,256]{1,0:T(8,128)(2,1)S(1)}, bf16[160,256]{1,0:T(8,128)(2,1)S(1)}, u32[]{:S(2)}, u32[]{:S(2)}) collective-permute-start(bf16[160,256]{1,0:T(8,128)(2,1)S(1)} %get-tuple-element.85), channel_id=1, source_target_pairs={{0,2},{1,3},{2,0},{3,1},{4,6},{5,7},{6,4},{7,5},{8,10},{9,11},{10,... | collective-permute-start | bytes 245768 | tf_op jit(solution)/shard_map/ppermute | solution.py:207
  18.9 8.0 %collective-permute-start = (bf16[160,256]{1,0:T(8,128)(2,1)S(1)}, bf16[160,256]{1,0:T(8,128)(2,1)S(1)}, u32[]{:S(2)}, u32[]{:S(2)}) collective-permute-start(bf16[160,256]{1,0:T(8,128)(2,1)S(1)} %get-tuple-element.86), channel_id=1, source_target_pairs={{0,1},{1,2},{2,3},{3,0},{4,5},{5,6},{6,7},{7,4},{8,9},{9,10},{10,1... | collective-permute-start | bytes 245768 | tf_op jit(solution)/shard_map/ppermute | solution.py:207
  28.4 8.6 %collective-permute-start.4 = (bf16[4,160,256]{2,1,0:T(8,128)(2,1)S(1)}, bf16[4,160,256]{2,1,0:T(8,128)(2,1)S(1)}, u32[]{:S(2)}, u32[]{:S(2)}) collective-permute-start(bf16[4,160,256]{2,1,0:T(8,128)(2,1)S(1)} %get-tuple-element.83), channel_id=1, source_target_pairs={{0,16},{4,20},{8,24},{12,28},{16,0},{20,4},{24,8},{28,12},{1,17},{... | collective-permute-start | bytes 983048 | tf_op jit(solution)/shard_map/ppermute | solution.py:200
  28.8 8.3 %collective-permute-start.3 = (bf16[4,160,256]{2,1,0:T(8,128)(2,1)S(1)}, bf16[4,160,256]{2,1,0:T(8,128)(2,1)S(1)}, u32[]{:S(2)}, u32[]{:S(2)}) collective-permute-start(bf16[4,160,256]{2,1,0:T(8,128)(2,1)S(1)} %get-tuple-element.83), channel_id=1, source_target_pairs={{0,8},{4,12},{8,0},{12,4},{16,24},{20,28},{24,16},{28,20},{1,9},{5... | collective-permute-start | bytes 983048 | tf_op jit(solution)/shard_map/ppermute | solution.py:200
  29.0 16.0 %collective-permute-start.5 = (bf16[4,160,256]{2,1,0:T(8,128)(2,1)S(1)}, bf16[4,160,256]{2,1,0:T(8,128)(2,1)S(1)}, u32[]{:S(2)}, u32[]{:S(2)}) collective-permute-start(bf16[4,160,256]{2,1,0:T(8,128)(2,1)S(1)} %get-tuple-element.83), channel_id=1, source_target_pairs={{0,24},{4,28},{8,16},{12,20},{16,8},{20,12},{24,0},{28,4},{1,25},{... | collective-permute-start | bytes 983048 | tf_op jit(solution)/shard_map/ppermute | solution.py:200
  45.2 18.2 %collective-permute-start.6 = (bf16[4,4,160,256]{3,2,1,0:T(8,128)(2,1)S(1)}, bf16[4,4,160,256]{3,2,1,0:T(8,128)(2,1)}, u32[]{:S(2)}, u32[]{:S(2)}) collective-permute-start(bf16[4,4,160,256]{3,2,1,0:T(8,128)(2,1)S(1)} %pad_maximum_fusion.2), channel_id=1, source_target_pairs={{0,4},{4,0},{8,12},{12,8},{16,20},{20,16},{24,28},{28,24},{1,5},{5... | collective-permute-start | bytes 3932168 | tf_op jit(solution)/shard_map/ppermute | solution.py:200
  47.0 16.4 %collective-permute-start.8 = (bf16[256,1280]{1,0:T(8,128)(2,1)S(1)}, bf16[256,1280]{1,0:T(8,128)(2,1)S(1)}, u32[]{:S(2)}, u32[]{:S(2)}) collective-permute-start(bf16[256,1280]{1,0:T(8,128)(2,1)S(1)} %bitcast.75), channel_id=1, source_target_pairs={{0,16},{4,20},{8,24},{12,28},{16,0},{20,4},{24,8},{28,12},{1,17},{... | collective-permute-start | bytes 1966088 | tf_op jit(solution)/shard_map/ppermute | solution.py:200
  47.3 16.1 %collective-permute-start.7 = (bf16[256,1280]{1,0:T(8,128)(2,1)S(1)}, bf16[256,1280]{1,0:T(8,128)(2,1)}, u32[]{:S(2)}, u32[]{:S(2)}) collective-permute-start(bf16[256,1280]{1,0:T(8,128)(2,1)S(1)} %bitcast.76), channel_id=1, source_target_pairs={{0,8},{4,12},{8,0},{12,4},{16,24},{20,28},{24,16},{28,20},{1,9},{5... | collective-permute-start | bytes 1966088 | tf_op jit(solution)/shard_map/ppermute | solution.py:200
  66.2 8.6 %collective-permute-start.10 = (bf16[128,1280]{1,0:T(8,128)(2,1)}, bf16[128,1280]{1,0:T(8,128)(2,1)}, u32[]{:S(2)}, u32[]{:S(2)}) collective-permute-start(bf16[128,1280]{1,0:T(8,128)(2,1)} %slice.51), channel_id=1, source_target_pairs={{0,8},{4,12},{8,0},{12,4},{16,24},{20,28},{24,16},{28,20},{1,9},{5... | collective-permute-start | bytes 983048 | tf_op jit(solution)/shard_map/ppermute | solution.py:200
  66.4 8.4 %collective-permute-start.9 = (bf16[128,1280]{1,0:T(8,128)(2,1)}, bf16[128,1280]{1,0:T(8,128)(2,1)}, u32[]{:S(2)}, u32[]{:S(2)}) collective-permute-start(bf16[128,1280]{1,0:T(8,128)(2,1)} %slice.50), channel_id=1, source_target_pairs={{0,16},{4,20},{8,24},{12,28},{16,0},{20,4},{24,8},{28,12},{1,17},{... | collective-permute-start | bytes 983048 | tf_op jit(solution)/shard_map/ppermute | solution.py:200
  84.8 15.7 %collective-permute-start.11 = (bf16[256,1280]{1,0:T(8,128)(2,1)S(1)}, bf16[256,1280]{1,0:T(8,128)(2,1)S(1)}, u32[]{:S(2)}, u32[]{:S(2)}) collective-permute-start(bf16[256,1280]{1,0:T(8,128)(2,1)S(1)} %get-tuple-element.54), channel_id=1, source_target_pairs={{0,8},{4,12},{8,0},{12,4},{16,24},{20,28},{24,16},{28,20},{1,9},{5... | collective-permute-start | bytes 1966088 | tf_op jit(solution)/shard_map/ppermute | solution.py:200
  85.1 15.3 %collective-permute-start.12 = (bf16[256,1280]{1,0:T(8,128)(2,1)S(1)}, bf16[256,1280]{1,0:T(8,128)(2,1)S(1)}, u32[]{:S(2)}, u32[]{:S(2)}) collective-permute-start(bf16[256,1280]{1,0:T(8,128)(2,1)S(1)} %get-tuple-element.55), channel_id=1, source_target_pairs={{0,16},{4,20},{8,24},{12,28},{16,0},{20,4},{24,8},{28,12},{1,17},{... | collective-permute-start | bytes 1966088 | tf_op jit(solution)/shard_map/ppermute | solution.py:200
  85.4 29.1 %collective-permute-start.13 = (bf16[256,1280]{1,0:T(8,128)(2,1)S(1)}, bf16[256,1280]{1,0:T(8,128)(2,1)S(1)}, u32[]{:S(2)}, u32[]{:S(2)}) collective-permute-start(bf16[256,1280]{1,0:T(8,128)(2,1)S(1)} %get-tuple-element.56), channel_id=1, source_target_pairs={{0,24},{4,28},{8,16},{12,20},{16,8},{20,12},{24,0},{28,4},{1,25},{... | collective-permute-start | bytes 1966088 | tf_op jit(solution)/shard_map/ppermute | solution.py:200
  115.8 12.0 %collective-permute-start.19 = (bf16[256,256]{1,0:T(8,128)(2,1)S(1)}, bf16[256,256]{1,0:T(8,128)(2,1)S(1)}, u32[]{:S(2)}, u32[]{:S(2)}) collective-permute-start(bf16[256,256]{1,0:T(8,128)(2,1)S(1)} %convert_element_type.36), channel_id=1, source_target_pairs={{0,2},{1,3},{2,0},{3,1},{4,6},{5,7},{6,4},{7,5},{8,10},{9,11},{10,... | collective-permute-start | bytes 393224 | tf_op jit(solution)/shard_map/ppermute | solution.py:207
  115.8 12.0 %collective-permute-start.18 = (bf16[256,256]{1,0:T(8,128)(2,1)S(1)}, bf16[256,256]{1,0:T(8,128)(2,1)S(1)}, u32[]{:S(2)}, u32[]{:S(2)}) collective-permute-start(bf16[256,256]{1,0:T(8,128)(2,1)S(1)} %convert_element_type.36), channel_id=1, source_target_pairs={{0,1},{1,2},{2,3},{3,0},{4,5},{5,6},{6,7},{7,4},{8,9},{9,10},{10,1... | collective-permute-start | bytes 393224 | tf_op jit(solution)/shard_map/ppermute | solution.py:207
  116.8 22.4 %collective-permute-start.16 = (bf16[256,1024]{1,0:T(8,128)(2,1)S(1)}, bf16[256,1024]{1,0:T(8,128)(2,1)S(1)}, u32[]{:S(2)}, u32[]{:S(2)}) collective-permute-start(bf16[256,1024]{1,0:T(8,128)(2,1)S(1)} %convert_element_type.35), channel_id=1, source_target_pairs={{0,16},{4,20},{8,24},{12,28},{16,0},{20,4},{24,8},{28,12},{1,17},{... | collective-permute-start | bytes 1572872 | tf_op jit(solution)/shard_map/ppermute | solution.py:200
  118.0 21.2 %collective-permute-start.15 = (bf16[256,1024]{1,0:T(8,128)(2,1)S(1)}, bf16[256,1024]{1,0:T(8,128)(2,1)S(1)}, u32[]{:S(2)}, u32[]{:S(2)}) collective-permute-start(bf16[256,1024]{1,0:T(8,128)(2,1)S(1)} %convert_element_type.35), channel_id=1, source_target_pairs={{0,8},{4,12},{8,0},{12,4},{16,24},{20,28},{24,16},{28,20},{1,9},{5... | collective-permute-start | bytes 1572872 | tf_op jit(solution)/shard_map/ppermute | solution.py:200
  129.2 7.9 %collective-permute-start.22 = (bf16[256,256]{1,0:T(8,128)(2,1)S(1)}, bf16[256,256]{1,0:T(8,128)(2,1)S(1)}, u32[]{:S(2)}, u32[]{:S(2)}) collective-permute-start(bf16[256,256]{1,0:T(8,128)(2,1)S(1)} %get-tuple-element.80), channel_id=1, source_target_pairs={{0,16},{4,20},{8,24},{12,28},{16,0},{20,4},{24,8},{28,12},{1,17},{... | collective-permute-start | bytes 393224 | tf_op jit(solution)/shard_map/ppermute | solution.py:200
  129.4 7.7 %collective-permute-start.21 = (bf16[256,256]{1,0:T(8,128)(2,1)S(1)}, bf16[256,256]{1,0:T(8,128)(2,1)S(1)}, u32[]{:S(2)}, u32[]{:S(2)}) collective-permute-start(bf16[256,256]{1,0:T(8,128)(2,1)S(1)} %get-tuple-element.81), channel_id=1, source_target_pairs={{0,8},{4,12},{8,0},{12,4},{16,24},{20,28},{24,16},{28,20},{1,9},{5... | collective-permute-start | bytes 393224 | tf_op jit(solution)/shard_map/ppermute | solution.py:200
  133.6 12.3 %collective-permute-start.14 = (bf16[256,1024]{1,0:T(8,128)(2,1)S(1)}, bf16[256,1024]{1,0:T(8,128)(2,1)S(1)}, u32[]{:S(2)}, u32[]{:S(2)}) collective-permute-start(bf16[256,1024]{1,0:T(8,128)(2,1)S(1)} %convert_element_type.35), channel_id=1, source_target_pairs={{0,24},{4,28},{8,16},{12,20},{16,8},{20,12},{24,0},{28,4},{1,25},{... | collective-permute-start | bytes 1572872 | tf_op jit(solution)/shard_map/ppermute | solution.py:200
  138.2 14.3 %collective-permute-start.24 = (bf16[1280,128]{0,1:T(8,128)(2,1)S(1)}, bf16[1280,128]{0,1:T(8,128)(2,1)S(1)}, u32[]{:S(2)}, u32[]{:S(2)}) collective-permute-start(bf16[1280,128]{0,1:T(8,128)(2,1)S(1)} %select_convert_fusion), channel_id=1, source_target_pairs={{0,4},{4,0},{8,12},{12,8},{16,20},{20,16},{24,28},{28,24},{1,5},{5... | collective-permute-start | bytes 983048 | tf_op jit(solution)/shard_map/ppermute | solution.py:200
  147.7 6.1 %collective-permute-start.17 = (bf16[640,1024]{1,0:T(8,128)(2,1)S(1)}, bf16[640,1024]{1,0:T(8,128)(2,1)S(1)}, u32[]{:S(2)}, u32[]{:S(2)}) collective-permute-start(bf16[640,1024]{1,0:T(8,128)(2,1)S(1)} %add_convert_fusion), channel_id=1, source_target_pairs={{0,4},{4,0},{8,12},{12,8},{16,20},{20,16},{24,28},{28,24},{1,5},{5... | collective-permute-start | bytes 3932168 | tf_op jit(solution)/shard_map/ppermute | solution.py:200
  (14 other events, 118.9 us)
Sparse Core Ops, SparseCore 0:
  28.4 54.2 all-gather.1

commit v5 on v4

--- a/solution.py
+++ b/solution.py
@@ -90,7 +90,7 @@
     kv_ref,
 ):
     step = pl.program_id(0)
-    x = x_ref[...]
+    x = x_ref[0]
     query_part = jnp.dot(x, wq_ref[...], preferred_element_type=F32)
     kv_part = jnp.dot(x, wkv_ref[...], preferred_element_type=F32)
 
@@ -129,18 +129,17 @@
 
 
 def attend(x, w_query, w_kv, d_out, query_gain, key_gain, length, device_cols):
-    tokens, depth = x.shape
+    blocks, tokens, width = x.shape
     cols = w_query.shape[1]
     kv_cols = w_kv.shape[1]
-    block = depth // 4
     whole = lambda shape: pl.BlockSpec(shape, lambda b: (0, 0))
     return pl.pallas_call(
         functools.partial(attend_kernel, length, device_cols),
-        grid=(depth // block,),
+        grid=(blocks,),
         in_specs=[
-            pl.BlockSpec((tokens, block), lambda b: (0, b)),
-            pl.BlockSpec((block, cols), lambda b: (b, 0)),
-            pl.BlockSpec((block, kv_cols), lambda b: (b, 0)),
+            pl.BlockSpec((1, tokens, width), lambda b: (b, 0, 0)),
+            pl.BlockSpec((width, cols), lambda b: (b, 0)),
+            pl.BlockSpec((width, kv_cols), lambda b: (b, 0)),
             whole(d_out.shape),
             whole(query_gain.shape),
             whole(key_gain.shape),
@@ -154,7 +153,7 @@
         scratch_shapes=[pltpu.VMEM((tokens, cols), F32), pltpu.VMEM((tokens, kv_cols), F32)],
         compiler_params=pltpu.CompilerParams(vmem_limit_bytes=40 * 1024 * 1024),
         cost_estimate=pl.CostEstimate(
-            flops=10 * tokens * depth * (cols + kv_cols),
+            flops=20 * x.size * (cols + kv_cols),
             bytes_accessed=8 * w_query.size,
             transcendentals=tokens * cols,
         ),
@@ -216,18 +215,18 @@
     def from_far(block, arrived):
         arrived = dict(zip(near, arrived))
         middle = block.shape[0] // 2
-        blocks = [block]
+        pieces = [[block]]
         for k in range(1, chips):
             bits = [n for n in near if k & n]
             if len(bits) == 1:
-                blocks.append(arrived[k])
+                pieces.append([arrived[k]])
             elif len(bits) == 2:
                 first = flip(arrived[bits[0]][:middle], 2 * bits[1])
                 second = flip(arrived[bits[1]][middle:], 2 * bits[0])
-                blocks.append(jnp.concatenate([first, second]))
+                pieces.append([first, second])
             else:
-                blocks.append(flip(block, 2 * k))
-        return blocks
+                pieces.append([flip(block, 2 * k)])
+        return pieces
 
     outgoing = pick(pool, jnp.maximum(send_table[0], 0))
     outgoing, w_key, w_value = together(outgoing, w_key, w_value)
@@ -243,58 +242,88 @@
     pairs = jnp.stack(pairs)
     heads = [(mp + k) % n_mp * KV_HEADS // n_mp for k in range(n_mp)]
     shares = around([lax.dynamic_index_in_dim(pairs, h, 0, False) for h in heads])
-    arrived, *shares = together(arrived, *shares)
     shares = jnp.stack(shares)
     rows = pick(arrived, slot_source).reshape(tokens, width)
 
-    x = lax.all_gather(rows, "mp", axis=1, tiled=True)
+    middle = tokens // 2
+    first_rows, second_rows = rows[:middle], rows[middle:]
+    x_first = lax.all_gather(first_rows, "mp", axis=0)
     shares = jnp.stack([shares] + other_chips([shares] * chips))
-    native, shares = together(rows, shares)
-    other_shares, *plane_rows = together(flip(shares, 1), *from_near(native))
-    plane_rows = jnp.stack(from_far(native, plane_rows)).reshape(chips * tokens, width)
+    native, second_rows, shares = together(rows, second_rows, shares)
+    x_second = lax.all_gather(second_rows, "mp", axis=0)
+    other_shares = flip(shares, 1)
+    plane_rows = together(*from_near(native))
+    plane_rows = from_far(native, plane_rows)
 
     shares = jnp.stack([shares, other_shares], axis=1).reshape(n_dp * n_mp, share, 2 * dim)
     order = (dp ^ jnp.arange(n_dp))[None, :] * n_mp + ((mp - jnp.arange(n_mp)) % n_mp)[:, None]
     w_kv = pick(shares, order.reshape(-1)).reshape(n_mp * width, 2 * dim)
 
-    x, w_kv, plane_rows = together(x, w_kv, plane_rows)
-
-    chip_width = n_mp * width // chips
-    chip_rows = [
-        lax.dynamic_slice_in_dim(x, (chip ^ k) * chip_width, chip_width, 1) for k in range(chips)
-    ]
-    x, *chip_rows = together(x, *chip_rows)
-    chip_rows = [chip_rows[0]] + other_chips(chip_rows)
-
     factor = multiplicity.astype(F32) * slot_weight / length
     d_out = (cotangent.astype(F32) * factor[:, None, None]).astype(BF16).astype(F32)
-    attended, d_query, d_kv = attend(
-        x,
-        w_query,
-        w_kv,
-        d_out.reshape(tokens, query_cols),
-        query_gain[None, :],
-        key_gain[None, :],
-        length,
-        key_cols // n_dp,
-    )
-    attended, d_query, d_kv = [value.astype(BF16) for value in (attended, d_query, d_kv)]
-    d_query, d_kv, *chip_rows = together(d_query, d_kv, *chip_rows)
-
-    d_all = [d_query] + other_chips([d_query] * chips)
+    d_out = d_out.reshape(tokens, query_cols)
+    chip_width = n_mp * width // chips
+
+    def chip_part(x, k):
+        if chip_width == width:
+            return lax.dynamic_index_in_dim(x, chip ^ k, 0, False)
+        flat = x.transpose(1, 0, 2).reshape(x.shape[1], -1)
+        return lax.dynamic_slice_in_dim(flat, (chip ^ k) * chip_width, chip_width, 1)
+
+    def half_step(x, d_out, beside):
+        x, *parts = together(x, *[chip_part(x, k) for k in range(chips)])
+        near_parts = [flip(parts[k], 2 * k) for k in near]
+        attended, d_query, d_kv = attend(
+            x, w_query, w_kv, d_out, query_gain[None, :], key_gain[None, :], length, key_cols // n_dp
+        )
+        d_query, d_kv, near_parts, beside = lax.optimization_barrier(
+            (d_query.astype(BF16), d_kv.astype(BF16), near_parts, beside)
+        )
+        near_parts = dict(zip(near, near_parts))
+        for k in range(1, chips):
+            parts[k] = near_parts[k] if k in near_parts else flip(parts[k], 2 * k)
+        d_query, *parts = together(d_query, *parts)
+        return attended.astype(BF16), d_query, d_kv, parts, beside
+
+    (x_first, *native_near) = together(x_first, *[plane_rows[k][0] for k in near])
+    for k, block in zip(near, native_near):
+        plane_rows[k] = [block]
+    attended, d_query, d_kv, first_parts, plane_rows = half_step(
+        x_first, d_out[:middle], plane_rows
+    )
+    first_all = [d_query] + other_chips([d_query] * chips)
+
+    half = chip_width // 2
+
+    def product(mine, theirs, which):
+        mine = lax.dynamic_slice_in_dim(jnp.concatenate(mine), which * half, half, 1)
+        return jnp.einsum("td,tc->dc", mine, jnp.concatenate(theirs), preferred_element_type=F32)
+
+    x_second, first_other, first_own = together(
+        x_second, product(first_parts, first_all, 1 - core), product(first_parts, first_all, core)
+    )
+    attended_second, d_query, d_kv_second, second_parts, _ = half_step(x_second, d_out[middle:], [])
+    second_all = [d_query] + other_chips([d_query] * chips)
+    attended = jnp.concatenate([attended, attended_second])
+    d_kv = jnp.concatenate([d_kv, d_kv_second])
     spread = jnp.stack(around([d_kv] * n_mp))
-    half = chip_width // 2
-    early = [0] + near
-    late = [k for k in range(chips) if k not in early]
-
-    def product(some, which):
-        mine = jnp.concatenate([chip_rows[k] for k in some])
-        mine = lax.dynamic_slice_in_dim(mine, which * half, half, 1)
-        theirs = jnp.concatenate([d_all[k] for k in some])
-        return jnp.einsum("td,tc->dc", mine, theirs, preferred_element_type=F32)
-
-    other = flip((product(early, 1 - core) + product(late, 1 - core)).astype(BF16), 1)
-    grad_query = product(late, core) + (product(early, core) + other.astype(F32))
+    spread, *second_near = together(spread, *[second_all[k] for k in near])
+    for k, block in zip(near, second_near):
+        second_all[k] = block
+
+    some = [0] + near
+    rest = [k for k in range(chips) if k not in some]
+
+    def second(which):
+        return [
+            product([second_parts[k] for k in ks], [second_all[k] for k in ks], which)
+            for ks in (some, rest)
+        ]
+
+    early, late = second(1 - core)
+    other = flip((late + (early + first_other)).astype(BF16), 1)
+    early, late = second(core)
+    grad_query = late + ((early + first_own) + other.astype(F32))
 
     if n_mp > KV_HEADS:
         spread = pick(spread, (mp - jnp.arange(n_mp)) % n_mp)
@@ -308,8 +337,13 @@
         spread = spread.reshape(KV_HEADS, tokens, chips // KV_HEADS, chip_cols)
         spread = spread.transpose(0, 2, 1, 3).reshape(chips, tokens, chip_cols)
     kv_all = [lax.dynamic_index_in_dim(spread, spread_at(chip ^ k), 0, False) for k in range(chips)]
-    kv_all = jnp.stack([kv_all[0]] + other_chips(kv_all)).reshape(chips * tokens, chip_cols)
-    partial = jnp.einsum("td,tc->dc", plane_rows, kv_all, preferred_element_type=F32)
+    kv_all = [kv_all[0]] + other_chips(kv_all)
+    partial = 0
+    for pieces, columns in zip(plane_rows, kv_all):
+        size = tokens // len(pieces)
+        for i, piece in enumerate(pieces):
+            part = columns[i * size : (i + 1) * size]
+            partial = partial + jnp.einsum("td,tc->dc", piece, part, preferred_element_type=F32)
     mine, theirs = partial[:, : chip_cols // 2], partial[:, chip_cols // 2 :]
     mine, theirs = jnp.where(core == 0, mine, theirs), jnp.where(core == 0, theirs, mine)
     grad_kv = mine + flip(theirs.astype(BF16), 1).astype(F32)

time: 165 us -> 172 us (1.042)
  waiting for transfers between devices: 77.6 us -> 59 us
  starting transfers between devices: 29.6 us -> 44.6 us
  matrix products: 6.02 us -> 14.2 us
  other arithmetic: 12.2 us -> 6.65 us
  Pallas kernels: 10.3 us -> 14.5 us
  local copies, waits for them, and re-layouts: 12.7 us -> 16.6 us
    ppermute x19 -> x25, starting transfers between devices: 18.8 us -> 33.8 us  [flip(): return lax.ppermute(block, 'dp', [(i, i ^ bits) for i in range(n_dp)])]
    ppermute x6, waiting for transfers between devices: 16.7 us -> 4.26 us  [around(): lax.ppermute(blocks[k], 'mp', [(i, (i + k) % n_mp) for i in range(n_mp)])]
    dot_general x5 -> x11, matrix products: 6.02 us -> 14.2 us  [the longest x6 9.06 us: product(): jnp.einsum('td,tc->dc', mine, jnp.concatenate(theirs), preferred_element_...]
    ppermute x19 -> x25, waiting for transfers between devices: 57.3 us -> 52 us  [flip(): return lax.ppermute(block, 'dp', [(i, i ^ bits) for i in range(n_dp)])]
    another operation x3 -> x0, other arithmetic: 4.48 us -> none  [the longest x2 4.42 us: local(): jnp.stack(from_far(native, plane_rows)).reshape(chips * tokens, width)]
    pallas_call x1 -> x2, Pallas kernels: 10.3 us -> 14.5 us  [attend(): pl.pallas_call(functools.partial(attend_kernel, length, device_cols), gri...]
    all_gather x1 -> x2, waiting for transfers between devices: 3.51 us -> 0.02 us  [the longest x1 0.02 us: local(): x_first = lax.all_gather(first_rows, 'mp', axis=0)]
    squeeze x1 -> x3, local copies, waits for them, and re-layouts: 0.03 us -> 2.99 us  [the longest x2 2.97 us: chip_part(): return lax.dynamic_index_in_dim(x, chip ^ k, 0, False)]
  transfers between devices with their start and end apart: 27 -> 34, of which waited for: 14 -> 14; matrix products, arithmetic and copies ran while one was open for 14% -> 18% of each run, Pallas kernels for 6% -> 8%
where the time goes in v5:
time: 172 us; the launch traced here: 170 us
  waiting for transfers between devices  59 us (34%)
  starting transfers between devices  44.6 us (26%)
  local copies, waits for them, and re-layouts  16.6 us (10%)
  between operations  14.7 us (9%)
  Pallas kernels  14.5 us (8%)
  matrix products  14.2 us (8%)
  other arithmetic  6.65 us (4%)
    ppermute x25, waiting for transfers between devices, flip(): return lax.ppermute(block, 'dp', [(i, i ^ bits) for i in range(n_dp)])  52 us
    ppermute x25, starting transfers between devices, flip(): return lax.ppermute(block, 'dp', [(i, i ^ bits) for i in range(n_dp)])  33.8 us
    pallas_call x2, Pallas kernels, attend(): pl.pallas_call(functools.partial(attend_kernel, length, device_cols), gri...  14.5 us
    dot_general x6, matrix products, product(): jnp.einsum('td,tc->dc', mine, jnp.concatenate(theirs), preferred_element_...  9.06 us
    ppermute x6, starting transfers between devices, around(): lax.ppermute(blocks[k], 'mp', [(i, (i + k) % n_mp) for i in range(n_mp)])  6.26 us
    dot_general x5, matrix products, local(): jnp.einsum('td,tc->dc', piece, part, preferred_element_type=F32)  5.18 us
    all_to_all x1, starting transfers between devices, local(): lax.all_to_all(outgoing, 'dp', split_axis=0, concat_axis=0, tiled=True)  4.51 us
    gather x3, local copies, waits for them, and re-layouts, pick(): return array.at[index].get(mode='promise_in_bounds')  4.46 us
  transfers between devices with their start and end apart: 34, of which 14 were waited for; matrix products, arithmetic and copies ran while one was open for 18% of the time, Pallas kernels for 8%

profile of v5, /device:TPU:7, one launch (start us, length us, event | category | flops | bytes accessed | tf_op | source)
XLA Modules:
  0.0 170.2 jit_solution(15018283645607776274)
XLA Ops:
  9.7 4.5 %all-to-all-start = ((bf16[8,32,1280]{2,1,0:T(8,128)(2,1)}), bf16[8,32,1280]{2,1,0:T(8,128)(2,1)S(1)}, u32[]{:S(2)}, u32[]{:S(2)}) async-start(bf16[8,32,1280]{2,1,0:T(8,128)(2,1)} %gather_fusion), calls=%async_computation | async-start | bytes 1310720 | tf_op jit(solution)/shard_map/all_to_all | solution.py:233
  16.2 3.4 %collective-permute-start.2 = (bf16[160,256]{1,0:T(8,128)(2,1)S(1)}, bf16[160,256]{1,0:T(8,128)(2,1)S(1)}, u32[]{:S(2)}, u32[]{:S(2)}) collective-permute-start(bf16[160,256]{1,0:T(8,128)(2,1)S(1)} %get-tuple-element.144), channel_id=1, source_target_pairs={{0,3},{1,0},{2,1},{3,2},{4,7},{5,4},{6,5},{7,6},{8,11},{9,8},{10,9... | collective-permute-start | bytes 245768 | tf_op jit(solution)/shard_map/ppermute | solution.py:206
  20.1 2.6 %all-to-all-done = bf16[8,32,1280]{2,1,0:T(8,128)(2,1)S(1)} async-done(((bf16[8,32,1280]{2,1,0:T(8,128)(2,1)}), bf16[8,32,1280]{2,1,0:T(8,128)(2,1)S(1)}, u32[]{:S(2)}, u32[]{:S(2)}) %all-to-all-start) | async-done | bytes 655392 | tf_op jit(solution)/shard_map/all_to_all | solution.py:233
  24.4 3.2 %collective-permute-done.1 = bf16[160,256]{1,0:T(8,128)(2,1)S(1)} collective-permute-done((bf16[160,256]{1,0:T(8,128)(2,1)S(1)}, bf16[160,256]{1,0:T(8,128)(2,1)S(1)}, u32[]{:S(2)}, u32[]{:S(2)}) %collective-permute-start.1) | collective-permute-done | bytes 81952 | tf_op jit(solution)/shard_map/ppermute | solution.py:206
  28.3 2.0 %collective-permute-start.5 = (bf16[4,160,256]{2,1,0:T(8,128)(2,1)S(1)}, bf16[4,160,256]{2,1,0:T(8,128)(2,1)S(1)}, u32[]{:S(2)}, u32[]{:S(2)}) collective-permute-start(bf16[4,160,256]{2,1,0:T(8,128)(2,1)S(1)} %get-tuple-element.142), channel_id=1, source_target_pairs={{0,24},{4,28},{8,16},{12,20},{16,8},{20,12},{24,0},{28,4},{1,25},{... | collective-permute-start | bytes 983048 | tf_op jit(solution)/shard_map/ppermute | solution.py:199
  30.4 5.9 %collective-permute-done.4 = bf16[4,160,256]{2,1,0:T(8,128)(2,1)S(1)} collective-permute-done((bf16[4,160,256]{2,1,0:T(8,128)(2,1)S(1)}, bf16[4,160,256]{2,1,0:T(8,128)(2,1)S(1)}, u32[]{:S(2)}, u32[]{:S(2)}) %collective-permute-start.4) | collective-permute-done | bytes 327712 | tf_op jit(solution)/shard_map/ppermute | solution.py:199
  36.3 8.0 %collective-permute-done.5 = bf16[4,160,256]{2,1,0:T(8,128)(2,1)S(1)} collective-permute-done((bf16[4,160,256]{2,1,0:T(8,128)(2,1)S(1)}, bf16[4,160,256]{2,1,0:T(8,128)(2,1)S(1)}, u32[]{:S(2)}, u32[]{:S(2)}) %collective-permute-start.5) | collective-permute-done | bytes 327712 | tf_op jit(solution)/shard_map/ppermute | solution.py:199
  44.5 1.8 %collective-permute-start.8 = (bf16[4,4,160,256]{3,2,1,0:T(8,128)(2,1)S(1)}, bf16[4,4,160,256]{3,2,1,0:T(8,128)(2,1)}, u32[]{:S(2)}, u32[]{:S(2)}) collective-permute-start(bf16[4,4,160,256]{3,2,1,0:T(8,128)(2,1)S(1)} %pad_maximum_fusion.1), channel_id=1, source_target_pairs={{0,4},{4,0},{8,12},{12,8},{16,20},{20,16},{24,28},{28,24},{1,5},{5... | collective-permute-start | bytes 3932168 | tf_op jit(solution)/shard_map/ppermute | solution.py:199
  49.0 13.5 %collective-permute-done.7 = bf16[256,1280]{1,0:T(8,128)(2,1)} collective-permute-done((bf16[256,1280]{1,0:T(8,128)(2,1)S(1)}, bf16[256,1280]{1,0:T(8,128)(2,1)}, u32[]{:S(2)}, u32[]{:S(2)}) %collective-permute-start.7) | collective-permute-done | bytes 655392 | tf_op jit(solution)/shard_map/ppermute | solution.py:199
  66.4 3.1 %pad_maximum_fusion = bf16[4,2,4,160,256]{4,3,2,1,0:T(8,128)(2,1)} fusion(bf16[4,1,4,160,256]{4,3,2,1,0:T(8,128)(2,1)} %bitcast.24, bf16[4,1,4,160,256]{4,3,2,1,0:T(8,128)(2,1)S(1)} %bitcast.97), kind=kLoop, calls=%fused_computation.7 | loop fusion | flops 1310720 | bytes 5242880 | tf_op jit(solution)/shard_map/stack | solution.py:258
  69.5 2.5 %gather_fusion.2 = bf16[32,160,256]{2,1,0:T(8,128)(2,1)S(1)} fusion(bf16[32,160,256]{2,1,0:T(8,128)(2,1)} %bitcast.93, s32[1024]{0:T(1024)S(1)} %get-tuple-element.147), kind=kCustom, calls=%fused_computation.2 | custom fusion | bytes 5243008 | tf_op jit(solution)/shard_map/gather | solution.py:168
  76.2 7.3 %shard_map.138 = (f32[128,1024]{1,0:T(8,128)S(1)}, f32[128,1024]{1,0:T(8,128)S(1)}, f32[128,256]{1,0:T(8,128)S(1)}) custom-call(bf16[4,128,1280]{2,1,0:T(8,128)(2,1)S(1)} %copy-done.2, bf16[5120,1024]{1,0:T(8,128)(2,1)} %wq_ref.3, bf16[5120,256]{1,0:T(8,128)(2,1)S(1)} %bitcast.83, f32[128,1024]{1,0:T(8,128)S(1)} %bitcast.88, f32[1,128]{1,0:T(1,128)S(1)} %bitcast.89, ...), custom_call_target="tpu_custom_call" | custom-call | flops 16777216000 | bytes 41943040 | tf_op jit(solution)/shard_map/pallas_call | solution.py:136
  83.6 4.6 %collective-permute-done.13 = bf16[128,1280]{1,0:T(8,128)(2,1)S(1)} collective-permute-done((bf16[128,1280]{1,0:T(8,128)(2,1)S(1)}, bf16[128,1280]{1,0:T(8,128)(2,1)S(1)}, u32[]{:S(2)}, u32[]{:S(2)}) %collective-permute-start.13) | collective-permute-done | bytes 327712 | tf_op jit(solution)/shard_map/ppermute | solution.py:199
  91.7 7.5 %collective-permute-done.14 = bf16[128,1024]{1,0:T(8,128)(2,1)S(1)} collective-permute-done((bf16[128,1024]{1,0:T(8,128)(2,1)S(1)}, bf16[128,1024]{1,0:T(8,128)(2,1)S(1)}, u32[]{:S(2)}, u32[]{:S(2)}) %collective-permute-start.14) | collective-permute-done | bytes 262176 | tf_op jit(solution)/shard_map/ppermute | solution.py:199
  99.2 2.4 %collective-permute-done.15 = bf16[128,1024]{1,0:T(8,128)(2,1)S(1)} collective-permute-done((bf16[128,1024]{1,0:T(8,128)(2,1)S(1)}, bf16[128,1024]{1,0:T(8,128)(2,1)S(1)}, u32[]{:S(2)}, u32[]{:S(2)}) %collective-permute-start.15) | collective-permute-done | bytes 262176 | tf_op jit(solution)/shard_map/ppermute | solution.py:199
  101.7 2.4 %fusion.3 = f32[640,1024]{1,0:T(8,128)} fusion(bf16[512,1024]{1,0:T(8,128)(2,1)S(1)} %constant_dynamic-update-slice_fusion.4, bf16[512,1280]{1,0:T(8,128)(2,1)S(1)} %constant_dynamic-update-slice_fusion, s32[]{:T(128)S(6)} %select_n.171), kind=kOutput, calls=%fused_computation.14 | convolution fusion | flops 671088640 | bytes 4325380 | tf_op jit(solution)/shard_map/td,tc->dc/dot_general | solution.py:300
  104.0 2.4 %fusion.5 = f32[640,1024]{1,0:T(8,128)} fusion(bf16[512,1024]{1,0:T(8,128)(2,1)S(1)} %constant_dynamic-update-slice_fusion.4, bf16[512,1280]{1,0:T(8,128)(2,1)S(1)} %constant_dynamic-update-slice_fusion, s32[]{:T(128)S(6)} %select_n.170), kind=kOutput, calls=%fused_computation.16 | convolution fusion | flops 671088640 | bytes 4325380 | tf_op jit(solution)/shard_map/td,tc->dc/dot_general | solution.py:300
  107.9 1.9 %collective-permute-start.17 = (bf16[128,1280]{1,0:T(8,128)(2,1)S(1)}, bf16[128,1280]{1,0:T(8,128)(2,1)S(1)}, u32[]{:S(2)}, u32[]{:S(2)}) collective-permute-start(bf16[128,1280]{1,0:T(8,128)(2,1)S(1)} %get-tuple-element.92), channel_id=1, source_target_pairs={{0,8},{4,12},{8,0},{12,4},{16,24},{20,28},{24,16},{28,20},{1,9},{5... | collective-permute-start | bytes 983048 | tf_op jit(solution)/shard_map/ppermute | solution.py:199
  111.1 7.2 %shard_map.139 = (f32[128,1024]{1,0:T(8,128)S(1)}, f32[128,1024]{1,0:T(8,128)S(1)}, f32[128,256]{1,0:T(8,128)S(1)}) custom-call(bf16[4,128,1280]{2,1,0:T(8,128)(2,1)S(1)} %bitcast.86, bf16[5120,1024]{1,0:T(8,128)(2,1)} %wq_ref.3, bf16[5120,256]{1,0:T(8,128)(2,1)S(1)} %bitcast.84, f32[128,1024]{1,0:T(8,128)S(1)} %bitcast.87, f32[1,128]{1,0:T(1,128)S(1)} %bitcast.90, ...), custom_call_target="tpu_custom_call" | custom-call | flops 16777216000 | bytes 41943040 | tf_op jit(solution)/shard_map/pallas_call | solution.py:136
  121.7 2.0 %collective-permute-done.19 = bf16[128,1280]{1,0:T(8,128)(2,1)S(1)} collective-permute-done((bf16[128,1280]{1,0:T(8,128)(2,1)S(1)}, bf16[128,1280]{1,0:T(8,128)(2,1)S(1)}, u32[]{:S(2)}, u32[]{:S(2)}) %collective-permute-start.19) | collective-permute-done | bytes 327712 | tf_op jit(solution)/shard_map/ppermute | solution.py:199
  129.8 1.8 %collective-permute-start.27 = (bf16[256,256]{1,0:T(8,128)(2,1)S(1)}, bf16[256,256]{1,0:T(8,128)(2,1)S(1)}, u32[]{:S(2)}, u32[]{:S(2)}) collective-permute-start(bf16[256,256]{1,0:T(8,128)(2,1)S(1)} %get-tuple-element.138), channel_id=1, source_target_pairs={{0,8},{4,12},{8,0},{12,4},{16,24},{20,28},{24,16},{28,20},{1,9},{5... | collective-permute-start | bytes 393224 | tf_op jit(solution)/shard_map/ppermute | solution.py:199
  133.8 5.2 %collective-permute-done.28 = bf16[256,256]{1,0:T(8,128)(2,1)S(1)} collective-permute-done((bf16[256,256]{1,0:T(8,128)(2,1)S(1)}, bf16[256,256]{1,0:T(8,128)(2,1)S(1)}, u32[]{:S(2)}, u32[]{:S(2)}) %collective-permute-start.28) | collective-permute-done | bytes 131104 | tf_op jit(solution)/shard_map/ppermute | solution.py:199
  144.9 11.9 %collective-permute-start.30 = (bf16[1280,128]{0,1:T(8,128)(2,1)S(1)}, bf16[1280,128]{0,1:T(8,128)(2,1)S(1)}, u32[]{:S(2)}, u32[]{:S(2)}) collective-permute-start(bf16[1280,128]{0,1:T(8,128)(2,1)S(1)} %select_convert_fusion), channel_id=1, source_target_pairs={{0,4},{4,0},{8,12},{12,8},{16,20},{20,16},{24,28},{28,24},{1,5},{5... | collective-permute-start | bytes 983048 | tf_op jit(solution)/shard_map/ppermute | solution.py:199
  161.3 2.0 %add_add_fusion = f32[640,1024]{1,0:T(8,128)} fusion(bf16[640,1024]{1,0:T(8,128)(2,1)S(1)} %collective-permute-done.26, f32[640,1024]{1,0:T(8,128)S(1)} %fusion.10, f32[640,1024]{1,0:T(8,128)S(1)} %copy-done.9, bf16[128,1024]{1,0:T(8,128)(2,1)S(1)} %collective-permute-done.20, bf16[128,1280]{1,0:T(8,128)(2,1)S(1)} %collective-permute-done.19, s32[]{:T(128)S(6)} %select_n.171), kind=kOutput, calls=%fused_computation.8 | convolution fusion | flops 170393600 | bytes 9601028 | tf_op jit(solution)/shard_map/td,tc->dc/dot_general | solution.py:300
  (152 shorter events, 46.4 us)
Async XLA Ops:
  9.7 13.0 %all-to-all-start = ((bf16[8,32,1280]{2,1,0:T(8,128)(2,1)}), bf16[8,32,1280]{2,1,0:T(8,128)(2,1)S(1)}, u32[]{:S(2)}, u32[]{:S(2)}) async-start(bf16[8,32,1280]{2,1,0:T(8,128)(2,1)} %gather_fusion), calls=%async_computation | async-start | bytes 1310720 | tf_op jit(solution)/shard_map/all_to_all | solution.py:233
  14.2 57.8 %all-gather.4.cloned.1.call-start = ((), (), s32[]{:S(2)}) async-start(), calls=%async_computation.1 | async-start | bytes 1638400 | tf_op jit(solution)/shard_map/all_gather | solution.py:250
  24.3 82.1 %all-gather.6.cloned.1.call-start = ((), (), s32[]{:S(2)}) async-start(), calls=%async_computation.2 | async-start | bytes 1638400 | tf_op jit(solution)/shard_map/all_gather | solution.py:253
  27.6 8.6 %collective-permute-start.4 = (bf16[4,160,256]{2,1,0:T(8,128)(2,1)S(1)}, bf16[4,160,256]{2,1,0:T(8,128)(2,1)S(1)}, u32[]{:S(2)}, u32[]{:S(2)}) collective-permute-start(bf16[4,160,256]{2,1,0:T(8,128)(2,1)S(1)} %get-tuple-element.142), channel_id=1, source_target_pairs={{0,16},{4,20},{8,24},{12,28},{16,0},{20,4},{24,8},{28,12},{1,17},{... | collective-permute-start | bytes 983048 | tf_op jit(solution)/shard_map/ppermute | solution.py:199
  28.0 8.3 %collective-permute-start.3 = (bf16[4,160,256]{2,1,0:T(8,128)(2,1)S(1)}, bf16[4,160,256]{2,1,0:T(8,128)(2,1)S(1)}, u32[]{:S(2)}, u32[]{:S(2)}) collective-permute-start(bf16[4,160,256]{2,1,0:T(8,128)(2,1)S(1)} %get-tuple-element.142), channel_id=1, source_target_pairs={{0,8},{4,12},{8,0},{12,4},{16,24},{20,28},{24,16},{28,20},{1,9},{5... | collective-permute-start | bytes 983048 | tf_op jit(solution)/shard_map/ppermute | solution.py:199
  28.3 16.0 %collective-permute-start.5 = (bf16[4,160,256]{2,1,0:T(8,128)(2,1)S(1)}, bf16[4,160,256]{2,1,0:T(8,128)(2,1)S(1)}, u32[]{:S(2)}, u32[]{:S(2)}) collective-permute-start(bf16[4,160,256]{2,1,0:T(8,128)(2,1)S(1)} %get-tuple-element.142), channel_id=1, source_target_pairs={{0,24},{4,28},{8,16},{12,20},{16,8},{20,12},{24,0},{28,4},{1,25},{... | collective-permute-start | bytes 983048 | tf_op jit(solution)/shard_map/ppermute | solution.py:199
  44.5 21.9 %collective-permute-start.8 = (bf16[4,4,160,256]{3,2,1,0:T(8,128)(2,1)S(1)}, bf16[4,4,160,256]{3,2,1,0:T(8,128)(2,1)}, u32[]{:S(2)}, u32[]{:S(2)}) collective-permute-start(bf16[4,4,160,256]{3,2,1,0:T(8,128)(2,1)S(1)} %pad_maximum_fusion.1), channel_id=1, source_target_pairs={{0,4},{4,0},{8,12},{12,8},{16,20},{20,16},{24,28},{28,24},{1,5},{5... | collective-permute-start | bytes 3932168 | tf_op jit(solution)/shard_map/ppermute | solution.py:199
  46.3 16.2 %collective-permute-start.7 = (bf16[256,1280]{1,0:T(8,128)(2,1)S(1)}, bf16[256,1280]{1,0:T(8,128)(2,1)}, u32[]{:S(2)}, u32[]{:S(2)}) collective-permute-start(bf16[256,1280]{1,0:T(8,128)(2,1)S(1)} %bitcast.94), channel_id=1, source_target_pairs={{0,16},{4,20},{8,24},{12,28},{16,0},{20,4},{24,8},{28,12},{1,17},{... | collective-permute-start | bytes 1966088 | tf_op jit(solution)/shard_map/ppermute | solution.py:199
  46.6 15.9 %collective-permute-start.6 = (bf16[256,1280]{1,0:T(8,128)(2,1)S(1)}, bf16[256,1280]{1,0:T(8,128)(2,1)S(1)}, u32[]{:S(2)}, u32[]{:S(2)}) collective-permute-start(bf16[256,1280]{1,0:T(8,128)(2,1)S(1)} %bitcast.95), channel_id=1, source_target_pairs={{0,8},{4,12},{8,0},{12,4},{16,24},{20,28},{24,16},{28,20},{1,9},{5... | collective-permute-start | bytes 1966088 | tf_op jit(solution)/shard_map/ppermute | solution.py:199
  65.0 18.5 %collective-permute-start.12 = (bf16[128,1280]{1,0:T(8,128)(2,1)}, bf16[128,1280]{1,0:T(8,128)(2,1)}, u32[]{:S(2)}, u32[]{:S(2)}) collective-permute-start(bf16[128,1280]{1,0:T(8,128)(2,1)} %slice.84), channel_id=1, source_target_pairs={{0,8},{4,12},{8,0},{12,4},{16,24},{20,28},{24,16},{28,20},{1,9},{5... | collective-permute-start | bytes 983048 | tf_op jit(solution)/shard_map/ppermute | solution.py:199
  65.3 18.3 %collective-permute-start.11 = (bf16[128,1280]{1,0:T(8,128)(2,1)}, bf16[128,1280]{1,0:T(8,128)(2,1)}, u32[]{:S(2)}, u32[]{:S(2)}) collective-permute-start(bf16[128,1280]{1,0:T(8,128)(2,1)} %slice.83), channel_id=1, source_target_pairs={{0,16},{4,20},{8,24},{12,28},{16,0},{20,4},{24,8},{28,12},{1,17},{... | collective-permute-start | bytes 983048 | tf_op jit(solution)/shard_map/ppermute | solution.py:199
  73.5 10.1 %collective-permute-start.9 = (bf16[128,1280]{1,0:T(8,128)(2,1)S(1)}, bf16[128,1280]{1,0:T(8,128)(2,1)S(1)}, u32[]{:S(2)}, u32[]{:S(2)}) collective-permute-start(bf16[128,1280]{1,0:T(8,128)(2,1)S(1)} %get-tuple-element.73), channel_id=1, source_target_pairs={{0,8},{4,12},{8,0},{12,4},{16,24},{20,28},{24,16},{28,20},{1,9},{5... | collective-permute-start | bytes 983048 | tf_op jit(solution)/shard_map/ppermute | solution.py:199
  74.7 8.9 %collective-permute-start.10 = (bf16[128,1280]{1,0:T(8,128)(2,1)S(1)}, bf16[128,1280]{1,0:T(8,128)(2,1)S(1)}, u32[]{:S(2)}, u32[]{:S(2)}) collective-permute-start(bf16[128,1280]{1,0:T(8,128)(2,1)S(1)} %get-tuple-element.74), channel_id=1, source_target_pairs={{0,16},{4,20},{8,24},{12,28},{16,0},{20,4},{24,8},{28,12},{1,17},{... | collective-permute-start | bytes 983048 | tf_op jit(solution)/shard_map/ppermute | solution.py:199
  75.2 13.1 %collective-permute-start.13 = (bf16[128,1280]{1,0:T(8,128)(2,1)S(1)}, bf16[128,1280]{1,0:T(8,128)(2,1)S(1)}, u32[]{:S(2)}, u32[]{:S(2)}) collective-permute-start(bf16[128,1280]{1,0:T(8,128)(2,1)S(1)} %get-tuple-element.81), channel_id=1, source_target_pairs={{0,24},{4,28},{8,16},{12,20},{16,8},{20,12},{24,0},{28,4},{1,25},{... | collective-permute-start | bytes 983048 | tf_op jit(solution)/shard_map/ppermute | solution.py:199
  88.3 13.4 %collective-permute-start.16 = (bf16[128,1024]{1,0:T(8,128)(2,1)S(1)}, bf16[128,1024]{1,0:T(8,128)(2,1)S(1)}, u32[]{:S(2)}, u32[]{:S(2)}) collective-permute-start(bf16[128,1024]{1,0:T(8,128)(2,1)S(1)} %convert_element_type.47), channel_id=1, source_target_pairs={{0,24},{4,28},{8,16},{12,20},{16,8},{20,12},{24,0},{28,4},{1,25},{... | collective-permute-start | bytes 786440 | tf_op jit(solution)/shard_map/ppermute | solution.py:199
  90.0 11.6 %collective-permute-start.15 = (bf16[128,1024]{1,0:T(8,128)(2,1)S(1)}, bf16[128,1024]{1,0:T(8,128)(2,1)S(1)}, u32[]{:S(2)}, u32[]{:S(2)}) collective-permute-start(bf16[128,1024]{1,0:T(8,128)(2,1)S(1)} %convert_element_type.47), channel_id=1, source_target_pairs={{0,16},{4,20},{8,24},{12,28},{16,0},{20,4},{24,8},{28,12},{1,17},{... | collective-permute-start | bytes 786440 | tf_op jit(solution)/shard_map/ppermute | solution.py:199
  90.8 8.4 %collective-permute-start.14 = (bf16[128,1024]{1,0:T(8,128)(2,1)S(1)}, bf16[128,1024]{1,0:T(8,128)(2,1)S(1)}, u32[]{:S(2)}, u32[]{:S(2)}) collective-permute-start(bf16[128,1024]{1,0:T(8,128)(2,1)S(1)} %convert_element_type.47), channel_id=1, source_target_pairs={{0,8},{4,12},{8,0},{12,4},{16,24},{20,28},{24,16},{28,20},{1,9},{5... | collective-permute-start | bytes 786440 | tf_op jit(solution)/shard_map/ppermute | solution.py:199
  107.9 11.3 %collective-permute-start.17 = (bf16[128,1280]{1,0:T(8,128)(2,1)S(1)}, bf16[128,1280]{1,0:T(8,128)(2,1)S(1)}, u32[]{:S(2)}, u32[]{:S(2)}) collective-permute-start(bf16[128,1280]{1,0:T(8,128)(2,1)S(1)} %get-tuple-element.92), channel_id=1, source_target_pairs={{0,8},{4,12},{8,0},{12,4},{16,24},{20,28},{24,16},{28,20},{1,9},{5... | collective-permute-start | bytes 983048 | tf_op jit(solution)/shard_map/ppermute | solution.py:199
  109.8 9.4 %collective-permute-start.18 = (bf16[128,1280]{1,0:T(8,128)(2,1)S(1)}, bf16[128,1280]{1,0:T(8,128)(2,1)S(1)}, u32[]{:S(2)}, u32[]{:S(2)}) collective-permute-start(bf16[128,1280]{1,0:T(8,128)(2,1)S(1)} %get-tuple-element.93), channel_id=1, source_target_pairs={{0,16},{4,20},{8,24},{12,28},{16,0},{20,4},{24,8},{28,12},{1,17},{... | collective-permute-start | bytes 983048 | tf_op jit(solution)/shard_map/ppermute | solution.py:199
  110.0 13.7 %collective-permute-start.19 = (bf16[128,1280]{1,0:T(8,128)(2,1)S(1)}, bf16[128,1280]{1,0:T(8,128)(2,1)S(1)}, u32[]{:S(2)}, u32[]{:S(2)}) collective-permute-start(bf16[128,1280]{1,0:T(8,128)(2,1)S(1)} %get-tuple-element.98), channel_id=1, source_target_pairs={{0,24},{4,28},{8,16},{12,20},{16,8},{20,12},{24,0},{28,4},{1,25},{... | collective-permute-start | bytes 983048 | tf_op jit(solution)/shard_map/ppermute | solution.py:199
  126.1 30.7 %collective-permute-start.20 = (bf16[128,1024]{1,0:T(8,128)(2,1)S(1)}, bf16[128,1024]{1,0:T(8,128)(2,1)S(1)}, u32[]{:S(2)}, u32[]{:S(2)}) collective-permute-start(bf16[128,1024]{1,0:T(8,128)(2,1)S(1)} %convert_element_type.50), channel_id=1, source_target_pairs={{0,24},{4,28},{8,16},{12,20},{16,8},{20,12},{24,0},{28,4},{1,25},{... | collective-permute-start | bytes 786440 | tf_op jit(solution)/shard_map/ppermute | solution.py:199
  129.8 13.4 %collective-permute-start.27 = (bf16[256,256]{1,0:T(8,128)(2,1)S(1)}, bf16[256,256]{1,0:T(8,128)(2,1)S(1)}, u32[]{:S(2)}, u32[]{:S(2)}) collective-permute-start(bf16[256,256]{1,0:T(8,128)(2,1)S(1)} %get-tuple-element.138), channel_id=1, source_target_pairs={{0,8},{4,12},{8,0},{12,4},{16,24},{20,28},{24,16},{28,20},{1,9},{5... | collective-permute-start | bytes 393224 | tf_op jit(solution)/shard_map/ppermute | solution.py:199
  131.6 8.8 %collective-permute-start.29 = (bf16[256,256]{1,0:T(8,128)(2,1)S(1)}, bf16[256,256]{1,0:T(8,128)(2,1)S(1)}, u32[]{:S(2)}, u32[]{:S(2)}) collective-permute-start(bf16[256,256]{1,0:T(8,128)(2,1)S(1)} %get-tuple-element.139), channel_id=1, source_target_pairs={{0,24},{4,28},{8,16},{12,20},{16,8},{20,12},{24,0},{28,4},{1,25},{... | collective-permute-start | bytes 393224 | tf_op jit(solution)/shard_map/ppermute | solution.py:199
  144.9 14.4 %collective-permute-start.30 = (bf16[1280,128]{0,1:T(8,128)(2,1)S(1)}, bf16[1280,128]{0,1:T(8,128)(2,1)S(1)}, u32[]{:S(2)}, u32[]{:S(2)}) collective-permute-start(bf16[1280,128]{0,1:T(8,128)(2,1)S(1)} %select_convert_fusion), channel_id=1, source_target_pairs={{0,4},{4,0},{8,12},{12,8},{16,20},{20,16},{24,28},{28,24},{1,5},{5... | collective-permute-start | bytes 983048 | tf_op jit(solution)/shard_map/ppermute | solution.py:199
  (27 other events, 153.1 us)
Sparse Core Ops, SparseCore 0:
  24.4 33.1 all-gather.3
  59.8 31.6 all-gather.5

commit v6 on v5

--- a/solution.py
+++ b/solution.py
@@ -153,8 +153,8 @@
         scratch_shapes=[pltpu.VMEM((tokens, cols), F32), pltpu.VMEM((tokens, kv_cols), F32)],
         compiler_params=pltpu.CompilerParams(vmem_limit_bytes=40 * 1024 * 1024),
         cost_estimate=pl.CostEstimate(
-            flops=20 * x.size * (cols + kv_cols),
-            bytes_accessed=8 * w_query.size,
+            flops=2 * x.size * (cols + kv_cols),
+            bytes_accessed=2 * w_query.size,
             transcendentals=tokens * cols,
         ),
     )(x, w_query, w_kv, d_out, query_gain, key_gain)
@@ -232,32 +232,45 @@
     outgoing, w_key, w_value = together(outgoing, w_key, w_value)
     arrived = lax.all_to_all(outgoing, "dp", split_axis=0, concat_axis=0, tiled=True)
 
-    share = width // n_dp
-    own_key = lax.dynamic_slice_in_dim(w_key, dp * share, share, 0)
-    own_value = lax.dynamic_slice_in_dim(w_value, dp * share, share, 0)
+    axes = len(near)
+    share = width // axes // 4
+    own = [
+        b * (width // axes) + ((chip >> b) % 2 * 2 + core) * share for b in range(axes)
+    ]
+    own_key = jnp.concatenate([lax.dynamic_slice_in_dim(w_key, i, share, 0) for i in own])
+    own_value = jnp.concatenate([lax.dynamic_slice_in_dim(w_value, i, share, 0) for i in own])
     pairs = []
     for head in range(KV_HEADS):
         columns = slice(head * dim, (head + 1) * dim)
         pairs.append(jnp.concatenate([own_key[:, columns], own_value[:, columns]], axis=1))
     pairs = jnp.stack(pairs)
     heads = [(mp + k) % n_mp * KV_HEADS // n_mp for k in range(n_mp)]
-    shares = around([lax.dynamic_index_in_dim(pairs, h, 0, False) for h in heads])
-    shares = jnp.stack(shares)
+    pairs = [lax.dynamic_index_in_dim(pairs, h, 0, False) for h in heads]
     rows = pick(arrived, slot_source).reshape(tokens, width)
+    rows, pairs = lax.optimization_barrier((rows, pairs))
+    shares = around(pairs)
+    shares = jnp.stack(shares).reshape(n_mp, axes, share, 2 * dim)
+    shares = [shares[:, b] for b in range(axes)]
 
     middle = tokens // 2
     first_rows, second_rows = rows[:middle], rows[middle:]
     x_first = lax.all_gather(first_rows, "mp", axis=0)
-    shares = jnp.stack([shares] + other_chips([shares] * chips))
-    native, second_rows, shares = together(rows, second_rows, shares)
+    other_shares = [flip(block, 2 * k) for k, block in zip(near, shares)]
+    native, second_rows, other_shares = lax.optimization_barrier((rows, second_rows, other_shares))
     x_second = lax.all_gather(second_rows, "mp", axis=0)
-    other_shares = flip(shares, 1)
-    plane_rows = together(*from_near(native))
+    shares = jnp.stack([block for pair in zip(shares, other_shares) for block in pair])
+    shares = jnp.stack([shares, flip(shares, 1)]).reshape(-1, share, 2 * dim)
+
+    places = []
+    for i in range(n_mp):
+        for b in range(axes):
+            for bit in range(2):
+                for c in range(2):
+                    place = ((c ^ core) * axes + b) * 2 + (bit ^ (chip >> b) % 2)
+                    places.append(place * n_mp + (mp - i) % n_mp)
+    w_kv = pick(shares, jnp.stack(places)).reshape(n_mp * width, 2 * dim)
+    w_kv, *plane_rows = together(w_kv, *from_near(native))
     plane_rows = from_far(native, plane_rows)
-
-    shares = jnp.stack([shares, other_shares], axis=1).reshape(n_dp * n_mp, share, 2 * dim)
-    order = (dp ^ jnp.arange(n_dp))[None, :] * n_mp + ((mp - jnp.arange(n_mp)) % n_mp)[:, None]
-    w_kv = pick(shares, order.reshape(-1)).reshape(n_mp * width, 2 * dim)
 
     factor = multiplicity.astype(F32) * slot_weight / length
     d_out = (cotangent.astype(F32) * factor[:, None, None]).astype(BF16).astype(F32)
@@ -270,9 +283,10 @@
         flat = x.transpose(1, 0, 2).reshape(x.shape[1], -1)
         return lax.dynamic_slice_in_dim(flat, (chip ^ k) * chip_width, chip_width, 1)
 
-    def half_step(x, d_out, beside):
+    def half_step(x, d_out, before, beside):
         x, *parts = together(x, *[chip_part(x, k) for k in range(chips)])
         near_parts = [flip(parts[k], 2 * k) for k in near]
+        x, before = lax.optimization_barrier((x, before))
         attended, d_query, d_kv = attend(
             x, w_query, w_kv, d_out, query_gain[None, :], key_gain[None, :], length, key_cols // n_dp
         )
@@ -282,15 +296,15 @@
         near_parts = dict(zip(near, near_parts))
         for k in range(1, chips):
             parts[k] = near_parts[k] if k in near_parts else flip(parts[k], 2 * k)
-        d_query, *parts = together(d_query, *parts)
-        return attended.astype(BF16), d_query, d_kv, parts, beside
-
-    (x_first, *native_near) = together(x_first, *[plane_rows[k][0] for k in near])
+        return attended.astype(BF16), d_query, d_kv, parts, before, beside
+
+    x_first, *native_near = together(x_first, *[plane_rows[k][0] for k in near])
     for k, block in zip(near, native_near):
         plane_rows[k] = [block]
-    attended, d_query, d_kv, first_parts, plane_rows = half_step(
-        x_first, d_out[:middle], plane_rows
+    attended, d_query, d_kv, first_parts, _, plane_rows = half_step(
+        x_first, d_out[:middle], [], plane_rows
     )
+    d_query, *first_parts = together(d_query, *first_parts)
     first_all = [d_query] + other_chips([d_query] * chips)
 
     half = chip_width // 2
@@ -299,31 +313,20 @@
         mine = lax.dynamic_slice_in_dim(jnp.concatenate(mine), which * half, half, 1)
         return jnp.einsum("td,tc->dc", mine, jnp.concatenate(theirs), preferred_element_type=F32)
 
-    x_second, first_other, first_own = together(
-        x_second, product(first_parts, first_all, 1 - core), product(first_parts, first_all, core)
+    x_second, *first_near = together(x_second, *[first_all[k] for k in near])
+    for k, block in zip(near, first_near):
+        first_all[k] = block
+    products = [product(first_parts, first_all, which) for which in (1 - core, core)]
+    attended_second, d_query, d_kv_second, second_parts, products, _ = half_step(
+        x_second, d_out[middle:], products, []
     )
-    attended_second, d_query, d_kv_second, second_parts, _ = half_step(x_second, d_out[middle:], [])
-    second_all = [d_query] + other_chips([d_query] * chips)
+    first_other, first_own = products
     attended = jnp.concatenate([attended, attended_second])
     d_kv = jnp.concatenate([d_kv, d_kv_second])
-    spread = jnp.stack(around([d_kv] * n_mp))
-    spread, *second_near = together(spread, *[second_all[k] for k in near])
-    for k, block in zip(near, second_near):
-        second_all[k] = block
-
-    some = [0] + near
-    rest = [k for k in range(chips) if k not in some]
-
-    def second(which):
-        return [
-            product([second_parts[k] for k in ks], [second_all[k] for k in ks], which)
-            for ks in (some, rest)
-        ]
-
-    early, late = second(1 - core)
-    other = flip((late + (early + first_other)).astype(BF16), 1)
-    early, late = second(core)
-    grad_query = late + ((early + first_own) + other.astype(F32))
+    spread = around([d_kv] * n_mp)
+    d_query, spread, second_parts = lax.optimization_barrier((d_query, spread, second_parts))
+    spread = jnp.stack(spread)
+    second_all = [d_query] + other_chips([d_query] * chips)
 
     if n_mp > KV_HEADS:
         spread = pick(spread, (mp - jnp.arange(n_mp)) % n_mp)
@@ -338,6 +341,24 @@
         spread = spread.transpose(0, 2, 1, 3).reshape(chips, tokens, chip_cols)
     kv_all = [lax.dynamic_index_in_dim(spread, spread_at(chip ^ k), 0, False) for k in range(chips)]
     kv_all = [kv_all[0]] + other_chips(kv_all)
+    second_near = [second_all[k] for k in near]
+    kv_all, second_near = lax.optimization_barrier((kv_all, second_near))
+    for k, block in zip(near, second_near):
+        second_all[k] = block
+    some = [0] + near
+    rest = [k for k in range(chips) if k not in some]
+
+    def second(which):
+        return [
+            product([second_parts[k] for k in ks], [second_all[k] for k in ks], which)
+            for ks in (some, rest)
+        ]
+
+    early, late = second(1 - core)
+    other = flip((late + (early + first_other)).astype(BF16), 1)
+    early, late = second(core)
+    grad_query = late + ((early + first_own) + other.astype(F32))
+
     partial = 0
     for pieces, columns in zip(plane_rows, kv_all):
         size = tokens // len(pieces)

time: 172 us -> 191 us (1.11)
  the two profiles are of different devices: /device:TPU:7 before, /device:TPU:0 now
where the time goes in v6:
time: 191 us; the launch traced here: 190 us
  waiting for transfers between devices  57.9 us (30%)
  starting transfers between devices  48.4 us (25%)
  local copies, waits for them, and re-layouts  27.5 us (14%)
  matrix products  19.4 us (10%)
  between operations  14.9 us (8%)
  Pallas kernels  14.5 us (8%)
  other arithmetic  7.43 us (4%)
    ppermute x24, waiting for transfers between devices, flip(): return lax.ppermute(block, 'dp', [(i, i ^ bits) for i in range(n_dp)])  38.8 us
    ppermute x24, starting transfers between devices, flip(): return lax.ppermute(block, 'dp', [(i, i ^ bits) for i in range(n_dp)])  22.7 us
    ppermute x6, starting transfers between devices, around(): lax.ppermute(blocks[k], 'mp', [(i, (i + k) % n_mp) for i in range(n_mp)])  20.5 us
    pallas_call x2, Pallas kernels, attend(): pl.pallas_call(functools.partial(attend_kernel, length, device_cols), gri...  14.5 us
    dot_general x6, matrix products, product(): jnp.einsum('td,tc->dc', mine, jnp.concatenate(theirs), preferred_element_...  13.2 us
    ppermute x6, waiting for transfers between devices, around(): lax.ppermute(blocks[k], 'mp', [(i, (i + k) % n_mp) for i in range(n_mp)])  10.6 us
    unnamed x63, local copies, waits for them, and re-layouts  9.09 us
    all_to_all x1, waiting for transfers between devices, local(): lax.all_to_all(outgoing, 'dp', split_axis=0, concat_axis=0, tiled=True)  8.46 us
  transfers between devices with their start and end apart: 33, of which 18 were waited for; matrix products, arithmetic and copies ran while one was open for 24% of the time, Pallas kernels for 8%

profile of v6, /device:TPU:0, one launch (start us, length us, event | category | flops | bytes accessed | tf_op | source)
XLA Modules:
  0.0 190.1 jit_solution(10786964065035073894)
XLA Ops:
  9.7 5.2 %all-to-all-start = ((bf16[8,32,1280]{2,1,0:T(8,128)(2,1)}), bf16[8,32,1280]{2,1,0:T(8,128)(2,1)S(1)}, u32[]{:S(2)}, u32[]{:S(2)}) async-start(bf16[8,32,1280]{2,1,0:T(8,128)(2,1)} %gather_fusion), calls=%async_computation | async-start | bytes 1310720 | tf_op jit(solution)/shard_map/all_to_all | solution.py:233
  17.5 8.5 %all-to-all-done = bf16[8,32,1280]{2,1,0:T(8,128)(2,1)S(1)} async-done(((bf16[8,32,1280]{2,1,0:T(8,128)(2,1)}), bf16[8,32,1280]{2,1,0:T(8,128)(2,1)S(1)}, u32[]{:S(2)}, u32[]{:S(2)}) %all-to-all-start) | async-done | bytes 655392 | tf_op jit(solution)/shard_map/all_to_all | solution.py:233
  28.2 2.6 %collective-permute-start.1 = (bf16[320,256]{1,0:T(8,128)(2,1)S(1)}, bf16[320,256]{1,0:T(8,128)(2,1)S(1)}, u32[]{:S(2)}, u32[]{:S(2)}) collective-permute-start(bf16[320,256]{1,0:T(8,128)(2,1)S(1)} %get-tuple-element.83), channel_id=1, source_target_pairs={{0,2},{1,3},{2,0},{3,1},{4,6},{5,7},{6,4},{7,5},{8,10},{9,11},{10,... | collective-permute-start | bytes 491528 | tf_op jit(solution)/shard_map/ppermute | solution.py:206
  33.1 2.2 %collective-permute-done = bf16[320,256]{1,0:T(8,128)(2,1)S(1)} collective-permute-done((bf16[320,256]{1,0:T(8,128)(2,1)S(1)}, bf16[320,256]{1,0:T(8,128)(2,1)S(1)}, u32[]{:S(2)}, u32[]{:S(2)}) %collective-permute-start) | collective-permute-done | bytes 163872 | tf_op jit(solution)/shard_map/ppermute | solution.py:206
  35.3 4.2 %collective-permute-done.1 = bf16[320,256]{1,0:T(8,128)(2,1)S(1)} collective-permute-done((bf16[320,256]{1,0:T(8,128)(2,1)S(1)}, bf16[320,256]{1,0:T(8,128)(2,1)S(1)}, u32[]{:S(2)}, u32[]{:S(2)}) %collective-permute-start.1) | collective-permute-done | bytes 163872 | tf_op jit(solution)/shard_map/ppermute | solution.py:206
  39.7 3.0 %collective-permute-start.3 = (bf16[4,160,256]{2,1,0:T(8,128)(2,1)S(1)}, bf16[4,160,256]{2,1,0:T(8,128)(2,1)S(1)}, u32[]{:S(2)}, u32[]{:S(2)}) collective-permute-start(bf16[4,160,256]{2,1,0:T(8,128)(2,1)S(1)} %get-tuple-element.169), channel_id=1, source_target_pairs={{0,8},{4,12},{8,0},{12,4},{16,24},{20,28},{24,16},{28,20},{1,9},{5... | collective-permute-start | bytes 983048 | tf_op jit(solution)/shard_map/ppermute | solution.py:199
  43.0 7.4 %collective-permute-done.3 = bf16[4,160,256]{2,1,0:T(8,128)(2,1)S(1)} collective-permute-done((bf16[4,160,256]{2,1,0:T(8,128)(2,1)S(1)}, bf16[4,160,256]{2,1,0:T(8,128)(2,1)S(1)}, u32[]{:S(2)}, u32[]{:S(2)}) %collective-permute-start.3) | collective-permute-done | bytes 327712 | tf_op jit(solution)/shard_map/ppermute | solution.py:199
  53.9 2.2 %fusion.7 = f32[8,32,1024]{2,1,0:T(8,128)} fusion(bf16[8,32,1024]{2,1,0:T(8,128)(2,1)} %param.16, f32[8]{0:T(128)S(1)} %multiply_multiply_fusion), kind=kLoop, calls=%fused_computation.20 | loop fusion | flops 1048576 | bytes 1572896 | tf_op jit(solution)/shard_map/convert_element_type | solution.py:276
  58.2 2.5 %gather_fusion.2 = bf16[32,160,256]{2,1,0:T(8,128)(2,1)S(1)} fusion(bf16[32,160,256]{2,1,0:T(8,128)(2,1)} %bitcast.136, s32[1024]{0:T(1024)S(1)} %get-tuple-element.188), kind=kCustom, calls=%fused_computation.2 | custom fusion | bytes 5243008 | tf_op jit(solution)/shard_map/gather | solution.py:168
  60.6 9.8 %collective-permute-done.6 = bf16[256,1280]{1,0:T(8,128)(2,1)} collective-permute-done((bf16[256,1280]{1,0:T(8,128)(2,1)S(1)}, bf16[256,1280]{1,0:T(8,128)(2,1)}, u32[]{:S(2)}, u32[]{:S(2)}) %collective-permute-start.6) | collective-permute-done | bytes 655392 | tf_op jit(solution)/shard_map/ppermute | solution.py:199
  82.0 7.3 %shard_map.138 = (f32[128,1024]{1,0:T(8,128)S(1)}, f32[128,1024]{1,0:T(8,128)S(1)}, f32[128,256]{1,0:T(8,128)S(1)}) custom-call(bf16[4,128,1280]{2,1,0:T(8,128)(2,1)S(1)} %bitcast.127, bf16[5120,1024]{1,0:T(8,128)(2,1)} %wq_ref.3, bf16[5120,256]{1,0:T(8,128)(2,1)S(1)} %bitcast.124, f32[128,1024]{1,0:T(8,128)S(1)} %bitcast.131, f32[1,128]{1,0:T(1,128)S(1)} %bitcast.132, ...), custom_call_target="tpu_custom_call" | custom-call | flops 1677721600 | bytes 10485760 | tf_op jit(solution)/shard_map/pallas_call | solution.py:136
  89.3 2.9 %collective-permute-done.8 = bf16[128,1280]{1,0:T(8,128)(2,1)S(1)} collective-permute-done((bf16[128,1280]{1,0:T(8,128)(2,1)S(1)}, bf16[128,1280]{1,0:T(8,128)(2,1)S(1)}, u32[]{:S(2)}, u32[]{:S(2)}) %collective-permute-start.8) | collective-permute-done | bytes 327712 | tf_op jit(solution)/shard_map/ppermute | solution.py:199
  92.2 6.5 %collective-permute-done.12 = bf16[128,1280]{1,0:T(8,128)(2,1)S(1)} collective-permute-done((bf16[128,1280]{1,0:T(8,128)(2,1)S(1)}, bf16[128,1280]{1,0:T(8,128)(2,1)S(1)}, u32[]{:S(2)}, u32[]{:S(2)}) %collective-permute-start.12) | collective-permute-done | bytes 327712 | tf_op jit(solution)/shard_map/ppermute | solution.py:199
  108.0 3.7 %collective-permute-done.14 = bf16[128,1024]{1,0:T(8,128)(2,1)} collective-permute-done((bf16[128,1024]{1,0:T(8,128)(2,1)S(1)}, bf16[128,1024]{1,0:T(8,128)(2,1)}, u32[]{:S(2)}, u32[]{:S(2)}) %collective-permute-start.14) | collective-permute-done | bytes 262176 | tf_op jit(solution)/shard_map/ppermute | solution.py:199
  111.7 2.3 %dynamic-slice_bitcast_fusion = (bf16[128,1280]{1,0:T(8,128)(2,1)}, bf16[128,1280]{1,0:T(8,128)(2,1)S(1)}, bf16[128,1280]{1,0:T(8,128)(2,1)S(1)}, bf16[128,1280]{1,0:T(8,128)(2,1)}) fusion(bf16[4,128,1280]{2,1,0:T(8,128)(2,1)} %bitcast.128, s32[]{:T(128)S(6)} %select_n.310, s32[]{:T(128)S(6)} %select_n.309, s32[]{:T(128)S(6)} %select_n.308, s32[]{:T(128)S(6)} %select_n.307), kind=kLoop, calls=%fused_computation.42 | loop fusion | bytes 2621456 | tf_op jit(solution)/shard_map/jit(dynamic_index_in_dim)/squeeze | solution.py:282
  116.9 3.4 %fusion.3 = f32[640,1024]{1,0:T(8,128)} fusion(bf16[512,1024]{1,0:T(8,128)(2,1)S(1)} %constant_dynamic-update-slice_fusion.4, bf16[512,1280]{1,0:T(8,128)(2,1)} %constant_dynamic-update-slice_fusion, s32[]{:T(128)S(6)} %select_n.312), kind=kOutput, calls=%fused_computation.16 | convolution fusion | flops 671088640 | bytes 4325380 | tf_op jit(solution)/shard_map/td,tc->dc/dot_general | solution.py:314
  120.4 3.6 %fusion.5 = f32[640,1024]{1,0:T(8,128)} fusion(bf16[512,1024]{1,0:T(8,128)(2,1)S(1)} %constant_dynamic-update-slice_fusion.4, bf16[512,1280]{1,0:T(8,128)(2,1)} %constant_dynamic-update-slice_fusion, s32[]{:T(128)S(6)} %select_n.311), kind=kOutput, calls=%fused_computation.18 | convolution fusion | flops 671088640 | bytes 4325380 | tf_op jit(solution)/shard_map/td,tc->dc/dot_general | solution.py:314
  124.0 3.5 %collective-permute-start.21 = (bf16[128,1280]{1,0:T(8,128)(2,1)}, bf16[128,1280]{1,0:T(8,128)(2,1)}, u32[]{:S(2)}, u32[]{:S(2)}) collective-permute-start(bf16[128,1280]{1,0:T(8,128)(2,1)} %get-tuple-element.127), channel_id=1, source_target_pairs={{0,24},{4,28},{8,16},{12,20},{16,8},{20,12},{24,0},{28,4},{1,25},{... | collective-permute-start | bytes 983048 | tf_op jit(solution)/shard_map/ppermute | solution.py:199
  127.4 7.3 %shard_map.139 = (f32[128,1024]{1,0:T(8,128)S(1)}, f32[128,1024]{1,0:T(8,128)S(1)}, f32[128,256]{1,0:T(8,128)S(1)}) custom-call(bf16[4,128,1280]{2,1,0:T(8,128)(2,1)S(1)} %bitcast.129, bf16[5120,1024]{1,0:T(8,128)(2,1)} %wq_ref.3, bf16[5120,256]{1,0:T(8,128)(2,1)S(1)} %bitcast.125, f32[128,1024]{1,0:T(8,128)S(1)} %bitcast.130, f32[1,128]{1,0:T(1,128)S(1)} %bitcast.133, ...), custom_call_target="tpu_custom_call" | custom-call | flops 1677721600 | bytes 10485760 | tf_op jit(solution)/shard_map/pallas_call | solution.py:136
  137.0 12.5 %collective-permute-start.18 = (bf16[256,256]{1,0:T(8,128)(2,1)S(1)}, bf16[256,256]{1,0:T(8,128)(2,1)S(1)}, u32[]{:S(2)}, u32[]{:S(2)}) collective-permute-start(bf16[256,256]{1,0:T(8,128)(2,1)S(1)} %constant_dynamic-update-slice_fusion.8), channel_id=1, source_target_pairs={{0,1},{1,2},{2,3},{3,0},{4,5},{5,6},{6,7},{7,4},{8,9},{9,10},{10,1... | collective-permute-start | bytes 393224 | tf_op jit(solution)/shard_map/ppermute | solution.py:206
  153.2 3.2 %collective-permute-done.19 = bf16[256,256]{1,0:T(8,128)(2,1)S(1)} collective-permute-done((bf16[256,256]{1,0:T(8,128)(2,1)S(1)}, bf16[256,256]{1,0:T(8,128)(2,1)S(1)}, u32[]{:S(2)}, u32[]{:S(2)}) %collective-permute-start.19) | collective-permute-done | bytes 131104 | tf_op jit(solution)/shard_map/ppermute | solution.py:206
  159.4 2.0 %collective-permute-start.24 = (bf16[256,256]{1,0:T(8,128)(2,1)S(1)}, bf16[256,256]{1,0:T(8,128)(2,1)S(1)}, u32[]{:S(2)}, u32[]{:S(2)}) collective-permute-start(bf16[256,256]{1,0:T(8,128)(2,1)S(1)} %get-tuple-element.179), channel_id=1, source_target_pairs={{0,16},{4,20},{8,24},{12,28},{16,0},{20,4},{24,8},{28,12},{1,17},{... | collective-permute-start | bytes 393224 | tf_op jit(solution)/shard_map/ppermute | solution.py:199
  161.5 3.4 %collective-permute-done.23 = bf16[256,256]{1,0:T(8,128)(2,1)S(1)} collective-permute-done((bf16[256,256]{1,0:T(8,128)(2,1)S(1)}, bf16[256,256]{1,0:T(8,128)(2,1)S(1)}, u32[]{:S(2)}, u32[]{:S(2)}) %collective-permute-start.23) | collective-permute-done | bytes 131104 | tf_op jit(solution)/shard_map/ppermute | solution.py:199
  180.3 3.0 %add_add_fusion = f32[640,1024]{1,0:T(8,128)} fusion(bf16[640,1024]{1,0:T(8,128)(2,1)S(1)} %collective-permute-done.28, f32[640,1024]{1,0:T(8,128)S(1)} %fusion.10, f32[640,1024]{1,0:T(8,128)S(1)} %copy-done.14, bf16[128,1024]{1,0:T(8,128)(2,1)S(1)} %collective-permute-done.22, bf16[128,1280]{1,0:T(8,128)(2,1)} %collective-permute-done.21, s32[]{:T(128)S(6)} %select_n.312), kind=kOutput, calls=%fused_computation.8 | convolution fusion | flops 170393600 | bytes 9601028 | tf_op jit(solution)/shard_map/td,tc->dc/dot_general | solution.py:314
  (168 shorter events, 63.3 us)
Async XLA Ops:
  9.7 16.3 %all-to-all-start = ((bf16[8,32,1280]{2,1,0:T(8,128)(2,1)}), bf16[8,32,1280]{2,1,0:T(8,128)(2,1)S(1)}, u32[]{:S(2)}, u32[]{:S(2)}) async-start(bf16[8,32,1280]{2,1,0:T(8,128)(2,1)} %gather_fusion), calls=%async_computation | async-start | bytes 1310720 | tf_op jit(solution)/shard_map/all_to_all | solution.py:233
  14.9 61.1 %all-gather.5.cloned.1.call-start = ((), (), s32[]{:S(2)}) async-start(), calls=%async_computation.1 | async-start | bytes 1638400 | tf_op jit(solution)/shard_map/all_gather | solution.py:257
  26.6 8.7 %collective-permute-start = (bf16[320,256]{1,0:T(8,128)(2,1)S(1)}, bf16[320,256]{1,0:T(8,128)(2,1)S(1)}, u32[]{:S(2)}, u32[]{:S(2)}) collective-permute-start(bf16[320,256]{1,0:T(8,128)(2,1)S(1)} %get-tuple-element.82), channel_id=1, source_target_pairs={{0,1},{1,2},{2,3},{3,0},{4,5},{5,6},{6,7},{7,4},{8,9},{9,10},{10,1... | collective-permute-start | bytes 491528 | tf_op jit(solution)/shard_map/ppermute | solution.py:206
  28.2 11.2 %collective-permute-start.1 = (bf16[320,256]{1,0:T(8,128)(2,1)S(1)}, bf16[320,256]{1,0:T(8,128)(2,1)S(1)}, u32[]{:S(2)}, u32[]{:S(2)}) collective-permute-start(bf16[320,256]{1,0:T(8,128)(2,1)S(1)} %get-tuple-element.83), channel_id=1, source_target_pairs={{0,2},{1,3},{2,0},{3,1},{4,6},{5,7},{6,4},{7,5},{8,10},{9,11},{10,... | collective-permute-start | bytes 491528 | tf_op jit(solution)/shard_map/ppermute | solution.py:206
  33.1 73.4 %all-gather.7.cloned.1.call-start = ((), (), s32[]{:S(2)}) async-start(), calls=%async_computation.2 | async-start | bytes 1638400 | tf_op jit(solution)/shard_map/all_gather | solution.py:260
  39.7 10.8 %collective-permute-start.3 = (bf16[4,160,256]{2,1,0:T(8,128)(2,1)S(1)}, bf16[4,160,256]{2,1,0:T(8,128)(2,1)S(1)}, u32[]{:S(2)}, u32[]{:S(2)}) collective-permute-start(bf16[4,160,256]{2,1,0:T(8,128)(2,1)S(1)} %get-tuple-element.169), channel_id=1, source_target_pairs={{0,8},{4,12},{8,0},{12,4},{16,24},{20,28},{24,16},{28,20},{1,9},{5... | collective-permute-start | bytes 983048 | tf_op jit(solution)/shard_map/ppermute | solution.py:199
  42.7 9.3 %collective-permute-start.4 = (bf16[4,160,256]{2,1,0:T(8,128)(2,1)S(1)}, bf16[4,160,256]{2,1,0:T(8,128)(2,1)S(1)}, u32[]{:S(2)}, u32[]{:S(2)}) collective-permute-start(bf16[4,160,256]{2,1,0:T(8,128)(2,1)S(1)} %get-tuple-element.170), channel_id=1, source_target_pairs={{0,16},{4,20},{8,24},{12,28},{16,0},{20,4},{24,8},{28,12},{1,17},{... | collective-permute-start | bytes 983048 | tf_op jit(solution)/shard_map/ppermute | solution.py:199
  53.2 17.3 %collective-permute-start.6 = (bf16[256,1280]{1,0:T(8,128)(2,1)S(1)}, bf16[256,1280]{1,0:T(8,128)(2,1)}, u32[]{:S(2)}, u32[]{:S(2)}) collective-permute-start(bf16[256,1280]{1,0:T(8,128)(2,1)S(1)} %bitcast.138), channel_id=1, source_target_pairs={{0,8},{4,12},{8,0},{12,4},{16,24},{20,28},{24,16},{28,20},{1,9},{5... | collective-permute-start | bytes 1966088 | tf_op jit(solution)/shard_map/ppermute | solution.py:199
  53.6 17.0 %collective-permute-start.7 = (bf16[256,1280]{1,0:T(8,128)(2,1)S(1)}, bf16[256,1280]{1,0:T(8,128)(2,1)}, u32[]{:S(2)}, u32[]{:S(2)}) collective-permute-start(bf16[256,1280]{1,0:T(8,128)(2,1)S(1)} %bitcast.139), channel_id=1, source_target_pairs={{0,16},{4,20},{8,24},{12,28},{16,0},{20,4},{24,8},{28,12},{1,17},{... | collective-permute-start | bytes 1966088 | tf_op jit(solution)/shard_map/ppermute | solution.py:199
  72.3 17.0 %collective-permute-start.10 = (bf16[128,1280]{1,0:T(8,128)(2,1)}, bf16[128,1280]{1,0:T(8,128)(2,1)}, u32[]{:S(2)}, u32[]{:S(2)}) collective-permute-start(bf16[128,1280]{1,0:T(8,128)(2,1)} %slice.86), channel_id=1, source_target_pairs={{0,16},{4,20},{8,24},{12,28},{16,0},{20,4},{24,8},{28,12},{1,17},{... | collective-permute-start | bytes 983048 | tf_op jit(solution)/shard_map/ppermute | solution.py:199
  74.3 15.0 %collective-permute-start.11 = (bf16[128,1280]{1,0:T(8,128)(2,1)}, bf16[128,1280]{1,0:T(8,128)(2,1)}, u32[]{:S(2)}, u32[]{:S(2)}) collective-permute-start(bf16[128,1280]{1,0:T(8,128)(2,1)} %slice.87), channel_id=1, source_target_pairs={{0,8},{4,12},{8,0},{12,4},{16,24},{20,28},{24,16},{28,20},{1,9},{5... | collective-permute-start | bytes 983048 | tf_op jit(solution)/shard_map/ppermute | solution.py:199
  77.5 14.7 %collective-permute-start.8 = (bf16[128,1280]{1,0:T(8,128)(2,1)S(1)}, bf16[128,1280]{1,0:T(8,128)(2,1)S(1)}, u32[]{:S(2)}, u32[]{:S(2)}) collective-permute-start(bf16[128,1280]{1,0:T(8,128)(2,1)S(1)} %get-tuple-element.97), channel_id=1, source_target_pairs={{0,8},{4,12},{8,0},{12,4},{16,24},{20,28},{24,16},{28,20},{1,9},{5... | collective-permute-start | bytes 983048 | tf_op jit(solution)/shard_map/ppermute | solution.py:199
  77.9 14.3 %collective-permute-start.9 = (bf16[128,1280]{1,0:T(8,128)(2,1)S(1)}, bf16[128,1280]{1,0:T(8,128)(2,1)S(1)}, u32[]{:S(2)}, u32[]{:S(2)}) collective-permute-start(bf16[128,1280]{1,0:T(8,128)(2,1)S(1)} %get-tuple-element.98), channel_id=1, source_target_pairs={{0,16},{4,20},{8,24},{12,28},{16,0},{20,4},{24,8},{28,12},{1,17},{... | collective-permute-start | bytes 983048 | tf_op jit(solution)/shard_map/ppermute | solution.py:199
  79.6 19.1 %collective-permute-start.12 = (bf16[128,1280]{1,0:T(8,128)(2,1)S(1)}, bf16[128,1280]{1,0:T(8,128)(2,1)S(1)}, u32[]{:S(2)}, u32[]{:S(2)}) collective-permute-start(bf16[128,1280]{1,0:T(8,128)(2,1)S(1)} %get-tuple-element.105), channel_id=1, source_target_pairs={{0,24},{4,28},{8,16},{12,20},{16,8},{20,12},{24,0},{28,4},{1,25},{... | collective-permute-start | bytes 983048 | tf_op jit(solution)/shard_map/ppermute | solution.py:199
  98.7 9.3 %collective-permute-start.13 = (bf16[128,1024]{1,0:T(8,128)(2,1)S(1)}, bf16[128,1024]{1,0:T(8,128)(2,1)}, u32[]{:S(2)}, u32[]{:S(2)}) collective-permute-start(bf16[128,1024]{1,0:T(8,128)(2,1)S(1)} %convert_element_type.47), channel_id=1, source_target_pairs={{0,8},{4,12},{8,0},{12,4},{16,24},{20,28},{24,16},{28,20},{1,9},{5... | collective-permute-start | bytes 786440 | tf_op jit(solution)/shard_map/ppermute | solution.py:199
  100.1 11.6 %collective-permute-start.14 = (bf16[128,1024]{1,0:T(8,128)(2,1)S(1)}, bf16[128,1024]{1,0:T(8,128)(2,1)}, u32[]{:S(2)}, u32[]{:S(2)}) collective-permute-start(bf16[128,1024]{1,0:T(8,128)(2,1)S(1)} %convert_element_type.47), channel_id=1, source_target_pairs={{0,16},{4,20},{8,24},{12,28},{16,0},{20,4},{24,8},{28,12},{1,17},{... | collective-permute-start | bytes 786440 | tf_op jit(solution)/shard_map/ppermute | solution.py:199
  100.5 15.5 %collective-permute-start.15 = (bf16[128,1024]{1,0:T(8,128)(2,1)S(1)}, bf16[128,1024]{1,0:T(8,128)(2,1)}, u32[]{:S(2)}, u32[]{:S(2)}) collective-permute-start(bf16[128,1024]{1,0:T(8,128)(2,1)S(1)} %convert_element_type.47), channel_id=1, source_target_pairs={{0,24},{4,28},{8,16},{12,20},{16,8},{20,12},{24,0},{28,4},{1,25},{... | collective-permute-start | bytes 786440 | tf_op jit(solution)/shard_map/ppermute | solution.py:199
  114.0 21.6 %collective-permute-start.16 = (bf16[128,1280]{1,0:T(8,128)(2,1)S(1)}, bf16[128,1280]{1,0:T(8,128)(2,1)S(1)}, u32[]{:S(2)}, u32[]{:S(2)}) collective-permute-start(bf16[128,1280]{1,0:T(8,128)(2,1)S(1)} %get-tuple-element.119), channel_id=1, source_target_pairs={{0,8},{4,12},{8,0},{12,4},{16,24},{20,28},{24,16},{28,20},{1,9},{5... | collective-permute-start | bytes 983048 | tf_op jit(solution)/shard_map/ppermute | solution.py:199
  114.0 21.6 %collective-permute-start.17 = (bf16[128,1280]{1,0:T(8,128)(2,1)S(1)}, bf16[128,1280]{1,0:T(8,128)(2,1)S(1)}, u32[]{:S(2)}, u32[]{:S(2)}) collective-permute-start(bf16[128,1280]{1,0:T(8,128)(2,1)S(1)} %get-tuple-element.120), channel_id=1, source_target_pairs={{0,16},{4,20},{8,24},{12,28},{16,0},{20,4},{24,8},{28,12},{1,17},{... | collective-permute-start | bytes 983048 | tf_op jit(solution)/shard_map/ppermute | solution.py:199
  124.0 28.9 %collective-permute-start.21 = (bf16[128,1280]{1,0:T(8,128)(2,1)}, bf16[128,1280]{1,0:T(8,128)(2,1)}, u32[]{:S(2)}, u32[]{:S(2)}) collective-permute-start(bf16[128,1280]{1,0:T(8,128)(2,1)} %get-tuple-element.127), channel_id=1, source_target_pairs={{0,24},{4,28},{8,16},{12,20},{16,8},{20,12},{24,0},{28,4},{1,25},{... | collective-permute-start | bytes 983048 | tf_op jit(solution)/shard_map/ppermute | solution.py:199
  137.0 16.1 %collective-permute-start.18 = (bf16[256,256]{1,0:T(8,128)(2,1)S(1)}, bf16[256,256]{1,0:T(8,128)(2,1)S(1)}, u32[]{:S(2)}, u32[]{:S(2)}) collective-permute-start(bf16[256,256]{1,0:T(8,128)(2,1)S(1)} %constant_dynamic-update-slice_fusion.8), channel_id=1, source_target_pairs={{0,1},{1,2},{2,3},{3,0},{4,5},{5,6},{6,7},{7,4},{8,9},{9,10},{10,1... | collective-permute-start | bytes 393224 | tf_op jit(solution)/shard_map/ppermute | solution.py:206
  157.1 10.1 %collective-permute-start.26 = (bf16[128,1024]{1,0:T(8,128)(2,1)S(1)}, bf16[128,1024]{1,0:T(8,128)(2,1)S(1)}, u32[]{:S(2)}, u32[]{:S(2)}) collective-permute-start(bf16[128,1024]{1,0:T(8,128)(2,1)S(1)} %convert_element_type.50), channel_id=1, source_target_pairs={{0,8},{4,12},{8,0},{12,4},{16,24},{20,28},{24,16},{28,20},{1,9},{5... | collective-permute-start | bytes 786440 | tf_op jit(solution)/shard_map/ppermute | solution.py:199
  157.2 10.1 %collective-permute-start.27 = (bf16[128,1024]{1,0:T(8,128)(2,1)S(1)}, bf16[128,1024]{1,0:T(8,128)(2,1)S(1)}, u32[]{:S(2)}, u32[]{:S(2)}) collective-permute-start(bf16[128,1024]{1,0:T(8,128)(2,1)S(1)} %convert_element_type.50), channel_id=1, source_target_pairs={{0,16},{4,20},{8,24},{12,28},{16,0},{20,4},{24,8},{28,12},{1,17},{... | collective-permute-start | bytes 786440 | tf_op jit(solution)/shard_map/ppermute | solution.py:199
  164.9 9.7 %collective-permute-start.22 = (bf16[128,1024]{1,0:T(8,128)(2,1)S(1)}, bf16[128,1024]{1,0:T(8,128)(2,1)S(1)}, u32[]{:S(2)}, u32[]{:S(2)}) collective-permute-start(bf16[128,1024]{1,0:T(8,128)(2,1)S(1)} %convert_element_type.50), channel_id=1, source_target_pairs={{0,24},{4,28},{8,16},{12,20},{16,8},{20,12},{24,0},{28,4},{1,25},{... | collective-permute-start | bytes 786440 | tf_op jit(solution)/shard_map/ppermute | solution.py:199
  (35 other events, 204.5 us)
Sparse Core Ops, SparseCore 0:
  33.2 30.4 all-gather.4
  65.8 34.5 all-gather.6

commit v7 on v4

--- a/solution.py
+++ b/solution.py
@@ -90,7 +90,7 @@
     kv_ref,
 ):
     step = pl.program_id(0)
-    x = x_ref[...]
+    x = x_ref[0]
     query_part = jnp.dot(x, wq_ref[...], preferred_element_type=F32)
     kv_part = jnp.dot(x, wkv_ref[...], preferred_element_type=F32)
 
@@ -129,18 +129,17 @@
 
 
 def attend(x, w_query, w_kv, d_out, query_gain, key_gain, length, device_cols):
-    tokens, depth = x.shape
+    blocks, tokens, width = x.shape
     cols = w_query.shape[1]
     kv_cols = w_kv.shape[1]
-    block = depth // 4
     whole = lambda shape: pl.BlockSpec(shape, lambda b: (0, 0))
     return pl.pallas_call(
         functools.partial(attend_kernel, length, device_cols),
-        grid=(depth // block,),
+        grid=(blocks,),
         in_specs=[
-            pl.BlockSpec((tokens, block), lambda b: (0, b)),
-            pl.BlockSpec((block, cols), lambda b: (b, 0)),
-            pl.BlockSpec((block, kv_cols), lambda b: (b, 0)),
+            pl.BlockSpec((1, tokens, width), lambda b: (b, 0, 0)),
+            pl.BlockSpec((width, cols), lambda b: (b, 0)),
+            pl.BlockSpec((width, kv_cols), lambda b: (b, 0)),
             whole(d_out.shape),
             whole(query_gain.shape),
             whole(key_gain.shape),
@@ -154,7 +153,7 @@
         scratch_shapes=[pltpu.VMEM((tokens, cols), F32), pltpu.VMEM((tokens, kv_cols), F32)],
         compiler_params=pltpu.CompilerParams(vmem_limit_bytes=40 * 1024 * 1024),
         cost_estimate=pl.CostEstimate(
-            flops=10 * tokens * depth * (cols + kv_cols),
+            flops=10 * x.size * (cols + kv_cols),
             bytes_accessed=8 * w_query.size,
             transcendentals=tokens * cols,
         ),
@@ -215,19 +214,10 @@
 
     def from_far(block, arrived):
         arrived = dict(zip(near, arrived))
-        middle = block.shape[0] // 2
-        blocks = [block]
-        for k in range(1, chips):
-            bits = [n for n in near if k & n]
-            if len(bits) == 1:
-                blocks.append(arrived[k])
-            elif len(bits) == 2:
-                first = flip(arrived[bits[0]][:middle], 2 * bits[1])
-                second = flip(arrived[bits[1]][middle:], 2 * bits[0])
-                blocks.append(jnp.concatenate([first, second]))
-            else:
-                blocks.append(flip(block, 2 * k))
-        return blocks
+        return [
+            block if k == 0 else arrived[k] if k in arrived else flip(block, 2 * k)
+            for k in range(chips)
+        ]
 
     outgoing = pick(pool, jnp.maximum(send_table[0], 0))
     outgoing, w_key, w_value = together(outgoing, w_key, w_value)
@@ -242,12 +232,12 @@
         pairs.append(jnp.concatenate([own_key[:, columns], own_value[:, columns]], axis=1))
     pairs = jnp.stack(pairs)
     heads = [(mp + k) % n_mp * KV_HEADS // n_mp for k in range(n_mp)]
-    shares = around([lax.dynamic_index_in_dim(pairs, h, 0, False) for h in heads])
-    arrived, *shares = together(arrived, *shares)
-    shares = jnp.stack(shares)
+    pairs = [lax.dynamic_index_in_dim(pairs, h, 0, False) for h in heads]
+    arrived, pairs = lax.optimization_barrier((arrived, pairs))
+    shares = jnp.stack(around(pairs))
     rows = pick(arrived, slot_source).reshape(tokens, width)
 
-    x = lax.all_gather(rows, "mp", axis=1, tiled=True)
+    x = lax.all_gather(rows, "mp", axis=0)
     shares = jnp.stack([shares] + other_chips([shares] * chips))
     native, shares = together(rows, shares)
     other_shares, *plane_rows = together(flip(shares, 1), *from_near(native))
@@ -260,11 +250,15 @@
     x, w_kv, plane_rows = together(x, w_kv, plane_rows)
 
     chip_width = n_mp * width // chips
-    chip_rows = [
-        lax.dynamic_slice_in_dim(x, (chip ^ k) * chip_width, chip_width, 1) for k in range(chips)
-    ]
-    x, *chip_rows = together(x, *chip_rows)
-    chip_rows = [chip_rows[0]] + other_chips(chip_rows)
+
+    def chip_part(k):
+        if chip_width == width:
+            return lax.dynamic_index_in_dim(x, chip ^ k, 0, False)
+        flat = x.transpose(1, 0, 2).reshape(tokens, -1)
+        return lax.dynamic_slice_in_dim(flat, (chip ^ k) * chip_width, chip_width, 1)
+
+    x, *chip_rows = together(x, *[chip_part(k) for k in range(chips)])
+    near_rows = [flip(chip_rows[k], 2 * k) for k in near]
 
     factor = multiplicity.astype(F32) * slot_weight / length
     d_out = (cotangent.astype(F32) * factor[:, None, None]).astype(BF16).astype(F32)
@@ -279,10 +273,16 @@
         key_cols // n_dp,
     )
     attended, d_query, d_kv = [value.astype(BF16) for value in (attended, d_query, d_kv)]
-    d_query, d_kv, *chip_rows = together(d_query, d_kv, *chip_rows)
+    d_query, d_kv, *near_rows = together(d_query, d_kv, *near_rows)
+    chip_rows = [
+        chip_rows[0] if k == 0 else near_rows[near.index(k)] if k in near else flip(chip_rows[k], 2 * k)
+        for k in range(chips)
+    ]
+    spread = around([d_kv] * n_mp)
+    d_query, spread, chip_rows = lax.optimization_barrier((d_query, spread, chip_rows))
+    spread = jnp.stack(spread)
 
     d_all = [d_query] + other_chips([d_query] * chips)
-    spread = jnp.stack(around([d_kv] * n_mp))
     half = chip_width // 2
     early = [0] + near
     late = [k for k in range(chips) if k not in early]

time: 165 us -> 176 us (1.067)
  starting transfers between devices: 29.6 us -> 51.8 us
  waiting for transfers between devices: 77.6 us -> 66.1 us
  other arithmetic: 12.2 us -> 9.93 us
  matrix products: 6.02 us -> 7.95 us
    ppermute x19 -> x18, starting transfers between devices: 18.8 us -> 38.9 us  [flip(): return lax.ppermute(block, 'dp', [(i, i ^ bits) for i in range(n_dp)])]
    ppermute x6, waiting for transfers between devices: 16.7 us -> 5 us  [around(): lax.ppermute(blocks[k], 'mp', [(i, (i + k) % n_mp) for i in range(n_mp)])]
    all_to_all x1, waiting for transfers between devices: 0.01 us -> 7.14 us  [local(): lax.all_to_all(outgoing, 'dp', split_axis=0, concat_axis=0, tiled=True)]
    all_gather x1, waiting for transfers between devices: 3.51 us -> 0.01 us  [local(): x = lax.all_gather(rows, 'mp', axis=0)]
    ppermute x19 -> x18, waiting for transfers between devices: 57.3 us -> 53.9 us  [flip(): return lax.ppermute(block, 'dp', [(i, i ^ bits) for i in range(n_dp)])]
    squeeze x1 -> x2, local copies, waits for them, and re-layouts: 0.03 us -> 3.14 us  [the longest x1 3.11 us: chip_part(): return lax.dynamic_index_in_dim(x, chip ^ k, 0, False)]
    slice x2 -> x0, local copies, waits for them, and re-layouts: 2.7 us -> none  [the longest x1 1.95 us: from_far(): first = flip(arrived[bits[0]][:middle], 2 * bits[1])]
    unnamed x26 -> x40, local copies, waits for them, and re-layouts: 0.57 us -> 3.23 us
  transfers between devices with their start and end apart: 27 -> 26, of which waited for: 14 -> 14; matrix products, arithmetic and copies ran while one was open for 14% -> 11% of each run, Pallas kernels for 6% -> 6%
where the time goes in v7:
time: 176 us; the launch traced here: 174 us
  waiting for transfers between devices  66.1 us (38%)
  starting transfers between devices  51.8 us (29%)
  between operations  14.4 us (8%)
  local copies, waits for them, and re-layouts  13.7 us (8%)
  Pallas kernels  10.1 us (6%)
  other arithmetic  9.93 us (6%)
  matrix products  7.95 us (5%)
    ppermute x18, waiting for transfers between devices, flip(): return lax.ppermute(block, 'dp', [(i, i ^ bits) for i in range(n_dp)])  53.9 us
    ppermute x18, starting transfers between devices, flip(): return lax.ppermute(block, 'dp', [(i, i ^ bits) for i in range(n_dp)])  38.9 us
    pallas_call x1, Pallas kernels, attend(): pl.pallas_call(functools.partial(attend_kernel, length, device_cols), gri...  10.1 us
    ppermute x6, starting transfers between devices, around(): lax.ppermute(blocks[k], 'mp', [(i, (i + k) % n_mp) for i in range(n_mp)])  8.39 us
    all_to_all x1, waiting for transfers between devices, local(): lax.all_to_all(outgoing, 'dp', split_axis=0, concat_axis=0, tiled=True)  7.14 us
    dot_general x4, matrix products, product(): return jnp.einsum('td,tc->dc', mine, theirs, preferred_element_type=F32)  7.06 us
    gather x3, local copies, waits for them, and re-layouts, pick(): return array.at[index].get(mode='promise_in_bounds')  5.32 us
    ppermute x6, waiting for transfers between devices, around(): lax.ppermute(blocks[k], 'mp', [(i, (i + k) % n_mp) for i in range(n_mp)])  5 us
  transfers between devices with their start and end apart: 26, of which 14 were waited for; matrix products, arithmetic and copies ran while one was open for 11% of the time, Pallas kernels for 6%

profile of v7, /device:TPU:7, one launch (start us, length us, event | category | flops | bytes accessed | tf_op | source)
XLA Modules:
  0.0 174.0 jit_solution(2013860500436345549)
XLA Ops:
  9.7 4.5 %all-to-all-start = ((bf16[8,32,1280]{2,1,0:T(8,128)(2,1)}), bf16[8,32,1280]{2,1,0:T(8,128)(2,1)S(1)}, u32[]{:S(2)}, u32[]{:S(2)}) async-start(bf16[8,32,1280]{2,1,0:T(8,128)(2,1)} %gather_fusion), calls=%async_computation | async-start | bytes 1310720 | tf_op jit(solution)/shard_map/all_to_all | solution.py:224
  15.6 7.1 %all-to-all-done = bf16[8,32,1280]{2,1,0:T(8,128)(2,1)S(1)} async-done(((bf16[8,32,1280]{2,1,0:T(8,128)(2,1)}), bf16[8,32,1280]{2,1,0:T(8,128)(2,1)S(1)}, u32[]{:S(2)}, u32[]{:S(2)}) %all-to-all-start) | async-done | bytes 655392 | tf_op jit(solution)/shard_map/all_to_all | solution.py:224
  22.7 1.4 gather_fusion.1
  25.6 2.3 %collective-permute-start.1 = (bf16[160,256]{1,0:T(8,128)(2,1)S(1)}, bf16[160,256]{1,0:T(8,128)(2,1)S(1)}, u32[]{:S(2)}, u32[]{:S(2)}) collective-permute-start(bf16[160,256]{1,0:T(8,128)(2,1)S(1)} %get-tuple-element.47), channel_id=1, source_target_pairs={{0,2},{1,3},{2,0},{3,1},{4,6},{5,7},{6,4},{7,5},{8,10},{9,11},{10,... | collective-permute-start | bytes 245768 | tf_op jit(solution)/shard_map/ppermute | solution.py:206
  29.5 4.5 %collective-permute-done.1 = bf16[160,256]{1,0:T(8,128)(2,1)S(1)} collective-permute-done((bf16[160,256]{1,0:T(8,128)(2,1)S(1)}, bf16[160,256]{1,0:T(8,128)(2,1)S(1)}, u32[]{:S(2)}, u32[]{:S(2)}) %collective-permute-start.1) | collective-permute-done | bytes 81952 | tf_op jit(solution)/shard_map/ppermute | solution.py:206
  34.0 1.5 collective-permute-start.4
  36.8 5.7 %collective-permute-done.4 = bf16[4,160,256]{2,1,0:T(8,128)(2,1)S(1)} collective-permute-done((bf16[4,160,256]{2,1,0:T(8,128)(2,1)S(1)}, bf16[4,160,256]{2,1,0:T(8,128)(2,1)S(1)}, u32[]{:S(2)}, u32[]{:S(2)}) %collective-permute-start.4) | collective-permute-done | bytes 327712 | tf_op jit(solution)/shard_map/ppermute | solution.py:199
  43.7 6.8 %collective-permute-done.5 = bf16[4,160,256]{2,1,0:T(8,128)(2,1)S(1)} collective-permute-done((bf16[4,160,256]{2,1,0:T(8,128)(2,1)S(1)}, bf16[4,160,256]{2,1,0:T(8,128)(2,1)S(1)}, u32[]{:S(2)}, u32[]{:S(2)}) %collective-permute-start.5) | collective-permute-done | bytes 327712 | tf_op jit(solution)/shard_map/ppermute | solution.py:199
  50.7 2.0 %collective-permute-start.6 = (bf16[4,4,160,256]{3,2,1,0:T(8,128)(2,1)S(1)}, bf16[4,4,160,256]{3,2,1,0:T(8,128)(2,1)S(1)}, u32[]{:S(2)}, u32[]{:S(2)}) collective-permute-start(bf16[4,4,160,256]{3,2,1,0:T(8,128)(2,1)S(1)} %pad_maximum_fusion.2), channel_id=1, source_target_pairs={{0,4},{4,0},{8,12},{12,8},{16,20},{20,16},{24,28},{28,24},{1,5},{5... | collective-permute-start | bytes 3932168 | tf_op jit(solution)/shard_map/ppermute | solution.py:199
  57.8 11.4 %collective-permute-done.8 = bf16[256,1280]{1,0:T(8,128)(2,1)S(1)} collective-permute-done((bf16[256,1280]{1,0:T(8,128)(2,1)}, bf16[256,1280]{1,0:T(8,128)(2,1)S(1)}, u32[]{:S(2)}, u32[]{:S(2)}) %collective-permute-start.8) | collective-permute-done | bytes 655392 | tf_op jit(solution)/shard_map/ppermute | solution.py:199
  71.1 1.7 pad_maximum_fusion
  72.8 2.5 %gather_fusion.2 = bf16[32,160,256]{2,1,0:T(8,128)(2,1)S(1)} fusion(bf16[32,160,256]{2,1,0:T(8,128)(2,1)} %bitcast.80, s32[1024]{0:T(1024)S(1)} %get-tuple-element.102), kind=kCustom, calls=%fused_computation.2 | custom fusion | bytes 5243008 | tf_op jit(solution)/shard_map/gather | solution.py:168
  75.3 8.8 %collective-permute-done.9 = bf16[256,1280]{1,0:T(8,128)(2,1)} collective-permute-done((bf16[256,1280]{1,0:T(8,128)(2,1)}, bf16[256,1280]{1,0:T(8,128)(2,1)}, u32[]{:S(2)}, u32[]{:S(2)}) %collective-permute-start.9) | collective-permute-done | bytes 655392 | tf_op jit(solution)/shard_map/ppermute | solution.py:199
  84.1 3.5 %pad_maximum_fusion.1 = bf16[4,256,1280]{2,1,0:T(8,128)(2,1)} fusion(bf16[1,256,1280]{2,1,0:T(8,128)(2,1)} %bitcast.28, bf16[1,256,1280]{2,1,0:T(8,128)(2,1)} %bitcast.84, bf16[1,256,1280]{2,1,0:T(8,128)(2,1)} %bitcast.85, bf16[1,256,1280]{2,1,0:T(8,128)(2,1)} %bitcast.25), kind=kLoop, calls=%fused_computation.4 | loop fusion | flops 3932160 | bytes 5242880 | tf_op jit(solution)/shard_map/stack | solution.py:244
  87.6 3.1 %dynamic-slice_bitcast_fusion = (bf16[256,1280]{1,0:T(8,128)(2,1)}, bf16[256,1280]{1,0:T(8,128)(2,1)S(1)}, bf16[256,1280]{1,0:T(8,128)(2,1)S(1)}, bf16[256,1280]{1,0:T(8,128)(2,1)}) fusion(bf16[4,256,1280]{2,1,0:T(8,128)(2,1)} %all-gather.2.cloned.1.call-done.x_ref, s32[]{:T(128)S(6)} %select_n.162, s32[]{:T(128)S(6)} %select_n.161, s32[]{:T(128)S(6)} %select_n.160, ...), kind=kLoop, calls=%fused_computation.14 | loop fusion | bytes 5242896 | tf_op jit(solution)/shard_map/jit(dynamic_index_in_dim)/squeeze | solution.py:256
  93.4 10.1 %shard_map.138 = (f32[256,1024]{1,0:T(8,128)S(1)}, f32[256,1024]{1,0:T(8,128)S(1)}, f32[256,256]{1,0:T(8,128)S(1)}) custom-call(bf16[4,256,1280]{2,1,0:T(8,128)(2,1)S(1)} %copy-done.1, bf16[5120,1024]{1,0:T(8,128)(2,1)} %wq_ref.1, bf16[5120,256]{1,0:T(8,128)(2,1)S(1)} %bitcast.76, f32[256,1024]{1,0:T(8,128)S(1)} %copy-done.4, f32[1,128]{1,0:T(1,128)S(1)} %bitcast.77, ...), custom_call_target="tpu_custom_call" | custom-call | flops 16777216000 | bytes 41943040 | tf_op jit(solution)/shard_map/pallas_call | solution.py:136
  106.5 2.5 %collective-permute-start.14 = (bf16[256,256]{1,0:T(8,128)(2,1)S(1)}, bf16[256,256]{1,0:T(8,128)(2,1)S(1)}, u32[]{:S(2)}, u32[]{:S(2)}) collective-permute-start(bf16[256,256]{1,0:T(8,128)(2,1)S(1)} %convert_element_type.36), channel_id=1, source_target_pairs={{0,3},{1,0},{2,1},{3,2},{4,7},{5,4},{6,5},{7,6},{8,11},{9,8},{10,9... | collective-permute-start | bytes 393224 | tf_op jit(solution)/shard_map/ppermute | solution.py:206
  111.1 9.9 %collective-permute-done.15 = bf16[256,1280]{1,0:T(8,128)(2,1)} collective-permute-done((bf16[256,1280]{1,0:T(8,128)(2,1)}, bf16[256,1280]{1,0:T(8,128)(2,1)}, u32[]{:S(2)}, u32[]{:S(2)}) %collective-permute-start.15) | collective-permute-done | bytes 655392 | tf_op jit(solution)/shard_map/ppermute | solution.py:199
  121.4 2.5 %collective-permute-start.22 = (bf16[256,256]{1,0:T(8,128)(2,1)S(1)}, bf16[256,256]{1,0:T(8,128)(2,1)S(1)}, u32[]{:S(2)}, u32[]{:S(2)}) collective-permute-start(bf16[256,256]{1,0:T(8,128)(2,1)S(1)} %get-tuple-element.93), channel_id=1, source_target_pairs={{0,24},{4,28},{8,16},{12,20},{16,8},{20,12},{24,0},{28,4},{1,25},{... | collective-permute-start | bytes 393224 | tf_op jit(solution)/shard_map/ppermute | solution.py:199
  124.5 7.3 %collective-permute-done.22 = bf16[256,256]{1,0:T(8,128)(2,1)S(1)} collective-permute-done((bf16[256,256]{1,0:T(8,128)(2,1)S(1)}, bf16[256,256]{1,0:T(8,128)(2,1)S(1)}, u32[]{:S(2)}, u32[]{:S(2)}) %collective-permute-start.22) | collective-permute-done | bytes 131104 | tf_op jit(solution)/shard_map/ppermute | solution.py:199
  133.1 17.8 %collective-permute-start.23 = (bf16[1280,128]{0,1:T(8,128)(2,1)S(1)}, bf16[1280,128]{0,1:T(8,128)(2,1)S(1)}, u32[]{:S(2)}, u32[]{:S(2)}) collective-permute-start(bf16[1280,128]{0,1:T(8,128)(2,1)S(1)} %select_convert_fusion), channel_id=1, source_target_pairs={{0,4},{4,0},{8,12},{12,8},{16,20},{20,16},{24,28},{28,24},{1,5},{5... | collective-permute-start | bytes 983048 | tf_op jit(solution)/shard_map/ppermute | solution.py:199
  151.0 1.5 fusion.3
  153.8 7.6 %collective-permute-start.19 = (bf16[640,1024]{1,0:T(8,128)(2,1)S(1)}, bf16[640,1024]{1,0:T(8,128)(2,1)S(1)}, u32[]{:S(2)}, u32[]{:S(2)}) collective-permute-start(bf16[640,1024]{1,0:T(8,128)(2,1)S(1)} %add_convert_fusion), channel_id=1, source_target_pairs={{0,4},{4,0},{8,12},{12,8},{16,20},{20,16},{24,28},{28,24},{1,5},{5... | collective-permute-start | bytes 3932168 | tf_op jit(solution)/shard_map/ppermute | solution.py:199
  164.1 3.0 %add_add_fusion = f32[640,1024]{1,0:T(8,128)} fusion(f32[640,1024]{1,0:T(8,128)S(1)} %fusion.1, bf16[640,1024]{1,0:T(8,128)(2,1)S(1)} %collective-permute-done.19, bf16[256,1024]{1,0:T(8,128)(2,1)S(1)} %collective-permute-done.16, bf16[256,1280]{1,0:T(8,128)(2,1)} %collective-permute-done.15, s32[]{:T(128)S(6)} %select_n.164), kind=kOutput, calls=%fused_computation.5 | convolution fusion | flops 337510400 | bytes 7405572 | tf_op jit(solution)/shard_map/td,tc->dc/dot_general | solution.py:294
  (113 shorter events, 30.3 us)
Async XLA Ops:
  9.7 13.0 %all-to-all-start = ((bf16[8,32,1280]{2,1,0:T(8,128)(2,1)}), bf16[8,32,1280]{2,1,0:T(8,128)(2,1)S(1)}, u32[]{:S(2)}, u32[]{:S(2)}) async-start(bf16[8,32,1280]{2,1,0:T(8,128)(2,1)} %gather_fusion), calls=%async_computation | async-start | bytes 1310720 | tf_op jit(solution)/shard_map/all_to_all | solution.py:224
  14.2 73.4 %all-gather.2.cloned.1.call-start = ((), (), s32[]{:S(2)}) async-start(), calls=%async_computation.1 | async-start | bytes 3276800 | tf_op jit(solution)/shard_map/all_gather | solution.py:240
  25.6 8.4 %collective-permute-start.1 = (bf16[160,256]{1,0:T(8,128)(2,1)S(1)}, bf16[160,256]{1,0:T(8,128)(2,1)S(1)}, u32[]{:S(2)}, u32[]{:S(2)}) collective-permute-start(bf16[160,256]{1,0:T(8,128)(2,1)S(1)} %get-tuple-element.47), channel_id=1, source_target_pairs={{0,2},{1,3},{2,0},{3,1},{4,6},{5,7},{6,4},{7,5},{8,10},{9,11},{10,... | collective-permute-start | bytes 245768 | tf_op jit(solution)/shard_map/ppermute | solution.py:206
  34.0 8.5 %collective-permute-start.4 = (bf16[4,160,256]{2,1,0:T(8,128)(2,1)S(1)}, bf16[4,160,256]{2,1,0:T(8,128)(2,1)S(1)}, u32[]{:S(2)}, u32[]{:S(2)}) collective-permute-start(bf16[4,160,256]{2,1,0:T(8,128)(2,1)S(1)} %get-tuple-element.97), channel_id=1, source_target_pairs={{0,16},{4,20},{8,24},{12,28},{16,0},{20,4},{24,8},{28,12},{1,17},{... | collective-permute-start | bytes 983048 | tf_op jit(solution)/shard_map/ppermute | solution.py:199
  35.5 8.2 %collective-permute-start.3 = (bf16[4,160,256]{2,1,0:T(8,128)(2,1)S(1)}, bf16[4,160,256]{2,1,0:T(8,128)(2,1)S(1)}, u32[]{:S(2)}, u32[]{:S(2)}) collective-permute-start(bf16[4,160,256]{2,1,0:T(8,128)(2,1)S(1)} %get-tuple-element.97), channel_id=1, source_target_pairs={{0,8},{4,12},{8,0},{12,4},{16,24},{20,28},{24,16},{28,20},{1,9},{5... | collective-permute-start | bytes 983048 | tf_op jit(solution)/shard_map/ppermute | solution.py:199
  35.5 15.0 %collective-permute-start.5 = (bf16[4,160,256]{2,1,0:T(8,128)(2,1)S(1)}, bf16[4,160,256]{2,1,0:T(8,128)(2,1)S(1)}, u32[]{:S(2)}, u32[]{:S(2)}) collective-permute-start(bf16[4,160,256]{2,1,0:T(8,128)(2,1)S(1)} %get-tuple-element.97), channel_id=1, source_target_pairs={{0,24},{4,28},{8,16},{12,20},{16,8},{20,12},{24,0},{28,4},{1,25},{... | collective-permute-start | bytes 983048 | tf_op jit(solution)/shard_map/ppermute | solution.py:199
  50.7 19.6 %collective-permute-start.6 = (bf16[4,4,160,256]{3,2,1,0:T(8,128)(2,1)S(1)}, bf16[4,4,160,256]{3,2,1,0:T(8,128)(2,1)S(1)}, u32[]{:S(2)}, u32[]{:S(2)}) collective-permute-start(bf16[4,4,160,256]{3,2,1,0:T(8,128)(2,1)S(1)} %pad_maximum_fusion.2), channel_id=1, source_target_pairs={{0,4},{4,0},{8,12},{12,8},{16,20},{20,16},{24,28},{28,24},{1,5},{5... | collective-permute-start | bytes 3932168 | tf_op jit(solution)/shard_map/ppermute | solution.py:199
  52.7 16.5 %collective-permute-start.8 = (bf16[256,1280]{1,0:T(8,128)(2,1)}, bf16[256,1280]{1,0:T(8,128)(2,1)S(1)}, u32[]{:S(2)}, u32[]{:S(2)}) collective-permute-start(bf16[256,1280]{1,0:T(8,128)(2,1)} %bitcast.10), channel_id=1, source_target_pairs={{0,16},{4,20},{8,24},{12,28},{16,0},{20,4},{24,8},{28,12},{1,17},{... | collective-permute-start | bytes 1966088 | tf_op jit(solution)/shard_map/ppermute | solution.py:199
  54.1 16.2 %collective-permute-start.7 = (bf16[256,1280]{1,0:T(8,128)(2,1)}, bf16[256,1280]{1,0:T(8,128)(2,1)S(1)}, u32[]{:S(2)}, u32[]{:S(2)}) collective-permute-start(bf16[256,1280]{1,0:T(8,128)(2,1)} %bitcast.10), channel_id=1, source_target_pairs={{0,8},{4,12},{8,0},{12,4},{16,24},{20,28},{24,16},{28,20},{1,9},{5... | collective-permute-start | bytes 1966088 | tf_op jit(solution)/shard_map/ppermute | solution.py:199
  54.1 30.0 %collective-permute-start.9 = (bf16[256,1280]{1,0:T(8,128)(2,1)}, bf16[256,1280]{1,0:T(8,128)(2,1)}, u32[]{:S(2)}, u32[]{:S(2)}) collective-permute-start(bf16[256,1280]{1,0:T(8,128)(2,1)} %bitcast.10), channel_id=1, source_target_pairs={{0,24},{4,28},{8,16},{12,20},{16,8},{20,12},{24,0},{28,4},{1,25},{... | collective-permute-start | bytes 1966088 | tf_op jit(solution)/shard_map/ppermute | solution.py:199
  90.8 15.0 %collective-permute-start.10 = (bf16[256,1280]{1,0:T(8,128)(2,1)S(1)}, bf16[256,1280]{1,0:T(8,128)(2,1)S(1)}, u32[]{:S(2)}, u32[]{:S(2)}) collective-permute-start(bf16[256,1280]{1,0:T(8,128)(2,1)S(1)} %get-tuple-element.60), channel_id=1, source_target_pairs={{0,8},{4,12},{8,0},{12,4},{16,24},{20,28},{24,16},{28,20},{1,9},{5... | collective-permute-start | bytes 1966088 | tf_op jit(solution)/shard_map/ppermute | solution.py:199
  90.8 14.9 %collective-permute-start.11 = (bf16[256,1280]{1,0:T(8,128)(2,1)S(1)}, bf16[256,1280]{1,0:T(8,128)(2,1)S(1)}, u32[]{:S(2)}, u32[]{:S(2)}) collective-permute-start(bf16[256,1280]{1,0:T(8,128)(2,1)S(1)} %get-tuple-element.61), channel_id=1, source_target_pairs={{0,16},{4,20},{8,24},{12,28},{16,0},{20,4},{24,8},{28,12},{1,17},{... | collective-permute-start | bytes 1966088 | tf_op jit(solution)/shard_map/ppermute | solution.py:199
  92.2 28.8 %collective-permute-start.15 = (bf16[256,1280]{1,0:T(8,128)(2,1)}, bf16[256,1280]{1,0:T(8,128)(2,1)}, u32[]{:S(2)}, u32[]{:S(2)}) collective-permute-start(bf16[256,1280]{1,0:T(8,128)(2,1)} %get-tuple-element.67), channel_id=1, source_target_pairs={{0,24},{4,28},{8,16},{12,20},{16,8},{20,12},{24,0},{28,4},{1,25},{... | collective-permute-start | bytes 1966088 | tf_op jit(solution)/shard_map/ppermute | solution.py:199
  106.5 14.4 %collective-permute-start.14 = (bf16[256,256]{1,0:T(8,128)(2,1)S(1)}, bf16[256,256]{1,0:T(8,128)(2,1)S(1)}, u32[]{:S(2)}, u32[]{:S(2)}) collective-permute-start(bf16[256,256]{1,0:T(8,128)(2,1)S(1)} %convert_element_type.36), channel_id=1, source_target_pairs={{0,3},{1,0},{2,1},{3,2},{4,7},{5,4},{6,5},{7,6},{8,11},{9,8},{10,9... | collective-permute-start | bytes 393224 | tf_op jit(solution)/shard_map/ppermute | solution.py:206
  109.1 11.9 %collective-permute-start.13 = (bf16[256,256]{1,0:T(8,128)(2,1)S(1)}, bf16[256,256]{1,0:T(8,128)(2,1)S(1)}, u32[]{:S(2)}, u32[]{:S(2)}) collective-permute-start(bf16[256,256]{1,0:T(8,128)(2,1)S(1)} %convert_element_type.36), channel_id=1, source_target_pairs={{0,2},{1,3},{2,0},{3,1},{4,6},{5,7},{6,4},{7,5},{8,10},{9,11},{10,... | collective-permute-start | bytes 393224 | tf_op jit(solution)/shard_map/ppermute | solution.py:206
  109.8 11.2 %collective-permute-start.12 = (bf16[256,256]{1,0:T(8,128)(2,1)S(1)}, bf16[256,256]{1,0:T(8,128)(2,1)S(1)}, u32[]{:S(2)}, u32[]{:S(2)}) collective-permute-start(bf16[256,256]{1,0:T(8,128)(2,1)S(1)} %convert_element_type.36), channel_id=1, source_target_pairs={{0,1},{1,2},{2,3},{3,0},{4,5},{5,6},{6,7},{7,4},{8,9},{9,10},{10,1... | collective-permute-start | bytes 393224 | tf_op jit(solution)/shard_map/ppermute | solution.py:206
  121.0 30.0 %collective-permute-start.18 = (bf16[256,1024]{1,0:T(8,128)(2,1)S(1)}, bf16[256,1024]{1,0:T(8,128)(2,1)S(1)}, u32[]{:S(2)}, u32[]{:S(2)}) collective-permute-start(bf16[256,1024]{1,0:T(8,128)(2,1)S(1)} %convert_element_type.35), channel_id=1, source_target_pairs={{0,16},{4,20},{8,24},{12,28},{16,0},{20,4},{24,8},{28,12},{1,17},{... | collective-permute-start | bytes 1572872 | tf_op jit(solution)/shard_map/ppermute | solution.py:199
  121.2 29.8 %collective-permute-start.17 = (bf16[256,1024]{1,0:T(8,128)(2,1)S(1)}, bf16[256,1024]{1,0:T(8,128)(2,1)S(1)}, u32[]{:S(2)}, u32[]{:S(2)}) collective-permute-start(bf16[256,1024]{1,0:T(8,128)(2,1)S(1)} %convert_element_type.35), channel_id=1, source_target_pairs={{0,8},{4,12},{8,0},{12,4},{16,24},{20,28},{24,16},{28,20},{1,9},{5... | collective-permute-start | bytes 1572872 | tf_op jit(solution)/shard_map/ppermute | solution.py:199
  121.4 10.4 %collective-permute-start.22 = (bf16[256,256]{1,0:T(8,128)(2,1)S(1)}, bf16[256,256]{1,0:T(8,128)(2,1)S(1)}, u32[]{:S(2)}, u32[]{:S(2)}) collective-permute-start(bf16[256,256]{1,0:T(8,128)(2,1)S(1)} %get-tuple-element.93), channel_id=1, source_target_pairs={{0,24},{4,28},{8,16},{12,20},{16,8},{20,12},{24,0},{28,4},{1,25},{... | collective-permute-start | bytes 393224 | tf_op jit(solution)/shard_map/ppermute | solution.py:199
  123.9 8.1 %collective-permute-start.21 = (bf16[256,256]{1,0:T(8,128)(2,1)S(1)}, bf16[256,256]{1,0:T(8,128)(2,1)S(1)}, u32[]{:S(2)}, u32[]{:S(2)}) collective-permute-start(bf16[256,256]{1,0:T(8,128)(2,1)S(1)} %get-tuple-element.94), channel_id=1, source_target_pairs={{0,16},{4,20},{8,24},{12,28},{16,0},{20,4},{24,8},{28,12},{1,17},{... | collective-permute-start | bytes 393224 | tf_op jit(solution)/shard_map/ppermute | solution.py:199
  124.0 8.0 %collective-permute-start.20 = (bf16[256,256]{1,0:T(8,128)(2,1)S(1)}, bf16[256,256]{1,0:T(8,128)(2,1)S(1)}, u32[]{:S(2)}, u32[]{:S(2)}) collective-permute-start(bf16[256,256]{1,0:T(8,128)(2,1)S(1)} %get-tuple-element.95), channel_id=1, source_target_pairs={{0,8},{4,12},{8,0},{12,4},{16,24},{20,28},{24,16},{28,20},{1,9},{5... | collective-permute-start | bytes 393224 | tf_op jit(solution)/shard_map/ppermute | solution.py:199
  131.8 19.3 %collective-permute-start.16 = (bf16[256,1024]{1,0:T(8,128)(2,1)S(1)}, bf16[256,1024]{1,0:T(8,128)(2,1)S(1)}, u32[]{:S(2)}, u32[]{:S(2)}) collective-permute-start(bf16[256,1024]{1,0:T(8,128)(2,1)S(1)} %convert_element_type.35), channel_id=1, source_target_pairs={{0,24},{4,28},{8,16},{12,20},{16,8},{20,12},{24,0},{28,4},{1,25},{... | collective-permute-start | bytes 1572872 | tf_op jit(solution)/shard_map/ppermute | solution.py:199
  133.1 28.4 %collective-permute-start.23 = (bf16[1280,128]{0,1:T(8,128)(2,1)S(1)}, bf16[1280,128]{0,1:T(8,128)(2,1)S(1)}, u32[]{:S(2)}, u32[]{:S(2)}) collective-permute-start(bf16[1280,128]{0,1:T(8,128)(2,1)S(1)} %select_convert_fusion), channel_id=1, source_target_pairs={{0,4},{4,0},{8,12},{12,8},{16,20},{20,16},{24,28},{28,24},{1,5},{5... | collective-permute-start | bytes 983048 | tf_op jit(solution)/shard_map/ppermute | solution.py:199
  153.8 10.3 %collective-permute-start.19 = (bf16[640,1024]{1,0:T(8,128)(2,1)S(1)}, bf16[640,1024]{1,0:T(8,128)(2,1)S(1)}, u32[]{:S(2)}, u32[]{:S(2)}) collective-permute-start(bf16[640,1024]{1,0:T(8,128)(2,1)S(1)} %add_convert_fusion), channel_id=1, source_target_pairs={{0,4},{4,0},{8,12},{12,8},{16,20},{20,16},{24,28},{28,24},{1,5},{5... | collective-permute-start | bytes 3932168 | tf_op jit(solution)/shard_map/ppermute | solution.py:199
  (20 other events, 158.0 us)
Sparse Core Ops, SparseCore 0:
  24.3 55.9 all-gather.1

commit v8 on v5

--- a/solution.py
+++ b/solution.py
@@ -291,39 +291,32 @@
     attended, d_query, d_kv, first_parts, plane_rows = half_step(
         x_first, d_out[:middle], plane_rows
     )
-    first_all = [d_query] + other_chips([d_query] * chips)
-
+    plane_rows = jnp.concatenate([piece for pieces in plane_rows for piece in pieces])
+    x_second, first_parts, plane_rows, d_query, d_kv = lax.optimization_barrier(
+        (x_second, first_parts, plane_rows, d_query, d_kv)
+    )
+    attended_second, d_query_second, d_kv_second, second_parts, beside = half_step(
+        x_second, d_out[middle:], (attended, first_parts, d_query, d_kv)
+    )
+    attended, first_parts, d_query, d_kv = beside
+    attended = jnp.concatenate([attended, attended_second])
+    d_query = jnp.concatenate([d_query, d_query_second])
+    d_kv = jnp.concatenate([d_kv, d_kv_second])
+
+    d_all = [d_query] + other_chips([d_query] * chips)
+    spread = jnp.stack(around([d_kv] * n_mp))
     half = chip_width // 2
-
-    def product(mine, theirs, which):
-        mine = lax.dynamic_slice_in_dim(jnp.concatenate(mine), which * half, half, 1)
-        return jnp.einsum("td,tc->dc", mine, jnp.concatenate(theirs), preferred_element_type=F32)
-
-    x_second, first_other, first_own = together(
-        x_second, product(first_parts, first_all, 1 - core), product(first_parts, first_all, core)
-    )
-    attended_second, d_query, d_kv_second, second_parts, _ = half_step(x_second, d_out[middle:], [])
-    second_all = [d_query] + other_chips([d_query] * chips)
-    attended = jnp.concatenate([attended, attended_second])
-    d_kv = jnp.concatenate([d_kv, d_kv_second])
-    spread = jnp.stack(around([d_kv] * n_mp))
-    spread, *second_near = together(spread, *[second_all[k] for k in near])
-    for k, block in zip(near, second_near):
-        second_all[k] = block
-
-    some = [0] + near
-    rest = [k for k in range(chips) if k not in some]
-
-    def second(which):
-        return [
-            product([second_parts[k] for k in ks], [second_all[k] for k in ks], which)
-            for ks in (some, rest)
-        ]
-
-    early, late = second(1 - core)
-    other = flip((late + (early + first_other)).astype(BF16), 1)
-    early, late = second(core)
-    grad_query = late + ((early + first_own) + other.astype(F32))
+    early = [0] + near
+    late = [k for k in range(chips) if k not in early]
+
+    def product(some, which):
+        mine = jnp.concatenate([part[k] for k in some for part in (first_parts, second_parts)])
+        mine = lax.dynamic_slice_in_dim(mine, which * half, half, 1)
+        theirs = jnp.concatenate([d_all[k] for k in some])
+        return jnp.einsum("td,tc->dc", mine, theirs, preferred_element_type=F32)
+
+    other = flip((product(early, 1 - core) + product(late, 1 - core)).astype(BF16), 1)
+    grad_query = product(late, core) + (product(early, core) + other.astype(F32))
 
     if n_mp > KV_HEADS:
         spread = pick(spread, (mp - jnp.arange(n_mp)) % n_mp)
@@ -337,13 +330,8 @@
         spread = spread.reshape(KV_HEADS, tokens, chips // KV_HEADS, chip_cols)
         spread = spread.transpose(0, 2, 1, 3).reshape(chips, tokens, chip_cols)
     kv_all = [lax.dynamic_index_in_dim(spread, spread_at(chip ^ k), 0, False) for k in range(chips)]
-    kv_all = [kv_all[0]] + other_chips(kv_all)
-    partial = 0
-    for pieces, columns in zip(plane_rows, kv_all):
-        size = tokens // len(pieces)
-        for i, piece in enumerate(pieces):
-            part = columns[i * size : (i + 1) * size]
-            partial = partial + jnp.einsum("td,tc->dc", piece, part, preferred_element_type=F32)
+    kv_all = jnp.concatenate([kv_all[0]] + other_chips(kv_all))
+    partial = jnp.einsum("td,tc->dc", plane_rows, kv_all, preferred_element_type=F32)
     mine, theirs = partial[:, : chip_cols // 2], partial[:, chip_cols // 2 :]
     mine, theirs = jnp.where(core == 0, mine, theirs), jnp.where(core == 0, theirs, mine)
     grad_kv = mine + flip(theirs.astype(BF16), 1).astype(F32)

time: 172 us -> 168 us (0.977)
  waiting for transfers between devices: 59 us -> 45.2 us
  starting transfers between devices: 44.6 us -> 54.4 us
  local copies, waits for them, and re-layouts: 16.6 us -> 23.2 us
  matrix products: 14.2 us -> 7.75 us
    ppermute x25 -> x22, waiting for transfers between devices: 52 us -> 41.7 us  [flip(): return lax.ppermute(block, 'dp', [(i, i ^ bits) for i in range(n_dp)])]
    dot_general x11 -> x5, matrix products: 14.2 us -> 7.75 us  [the longest x4 5.11 us: product(): return jnp.einsum('td,tc->dc', mine, theirs, preferred_element_type=F32)]
    ppermute x25 -> x22, starting transfers between devices: 33.8 us -> 39.7 us  [flip(): return lax.ppermute(block, 'dp', [(i, i ^ bits) for i in range(n_dp)])]
    unnamed x45 -> x57, local copies, waits for them, and re-layouts: 1.96 us -> 6.09 us
    ppermute x6, starting transfers between devices: 6.26 us -> 10 us  [around(): lax.ppermute(blocks[k], 'mp', [(i, (i + k) % n_mp) for i in range(n_mp)])]
    ppermute x6, waiting for transfers between devices: 4.26 us -> 0.73 us  [around(): lax.ppermute(blocks[k], 'mp', [(i, (i + k) % n_mp) for i in range(n_mp)])]
    concatenate x4 -> x5, local copies, waits for them, and re-layouts: 0.09 us -> 1.84 us  [the longest x1 1.72 us: local(): jnp.concatenate([piece for pieces in plane_rows for piece in pieces])]
  transfers between devices with their start and end apart: 34 -> 31, of which waited for: 14 -> 10; matrix products, arithmetic and copies ran while one was open for 18% -> 19% of each run, Pallas kernels for 8% -> 9%
where the time goes in v8:
time: 168 us; the launch traced here: 167 us
  starting transfers between devices  54.4 us (32%)
  waiting for transfers between devices  45.2 us (27%)
  local copies, waits for them, and re-layouts  23.2 us (14%)
  between operations  14.7 us (9%)
  Pallas kernels  14.5 us (9%)
  matrix products  7.75 us (5%)
  other arithmetic  7.24 us (4%)
    ppermute x22, waiting for transfers between devices, flip(): return lax.ppermute(block, 'dp', [(i, i ^ bits) for i in range(n_dp)])  41.7 us
    ppermute x22, starting transfers between devices, flip(): return lax.ppermute(block, 'dp', [(i, i ^ bits) for i in range(n_dp)])  39.7 us
    pallas_call x2, Pallas kernels, attend(): pl.pallas_call(functools.partial(attend_kernel, length, device_cols), gri...  14.5 us
    ppermute x6, starting transfers between devices, around(): lax.ppermute(blocks[k], 'mp', [(i, (i + k) % n_mp) for i in range(n_mp)])  10 us
    unnamed x57, local copies, waits for them, and re-layouts  6.09 us
    dot_general x4, matrix products, product(): return jnp.einsum('td,tc->dc', mine, theirs, preferred_element_type=F32)  5.11 us
    all_to_all x1, starting transfers between devices, local(): lax.all_to_all(outgoing, 'dp', split_axis=0, concat_axis=0, tiled=True)  4.64 us
    gather x3, local copies, waits for them, and re-layouts, pick(): return array.at[index].get(mode='promise_in_bounds')  4.55 us
  transfers between devices with their start and end apart: 31, of which 10 were waited for; matrix products, arithmetic and copies ran while one was open for 19% of the time, Pallas kernels for 9%

profile of v8, /device:TPU:7, one launch (start us, length us, event | category | flops | bytes accessed | tf_op | source)
XLA Modules:
  0.0 167.0 jit_solution(13017318335667529302)
XLA Ops:
  9.7 4.6 %all-to-all-start = ((bf16[8,32,1280]{2,1,0:T(8,128)(2,1)}), bf16[8,32,1280]{2,1,0:T(8,128)(2,1)S(1)}, u32[]{:S(2)}, u32[]{:S(2)}) async-start(bf16[8,32,1280]{2,1,0:T(8,128)(2,1)} %gather_fusion), calls=%async_computation | async-start | bytes 1310720 | tf_op jit(solution)/shard_map/all_to_all | solution.py:233
  16.3 2.4 %collective-permute-start.1 = (bf16[160,256]{1,0:T(8,128)(2,1)S(1)}, bf16[160,256]{1,0:T(8,128)(2,1)S(1)}, u32[]{:S(2)}, u32[]{:S(2)}) collective-permute-start(bf16[160,256]{1,0:T(8,128)(2,1)S(1)} %get-tuple-element.164), channel_id=1, source_target_pairs={{0,2},{1,3},{2,0},{3,1},{4,6},{5,7},{6,4},{7,5},{8,10},{9,11},{10,... | collective-permute-start | bytes 245768 | tf_op jit(solution)/shard_map/ppermute | solution.py:206
  20.2 2.7 %all-to-all-done = bf16[8,32,1280]{2,1,0:T(8,128)(2,1)S(1)} async-done(((bf16[8,32,1280]{2,1,0:T(8,128)(2,1)}), bf16[8,32,1280]{2,1,0:T(8,128)(2,1)S(1)}, u32[]{:S(2)}, u32[]{:S(2)}) %all-to-all-start) | async-done | bytes 655392 | tf_op jit(solution)/shard_map/all_to_all | solution.py:233
  26.1 1.9 %collective-permute-start.5 = (bf16[4,160,256]{2,1,0:T(8,128)(2,1)S(1)}, bf16[4,160,256]{2,1,0:T(8,128)(2,1)S(1)}, u32[]{:S(2)}, u32[]{:S(2)}) collective-permute-start(bf16[4,160,256]{2,1,0:T(8,128)(2,1)S(1)} %get-tuple-element.161), channel_id=1, source_target_pairs={{0,24},{4,28},{8,16},{12,20},{16,8},{20,12},{24,0},{28,4},{1,25},{... | collective-permute-start | bytes 983048 | tf_op jit(solution)/shard_map/ppermute | solution.py:199
  28.0 4.8 %collective-permute-done.3 = bf16[4,160,256]{2,1,0:T(8,128)(2,1)S(1)} collective-permute-done((bf16[4,160,256]{2,1,0:T(8,128)(2,1)S(1)}, bf16[4,160,256]{2,1,0:T(8,128)(2,1)S(1)}, u32[]{:S(2)}, u32[]{:S(2)}) %collective-permute-start.3) | collective-permute-done | bytes 327712 | tf_op jit(solution)/shard_map/ppermute | solution.py:199
  32.8 7.9 %collective-permute-done.5 = bf16[4,160,256]{2,1,0:T(8,128)(2,1)S(1)} collective-permute-done((bf16[4,160,256]{2,1,0:T(8,128)(2,1)S(1)}, bf16[4,160,256]{2,1,0:T(8,128)(2,1)S(1)}, u32[]{:S(2)}, u32[]{:S(2)}) %collective-permute-start.5) | collective-permute-done | bytes 327712 | tf_op jit(solution)/shard_map/ppermute | solution.py:199
  40.9 2.2 %collective-permute-start.8 = (bf16[4,4,160,256]{3,2,1,0:T(8,128)(2,1)S(1)}, bf16[4,4,160,256]{3,2,1,0:T(8,128)(2,1)}, u32[]{:S(2)}, u32[]{:S(2)}) collective-permute-start(bf16[4,4,160,256]{3,2,1,0:T(8,128)(2,1)S(1)} %pad_maximum_fusion.1), channel_id=1, source_target_pairs={{0,4},{4,0},{8,12},{12,8},{16,20},{20,16},{24,28},{28,24},{1,5},{5... | collective-permute-start | bytes 3932168 | tf_op jit(solution)/shard_map/ppermute | solution.py:199
  47.1 12.3 %collective-permute-done.6 = bf16[256,1280]{1,0:T(8,128)(2,1)S(1)} collective-permute-done((bf16[256,1280]{1,0:T(8,128)(2,1)S(1)}, bf16[256,1280]{1,0:T(8,128)(2,1)S(1)}, u32[]{:S(2)}, u32[]{:S(2)}) %collective-permute-start.6) | collective-permute-done | bytes 655392 | tf_op jit(solution)/shard_map/ppermute | solution.py:199
  63.8 3.0 %pad_maximum_fusion = bf16[4,2,4,160,256]{4,3,2,1,0:T(8,128)(2,1)} fusion(bf16[4,1,4,160,256]{4,3,2,1,0:T(8,128)(2,1)} %bitcast.25, bf16[4,1,4,160,256]{4,3,2,1,0:T(8,128)(2,1)S(1)} %bitcast.88), kind=kLoop, calls=%fused_computation.3 | loop fusion | flops 1310720 | bytes 5242880 | tf_op jit(solution)/shard_map/stack | solution.py:258
  66.9 2.5 %gather_fusion.2 = bf16[32,160,256]{2,1,0:T(8,128)(2,1)S(1)} fusion(bf16[32,160,256]{2,1,0:T(8,128)(2,1)} %bitcast.84, s32[1024]{0:T(1024)S(1)} %get-tuple-element.170), kind=kCustom, calls=%fused_computation.2 | custom fusion | bytes 5243008 | tf_op jit(solution)/shard_map/gather | solution.py:168
  69.5 2.2 %dynamic-slice_bitcast_fusion.4 = (bf16[128,1280]{1,0:T(8,128)(2,1)S(1)}, bf16[128,1280]{1,0:T(8,128)(2,1)S(1)}, bf16[128,1280]{1,0:T(8,128)(2,1)S(1)}, bf16[128,1280]{1,0:T(8,128)(2,1)}) fusion(bf16[4,128,1280]{2,1,0:T(8,128)(2,1)} %all-gather.4.cloned.1.call-done.x_ref, s32[]{:T(128)S(6)} %select_n.164, s32[]{:T(128)S(6)} %select_n.163, s32[]{:T(128)S(6)} %select_n.162, ...), kind=kLoop, calls=%fused_computation.33 | loop fusion | bytes 2621456 | tf_op jit(solution)/shard_map/jit(dynamic_index_in_dim)/squeeze | solution.py:269
  74.4 7.3 %shard_map.138 = (f32[128,1024]{1,0:T(8,128)S(1)}, f32[128,1024]{1,0:T(8,128)S(1)}, f32[128,256]{1,0:T(8,128)S(1)}) custom-call(bf16[4,128,1280]{2,1,0:T(8,128)(2,1)S(1)} %copy-done.2, bf16[5120,1024]{1,0:T(8,128)(2,1)} %wq_ref.3, bf16[5120,256]{1,0:T(8,128)(2,1)S(1)} %bitcast.74, f32[128,1024]{1,0:T(8,128)S(1)} %bitcast.79, f32[1,128]{1,0:T(1,128)S(1)} %bitcast.80, ...), custom_call_target="tpu_custom_call" | custom-call | flops 16777216000 | bytes 41943040 | tf_op jit(solution)/shard_map/pallas_call | solution.py:136
  82.5 4.7 %collective-permute-done.13 = bf16[128,1280]{1,0:T(8,128)(2,1)S(1)} collective-permute-done((bf16[128,1280]{1,0:T(8,128)(2,1)S(1)}, bf16[128,1280]{1,0:T(8,128)(2,1)S(1)}, u32[]{:S(2)}, u32[]{:S(2)}) %collective-permute-start.13) | collective-permute-done | bytes 327712 | tf_op jit(solution)/shard_map/ppermute | solution.py:199
  89.0 2.0 %constant_dynamic-update-slice_fusion.2 = bf16[1024,1280]{1,0:T(8,128)(2,1)} fusion(bf16[1024,1280]{1,0:T(8,128)(2,1)} %constant_dynamic-update-slice_fusion.3, bf16[256,1280]{1,0:T(8,128)(2,1)} %collective-permute-done.7), kind=kLoop, calls=%fused_computation.50 | loop fusion | bytes 1310720
  91.0 1.8 %constant_dynamic-update-slice_fusion.1 = bf16[1024,1280]{1,0:T(8,128)(2,1)} fusion(bf16[1024,1280]{1,0:T(8,128)(2,1)} %constant_dynamic-update-slice_fusion.2, bf16[128,1280]{1,0:T(8,128)(2,1)} %collective-permute-done.11), kind=kLoop, calls=%fused_computation.49 | loop fusion | bytes 655360
  98.6 7.2 %shard_map.139 = (f32[128,1024]{1,0:T(8,128)S(1)}, f32[128,1024]{1,0:T(8,128)S(1)}, f32[128,256]{1,0:T(8,128)S(1)}) custom-call(bf16[4,128,1280]{2,1,0:T(8,128)(2,1)S(1)} %bitcast.77, bf16[5120,1024]{1,0:T(8,128)(2,1)} %wq_ref.3, bf16[5120,256]{1,0:T(8,128)(2,1)S(1)} %bitcast.75, f32[128,1024]{1,0:T(8,128)S(1)} %bitcast.78, f32[1,128]{1,0:T(1,128)S(1)} %bitcast.81, ...), custom_call_target="tpu_custom_call" | custom-call | flops 16777216000 | bytes 41943040 | tf_op jit(solution)/shard_map/pallas_call | solution.py:136
  106.0 2.1 %collective-permute-start.21 = (bf16[256,256]{1,0:T(8,128)(2,1)S(1)}, bf16[256,256]{1,0:T(8,128)(2,1)S(1)}, u32[]{:S(2)}, u32[]{:S(2)}) collective-permute-start(bf16[256,256]{1,0:T(8,128)(2,1)S(1)} %constant_dynamic-update-slice_fusion.19), channel_id=1, source_target_pairs={{0,1},{1,2},{2,3},{3,0},{4,5},{5,6},{6,7},{7,4},{8,9},{9,10},{10,1... | collective-permute-start | bytes 393224 | tf_op jit(solution)/shard_map/ppermute | solution.py:206
  108.1 1.8 %collective-permute-start.22 = (bf16[256,256]{1,0:T(8,128)(2,1)S(1)}, bf16[256,256]{1,0:T(8,128)(2,1)S(1)}, u32[]{:S(2)}, u32[]{:S(2)}) collective-permute-start(bf16[256,256]{1,0:T(8,128)(2,1)S(1)} %constant_dynamic-update-slice_fusion.19), channel_id=1, source_target_pairs={{0,2},{1,3},{2,0},{3,1},{4,6},{5,7},{6,4},{7,5},{8,10},{9,11},{10,... | collective-permute-start | bytes 393224 | tf_op jit(solution)/shard_map/ppermute | solution.py:206
  109.9 2.3 %collective-permute-start.23 = (bf16[256,256]{1,0:T(8,128)(2,1)S(1)}, bf16[256,256]{1,0:T(8,128)(2,1)S(1)}, u32[]{:S(2)}, u32[]{:S(2)}) collective-permute-start(bf16[256,256]{1,0:T(8,128)(2,1)S(1)} %constant_dynamic-update-slice_fusion.19), channel_id=1, source_target_pairs={{0,3},{1,0},{2,1},{3,2},{4,7},{5,4},{6,5},{7,6},{8,11},{9,8},{10,9... | collective-permute-start | bytes 393224 | tf_op jit(solution)/shard_map/ppermute | solution.py:206
  118.4 9.9 %collective-permute-done.24 = bf16[256,256]{1,0:T(8,128)(2,1)S(1)} collective-permute-done((bf16[256,256]{1,0:T(8,128)(2,1)S(1)}, bf16[256,256]{1,0:T(8,128)(2,1)S(1)}, u32[]{:S(2)}, u32[]{:S(2)}) %collective-permute-start.24) | collective-permute-done | bytes 131104 | tf_op jit(solution)/shard_map/ppermute | solution.py:199
  129.8 2.6 %fusion.4 = f32[1280,256]{0,1:T(8,128)S(1)} fusion(bf16[1024,1280]{1,0:T(8,128)(2,1)} %constant_dynamic-update-slice_fusion, bf16[256,256]{1,0:T(8,128)(2,1)S(1)} %collective-permute-done.26, bf16[256,256]{1,0:T(8,128)(2,1)S(1)} %collective-permute-done.25, bf16[256,256]{1,0:T(8,128)(2,1)S(1)} %collective-permute-done.24, ...), kind=kOutput, calls=%fused_computation.16 | convolution fusion | flops 673185792 | bytes 4456448 | tf_op jit(solution)/shard_map/td,tc->dc/dot_general | solution.py:334
  132.5 15.0 %collective-permute-start.27 = (bf16[1280,128]{0,1:T(8,128)(2,1)S(1)}, bf16[1280,128]{0,1:T(8,128)(2,1)S(1)}, u32[]{:S(2)}, u32[]{:S(2)}) collective-permute-start(bf16[1280,128]{0,1:T(8,128)(2,1)S(1)} %select_convert_fusion), channel_id=1, source_target_pairs={{0,4},{4,0},{8,12},{12,8},{16,20},{20,16},{24,28},{28,24},{1,5},{5... | collective-permute-start | bytes 983048 | tf_op jit(solution)/shard_map/ppermute | solution.py:199
  149.4 6.1 %collective-permute-start.20 = (bf16[640,1024]{1,0:T(8,128)(2,1)S(1)}, bf16[640,1024]{1,0:T(8,128)(2,1)S(1)}, u32[]{:S(2)}, u32[]{:S(2)}) collective-permute-start(bf16[640,1024]{1,0:T(8,128)(2,1)S(1)} %add_convert_fusion), channel_id=1, source_target_pairs={{0,4},{4,0},{8,12},{12,8},{16,20},{20,16},{24,28},{28,24},{1,5},{5... | collective-permute-start | bytes 3932168 | tf_op jit(solution)/shard_map/ppermute | solution.py:199
  158.1 2.1 %add_add_fusion = f32[640,1024]{1,0:T(8,128)} fusion(f32[640,1024]{1,0:T(8,128)S(1)} %fusion.1, bf16[640,1024]{1,0:T(8,128)(2,1)S(1)} %collective-permute-done.20, bf16[256,1024]{1,0:T(8,128)(2,1)S(1)} %collective-permute-done.17, bf16[256,1280]{1,0:T(8,128)(2,1)S(1)} %constant_dynamic-update-slice_fusion.5, s32[]{:T(128)S(6)} %select_n.168), kind=kOutput, calls=%fused_computation.4 | convolution fusion | flops 337510400 | bytes 7405572 | tf_op jit(solution)/shard_map/td,tc->dc/dot_general | solution.py:316
  (153 shorter events, 40.9 us)
Async XLA Ops:
  9.7 13.1 %all-to-all-start = ((bf16[8,32,1280]{2,1,0:T(8,128)(2,1)}), bf16[8,32,1280]{2,1,0:T(8,128)(2,1)S(1)}, u32[]{:S(2)}, u32[]{:S(2)}) async-start(bf16[8,32,1280]{2,1,0:T(8,128)(2,1)} %gather_fusion), calls=%async_computation | async-start | bytes 1310720 | tf_op jit(solution)/shard_map/all_to_all | solution.py:233
  14.3 55.2 %all-gather.4.cloned.1.call-start = ((), (), s32[]{:S(2)}) async-start(), calls=%async_computation.1 | async-start | bytes 1638400 | tf_op jit(solution)/shard_map/all_gather | solution.py:250
  24.5 70.0 %all-gather.6.cloned.1.call-start = ((), (), s32[]{:S(2)}) async-start(), calls=%async_computation.2 | async-start | bytes 1638400 | tf_op jit(solution)/shard_map/all_gather | solution.py:253
  26.1 14.6 %collective-permute-start.5 = (bf16[4,160,256]{2,1,0:T(8,128)(2,1)S(1)}, bf16[4,160,256]{2,1,0:T(8,128)(2,1)S(1)}, u32[]{:S(2)}, u32[]{:S(2)}) collective-permute-start(bf16[4,160,256]{2,1,0:T(8,128)(2,1)S(1)} %get-tuple-element.161), channel_id=1, source_target_pairs={{0,24},{4,28},{8,16},{12,20},{16,8},{20,12},{24,0},{28,4},{1,25},{... | collective-permute-start | bytes 983048 | tf_op jit(solution)/shard_map/ppermute | solution.py:199
  40.9 22.9 %collective-permute-start.8 = (bf16[4,4,160,256]{3,2,1,0:T(8,128)(2,1)S(1)}, bf16[4,4,160,256]{3,2,1,0:T(8,128)(2,1)}, u32[]{:S(2)}, u32[]{:S(2)}) collective-permute-start(bf16[4,4,160,256]{3,2,1,0:T(8,128)(2,1)S(1)} %pad_maximum_fusion.1), channel_id=1, source_target_pairs={{0,4},{4,0},{8,12},{12,8},{16,20},{20,16},{24,28},{28,24},{1,5},{5... | collective-permute-start | bytes 3932168 | tf_op jit(solution)/shard_map/ppermute | solution.py:199
  43.1 16.2 %collective-permute-start.6 = (bf16[256,1280]{1,0:T(8,128)(2,1)S(1)}, bf16[256,1280]{1,0:T(8,128)(2,1)S(1)}, u32[]{:S(2)}, u32[]{:S(2)}) collective-permute-start(bf16[256,1280]{1,0:T(8,128)(2,1)S(1)} %bitcast.85), channel_id=1, source_target_pairs={{0,8},{4,12},{8,0},{12,4},{16,24},{20,28},{24,16},{28,20},{1,9},{5... | collective-permute-start | bytes 1966088 | tf_op jit(solution)/shard_map/ppermute | solution.py:199
  44.2 15.9 %collective-permute-start.7 = (bf16[256,1280]{1,0:T(8,128)(2,1)S(1)}, bf16[256,1280]{1,0:T(8,128)(2,1)}, u32[]{:S(2)}, u32[]{:S(2)}) collective-permute-start(bf16[256,1280]{1,0:T(8,128)(2,1)S(1)} %bitcast.86), channel_id=1, source_target_pairs={{0,16},{4,20},{8,24},{12,28},{16,0},{20,4},{24,8},{28,12},{1,17},{... | collective-permute-start | bytes 1966088 | tf_op jit(solution)/shard_map/ppermute | solution.py:199
  60.9 21.6 %collective-permute-start.11 = (bf16[128,1280]{1,0:T(8,128)(2,1)}, bf16[128,1280]{1,0:T(8,128)(2,1)}, u32[]{:S(2)}, u32[]{:S(2)}) collective-permute-start(bf16[128,1280]{1,0:T(8,128)(2,1)} %slice.77), channel_id=1, source_target_pairs={{0,16},{4,20},{8,24},{12,28},{16,0},{20,4},{24,8},{28,12},{1,17},{... | collective-permute-start | bytes 983048 | tf_op jit(solution)/shard_map/ppermute | solution.py:199
  63.3 19.1 %collective-permute-start.12 = (bf16[128,1280]{1,0:T(8,128)(2,1)}, bf16[128,1280]{1,0:T(8,128)(2,1)}, u32[]{:S(2)}, u32[]{:S(2)}) collective-permute-start(bf16[128,1280]{1,0:T(8,128)(2,1)} %slice.78), channel_id=1, source_target_pairs={{0,8},{4,12},{8,0},{12,4},{16,24},{20,28},{24,16},{28,20},{1,9},{5... | collective-permute-start | bytes 983048 | tf_op jit(solution)/shard_map/ppermute | solution.py:199
  71.7 10.7 %collective-permute-start.10 = (bf16[128,1280]{1,0:T(8,128)(2,1)S(1)}, bf16[128,1280]{1,0:T(8,128)(2,1)S(1)}, u32[]{:S(2)}, u32[]{:S(2)}) collective-permute-start(bf16[128,1280]{1,0:T(8,128)(2,1)S(1)} %get-tuple-element.82), channel_id=1, source_target_pairs={{0,16},{4,20},{8,24},{12,28},{16,0},{20,4},{24,8},{28,12},{1,17},{... | collective-permute-start | bytes 983048 | tf_op jit(solution)/shard_map/ppermute | solution.py:199
  72.5 9.9 %collective-permute-start.9 = (bf16[128,1280]{1,0:T(8,128)(2,1)S(1)}, bf16[128,1280]{1,0:T(8,128)(2,1)S(1)}, u32[]{:S(2)}, u32[]{:S(2)}) collective-permute-start(bf16[128,1280]{1,0:T(8,128)(2,1)S(1)} %get-tuple-element.81), channel_id=1, source_target_pairs={{0,8},{4,12},{8,0},{12,4},{16,24},{20,28},{24,16},{28,20},{1,9},{5... | collective-permute-start | bytes 983048 | tf_op jit(solution)/shard_map/ppermute | solution.py:199
  73.3 13.8 %collective-permute-start.13 = (bf16[128,1280]{1,0:T(8,128)(2,1)S(1)}, bf16[128,1280]{1,0:T(8,128)(2,1)S(1)}, u32[]{:S(2)}, u32[]{:S(2)}) collective-permute-start(bf16[128,1280]{1,0:T(8,128)(2,1)S(1)} %get-tuple-element.89), channel_id=1, source_target_pairs={{0,24},{4,28},{8,16},{12,20},{16,8},{20,12},{24,0},{28,4},{1,25},{... | collective-permute-start | bytes 983048 | tf_op jit(solution)/shard_map/ppermute | solution.py:199
  95.9 10.1 %collective-permute-start.14 = (bf16[128,1280]{1,0:T(8,128)(2,1)S(1)}, bf16[128,1280]{1,0:T(8,128)(2,1)S(1)}, u32[]{:S(2)}, u32[]{:S(2)}) collective-permute-start(bf16[128,1280]{1,0:T(8,128)(2,1)S(1)} %get-tuple-element.105), channel_id=1, source_target_pairs={{0,8},{4,12},{8,0},{12,4},{16,24},{20,28},{24,16},{28,20},{1,9},{5... | collective-permute-start | bytes 983048 | tf_op jit(solution)/shard_map/ppermute | solution.py:199
  96.9 9.1 %collective-permute-start.15 = (bf16[128,1280]{1,0:T(8,128)(2,1)S(1)}, bf16[128,1280]{1,0:T(8,128)(2,1)S(1)}, u32[]{:S(2)}, u32[]{:S(2)}) collective-permute-start(bf16[128,1280]{1,0:T(8,128)(2,1)S(1)} %get-tuple-element.106), channel_id=1, source_target_pairs={{0,16},{4,20},{8,24},{12,28},{16,0},{20,4},{24,8},{28,12},{1,17},{... | collective-permute-start | bytes 983048 | tf_op jit(solution)/shard_map/ppermute | solution.py:199
  97.5 14.7 %collective-permute-start.16 = (bf16[128,1280]{1,0:T(8,128)(2,1)S(1)}, bf16[128,1280]{1,0:T(8,128)(2,1)S(1)}, u32[]{:S(2)}, u32[]{:S(2)}) collective-permute-start(bf16[128,1280]{1,0:T(8,128)(2,1)S(1)} %get-tuple-element.121), channel_id=1, source_target_pairs={{0,24},{4,28},{8,16},{12,20},{16,8},{20,12},{24,0},{28,4},{1,25},{... | collective-permute-start | bytes 983048 | tf_op jit(solution)/shard_map/ppermute | solution.py:199
  106.0 8.6 %collective-permute-start.21 = (bf16[256,256]{1,0:T(8,128)(2,1)S(1)}, bf16[256,256]{1,0:T(8,128)(2,1)S(1)}, u32[]{:S(2)}, u32[]{:S(2)}) collective-permute-start(bf16[256,256]{1,0:T(8,128)(2,1)S(1)} %constant_dynamic-update-slice_fusion.19), channel_id=1, source_target_pairs={{0,1},{1,2},{2,3},{3,0},{4,5},{5,6},{6,7},{7,4},{8,9},{9,10},{10,1... | collective-permute-start | bytes 393224 | tf_op jit(solution)/shard_map/ppermute | solution.py:206
  112.3 35.3 %collective-permute-start.17 = (bf16[256,1024]{1,0:T(8,128)(2,1)S(1)}, bf16[256,1024]{1,0:T(8,128)(2,1)S(1)}, u32[]{:S(2)}, u32[]{:S(2)}) collective-permute-start(bf16[256,1024]{1,0:T(8,128)(2,1)S(1)} %get-tuple-element.166), channel_id=1, source_target_pairs={{0,24},{4,28},{8,16},{12,20},{16,8},{20,12},{24,0},{28,4},{1,25},{... | collective-permute-start | bytes 1572872 | tf_op jit(solution)/shard_map/ppermute | solution.py:199
  113.9 33.5 %collective-permute-start.18 = (bf16[256,1024]{1,0:T(8,128)(2,1)S(1)}, bf16[256,1024]{1,0:T(8,128)(2,1)S(1)}, u32[]{:S(2)}, u32[]{:S(2)}) collective-permute-start(bf16[256,1024]{1,0:T(8,128)(2,1)S(1)} %get-tuple-element.166), channel_id=1, source_target_pairs={{0,8},{4,12},{8,0},{12,4},{16,24},{20,28},{24,16},{28,20},{1,9},{5... | collective-permute-start | bytes 1572872 | tf_op jit(solution)/shard_map/ppermute | solution.py:199
  114.8 13.5 %collective-permute-start.24 = (bf16[256,256]{1,0:T(8,128)(2,1)S(1)}, bf16[256,256]{1,0:T(8,128)(2,1)S(1)}, u32[]{:S(2)}, u32[]{:S(2)}) collective-permute-start(bf16[256,256]{1,0:T(8,128)(2,1)S(1)} %get-tuple-element.159), channel_id=1, source_target_pairs={{0,8},{4,12},{8,0},{12,4},{16,24},{20,28},{24,16},{28,20},{1,9},{5... | collective-permute-start | bytes 393224 | tf_op jit(solution)/shard_map/ppermute | solution.py:199
  115.9 13.1 %collective-permute-start.25 = (bf16[256,256]{1,0:T(8,128)(2,1)S(1)}, bf16[256,256]{1,0:T(8,128)(2,1)S(1)}, u32[]{:S(2)}, u32[]{:S(2)}) collective-permute-start(bf16[256,256]{1,0:T(8,128)(2,1)S(1)} %get-tuple-element.158), channel_id=1, source_target_pairs={{0,16},{4,20},{8,24},{12,28},{16,0},{20,4},{24,8},{28,12},{1,17},{... | collective-permute-start | bytes 393224 | tf_op jit(solution)/shard_map/ppermute | solution.py:199
  116.2 13.6 %collective-permute-start.26 = (bf16[256,256]{1,0:T(8,128)(2,1)S(1)}, bf16[256,256]{1,0:T(8,128)(2,1)S(1)}, u32[]{:S(2)}, u32[]{:S(2)}) collective-permute-start(bf16[256,256]{1,0:T(8,128)(2,1)S(1)} %get-tuple-element.157), channel_id=1, source_target_pairs={{0,24},{4,28},{8,16},{12,20},{16,8},{20,12},{24,0},{28,4},{1,25},{... | collective-permute-start | bytes 393224 | tf_op jit(solution)/shard_map/ppermute | solution.py:199
  128.3 19.2 %collective-permute-start.19 = (bf16[256,1024]{1,0:T(8,128)(2,1)S(1)}, bf16[256,1024]{1,0:T(8,128)(2,1)S(1)}, u32[]{:S(2)}, u32[]{:S(2)}) collective-permute-start(bf16[256,1024]{1,0:T(8,128)(2,1)S(1)} %get-tuple-element.166), channel_id=1, source_target_pairs={{0,16},{4,20},{8,24},{12,28},{16,0},{20,4},{24,8},{28,12},{1,17},{... | collective-permute-start | bytes 1572872 | tf_op jit(solution)/shard_map/ppermute | solution.py:199
  132.5 24.2 %collective-permute-start.27 = (bf16[1280,128]{0,1:T(8,128)(2,1)S(1)}, bf16[1280,128]{0,1:T(8,128)(2,1)S(1)}, u32[]{:S(2)}, u32[]{:S(2)}) collective-permute-start(bf16[1280,128]{0,1:T(8,128)(2,1)S(1)} %select_convert_fusion), channel_id=1, source_target_pairs={{0,4},{4,0},{8,12},{12,8},{16,20},{20,16},{24,28},{28,24},{1,5},{5... | collective-permute-start | bytes 983048 | tf_op jit(solution)/shard_map/ppermute | solution.py:199
  149.4 8.7 %collective-permute-start.20 = (bf16[640,1024]{1,0:T(8,128)(2,1)S(1)}, bf16[640,1024]{1,0:T(8,128)(2,1)S(1)}, u32[]{:S(2)}, u32[]{:S(2)}) collective-permute-start(bf16[640,1024]{1,0:T(8,128)(2,1)S(1)} %add_convert_fusion), channel_id=1, source_target_pairs={{0,4},{4,0},{8,12},{12,8},{16,20},{20,16},{24,28},{28,24},{1,5},{5... | collective-permute-start | bytes 3932168 | tf_op jit(solution)/shard_map/ppermute | solution.py:199
  (29 other events, 220.0 us)
Sparse Core Ops, SparseCore 0:
  24.5 33.1 all-gather.3
  59.9 31.6 all-gather.5

commit v9 on v4

--- a/solution.py
+++ b/solution.py
@@ -245,7 +245,13 @@
     shares = around([lax.dynamic_index_in_dim(pairs, h, 0, False) for h in heads])
     arrived, *shares = together(arrived, *shares)
     shares = jnp.stack(shares)
-    rows = pick(arrived, slot_source).reshape(tokens, width)
+    if n_dp == slots:
+        slot_of = jnp.argmax(slot_source[None, :] == jnp.arange(n_dp)[:, None], axis=1)
+        place_of = slot_source
+    else:
+        arrived = pick(arrived, slot_source)
+        slot_of = place_of = jnp.arange(slots)
+    rows = arrived.reshape(tokens, width)
 
     x = lax.all_gather(rows, "mp", axis=1, tiled=True)
     shares = jnp.stack([shares] + other_chips([shares] * chips))
@@ -267,7 +273,8 @@
     chip_rows = [chip_rows[0]] + other_chips(chip_rows)
 
     factor = multiplicity.astype(F32) * slot_weight / length
-    d_out = (cotangent.astype(F32) * factor[:, None, None]).astype(BF16).astype(F32)
+    d_out = pick(cotangent, slot_of).astype(F32) * pick(factor, slot_of)[:, None, None]
+    d_out = d_out.astype(BF16).astype(F32)
     attended, d_query, d_kv = attend(
         x,
         w_query,
@@ -279,10 +286,11 @@
         key_cols // n_dp,
     )
     attended, d_query, d_kv = [value.astype(BF16) for value in (attended, d_query, d_kv)]
-    d_query, d_kv, *chip_rows = together(d_query, d_kv, *chip_rows)
+    spread = around([d_kv] * n_mp)
+    d_query, spread, chip_rows = lax.optimization_barrier((d_query, spread, chip_rows))
+    spread = jnp.stack(spread)
 
     d_all = [d_query] + other_chips([d_query] * chips)
-    spread = jnp.stack(around([d_kv] * n_mp))
     half = chip_width // 2
     early = [0] + near
     late = [k for k in range(chips) if k not in early]
@@ -316,7 +324,7 @@
     device_cols = chip_cols // 4
 
     return (
-        attended.reshape(slots, length, query_cols),
+        pick(attended.reshape(slots, length, query_cols), place_of),
         grad_query,
         grad_kv[:, :device_cols],
         grad_kv[:, device_cols:],

time: 165 us -> 176 us (1.067)
  local copies, waits for them, and re-layouts: 12.7 us -> 22.9 us
  waiting for transfers between devices: 77.6 us -> 74.1 us
  starting transfers between devices: 29.6 us -> 32.3 us
  matrix products: 6.02 us -> 7.95 us
    ppermute x6, waiting for transfers between devices: 16.7 us -> 12.4 us  [around(): lax.ppermute(blocks[k], 'mp', [(i, (i + k) % n_mp) for i in range(n_mp)])]
    unnamed x26 -> x34, local copies, waits for them, and re-layouts: 0.57 us -> 4.34 us
    ppermute x19, starting transfers between devices: 18.8 us -> 21.7 us  [flip(): return lax.ppermute(block, 'dp', [(i, i ^ bits) for i in range(n_dp)])]
    gather x3 -> x5, local copies, waits for them, and re-layouts: 5.32 us -> 7.51 us  [pick(): return array.at[index].get(mode='promise_in_bounds')]
    dot_general x4, matrix products: 5.12 us -> 7.06 us  [product(): return jnp.einsum('td,tc->dc', mine, theirs, preferred_element_type=F32)]
  transfers between devices with their start and end apart: 27 -> 27, of which waited for: 14 -> 16; matrix products, arithmetic and copies ran while one was open for 14% -> 18% of each run, Pallas kernels for 6% -> 6%
where the time goes in v9:
time: 176 us; the launch traced here: 174 us
  waiting for transfers between devices  74.1 us (42%)
  starting transfers between devices  32.3 us (18%)
  local copies, waits for them, and re-layouts  22.9 us (13%)
  between operations  14.5 us (8%)
  other arithmetic  12 us (7%)
  Pallas kernels  10.3 us (6%)
  matrix products  7.95 us (5%)
    ppermute x19, waiting for transfers between devices, flip(): return lax.ppermute(block, 'dp', [(i, i ^ bits) for i in range(n_dp)])  57.4 us
    ppermute x19, starting transfers between devices, flip(): return lax.ppermute(block, 'dp', [(i, i ^ bits) for i in range(n_dp)])  21.7 us
    ppermute x6, waiting for transfers between devices, around(): lax.ppermute(blocks[k], 'mp', [(i, (i + k) % n_mp) for i in range(n_mp)])  12.4 us
    pallas_call x1, Pallas kernels, attend(): pl.pallas_call(functools.partial(attend_kernel, length, device_cols), gri...  10.3 us
    gather x5, local copies, waits for them, and re-layouts, pick(): return array.at[index].get(mode='promise_in_bounds')  7.51 us
    dot_general x4, matrix products, product(): return jnp.einsum('td,tc->dc', mine, theirs, preferred_element_type=F32)  7.06 us
    ppermute x6, starting transfers between devices, around(): lax.ppermute(blocks[k], 'mp', [(i, (i + k) % n_mp) for i in range(n_mp)])  6.11 us
    all_to_all x1, starting transfers between devices, local(): lax.all_to_all(outgoing, 'dp', split_axis=0, concat_axis=0, tiled=True)  4.51 us
  transfers between devices with their start and end apart: 27, of which 16 were waited for; matrix products, arithmetic and copies ran while one was open for 18% of the time, Pallas kernels for 6%

profile of v9, /device:TPU:7, one launch (start us, length us, event | category | flops | bytes accessed | tf_op | source)
XLA Modules:
  0.0 174.1 jit_solution(3645735281117201823)
XLA Ops:
  9.7 4.5 %all-to-all-start = ((bf16[8,32,1280]{2,1,0:T(8,128)(2,1)}), bf16[8,32,1280]{2,1,0:T(8,128)(2,1)S(1)}, u32[]{:S(2)}, u32[]{:S(2)}) async-start(bf16[8,32,1280]{2,1,0:T(8,128)(2,1)} %gather_fusion), calls=%async_computation | async-start | bytes 1310720 | tf_op jit(solution)/shard_map/all_to_all | solution.py:234
  17.6 2.3 %collective-permute-start.1 = (bf16[160,256]{1,0:T(8,128)(2,1)S(1)}, bf16[160,256]{1,0:T(8,128)(2,1)S(1)}, u32[]{:S(2)}, u32[]{:S(2)}) collective-permute-start(bf16[160,256]{1,0:T(8,128)(2,1)S(1)} %get-tuple-element.93), channel_id=1, source_target_pairs={{0,2},{1,3},{2,0},{3,1},{4,6},{5,7},{6,4},{7,5},{8,10},{9,11},{10,... | collective-permute-start | bytes 245768 | tf_op jit(solution)/shard_map/ppermute | solution.py:207
  21.9 4.1 %collective-permute-done.1 = bf16[160,256]{1,0:T(8,128)(2,1)S(1)} collective-permute-done((bf16[160,256]{1,0:T(8,128)(2,1)S(1)}, bf16[160,256]{1,0:T(8,128)(2,1)S(1)}, u32[]{:S(2)}, u32[]{:S(2)}) %collective-permute-start.1) | collective-permute-done | bytes 81952 | tf_op jit(solution)/shard_map/ppermute | solution.py:207
  27.5 2.2 %collective-permute-start.5 = (bf16[4,160,256]{2,1,0:T(8,128)(2,1)S(1)}, bf16[4,160,256]{2,1,0:T(8,128)(2,1)S(1)}, u32[]{:S(2)}, u32[]{:S(2)}) collective-permute-start(bf16[4,160,256]{2,1,0:T(8,128)(2,1)S(1)} %get-tuple-element.91), channel_id=1, source_target_pairs={{0,24},{4,28},{8,16},{12,20},{16,8},{20,12},{24,0},{28,4},{1,25},{... | collective-permute-start | bytes 983048 | tf_op jit(solution)/shard_map/ppermute | solution.py:200
  29.7 5.8 %collective-permute-done.3 = bf16[4,160,256]{2,1,0:T(8,128)(2,1)S(1)} collective-permute-done((bf16[4,160,256]{2,1,0:T(8,128)(2,1)S(1)}, bf16[4,160,256]{2,1,0:T(8,128)(2,1)S(1)}, u32[]{:S(2)}, u32[]{:S(2)}) %collective-permute-start.3) | collective-permute-done | bytes 327712 | tf_op jit(solution)/shard_map/ppermute | solution.py:200
  35.5 7.2 %collective-permute-done.5 = bf16[4,160,256]{2,1,0:T(8,128)(2,1)S(1)} collective-permute-done((bf16[4,160,256]{2,1,0:T(8,128)(2,1)S(1)}, bf16[4,160,256]{2,1,0:T(8,128)(2,1)S(1)}, u32[]{:S(2)}, u32[]{:S(2)}) %collective-permute-start.5) | collective-permute-done | bytes 327712 | tf_op jit(solution)/shard_map/ppermute | solution.py:200
  42.8 1.9 %collective-permute-start.6 = (bf16[4,4,160,256]{3,2,1,0:T(8,128)(2,1)S(1)}, bf16[4,4,160,256]{3,2,1,0:T(8,128)(2,1)}, u32[]{:S(2)}, u32[]{:S(2)}) collective-permute-start(bf16[4,4,160,256]{3,2,1,0:T(8,128)(2,1)S(1)} %pad_maximum_fusion.2), channel_id=1, source_target_pairs={{0,4},{4,0},{8,12},{12,8},{16,20},{20,16},{24,28},{28,24},{1,5},{5... | collective-permute-start | bytes 3932168 | tf_op jit(solution)/shard_map/ppermute | solution.py:200
  49.4 11.8 %collective-permute-done.7 = bf16[256,1280]{1,0:T(8,128)(2,1)} collective-permute-done((bf16[256,1280]{1,0:T(8,128)(2,1)S(1)}, bf16[256,1280]{1,0:T(8,128)(2,1)}, u32[]{:S(2)}, u32[]{:S(2)}) %collective-permute-start.7) | collective-permute-done | bytes 655392 | tf_op jit(solution)/shard_map/ppermute | solution.py:200
  67.8 3.0 %pad_maximum_fusion = bf16[4,2,4,160,256]{4,3,2,1,0:T(8,128)(2,1)} fusion(bf16[4,1,4,160,256]{4,3,2,1,0:T(8,128)(2,1)} %bitcast.20, bf16[4,1,4,160,256]{4,3,2,1,0:T(8,128)(2,1)S(1)} %bitcast.77), kind=kLoop, calls=%fused_computation.5 | loop fusion | flops 1310720 | bytes 5242880 | tf_op jit(solution)/shard_map/stack | solution.py:262
  70.9 2.5 %gather_fusion.1 = bf16[32,160,256]{2,1,0:T(8,128)(2,1)S(1)} fusion(bf16[32,160,256]{2,1,0:T(8,128)(2,1)} %bitcast.72, s32[1024]{0:T(1024)S(1)} %get-tuple-element.98), kind=kCustom, calls=%fused_computation.1 | custom fusion | bytes 5243008 | tf_op jit(solution)/shard_map/gather | solution.py:169
  75.0 3.3 %pad_maximum_fusion.1 = bf16[4,256,1280]{2,1,0:T(8,128)(2,1)} fusion(bf16[1,256,1280]{2,1,0:T(8,128)(2,1)S(1)} %maximum_bitcast_fusion, bf16[1,256,1280]{2,1,0:T(8,128)(2,1)} %bitcast.26, bf16[1,256,1280]{2,1,0:T(8,128)(2,1)} %bitcast.25, bf16[1,256,1280]{2,1,0:T(8,128)(2,1)} %bitcast.74), kind=kLoop, calls=%fused_computation.6 | loop fusion | flops 3932160 | bytes 5242880 | tf_op jit(solution)/shard_map/stack | solution.py:260
  78.3 4.3 %all-gather.2.cloned.1.call-done.x_ref = bf16[256,5120]{1,0:T(8,128)(2,1)} async-done(((bf16[256,1280]{1,0:T(8,128)(2,1)}), bf16[256,5120]{1,0:T(8,128)(2,1)}) %all-gather.2.cloned.1.call-update) | async-done | bytes 2621456 | tf_op jit(solution)/shard_map/all_gather | solution.py:256
  82.6 3.4 %constant_dynamic-slice_fusion.3 = (bf16[256,1280]{1,0:T(8,128)(2,1)}, bf16[256,1280]{1,0:T(8,128)(2,1)}, bf16[256,1280]{1,0:T(8,128)(2,1)}, bf16[256,1280]{1,0:T(8,128)(2,1)}) fusion(bf16[256,5120]{1,0:T(8,128)(2,1)} %all-gather.2.cloned.1.call-done.x_ref, s32[]{:T(128)S(6)} %select_n.168, s32[]{:T(128)S(6)} %select_n.167, s32[]{:T(128)S(6)} %select_n.166, ...), kind=kLoop, calls=%fused_computation.50 | loop fusion | bytes 5242896 | tf_op jit(solution)/shard_map/dynamic_slice | solution.py:270
  86.6 2.1 %collective-permute-start.16 = (bf16[256,1280]{1,0:T(8,128)(2,1)}, bf16[256,1280]{1,0:T(8,128)(2,1)}, u32[]{:S(2)}, u32[]{:S(2)}) collective-permute-start(bf16[256,1280]{1,0:T(8,128)(2,1)} %get-tuple-element.61), channel_id=1, source_target_pairs={{0,24},{4,28},{8,16},{12,20},{16,8},{20,12},{24,0},{28,4},{1,25},{... | collective-permute-start | bytes 1966088 | tf_op jit(solution)/shard_map/ppermute | solution.py:200
  88.7 10.3 %shard_map.138 = (f32[256,1024]{1,0:T(8,128)S(1)}, f32[256,1024]{1,0:T(8,128)S(1)}, f32[256,256]{1,0:T(8,128)S(1)}) custom-call(bf16[256,5120]{1,0:T(8,128)(2,1)S(1)} %copy-done.1, bf16[5120,1024]{1,0:T(8,128)(2,1)} %wq_ref.1, bf16[5120,256]{1,0:T(8,128)(2,1)S(1)} %bitcast.68, f32[256,1024]{1,0:T(8,128)S(1)} %copy-done.5, f32[1,128]{1,0:T(1,128)S(1)} %bitcast.69, ...), custom_call_target="tpu_custom_call" | custom-call | flops 16777216000 | bytes 41943040 | tf_op jit(solution)/shard_map/pallas_call | solution.py:137
  102.3 4.4 %collective-permute-done.11 = bf16[256,256]{1,0:T(8,128)(2,1)S(1)} collective-permute-done((bf16[256,256]{1,0:T(8,128)(2,1)S(1)}, bf16[256,256]{1,0:T(8,128)(2,1)S(1)}, u32[]{:S(2)}, u32[]{:S(2)}) %collective-permute-start.11) | collective-permute-done | bytes 131104 | tf_op jit(solution)/shard_map/ppermute | solution.py:207
  112.5 3.6 %collective-permute-done.16 = bf16[256,1280]{1,0:T(8,128)(2,1)} collective-permute-done((bf16[256,1280]{1,0:T(8,128)(2,1)}, bf16[256,1280]{1,0:T(8,128)(2,1)}, u32[]{:S(2)}, u32[]{:S(2)}) %collective-permute-start.16) | collective-permute-done | bytes 655392 | tf_op jit(solution)/shard_map/ppermute | solution.py:200
  119.2 2.1 %collective-permute-start.23 = (bf16[256,256]{1,0:T(8,128)(2,1)S(1)}, bf16[256,256]{1,0:T(8,128)(2,1)S(1)}, u32[]{:S(2)}, u32[]{:S(2)}) collective-permute-start(bf16[256,256]{1,0:T(8,128)(2,1)S(1)} %get-tuple-element.87), channel_id=1, source_target_pairs={{0,24},{4,28},{8,16},{12,20},{16,8},{20,12},{24,0},{28,4},{1,25},{... | collective-permute-start | bytes 393224 | tf_op jit(solution)/shard_map/ppermute | solution.py:200
  123.7 19.1 %collective-permute-done.21 = bf16[256,256]{1,0:T(8,128)(2,1)S(1)} collective-permute-done((bf16[256,256]{1,0:T(8,128)(2,1)S(1)}, bf16[256,256]{1,0:T(8,128)(2,1)S(1)}, u32[]{:S(2)}, u32[]{:S(2)}) %collective-permute-start.21) | collective-permute-done | bytes 131104 | tf_op jit(solution)/shard_map/ppermute | solution.py:200
  142.9 2.2 %collective-permute-done.23 = bf16[256,256]{1,0:T(8,128)(2,1)S(1)} collective-permute-done((bf16[256,256]{1,0:T(8,128)(2,1)S(1)}, bf16[256,256]{1,0:T(8,128)(2,1)S(1)}, u32[]{:S(2)}, u32[]{:S(2)}) %collective-permute-start.23) | collective-permute-done | bytes 131104 | tf_op jit(solution)/shard_map/ppermute | solution.py:200
  146.2 3.2 %collective-permute-start.24 = (bf16[1280,128]{0,1:T(8,128)(2,1)S(1)}, bf16[1280,128]{0,1:T(8,128)(2,1)S(1)}, u32[]{:S(2)}, u32[]{:S(2)}) collective-permute-start(bf16[1280,128]{0,1:T(8,128)(2,1)S(1)} %select_convert_fusion), channel_id=1, source_target_pairs={{0,4},{4,0},{8,12},{12,8},{16,20},{20,16},{24,28},{28,24},{1,5},{5... | collective-permute-start | bytes 983048 | tf_op jit(solution)/shard_map/ppermute | solution.py:200
  149.4 5.8 %collective-permute-done.19 = bf16[256,1024]{1,0:T(8,128)(2,1)S(1)} collective-permute-done((bf16[256,1024]{1,0:T(8,128)(2,1)S(1)}, bf16[256,1024]{1,0:T(8,128)(2,1)S(1)}, u32[]{:S(2)}, u32[]{:S(2)}) %collective-permute-start.19) | collective-permute-done | bytes 524320 | tf_op jit(solution)/shard_map/ppermute | solution.py:200
  158.1 3.5 %collective-permute-start.20 = (bf16[640,1024]{1,0:T(8,128)(2,1)S(1)}, bf16[640,1024]{1,0:T(8,128)(2,1)S(1)}, u32[]{:S(2)}, u32[]{:S(2)}) collective-permute-start(bf16[640,1024]{1,0:T(8,128)(2,1)S(1)} %add_convert_fusion), channel_id=1, source_target_pairs={{0,4},{4,0},{8,12},{12,8},{16,20},{20,16},{24,28},{28,24},{1,5},{5... | collective-permute-start | bytes 3932168 | tf_op jit(solution)/shard_map/ppermute | solution.py:200
  164.2 3.0 %add_add_fusion = f32[640,1024]{1,0:T(8,128)} fusion(f32[640,1024]{1,0:T(8,128)S(1)} %fusion.2, bf16[640,1024]{1,0:T(8,128)(2,1)S(1)} %collective-permute-done.20, bf16[256,1024]{1,0:T(8,128)(2,1)S(1)} %collective-permute-done.17, bf16[256,1280]{1,0:T(8,128)(2,1)} %collective-permute-done.16, s32[]{:T(128)S(6)} %select_n.172), kind=kOutput, calls=%fused_computation.7 | convolution fusion | flops 337510400 | bytes 7405572 | tf_op jit(solution)/shard_map/td,tc->dc/dot_general | solution.py:302
  (118 shorter events, 44.0 us)
Async XLA Ops:
  9.7 16.4 %all-to-all-start = ((bf16[8,32,1280]{2,1,0:T(8,128)(2,1)}), bf16[8,32,1280]{2,1,0:T(8,128)(2,1)S(1)}, u32[]{:S(2)}, u32[]{:S(2)}) async-start(bf16[8,32,1280]{2,1,0:T(8,128)(2,1)} %gather_fusion), calls=%async_computation | async-start | bytes 1310720 | tf_op jit(solution)/shard_map/all_to_all | solution.py:234
  14.2 68.4 %all-gather.2.cloned.1.call-start = ((), (), s32[]{:S(2)}) async-start(), calls=%async_computation.1 | async-start | bytes 3276800 | tf_op jit(solution)/shard_map/all_gather | solution.py:256
  17.6 8.4 %collective-permute-start.1 = (bf16[160,256]{1,0:T(8,128)(2,1)S(1)}, bf16[160,256]{1,0:T(8,128)(2,1)S(1)}, u32[]{:S(2)}, u32[]{:S(2)}) collective-permute-start(bf16[160,256]{1,0:T(8,128)(2,1)S(1)} %get-tuple-element.93), channel_id=1, source_target_pairs={{0,2},{1,3},{2,0},{3,1},{4,6},{5,7},{6,4},{7,5},{8,10},{9,11},{10,... | collective-permute-start | bytes 245768 | tf_op jit(solution)/shard_map/ppermute | solution.py:207
  19.9 6.1 %collective-permute-start.2 = (bf16[160,256]{1,0:T(8,128)(2,1)S(1)}, bf16[160,256]{1,0:T(8,128)(2,1)S(1)}, u32[]{:S(2)}, u32[]{:S(2)}) collective-permute-start(bf16[160,256]{1,0:T(8,128)(2,1)S(1)} %get-tuple-element.92), channel_id=1, source_target_pairs={{0,3},{1,0},{2,1},{3,2},{4,7},{5,4},{6,5},{7,6},{8,11},{9,8},{10,9... | collective-permute-start | bytes 245768 | tf_op jit(solution)/shard_map/ppermute | solution.py:207
  27.0 8.5 %collective-permute-start.3 = (bf16[4,160,256]{2,1,0:T(8,128)(2,1)S(1)}, bf16[4,160,256]{2,1,0:T(8,128)(2,1)S(1)}, u32[]{:S(2)}, u32[]{:S(2)}) collective-permute-start(bf16[4,160,256]{2,1,0:T(8,128)(2,1)S(1)} %get-tuple-element.91), channel_id=1, source_target_pairs={{0,8},{4,12},{8,0},{12,4},{16,24},{20,28},{24,16},{28,20},{1,9},{5... | collective-permute-start | bytes 983048 | tf_op jit(solution)/shard_map/ppermute | solution.py:200
  27.4 8.1 %collective-permute-start.4 = (bf16[4,160,256]{2,1,0:T(8,128)(2,1)S(1)}, bf16[4,160,256]{2,1,0:T(8,128)(2,1)S(1)}, u32[]{:S(2)}, u32[]{:S(2)}) collective-permute-start(bf16[4,160,256]{2,1,0:T(8,128)(2,1)S(1)} %get-tuple-element.91), channel_id=1, source_target_pairs={{0,16},{4,20},{8,24},{12,28},{16,0},{20,4},{24,8},{28,12},{1,17},{... | collective-permute-start | bytes 983048 | tf_op jit(solution)/shard_map/ppermute | solution.py:200
  27.5 15.2 %collective-permute-start.5 = (bf16[4,160,256]{2,1,0:T(8,128)(2,1)S(1)}, bf16[4,160,256]{2,1,0:T(8,128)(2,1)S(1)}, u32[]{:S(2)}, u32[]{:S(2)}) collective-permute-start(bf16[4,160,256]{2,1,0:T(8,128)(2,1)S(1)} %get-tuple-element.91), channel_id=1, source_target_pairs={{0,24},{4,28},{8,16},{12,20},{16,8},{20,12},{24,0},{28,4},{1,25},{... | collective-permute-start | bytes 983048 | tf_op jit(solution)/shard_map/ppermute | solution.py:200
  42.8 19.2 %collective-permute-start.6 = (bf16[4,4,160,256]{3,2,1,0:T(8,128)(2,1)S(1)}, bf16[4,4,160,256]{3,2,1,0:T(8,128)(2,1)}, u32[]{:S(2)}, u32[]{:S(2)}) collective-permute-start(bf16[4,4,160,256]{3,2,1,0:T(8,128)(2,1)S(1)} %pad_maximum_fusion.2), channel_id=1, source_target_pairs={{0,4},{4,0},{8,12},{12,8},{16,20},{20,16},{24,28},{28,24},{1,5},{5... | collective-permute-start | bytes 3932168 | tf_op jit(solution)/shard_map/ppermute | solution.py:200
  44.8 16.4 %collective-permute-start.7 = (bf16[256,1280]{1,0:T(8,128)(2,1)S(1)}, bf16[256,1280]{1,0:T(8,128)(2,1)}, u32[]{:S(2)}, u32[]{:S(2)}) collective-permute-start(bf16[256,1280]{1,0:T(8,128)(2,1)S(1)} %bitcast.75), channel_id=1, source_target_pairs={{0,8},{4,12},{8,0},{12,4},{16,24},{20,28},{24,16},{28,20},{1,9},{5... | collective-permute-start | bytes 1966088 | tf_op jit(solution)/shard_map/ppermute | solution.py:200
  46.0 16.1 %collective-permute-start.8 = (bf16[256,1280]{1,0:T(8,128)(2,1)S(1)}, bf16[256,1280]{1,0:T(8,128)(2,1)}, u32[]{:S(2)}, u32[]{:S(2)}) collective-permute-start(bf16[256,1280]{1,0:T(8,128)(2,1)S(1)} %bitcast.76), channel_id=1, source_target_pairs={{0,16},{4,20},{8,24},{12,28},{16,0},{20,4},{24,8},{28,12},{1,17},{... | collective-permute-start | bytes 1966088 | tf_op jit(solution)/shard_map/ppermute | solution.py:200
  63.8 9.6 %collective-permute-start.10 = (bf16[128,1280]{1,0:T(8,128)(2,1)}, bf16[128,1280]{1,0:T(8,128)(2,1)}, u32[]{:S(2)}, u32[]{:S(2)}) collective-permute-start(bf16[128,1280]{1,0:T(8,128)(2,1)} %slice.51), channel_id=1, source_target_pairs={{0,8},{4,12},{8,0},{12,4},{16,24},{20,28},{24,16},{28,20},{1,9},{5... | collective-permute-start | bytes 983048 | tf_op jit(solution)/shard_map/ppermute | solution.py:200
  65.8 8.1 %collective-permute-start.9 = (bf16[128,1280]{1,0:T(8,128)(2,1)}, bf16[128,1280]{1,0:T(8,128)(2,1)}, u32[]{:S(2)}, u32[]{:S(2)}) collective-permute-start(bf16[128,1280]{1,0:T(8,128)(2,1)} %slice.50), channel_id=1, source_target_pairs={{0,16},{4,20},{8,24},{12,28},{16,0},{20,4},{24,8},{28,12},{1,17},{... | collective-permute-start | bytes 983048 | tf_op jit(solution)/shard_map/ppermute | solution.py:200
  86.0 26.4 %collective-permute-start.14 = (bf16[256,1280]{1,0:T(8,128)(2,1)}, bf16[256,1280]{1,0:T(8,128)(2,1)}, u32[]{:S(2)}, u32[]{:S(2)}) collective-permute-start(bf16[256,1280]{1,0:T(8,128)(2,1)} %get-tuple-element.59), channel_id=1, source_target_pairs={{0,8},{4,12},{8,0},{12,4},{16,24},{20,28},{24,16},{28,20},{1,9},{5... | collective-permute-start | bytes 1966088 | tf_op jit(solution)/shard_map/ppermute | solution.py:200
  86.3 26.2 %collective-permute-start.15 = (bf16[256,1280]{1,0:T(8,128)(2,1)}, bf16[256,1280]{1,0:T(8,128)(2,1)}, u32[]{:S(2)}, u32[]{:S(2)}) collective-permute-start(bf16[256,1280]{1,0:T(8,128)(2,1)} %get-tuple-element.60), channel_id=1, source_target_pairs={{0,16},{4,20},{8,24},{12,28},{16,0},{20,4},{24,8},{28,12},{1,17},{... | collective-permute-start | bytes 1966088 | tf_op jit(solution)/shard_map/ppermute | solution.py:200
  86.6 29.4 %collective-permute-start.16 = (bf16[256,1280]{1,0:T(8,128)(2,1)}, bf16[256,1280]{1,0:T(8,128)(2,1)}, u32[]{:S(2)}, u32[]{:S(2)}) collective-permute-start(bf16[256,1280]{1,0:T(8,128)(2,1)} %get-tuple-element.61), channel_id=1, source_target_pairs={{0,24},{4,28},{8,16},{12,20},{16,8},{20,12},{24,0},{28,4},{1,25},{... | collective-permute-start | bytes 1966088 | tf_op jit(solution)/shard_map/ppermute | solution.py:200
  101.0 10.2 %collective-permute-start.12 = (bf16[256,256]{1,0:T(8,128)(2,1)S(1)}, bf16[256,256]{1,0:T(8,128)(2,1)S(1)}, u32[]{:S(2)}, u32[]{:S(2)}) collective-permute-start(bf16[256,256]{1,0:T(8,128)(2,1)S(1)} %convert_element_type.46), channel_id=1, source_target_pairs={{0,2},{1,3},{2,0},{3,1},{4,6},{5,7},{6,4},{7,5},{8,10},{9,11},{10,... | collective-permute-start | bytes 393224 | tf_op jit(solution)/shard_map/ppermute | solution.py:207
  116.0 39.2 %collective-permute-start.17 = (bf16[256,1024]{1,0:T(8,128)(2,1)S(1)}, bf16[256,1024]{1,0:T(8,128)(2,1)S(1)}, u32[]{:S(2)}, u32[]{:S(2)}) collective-permute-start(bf16[256,1024]{1,0:T(8,128)(2,1)S(1)} %convert_element_type.45), channel_id=1, source_target_pairs={{0,24},{4,28},{8,16},{12,20},{16,8},{20,12},{24,0},{28,4},{1,25},{... | collective-permute-start | bytes 1572872 | tf_op jit(solution)/shard_map/ppermute | solution.py:200
  117.2 32.2 %collective-permute-start.18 = (bf16[256,1024]{1,0:T(8,128)(2,1)S(1)}, bf16[256,1024]{1,0:T(8,128)(2,1)S(1)}, u32[]{:S(2)}, u32[]{:S(2)}) collective-permute-start(bf16[256,1024]{1,0:T(8,128)(2,1)S(1)} %convert_element_type.45), channel_id=1, source_target_pairs={{0,8},{4,12},{8,0},{12,4},{16,24},{20,28},{24,16},{28,20},{1,9},{5... | collective-permute-start | bytes 1572872 | tf_op jit(solution)/shard_map/ppermute | solution.py:200
  118.5 24.4 %collective-permute-start.21 = (bf16[256,256]{1,0:T(8,128)(2,1)S(1)}, bf16[256,256]{1,0:T(8,128)(2,1)S(1)}, u32[]{:S(2)}, u32[]{:S(2)}) collective-permute-start(bf16[256,256]{1,0:T(8,128)(2,1)S(1)} %get-tuple-element.89), channel_id=1, source_target_pairs={{0,8},{4,12},{8,0},{12,4},{16,24},{20,28},{24,16},{28,20},{1,9},{5... | collective-permute-start | bytes 393224 | tf_op jit(solution)/shard_map/ppermute | solution.py:200
  118.9 24.1 %collective-permute-start.22 = (bf16[256,256]{1,0:T(8,128)(2,1)S(1)}, bf16[256,256]{1,0:T(8,128)(2,1)S(1)}, u32[]{:S(2)}, u32[]{:S(2)}) collective-permute-start(bf16[256,256]{1,0:T(8,128)(2,1)S(1)} %get-tuple-element.88), channel_id=1, source_target_pairs={{0,16},{4,20},{8,24},{12,28},{16,0},{20,4},{24,8},{28,12},{1,17},{... | collective-permute-start | bytes 393224 | tf_op jit(solution)/shard_map/ppermute | solution.py:200
  119.2 26.0 %collective-permute-start.23 = (bf16[256,256]{1,0:T(8,128)(2,1)S(1)}, bf16[256,256]{1,0:T(8,128)(2,1)S(1)}, u32[]{:S(2)}, u32[]{:S(2)}) collective-permute-start(bf16[256,256]{1,0:T(8,128)(2,1)S(1)} %get-tuple-element.87), channel_id=1, source_target_pairs={{0,24},{4,28},{8,16},{12,20},{16,8},{20,12},{24,0},{28,4},{1,25},{... | collective-permute-start | bytes 393224 | tf_op jit(solution)/shard_map/ppermute | solution.py:200
  142.9 12.4 %collective-permute-start.19 = (bf16[256,1024]{1,0:T(8,128)(2,1)S(1)}, bf16[256,1024]{1,0:T(8,128)(2,1)S(1)}, u32[]{:S(2)}, u32[]{:S(2)}) collective-permute-start(bf16[256,1024]{1,0:T(8,128)(2,1)S(1)} %convert_element_type.45), channel_id=1, source_target_pairs={{0,16},{4,20},{8,24},{12,28},{16,0},{20,4},{24,8},{28,12},{1,17},{... | collective-permute-start | bytes 1572872 | tf_op jit(solution)/shard_map/ppermute | solution.py:200
  146.2 15.3 %collective-permute-start.24 = (bf16[1280,128]{0,1:T(8,128)(2,1)S(1)}, bf16[1280,128]{0,1:T(8,128)(2,1)S(1)}, u32[]{:S(2)}, u32[]{:S(2)}) collective-permute-start(bf16[1280,128]{0,1:T(8,128)(2,1)S(1)} %select_convert_fusion), channel_id=1, source_target_pairs={{0,4},{4,0},{8,12},{12,8},{16,20},{20,16},{24,28},{28,24},{1,5},{5... | collective-permute-start | bytes 983048 | tf_op jit(solution)/shard_map/ppermute | solution.py:200
  158.1 6.1 %collective-permute-start.20 = (bf16[640,1024]{1,0:T(8,128)(2,1)S(1)}, bf16[640,1024]{1,0:T(8,128)(2,1)S(1)}, u32[]{:S(2)}, u32[]{:S(2)}) collective-permute-start(bf16[640,1024]{1,0:T(8,128)(2,1)S(1)} %add_convert_fusion), channel_id=1, source_target_pairs={{0,4},{4,0},{8,12},{12,8},{16,20},{20,16},{24,28},{28,24},{1,5},{5... | collective-permute-start | bytes 3932168 | tf_op jit(solution)/shard_map/ppermute | solution.py:200
  (18 other events, 168.6 us)
Sparse Core Ops, SparseCore 0:
  27.0 55.5 all-gather.1

commit v10 on v4

--- a/solution.py
+++ b/solution.py
@@ -251,20 +251,38 @@
     shares = jnp.stack([shares] + other_chips([shares] * chips))
     native, shares = together(rows, shares)
     other_shares, *plane_rows = together(flip(shares, 1), *from_near(native))
-    plane_rows = jnp.stack(from_far(native, plane_rows)).reshape(chips * tokens, width)
+    plane_rows = from_far(native, plane_rows)
+    rest = [k for k in range(1, chips) if k not in near]
+    far_rows = jnp.concatenate([plane_rows[k] for k in rest])
+    plane_rows = jnp.concatenate(plane_rows)
 
     shares = jnp.stack([shares, other_shares], axis=1).reshape(n_dp * n_mp, share, 2 * dim)
     order = (dp ^ jnp.arange(n_dp))[None, :] * n_mp + ((mp - jnp.arange(n_mp)) % n_mp)[:, None]
     w_kv = pick(shares, order.reshape(-1)).reshape(n_mp * width, 2 * dim)
 
-    x, w_kv, plane_rows = together(x, w_kv, plane_rows)
+    x, w_kv, plane_rows, far_rows = together(x, w_kv, plane_rows, far_rows)
 
     chip_width = n_mp * width // chips
-    chip_rows = [
-        lax.dynamic_slice_in_dim(x, (chip ^ k) * chip_width, chip_width, 1) for k in range(chips)
-    ]
-    x, *chip_rows = together(x, *chip_rows)
-    chip_rows = [chip_rows[0]] + other_chips(chip_rows)
+    by_plane = chips == n_mp
+    chip_rows = {
+        k: lax.dynamic_slice_in_dim(x, (chip ^ k) * chip_width, chip_width, 1)
+        for k in range(chips)
+        if k in [0] + near or not by_plane
+    }
+    x, chip_rows = lax.optimization_barrier((x, chip_rows))
+    near_rows = [flip(chip_rows[k], 2 * k) for k in near]
+
+    def along(block, steps):
+        pairs = [
+            (d * n_mp + d // 2 + a, d * n_mp + d // 2 + b)
+            for d in range(n_dp)
+            for a, b in steps
+            if 0 <= d // 2 + a < n_mp and 0 <= d // 2 + b < n_mp
+        ]
+        return lax.ppermute(block, ("dp", "mp"), pairs)
+
+    if by_plane:
+        near_rows += [along(far_rows, [(0, 1)]), along(far_rows, [(0, -1)])]
 
     factor = multiplicity.astype(F32) * slot_weight / length
     d_out = (cotangent.astype(F32) * factor[:, None, None]).astype(BF16).astype(F32)
@@ -279,10 +297,30 @@
         key_cols // n_dp,
     )
     attended, d_query, d_kv = [value.astype(BF16) for value in (attended, d_query, d_kv)]
-    d_query, d_kv, *chip_rows = together(d_query, d_kv, *chip_rows)
+    d_query, d_kv, *near_rows = together(d_query, d_kv, *near_rows)
+    if by_plane:
+        above, below = near_rows[len(near) :]
+        hops = [jnp.where(mp > chip, above, below)]
+        if n_mp > 2:
+            hops.append(along(hops[0], [(1, 2), (-1, -2)]))
 
     d_all = [d_query] + other_chips([d_query] * chips)
     spread = jnp.stack(around([d_kv] * n_mp))
+    d_near = [d_all[k] for k in near]
+    d_near, spread, last = lax.optimization_barrier((d_near, spread, hops[-1] if by_plane else x))
+    for k, block in zip(near, d_near):
+        d_all[k] = block
+    for k, block in zip(near, near_rows):
+        chip_rows[k] = block
+    if by_plane:
+        hops[-1] = last
+        for hop in range(3, n_mp):
+            hops.append(along(hops[-1], [(hop - 1, hop), (1 - hop, -hop)]))
+        for hop, block in enumerate(hops, 1):
+            far_rows = jnp.where(jnp.abs(mp - chip) == hop, block, far_rows)
+        chip_rows.update(zip(rest, jnp.split(far_rows, len(rest))))
+    else:
+        chip_rows.update({k: flip(chip_rows[k], 2 * k) for k in rest})
     half = chip_width // 2
     early = [0] + near
     late = [k for k in range(chips) if k not in early]

time: 165 us -> 166 us (level); the launches traced: 163 us -> 166 us
  starting transfers between devices: 29.6 us -> 53.3 us
  waiting for transfers between devices: 77.6 us -> 57.1 us
  other arithmetic: 12.2 us -> 7.5 us
  local copies, waits for them, and re-layouts: 12.7 us -> 15.1 us
  matrix products: 6.02 us -> 7.81 us
    ppermute x19 -> x18, waiting for transfers between devices: 57.3 us -> 33.3 us  [flip(): return lax.ppermute(block, 'dp', [(i, i ^ bits) for i in range(n_dp)])]
    ppermute x19 -> x18, starting transfers between devices: 18.8 us -> 34.6 us  [flip(): return lax.ppermute(block, 'dp', [(i, i ^ bits) for i in range(n_dp)])]
    ppermute x6, waiting for transfers between devices: 16.7 us -> 4.98 us  [around(): lax.ppermute(blocks[k], 'mp', [(i, (i + k) % n_mp) for i in range(n_mp)])]
    all_to_all x1, waiting for transfers between devices: 0.01 us -> 8.26 us  [local(): lax.all_to_all(outgoing, 'dp', split_axis=0, concat_axis=0, tiled=True)]
    ppermute x0 -> x4, waiting for transfers between devices: none -> 5.11 us  [along(): return lax.ppermute(block, ('dp', 'mp'), pairs)]
    another operation x2 -> x0, other arithmetic: 4.42 us -> none  [local(): jnp.stack(from_far(native, plane_rows)).reshape(chips * tokens, width)]
    ppermute x0 -> x4, starting transfers between devices: none -> 3.83 us  [along(): return lax.ppermute(block, ('dp', 'mp'), pairs)]
    ppermute x6, starting transfers between devices: 6.15 us -> 9.54 us  [around(): lax.ppermute(blocks[k], 'mp', [(i, (i + k) % n_mp) for i in range(n_mp)])]
  transfers between devices with their start and end apart: 27 -> 30, of which waited for: 14 -> 13; matrix products, arithmetic and copies ran while one was open for 14% -> 14% of each run, Pallas kernels for 6% -> 6%
where the time goes in v10:
time: 166 us
  waiting for transfers between devices  57.1 us (34%)
  starting transfers between devices  53.3 us (32%)
  local copies, waits for them, and re-layouts  15.1 us (9%)
  between operations  14.6 us (9%)
  Pallas kernels  10.3 us (6%)
  matrix products  7.81 us (5%)
  other arithmetic  7.5 us (5%)
    ppermute x18, starting transfers between devices, flip(): return lax.ppermute(block, 'dp', [(i, i ^ bits) for i in range(n_dp)])  34.6 us
    ppermute x18, waiting for transfers between devices, flip(): return lax.ppermute(block, 'dp', [(i, i ^ bits) for i in range(n_dp)])  33.3 us
    pallas_call x1, Pallas kernels, attend(): pl.pallas_call(functools.partial(attend_kernel, length, device_cols), gri...  10.3 us
    ppermute x6, starting transfers between devices, around(): lax.ppermute(blocks[k], 'mp', [(i, (i + k) % n_mp) for i in range(n_mp)])  9.54 us
    all_to_all x1, waiting for transfers between devices, local(): lax.all_to_all(outgoing, 'dp', split_axis=0, concat_axis=0, tiled=True)  8.26 us
    all_gather x1, waiting for transfers between devices, local(): x = lax.all_gather(rows, 'mp', axis=1, tiled=True)  5.54 us
    all_to_all x1, starting transfers between devices, local(): lax.all_to_all(outgoing, 'dp', split_axis=0, concat_axis=0, tiled=True)  5.35 us
    gather x3, local copies, waits for them, and re-layouts, pick(): return array.at[index].get(mode='promise_in_bounds')  5.3 us
  transfers between devices with their start and end apart: 30, of which 13 were waited for; matrix products, arithmetic and copies ran while one was open for 14% of the time, Pallas kernels for 6%

profile of v10, /device:TPU:7, one launch (start us, length us, event | category | flops | bytes accessed | tf_op | source)
XLA Modules:
  0.0 165.7 jit_solution(2946515475434208460)
XLA Ops:
  12.2 2.3 %collective-permute-start.1 = (bf16[160,256]{1,0:T(8,128)(2,1)S(1)}, bf16[160,256]{1,0:T(8,128)(2,1)S(1)}, u32[]{:S(2)}, u32[]{:S(2)}) collective-permute-start(bf16[160,256]{1,0:T(8,128)(2,1)S(1)} %get-tuple-element.92), channel_id=1, source_target_pairs={{0,2},{1,3},{2,0},{3,1},{4,6},{5,7},{6,4},{7,5},{8,10},{9,11},{10,... | collective-permute-start | bytes 245768 | tf_op jit(solution)/shard_map/ppermute | solution.py:207
  15.6 5.4 %all-to-all-start = ((bf16[8,32,1280]{2,1,0:T(8,128)(2,1)}), bf16[8,32,1280]{2,1,0:T(8,128)(2,1)S(1)}, u32[]{:S(2)}, u32[]{:S(2)}) async-start(bf16[8,32,1280]{2,1,0:T(8,128)(2,1)} %gather_fusion), calls=%async_computation | async-start | bytes 1310720 | tf_op jit(solution)/shard_map/all_to_all | solution.py:234
  21.2 8.3 %all-to-all-done = bf16[8,32,1280]{2,1,0:T(8,128)(2,1)S(1)} async-done(((bf16[8,32,1280]{2,1,0:T(8,128)(2,1)}), bf16[8,32,1280]{2,1,0:T(8,128)(2,1)S(1)}, u32[]{:S(2)}, u32[]{:S(2)}) %all-to-all-start) | async-done | bytes 655392 | tf_op jit(solution)/shard_map/all_to_all | solution.py:234
  33.7 6.0 %collective-permute-done.3 = bf16[4,160,256]{2,1,0:T(8,128)(2,1)S(1)} collective-permute-done((bf16[4,160,256]{2,1,0:T(8,128)(2,1)S(1)}, bf16[4,160,256]{2,1,0:T(8,128)(2,1)S(1)}, u32[]{:S(2)}, u32[]{:S(2)}) %collective-permute-start.3) | collective-permute-done | bytes 327712 | tf_op jit(solution)/shard_map/ppermute | solution.py:200
  39.6 8.5 %collective-permute-done.5 = bf16[4,160,256]{2,1,0:T(8,128)(2,1)S(1)} collective-permute-done((bf16[4,160,256]{2,1,0:T(8,128)(2,1)S(1)}, bf16[4,160,256]{2,1,0:T(8,128)(2,1)S(1)}, u32[]{:S(2)}, u32[]{:S(2)}) %collective-permute-start.5) | collective-permute-done | bytes 327712 | tf_op jit(solution)/shard_map/ppermute | solution.py:200
  54.6 11.3 %collective-permute-done.7 = bf16[256,1280]{1,0:T(8,128)(2,1)S(1)} collective-permute-done((bf16[256,1280]{1,0:T(8,128)(2,1)S(1)}, bf16[256,1280]{1,0:T(8,128)(2,1)S(1)}, u32[]{:S(2)}, u32[]{:S(2)}) %collective-permute-start.7) | collective-permute-done | bytes 655392 | tf_op jit(solution)/shard_map/ppermute | solution.py:200
  70.9 1.7 %pad_maximum_fusion = bf16[4,2,4,160,256]{4,3,2,1,0:T(8,128)(2,1)} fusion(bf16[4,1,4,160,256]{4,3,2,1,0:T(8,128)(2,1)S(1)} %bitcast.72, bf16[4,1,4,160,256]{4,3,2,1,0:T(8,128)(2,1)S(1)} %bitcast.70), kind=kLoop, calls=%fused_computation.3 | loop fusion | flops 1310720 | bytes 5242880 | tf_op jit(solution)/shard_map/stack | solution.py:259
  72.6 2.5 %gather_fusion.2 = bf16[32,160,256]{2,1,0:T(8,128)(2,1)S(1)} fusion(bf16[32,160,256]{2,1,0:T(8,128)(2,1)} %bitcast.65, s32[1024]{0:T(1024)S(1)} %get-tuple-element.95), kind=kCustom, calls=%fused_computation.2 | custom fusion | bytes 5243008 | tf_op jit(solution)/shard_map/gather | solution.py:169
  78.5 5.5 %all-gather.2.cloned.1.call-done.x_ref = bf16[256,5120]{1,0:T(8,128)(2,1)} async-done(((bf16[256,1280]{1,0:T(8,128)(2,1)}), bf16[256,5120]{1,0:T(8,128)(2,1)}) %all-gather.2.cloned.1.call-update) | async-done | bytes 2621456 | tf_op jit(solution)/shard_map/all_gather | solution.py:250
  85.7 1.6 constant_dynamic-slice_fusion.3
  88.6 10.3 %shard_map.138 = (f32[256,1024]{1,0:T(8,128)S(1)}, f32[256,1024]{1,0:T(8,128)S(1)}, f32[256,256]{1,0:T(8,128)S(1)}) custom-call(bf16[256,5120]{1,0:T(8,128)(2,1)S(1)} %copy-done.2, bf16[5120,1024]{1,0:T(8,128)(2,1)} %wq_ref.1, bf16[5120,256]{1,0:T(8,128)(2,1)S(1)} %bitcast.62, f32[256,1024]{1,0:T(8,128)S(1)} %copy-done.3, f32[1,128]{1,0:T(1,128)S(1)} %bitcast.63, ...), custom_call_target="tpu_custom_call" | custom-call | flops 16777216000 | bytes 41943040 | tf_op jit(solution)/shard_map/pallas_call | solution.py:137
  99.9 3.1 %collective-permute-done.11 = bf16[256,1280]{1,0:T(8,128)(2,1)S(1)} collective-permute-done((bf16[256,1280]{1,0:T(8,128)(2,1)S(1)}, bf16[256,1280]{1,0:T(8,128)(2,1)S(1)}, u32[]{:S(2)}, u32[]{:S(2)}) %collective-permute-start.11) | collective-permute-done | bytes 655392 | tf_op jit(solution)/shard_map/ppermute | solution.py:200
  103.0 1.9 %collective-permute-start.17 = (bf16[256,256]{1,0:T(8,128)(2,1)S(1)}, bf16[256,256]{1,0:T(8,128)(2,1)S(1)}, u32[]{:S(2)}, u32[]{:S(2)}) collective-permute-start(bf16[256,256]{1,0:T(8,128)(2,1)S(1)} %convert_element_type.36), channel_id=1, source_target_pairs={{0,1},{1,2},{2,3},{3,0},{4,5},{5,6},{6,7},{7,4},{8,9},{9,10},{10,1... | collective-permute-start | bytes 393224 | tf_op jit(solution)/shard_map/ppermute | solution.py:207
  108.7 1.5 collective-permute-start.19
  110.3 4.8 %collective-permute-done.18 = bf16[256,256]{1,0:T(8,128)(2,1)S(1)} collective-permute-done((bf16[256,256]{1,0:T(8,128)(2,1)S(1)}, bf16[256,256]{1,0:T(8,128)(2,1)S(1)}, u32[]{:S(2)}, u32[]{:S(2)}) %collective-permute-start.18) | collective-permute-done | bytes 131104 | tf_op jit(solution)/shard_map/ppermute | solution.py:207
  115.1 2.5 %collective-permute-start.22 = (bf16[256,1024]{1,0:T(8,128)(2,1)S(1)}, bf16[256,1024]{1,0:T(8,128)(2,1)S(1)}, u32[]{:S(2)}, u32[]{:S(2)}) collective-permute-start(bf16[256,1024]{1,0:T(8,128)(2,1)S(1)} %convert_element_type.35), channel_id=1, source_target_pairs={{0,24},{4,28},{8,16},{12,20},{16,8},{20,12},{24,0},{28,4},{1,25},{... | collective-permute-start | bytes 1572872 | tf_op jit(solution)/shard_map/ppermute | solution.py:200
  117.9 13.4 %collective-permute-start.24 = (bf16[256,256]{1,0:T(8,128)(2,1)S(1)}, bf16[256,256]{1,0:T(8,128)(2,1)S(1)}, u32[]{:S(2)}, u32[]{:S(2)}) collective-permute-start(bf16[256,256]{1,0:T(8,128)(2,1)S(1)} %get-tuple-element.88), channel_id=1, source_target_pairs={{0,8},{4,12},{8,0},{12,4},{16,24},{20,28},{24,16},{28,20},{1,9},{5... | collective-permute-start | bytes 393224 | tf_op jit(solution)/shard_map/ppermute | solution.py:200
  132.5 1.5 collective-permute-start.21
  134.1 2.8 %collective-permute-done.25 = bf16[256,256]{1,0:T(8,128)(2,1)S(1)} collective-permute-done((bf16[256,256]{1,0:T(8,128)(2,1)S(1)}, bf16[256,256]{1,0:T(8,128)(2,1)S(1)}, u32[]{:S(2)}, u32[]{:S(2)}) %collective-permute-start.25) | collective-permute-done | bytes 131104 | tf_op jit(solution)/shard_map/ppermute | solution.py:200
  136.9 2.7 %fusion.14 = f32[1280,256]{0,1:T(8,128)S(1)} fusion(bf16[1024,1280]{1,0:T(8,128)(2,1)} %constant_dynamic-update-slice_fusion, bf16[1024,256]{1,0:T(8,128)(2,1)S(1)} %bitcast.71), kind=kOutput, calls=%fused_computation.72 | convolution fusion | flops 671088640 | bytes 4456448 | tf_op jit(solution)/shard_map/td,tc->dc/dot_general | solution.py:350
  139.7 3.2 %collective-permute-start.27 = (bf16[1280,128]{0,1:T(8,128)(2,1)S(1)}, bf16[1280,128]{0,1:T(8,128)(2,1)S(1)}, u32[]{:S(2)}, u32[]{:S(2)}) collective-permute-start(bf16[1280,128]{0,1:T(8,128)(2,1)S(1)} %select_convert_fusion), channel_id=1, source_target_pairs={{0,4},{4,0},{8,12},{12,8},{16,20},{20,16},{24,28},{28,24},{1,5},{5... | collective-permute-start | bytes 983048 | tf_op jit(solution)/shard_map/ppermute | solution.py:200
  142.9 5.1 %collective-permute-done.21 = bf16[256,1280]{1,0:T(8,128)(2,1)S(1)} collective-permute-done((bf16[256,1280]{1,0:T(8,128)(2,1)S(1)}, bf16[256,1280]{1,0:T(8,128)(2,1)S(1)}, u32[]{:S(2)}, u32[]{:S(2)}) %collective-permute-start.21) | collective-permute-done | bytes 655392 | tf_op jit(solution)/shard_map/ppermute | solution.py:282
  149.9 4.2 %collective-permute-start.23 = (bf16[640,1024]{1,0:T(8,128)(2,1)S(1)}, bf16[640,1024]{1,0:T(8,128)(2,1)S(1)}, u32[]{:S(2)}, u32[]{:S(2)}) collective-permute-start(bf16[640,1024]{1,0:T(8,128)(2,1)S(1)} %add_convert_fusion), channel_id=1, source_target_pairs={{0,4},{4,0},{8,12},{12,8},{16,20},{20,16},{24,28},{28,24},{1,5},{5... | collective-permute-start | bytes 3932168 | tf_op jit(solution)/shard_map/ppermute | solution.py:200
  156.8 2.1 %add_add_fusion = f32[640,1024]{1,0:T(8,128)} fusion(f32[640,1024]{1,0:T(8,128)S(1)} %fusion.1, bf16[640,1024]{1,0:T(8,128)(2,1)S(1)} %collective-permute-done.23, bf16[256,1024]{1,0:T(8,128)(2,1)S(1)} %collective-permute-done.22, bf16[256,1280]{1,0:T(8,128)(2,1)S(1)} %select_select_fusion, s32[]{:T(128)S(6)} %select_n.193), kind=kOutput, calls=%fused_computation.4 | convolution fusion | flops 337510400 | bytes 7405572 | tf_op jit(solution)/shard_map/td,tc->dc/dot_general | solution.py:332
  (116 shorter events, 39.3 us)
Async XLA Ops:
  10.8 10.3 %collective-permute-start = (bf16[160,256]{1,0:T(8,128)(2,1)S(1)}, bf16[160,256]{1,0:T(8,128)(2,1)S(1)}, u32[]{:S(2)}, u32[]{:S(2)}) collective-permute-start(bf16[160,256]{1,0:T(8,128)(2,1)S(1)} %get-tuple-element.93), channel_id=1, source_target_pairs={{0,1},{1,2},{2,3},{3,0},{4,5},{5,6},{6,7},{7,4},{8,9},{9,10},{10,1... | collective-permute-start | bytes 245768 | tf_op jit(solution)/shard_map/ppermute | solution.py:207
  12.2 9.0 %collective-permute-start.1 = (bf16[160,256]{1,0:T(8,128)(2,1)S(1)}, bf16[160,256]{1,0:T(8,128)(2,1)S(1)}, u32[]{:S(2)}, u32[]{:S(2)}) collective-permute-start(bf16[160,256]{1,0:T(8,128)(2,1)S(1)} %get-tuple-element.92), channel_id=1, source_target_pairs={{0,2},{1,3},{2,0},{3,1},{4,6},{5,7},{6,4},{7,5},{8,10},{9,11},{10,... | collective-permute-start | bytes 245768 | tf_op jit(solution)/shard_map/ppermute | solution.py:207
  15.6 13.9 %all-to-all-start = ((bf16[8,32,1280]{2,1,0:T(8,128)(2,1)}), bf16[8,32,1280]{2,1,0:T(8,128)(2,1)S(1)}, u32[]{:S(2)}, u32[]{:S(2)}) async-start(bf16[8,32,1280]{2,1,0:T(8,128)(2,1)} %gather_fusion), calls=%async_computation | async-start | bytes 1310720 | tf_op jit(solution)/shard_map/all_to_all | solution.py:234
  20.9 63.1 %all-gather.2.cloned.1.call-start = ((), (), s32[]{:S(2)}) async-start(), calls=%async_computation.1 | async-start | bytes 3276800 | tf_op jit(solution)/shard_map/all_gather | solution.py:250
  31.0 8.7 %collective-permute-start.3 = (bf16[4,160,256]{2,1,0:T(8,128)(2,1)S(1)}, bf16[4,160,256]{2,1,0:T(8,128)(2,1)S(1)}, u32[]{:S(2)}, u32[]{:S(2)}) collective-permute-start(bf16[4,160,256]{2,1,0:T(8,128)(2,1)S(1)} %get-tuple-element.90), channel_id=1, source_target_pairs={{0,8},{4,12},{8,0},{12,4},{16,24},{20,28},{24,16},{28,20},{1,9},{5... | collective-permute-start | bytes 983048 | tf_op jit(solution)/shard_map/ppermute | solution.py:200
  31.0 8.6 %collective-permute-start.4 = (bf16[4,160,256]{2,1,0:T(8,128)(2,1)S(1)}, bf16[4,160,256]{2,1,0:T(8,128)(2,1)S(1)}, u32[]{:S(2)}, u32[]{:S(2)}) collective-permute-start(bf16[4,160,256]{2,1,0:T(8,128)(2,1)S(1)} %get-tuple-element.90), channel_id=1, source_target_pairs={{0,16},{4,20},{8,24},{12,28},{16,0},{20,4},{24,8},{28,12},{1,17},{... | collective-permute-start | bytes 983048 | tf_op jit(solution)/shard_map/ppermute | solution.py:200
  32.5 15.6 %collective-permute-start.5 = (bf16[4,160,256]{2,1,0:T(8,128)(2,1)S(1)}, bf16[4,160,256]{2,1,0:T(8,128)(2,1)S(1)}, u32[]{:S(2)}, u32[]{:S(2)}) collective-permute-start(bf16[4,160,256]{2,1,0:T(8,128)(2,1)S(1)} %get-tuple-element.90), channel_id=1, source_target_pairs={{0,24},{4,28},{8,16},{12,20},{16,8},{20,12},{24,0},{28,4},{1,25},{... | collective-permute-start | bytes 983048 | tf_op jit(solution)/shard_map/ppermute | solution.py:200
  48.3 17.7 %collective-permute-start.6 = (bf16[4,4,160,256]{3,2,1,0:T(8,128)(2,1)S(1)}, bf16[4,4,160,256]{3,2,1,0:T(8,128)(2,1)S(1)}, u32[]{:S(2)}, u32[]{:S(2)}) collective-permute-start(bf16[4,4,160,256]{3,2,1,0:T(8,128)(2,1)S(1)} %pad_maximum_fusion.1), channel_id=1, source_target_pairs={{0,4},{4,0},{8,12},{12,8},{16,20},{20,16},{24,28},{28,24},{1,5},{5... | collective-permute-start | bytes 3932168 | tf_op jit(solution)/shard_map/ppermute | solution.py:200
  49.5 16.3 %collective-permute-start.7 = (bf16[256,1280]{1,0:T(8,128)(2,1)S(1)}, bf16[256,1280]{1,0:T(8,128)(2,1)S(1)}, u32[]{:S(2)}, u32[]{:S(2)}) collective-permute-start(bf16[256,1280]{1,0:T(8,128)(2,1)S(1)} %bitcast.67), channel_id=1, source_target_pairs={{0,8},{4,12},{8,0},{12,4},{16,24},{20,28},{24,16},{28,20},{1,9},{5... | collective-permute-start | bytes 1966088 | tf_op jit(solution)/shard_map/ppermute | solution.py:200
  50.0 16.0 %collective-permute-start.8 = (bf16[256,1280]{1,0:T(8,128)(2,1)S(1)}, bf16[256,1280]{1,0:T(8,128)(2,1)S(1)}, u32[]{:S(2)}, u32[]{:S(2)}) collective-permute-start(bf16[256,1280]{1,0:T(8,128)(2,1)S(1)} %bitcast.68), channel_id=1, source_target_pairs={{0,16},{4,20},{8,24},{12,28},{16,0},{20,4},{24,8},{28,12},{1,17},{... | collective-permute-start | bytes 1966088 | tf_op jit(solution)/shard_map/ppermute | solution.py:200
  66.7 8.4 %collective-permute-start.9 = (bf16[128,1280]{1,0:T(8,128)(2,1)}, bf16[128,1280]{1,0:T(8,128)(2,1)S(1)}, u32[]{:S(2)}, u32[]{:S(2)}) collective-permute-start(bf16[128,1280]{1,0:T(8,128)(2,1)} %slice.50), channel_id=1, source_target_pairs={{0,16},{4,20},{8,24},{12,28},{16,0},{20,4},{24,8},{28,12},{1,17},{... | collective-permute-start | bytes 983048 | tf_op jit(solution)/shard_map/ppermute | solution.py:200
  84.0 19.0 %collective-permute-start.13 = (bf16[256,1280]{1,0:T(8,128)(2,1)}, bf16[256,1280]{1,0:T(8,128)(2,1)S(1)}, u32[]{:S(2)}, u32[]{:S(2)}) collective-permute-start(bf16[256,1280]{1,0:T(8,128)(2,1)} %pad_maximum_fusion.2), channel_id=1, source_target_pairs={{0,1},{4,5},{9,10},{13,14},{18,19},{22,23}} | collective-permute-start | bytes 1966088 | tf_op jit(solution)/shard_map/ppermute | solution.py:282
  84.9 18.1 %collective-permute-start.14 = (bf16[256,1280]{1,0:T(8,128)(2,1)}, bf16[256,1280]{1,0:T(8,128)(2,1)S(1)}, u32[]{:S(2)}, u32[]{:S(2)}) collective-permute-start(bf16[256,1280]{1,0:T(8,128)(2,1)} %pad_maximum_fusion.2), channel_id=1, source_target_pairs={{9,8},{13,12},{18,17},{22,21},{27,26},{31,30}} | collective-permute-start | bytes 1966088 | tf_op jit(solution)/shard_map/ppermute | solution.py:282
  87.3 15.7 %collective-permute-start.11 = (bf16[256,1280]{1,0:T(8,128)(2,1)S(1)}, bf16[256,1280]{1,0:T(8,128)(2,1)S(1)}, u32[]{:S(2)}, u32[]{:S(2)}) collective-permute-start(bf16[256,1280]{1,0:T(8,128)(2,1)S(1)} %get-tuple-element.57), channel_id=1, source_target_pairs={{0,8},{4,12},{8,0},{12,4},{16,24},{20,28},{24,16},{28,20},{1,9},{5... | collective-permute-start | bytes 1966088 | tf_op jit(solution)/shard_map/ppermute | solution.py:200
  87.7 15.3 %collective-permute-start.12 = (bf16[256,1280]{1,0:T(8,128)(2,1)S(1)}, bf16[256,1280]{1,0:T(8,128)(2,1)S(1)}, u32[]{:S(2)}, u32[]{:S(2)}) collective-permute-start(bf16[256,1280]{1,0:T(8,128)(2,1)S(1)} %get-tuple-element.58), channel_id=1, source_target_pairs={{0,16},{4,20},{8,24},{12,28},{16,0},{20,4},{24,8},{28,12},{1,17},{... | collective-permute-start | bytes 1966088 | tf_op jit(solution)/shard_map/ppermute | solution.py:200
  104.9 10.2 %collective-permute-start.18 = (bf16[256,256]{1,0:T(8,128)(2,1)S(1)}, bf16[256,256]{1,0:T(8,128)(2,1)S(1)}, u32[]{:S(2)}, u32[]{:S(2)}) collective-permute-start(bf16[256,256]{1,0:T(8,128)(2,1)S(1)} %convert_element_type.36), channel_id=1, source_target_pairs={{0,2},{1,3},{2,0},{3,1},{4,6},{5,7},{6,4},{7,5},{8,10},{9,11},{10,... | collective-permute-start | bytes 393224 | tf_op jit(solution)/shard_map/ppermute | solution.py:207
  106.3 11.3 %collective-permute-start.15 = (bf16[256,1024]{1,0:T(8,128)(2,1)S(1)}, bf16[256,1024]{1,0:T(8,128)(2,1)S(1)}, u32[]{:S(2)}, u32[]{:S(2)}) collective-permute-start(bf16[256,1024]{1,0:T(8,128)(2,1)S(1)} %convert_element_type.35), channel_id=1, source_target_pairs={{0,8},{4,12},{8,0},{12,4},{16,24},{20,28},{24,16},{28,20},{1,9},{5... | collective-permute-start | bytes 1572872 | tf_op jit(solution)/shard_map/ppermute | solution.py:200
  107.4 10.4 %collective-permute-start.16 = (bf16[256,1024]{1,0:T(8,128)(2,1)S(1)}, bf16[256,1024]{1,0:T(8,128)(2,1)S(1)}, u32[]{:S(2)}, u32[]{:S(2)}) collective-permute-start(bf16[256,1024]{1,0:T(8,128)(2,1)S(1)} %convert_element_type.35), channel_id=1, source_target_pairs={{0,16},{4,20},{8,24},{12,28},{16,0},{20,4},{24,8},{28,12},{1,17},{... | collective-permute-start | bytes 1572872 | tf_op jit(solution)/shard_map/ppermute | solution.py:200
  107.8 10.0 %collective-permute-start.20 = (bf16[256,1280]{1,0:T(8,128)(2,1)S(1)}, bf16[256,1280]{1,0:T(8,128)(2,1)S(1)}, u32[]{:S(2)}, u32[]{:S(2)}) collective-permute-start(bf16[256,1280]{1,0:T(8,128)(2,1)S(1)} %broadcast_select_fusion), channel_id=1, source_target_pairs={{1,2},{5,6},{10,11},{14,15},{17,16},{21,20},{26,25},{30,29}} | collective-permute-start | bytes 1966088 | tf_op jit(solution)/shard_map/ppermute | solution.py:282
  108.7 8.8 %collective-permute-start.19 = (bf16[256,256]{1,0:T(8,128)(2,1)S(1)}, bf16[256,256]{1,0:T(8,128)(2,1)S(1)}, u32[]{:S(2)}, u32[]{:S(2)}) collective-permute-start(bf16[256,256]{1,0:T(8,128)(2,1)S(1)} %convert_element_type.36), channel_id=1, source_target_pairs={{0,3},{1,0},{2,1},{3,2},{4,7},{5,4},{6,5},{7,6},{8,11},{9,8},{10,9... | collective-permute-start | bytes 393224 | tf_op jit(solution)/shard_map/ppermute | solution.py:207
  115.1 33.0 %collective-permute-start.22 = (bf16[256,1024]{1,0:T(8,128)(2,1)S(1)}, bf16[256,1024]{1,0:T(8,128)(2,1)S(1)}, u32[]{:S(2)}, u32[]{:S(2)}) collective-permute-start(bf16[256,1024]{1,0:T(8,128)(2,1)S(1)} %convert_element_type.35), channel_id=1, source_target_pairs={{0,24},{4,28},{8,16},{12,20},{16,8},{20,12},{24,0},{28,4},{1,25},{... | collective-permute-start | bytes 1572872 | tf_op jit(solution)/shard_map/ppermute | solution.py:200
  117.9 16.2 %collective-permute-start.24 = (bf16[256,256]{1,0:T(8,128)(2,1)S(1)}, bf16[256,256]{1,0:T(8,128)(2,1)S(1)}, u32[]{:S(2)}, u32[]{:S(2)}) collective-permute-start(bf16[256,256]{1,0:T(8,128)(2,1)S(1)} %get-tuple-element.88), channel_id=1, source_target_pairs={{0,8},{4,12},{8,0},{12,4},{16,24},{20,28},{24,16},{28,20},{1,9},{5... | collective-permute-start | bytes 393224 | tf_op jit(solution)/shard_map/ppermute | solution.py:200
  132.5 15.5 %collective-permute-start.21 = (bf16[256,1280]{1,0:T(8,128)(2,1)S(1)}, bf16[256,1280]{1,0:T(8,128)(2,1)S(1)}, u32[]{:S(2)}, u32[]{:S(2)}) collective-permute-start(bf16[256,1280]{1,0:T(8,128)(2,1)S(1)} %collective-permute-done.20), channel_id=1, source_target_pairs={{2,3},{6,7},{25,24},{29,28}} | collective-permute-start | bytes 1966088 | tf_op jit(solution)/shard_map/ppermute | solution.py:282
  139.7 15.7 %collective-permute-start.27 = (bf16[1280,128]{0,1:T(8,128)(2,1)S(1)}, bf16[1280,128]{0,1:T(8,128)(2,1)S(1)}, u32[]{:S(2)}, u32[]{:S(2)}) collective-permute-start(bf16[1280,128]{0,1:T(8,128)(2,1)S(1)} %select_convert_fusion), channel_id=1, source_target_pairs={{0,4},{4,0},{8,12},{12,8},{16,20},{20,16},{24,28},{28,24},{1,5},{5... | collective-permute-start | bytes 983048 | tf_op jit(solution)/shard_map/ppermute | solution.py:200
  (17 other events, 139.6 us)
Sparse Core Ops, SparseCore 0:
  31.0 52.9 all-gather.1

commit v11 on v10

--- a/solution.py
+++ b/solution.py
@@ -242,9 +242,9 @@
         pairs.append(jnp.concatenate([own_key[:, columns], own_value[:, columns]], axis=1))
     pairs = jnp.stack(pairs)
     heads = [(mp + k) % n_mp * KV_HEADS // n_mp for k in range(n_mp)]
-    shares = around([lax.dynamic_index_in_dim(pairs, h, 0, False) for h in heads])
-    arrived, *shares = together(arrived, *shares)
-    shares = jnp.stack(shares)
+    pairs = [lax.dynamic_index_in_dim(pairs, h, 0, False) for h in heads]
+    arrived, pairs = lax.optimization_barrier((arrived, pairs))
+    shares = jnp.stack(around(pairs))
     rows = pick(arrived, slot_source).reshape(tokens, width)
 
     x = lax.all_gather(rows, "mp", axis=1, tiled=True)
@@ -253,7 +253,9 @@
     other_shares, *plane_rows = together(flip(shares, 1), *from_near(native))
     plane_rows = from_far(native, plane_rows)
     rest = [k for k in range(1, chips) if k not in near]
-    far_rows = jnp.concatenate([plane_rows[k] for k in rest])
+    by_plane = chips == n_mp
+    cut = tokens * 3 // 4 if by_plane else 0
+    far_rows = jnp.concatenate([plane_rows[k][:cut] for k in rest])
     plane_rows = jnp.concatenate(plane_rows)
 
     shares = jnp.stack([shares, other_shares], axis=1).reshape(n_dp * n_mp, share, 2 * dim)
@@ -263,11 +265,11 @@
     x, w_kv, plane_rows, far_rows = together(x, w_kv, plane_rows, far_rows)
 
     chip_width = n_mp * width // chips
-    by_plane = chips == n_mp
     chip_rows = {
-        k: lax.dynamic_slice_in_dim(x, (chip ^ k) * chip_width, chip_width, 1)
+        k: lax.dynamic_slice_in_dim(
+            x[cut:] if k in rest else x, (chip ^ k) * chip_width, chip_width, 1
+        )
         for k in range(chips)
-        if k in [0] + near or not by_plane
     }
     x, chip_rows = lax.optimization_barrier((x, chip_rows))
     near_rows = [flip(chip_rows[k], 2 * k) for k in near]
@@ -307,7 +309,10 @@
     d_all = [d_query] + other_chips([d_query] * chips)
     spread = jnp.stack(around([d_kv] * n_mp))
     d_near = [d_all[k] for k in near]
-    d_near, spread, last = lax.optimization_barrier((d_near, spread, hops[-1] if by_plane else x))
+    direct = [flip(chip_rows[k], 2 * k) for k in rest]
+    d_near, spread, direct, last = lax.optimization_barrier(
+        (d_near, spread, direct, hops[-1] if by_plane else x)
+    )
     for k, block in zip(near, d_near):
         d_all[k] = block
     for k, block in zip(near, near_rows):
@@ -318,9 +323,10 @@
             hops.append(along(hops[-1], [(hop - 1, hop), (1 - hop, -hop)]))
         for hop, block in enumerate(hops, 1):
             far_rows = jnp.where(jnp.abs(mp - chip) == hop, block, far_rows)
-        chip_rows.update(zip(rest, jnp.split(far_rows, len(rest))))
-    else:
-        chip_rows.update({k: flip(chip_rows[k], 2 * k) for k in rest})
+        direct = [
+            jnp.concatenate(parts) for parts in zip(jnp.split(far_rows, len(rest)), direct)
+        ]
+    chip_rows.update(zip(rest, direct))
     half = chip_width // 2
     early = [0] + near
     late = [k for k in range(chips) if k not in early]

time: 166 us -> 168 us (1.012)
  starting transfers between devices: 53.3 us -> 48.9 us
  waiting for transfers between devices: 57.1 us -> 60.9 us
    ppermute x18 -> x19, waiting for transfers between devices: 33.3 us -> 46.5 us  [flip(): return lax.ppermute(block, 'dp', [(i, i ^ bits) for i in range(n_dp)])]
    all_gather x1, waiting for transfers between devices: 5.54 us -> 0.01 us  [local(): x = lax.all_gather(rows, 'mp', axis=1, tiled=True)]
    ppermute x4, waiting for transfers between devices: 5.11 us -> 0.01 us  [along(): return lax.ppermute(block, ('dp', 'mp'), pairs)]
    ppermute x18 -> x19, starting transfers between devices: 34.6 us -> 31.5 us  [flip(): return lax.ppermute(block, 'dp', [(i, i ^ bits) for i in range(n_dp)])]
    ppermute x6, waiting for transfers between devices: 4.98 us -> 7.23 us  [around(): lax.ppermute(blocks[k], 'mp', [(i, (i + k) % n_mp) for i in range(n_mp)])]
    unnamed x30 -> x28, local copies, waits for them, and re-layouts: 3.88 us -> 4.01 us
  transfers between devices with their start and end apart: 30 -> 31, of which waited for: 13 -> 14; matrix products, arithmetic and copies ran while one was open for 14% -> 16% of each run, Pallas kernels for 6% -> 6%
where the time goes in v11:
time: 168 us; the launch traced here: 167 us
  waiting for transfers between devices  60.9 us (36%)
  starting transfers between devices  48.9 us (29%)
  local copies, waits for them, and re-layouts  16.6 us (10%)
  between operations  14.5 us (9%)
  Pallas kernels  10.2 us (6%)
  other arithmetic  8.43 us (5%)
  matrix products  7.75 us (5%)
    ppermute x19, waiting for transfers between devices, flip(): return lax.ppermute(block, 'dp', [(i, i ^ bits) for i in range(n_dp)])  46.5 us
    ppermute x19, starting transfers between devices, flip(): return lax.ppermute(block, 'dp', [(i, i ^ bits) for i in range(n_dp)])  31.5 us
    pallas_call x1, Pallas kernels, attend(): pl.pallas_call(functools.partial(attend_kernel, length, device_cols), gri...  10.2 us
    ppermute x6, starting transfers between devices, around(): lax.ppermute(blocks[k], 'mp', [(i, (i + k) % n_mp) for i in range(n_mp)])  9.33 us
    ppermute x6, waiting for transfers between devices, around(): lax.ppermute(blocks[k], 'mp', [(i, (i + k) % n_mp) for i in range(n_mp)])  7.23 us
    all_to_all x1, waiting for transfers between devices, local(): lax.all_to_all(outgoing, 'dp', split_axis=0, concat_axis=0, tiled=True)  7.12 us
    gather x3, local copies, waits for them, and re-layouts, pick(): return array.at[index].get(mode='promise_in_bounds')  5.3 us
    dot_general x4, matrix products, product(): return jnp.einsum('td,tc->dc', mine, theirs, preferred_element_type=F32)  5.12 us
  transfers between devices with their start and end apart: 31, of which 14 were waited for; matrix products, arithmetic and copies ran while one was open for 16% of the time, Pallas kernels for 6%

profile of v11, /device:TPU:7, one launch (start us, length us, event | category | flops | bytes accessed | tf_op | source)
XLA Modules:
  0.0 167.3 jit_solution(3029334052138315880)
XLA Ops:
  9.7 4.5 %all-to-all-start = ((bf16[8,32,1280]{2,1,0:T(8,128)(2,1)}), bf16[8,32,1280]{2,1,0:T(8,128)(2,1)S(1)}, u32[]{:S(2)}, u32[]{:S(2)}) async-start(bf16[8,32,1280]{2,1,0:T(8,128)(2,1)} %gather_fusion), calls=%async_computation | async-start | bytes 1310720 | tf_op jit(solution)/shard_map/all_to_all | solution.py:234
  15.6 7.1 %all-to-all-done = bf16[8,32,1280]{2,1,0:T(8,128)(2,1)S(1)} async-done(((bf16[8,32,1280]{2,1,0:T(8,128)(2,1)}), bf16[8,32,1280]{2,1,0:T(8,128)(2,1)S(1)}, u32[]{:S(2)}, u32[]{:S(2)}) %all-to-all-start) | async-done | bytes 655392 | tf_op jit(solution)/shard_map/all_to_all | solution.py:234
  25.5 2.3 %collective-permute-start.1 = (bf16[160,256]{1,0:T(8,128)(2,1)S(1)}, bf16[160,256]{1,0:T(8,128)(2,1)S(1)}, u32[]{:S(2)}, u32[]{:S(2)}) collective-permute-start(bf16[160,256]{1,0:T(8,128)(2,1)S(1)} %get-tuple-element.46), channel_id=1, source_target_pairs={{0,2},{1,3},{2,0},{3,1},{4,6},{5,7},{6,4},{7,5},{8,10},{9,11},{10,... | collective-permute-start | bytes 245768 | tf_op jit(solution)/shard_map/ppermute | solution.py:207
  29.5 4.5 %collective-permute-done.1 = bf16[160,256]{1,0:T(8,128)(2,1)S(1)} collective-permute-done((bf16[160,256]{1,0:T(8,128)(2,1)S(1)}, bf16[160,256]{1,0:T(8,128)(2,1)S(1)}, u32[]{:S(2)}, u32[]{:S(2)}) %collective-permute-start.1) | collective-permute-done | bytes 81952 | tf_op jit(solution)/shard_map/ppermute | solution.py:207
  36.7 5.8 %collective-permute-done.3 = bf16[4,160,256]{2,1,0:T(8,128)(2,1)S(1)} collective-permute-done((bf16[4,160,256]{2,1,0:T(8,128)(2,1)S(1)}, bf16[4,160,256]{2,1,0:T(8,128)(2,1)S(1)}, u32[]{:S(2)}, u32[]{:S(2)}) %collective-permute-start.3) | collective-permute-done | bytes 327712 | tf_op jit(solution)/shard_map/ppermute | solution.py:200
  42.5 8.3 %collective-permute-done.5 = bf16[4,160,256]{2,1,0:T(8,128)(2,1)S(1)} collective-permute-done((bf16[4,160,256]{2,1,0:T(8,128)(2,1)S(1)}, bf16[4,160,256]{2,1,0:T(8,128)(2,1)S(1)}, u32[]{:S(2)}, u32[]{:S(2)}) %collective-permute-start.5) | collective-permute-done | bytes 327712 | tf_op jit(solution)/shard_map/ppermute | solution.py:200
  50.9 1.7 %collective-permute-start.6 = (bf16[4,4,160,256]{3,2,1,0:T(8,128)(2,1)S(1)}, bf16[4,4,160,256]{3,2,1,0:T(8,128)(2,1)S(1)}, u32[]{:S(2)}, u32[]{:S(2)}) collective-permute-start(bf16[4,4,160,256]{3,2,1,0:T(8,128)(2,1)S(1)} %pad_maximum_fusion.1), channel_id=1, source_target_pairs={{0,4},{4,0},{8,12},{12,8},{16,20},{20,16},{24,28},{28,24},{1,5},{5... | collective-permute-start | bytes 3932168 | tf_op jit(solution)/shard_map/ppermute | solution.py:200
  57.7 11.3 %collective-permute-done.7 = bf16[256,1280]{1,0:T(8,128)(2,1)S(1)} collective-permute-done((bf16[256,1280]{1,0:T(8,128)(2,1)S(1)}, bf16[256,1280]{1,0:T(8,128)(2,1)S(1)}, u32[]{:S(2)}, u32[]{:S(2)}) %collective-permute-start.7) | collective-permute-done | bytes 655392 | tf_op jit(solution)/shard_map/ppermute | solution.py:200
  74.0 1.7 %pad_maximum_fusion = bf16[4,2,4,160,256]{4,3,2,1,0:T(8,128)(2,1)} fusion(bf16[4,1,4,160,256]{4,3,2,1,0:T(8,128)(2,1)S(1)} %bitcast.72, bf16[4,1,4,160,256]{4,3,2,1,0:T(8,128)(2,1)S(1)} %bitcast.70), kind=kLoop, calls=%fused_computation.3 | loop fusion | flops 1310720 | bytes 5242880 | tf_op jit(solution)/shard_map/stack | solution.py:261
  75.7 2.5 %gather_fusion.2 = bf16[32,160,256]{2,1,0:T(8,128)(2,1)S(1)} fusion(bf16[32,160,256]{2,1,0:T(8,128)(2,1)} %bitcast.65, s32[1024]{0:T(1024)S(1)} %get-tuple-element.99), kind=kCustom, calls=%fused_computation.2 | custom fusion | bytes 5243008 | tf_op jit(solution)/shard_map/gather | solution.py:169
  84.1 1.8 %constant_dynamic-slice_fusion.4 = (bf16[256,1280]{1,0:T(8,128)(2,1)S(1)}, bf16[256,1280]{1,0:T(8,128)(2,1)S(1)}, bf16[256,1280]{1,0:T(8,128)(2,1)S(1)}) fusion(bf16[256,5120]{1,0:T(8,128)(2,1)} %all-gather.2.cloned.1.call-done.x_ref, s32[]{:T(128)S(6)} %select_n.186, s32[]{:T(128)S(6)} %select_n.185, s32[]{:T(128)S(6)} %select_n.184), kind=kLoop, calls=%fused_computation.57 | loop fusion | bytes 3932172 | tf_op jit(solution)/shard_map/dynamic_slice | solution.py:269
  86.5 3.8 %collective-permute-start.12 = (bf16[256,1280]{1,0:T(8,128)(2,1)S(1)}, bf16[256,1280]{1,0:T(8,128)(2,1)S(1)}, u32[]{:S(2)}, u32[]{:S(2)}) collective-permute-start(bf16[256,1280]{1,0:T(8,128)(2,1)S(1)} %get-tuple-element.60), channel_id=1, source_target_pairs={{0,16},{4,20},{8,24},{12,28},{16,0},{20,4},{24,8},{28,12},{1,17},{... | collective-permute-start | bytes 1966088 | tf_op jit(solution)/shard_map/ppermute | solution.py:200
  90.3 10.2 %shard_map.138 = (f32[256,1024]{1,0:T(8,128)S(1)}, f32[256,1024]{1,0:T(8,128)S(1)}, f32[256,256]{1,0:T(8,128)S(1)}) custom-call(bf16[256,5120]{1,0:T(8,128)(2,1)S(1)} %copy-done.2, bf16[5120,1024]{1,0:T(8,128)(2,1)} %wq_ref.1, bf16[5120,256]{1,0:T(8,128)(2,1)S(1)} %bitcast.62, f32[256,1024]{1,0:T(8,128)S(1)} %copy-done.3, f32[1,128]{1,0:T(1,128)S(1)} %bitcast.63, ...), custom_call_target="tpu_custom_call" | custom-call | flops 16777216000 | bytes 41943040 | tf_op jit(solution)/shard_map/pallas_call | solution.py:137
  102.8 1.8 %collective-permute-start.18 = (bf16[256,256]{1,0:T(8,128)(2,1)S(1)}, bf16[256,256]{1,0:T(8,128)(2,1)S(1)}, u32[]{:S(2)}, u32[]{:S(2)}) collective-permute-start(bf16[256,256]{1,0:T(8,128)(2,1)S(1)} %convert_element_type.36), channel_id=1, source_target_pairs={{0,2},{1,3},{2,0},{3,1},{4,6},{5,7},{6,4},{7,5},{8,10},{9,11},{10,... | collective-permute-start | bytes 393224 | tf_op jit(solution)/shard_map/ppermute | solution.py:207
  104.6 2.4 %collective-permute-start.19 = (bf16[256,256]{1,0:T(8,128)(2,1)S(1)}, bf16[256,256]{1,0:T(8,128)(2,1)S(1)}, u32[]{:S(2)}, u32[]{:S(2)}) collective-permute-start(bf16[256,256]{1,0:T(8,128)(2,1)S(1)} %convert_element_type.36), channel_id=1, source_target_pairs={{0,3},{1,0},{2,1},{3,2},{4,7},{5,4},{6,5},{7,6},{8,11},{9,8},{10,9... | collective-permute-start | bytes 393224 | tf_op jit(solution)/shard_map/ppermute | solution.py:207
  108.9 1.8 %collective-permute-done.18 = bf16[256,256]{1,0:T(8,128)(2,1)S(1)} collective-permute-done((bf16[256,256]{1,0:T(8,128)(2,1)S(1)}, bf16[256,256]{1,0:T(8,128)(2,1)S(1)}, u32[]{:S(2)}, u32[]{:S(2)}) %collective-permute-start.18) | collective-permute-done | bytes 131104 | tf_op jit(solution)/shard_map/ppermute | solution.py:207
  113.3 6.2 %collective-permute-done.20 = bf16[64,1280]{1,0:T(8,128)(2,1)S(1)} collective-permute-done((bf16[64,1280]{1,0:T(8,128)(2,1)S(1)}, bf16[64,1280]{1,0:T(8,128)(2,1)S(1)}, u32[]{:S(2)}, u32[]{:S(2)}) %collective-permute-start.20) | collective-permute-done | bytes 163872 | tf_op jit(solution)/shard_map/ppermute | solution.py:200
  119.5 3.4 %collective-permute-start.25 = (bf16[256,256]{1,0:T(8,128)(2,1)S(1)}, bf16[256,256]{1,0:T(8,128)(2,1)S(1)}, u32[]{:S(2)}, u32[]{:S(2)}) collective-permute-start(bf16[256,256]{1,0:T(8,128)(2,1)S(1)} %get-tuple-element.92), channel_id=1, source_target_pairs={{0,8},{4,12},{8,0},{12,4},{16,24},{20,28},{24,16},{28,20},{1,9},{5... | collective-permute-start | bytes 393224 | tf_op jit(solution)/shard_map/ppermute | solution.py:200
  125.7 7.8 %collective-permute-done.25 = bf16[256,256]{1,0:T(8,128)(2,1)S(1)} collective-permute-done((bf16[256,256]{1,0:T(8,128)(2,1)S(1)}, bf16[256,256]{1,0:T(8,128)(2,1)S(1)}, u32[]{:S(2)}, u32[]{:S(2)}) %collective-permute-start.25) | collective-permute-done | bytes 131104 | tf_op jit(solution)/shard_map/ppermute | solution.py:200
  133.5 5.0 %collective-permute-done.26 = bf16[256,256]{1,0:T(8,128)(2,1)S(1)} collective-permute-done((bf16[256,256]{1,0:T(8,128)(2,1)S(1)}, bf16[256,256]{1,0:T(8,128)(2,1)S(1)}, u32[]{:S(2)}, u32[]{:S(2)}) %collective-permute-start.26) | collective-permute-done | bytes 131104 | tf_op jit(solution)/shard_map/ppermute | solution.py:200
  138.6 2.6 %fusion.18 = f32[1280,256]{0,1:T(8,128)S(1)} fusion(bf16[1024,1280]{1,0:T(8,128)(2,1)} %constant_dynamic-update-slice_fusion, bf16[1024,256]{1,0:T(8,128)(2,1)S(1)} %bitcast.71), kind=kOutput, calls=%fused_computation.79 | convolution fusion | flops 671088640 | bytes 4456448 | tf_op jit(solution)/shard_map/td,tc->dc/dot_general | solution.py:356
  141.3 8.3 %collective-permute-start.28 = (bf16[1280,128]{0,1:T(8,128)(2,1)S(1)}, bf16[1280,128]{0,1:T(8,128)(2,1)S(1)}, u32[]{:S(2)}, u32[]{:S(2)}) collective-permute-start(bf16[1280,128]{0,1:T(8,128)(2,1)S(1)} %select_convert_fusion), channel_id=1, source_target_pairs={{0,4},{4,0},{8,12},{12,8},{16,20},{20,16},{24,28},{28,24},{1,5},{5... | collective-permute-start | bytes 983048 | tf_op jit(solution)/shard_map/ppermute | solution.py:200
  152.6 3.1 %collective-permute-start.24 = (bf16[640,1024]{1,0:T(8,128)(2,1)S(1)}, bf16[640,1024]{1,0:T(8,128)(2,1)S(1)}, u32[]{:S(2)}, u32[]{:S(2)}) collective-permute-start(bf16[640,1024]{1,0:T(8,128)(2,1)S(1)} %add_convert_fusion), channel_id=1, source_target_pairs={{0,4},{4,0},{8,12},{12,8},{16,20},{20,16},{24,28},{28,24},{1,5},{5... | collective-permute-start | bytes 3932168 | tf_op jit(solution)/shard_map/ppermute | solution.py:200
  158.4 2.1 %add_add_fusion = f32[640,1024]{1,0:T(8,128)} fusion(f32[640,1024]{1,0:T(8,128)S(1)} %fusion.1, bf16[640,1024]{1,0:T(8,128)(2,1)S(1)} %collective-permute-done.24, bf16[256,1024]{1,0:T(8,128)(2,1)S(1)} %collective-permute-done.23, s32[]{:T(128)S(6)} %select_n.197, bf16[192,1280]{1,0:T(8,128)(2,1)S(1)} %select_select_fusion, ...), kind=kOutput, calls=%fused_computation.4 | convolution fusion | flops 338165760 | bytes 7733252 | tf_op jit(solution)/shard_map/td,tc->dc/dot_general | solution.py:338
  (118 shorter events, 43.0 us)
Async XLA Ops:
  9.7 13.0 %all-to-all-start = ((bf16[8,32,1280]{2,1,0:T(8,128)(2,1)}), bf16[8,32,1280]{2,1,0:T(8,128)(2,1)S(1)}, u32[]{:S(2)}, u32[]{:S(2)}) async-start(bf16[8,32,1280]{2,1,0:T(8,128)(2,1)} %gather_fusion), calls=%async_computation | async-start | bytes 1310720 | tf_op jit(solution)/shard_map/all_to_all | solution.py:234
  14.2 67.3 %all-gather.2.cloned.1.call-start = ((), (), s32[]{:S(2)}) async-start(), calls=%async_computation.1 | async-start | bytes 3276800 | tf_op jit(solution)/shard_map/all_gather | solution.py:250
  25.5 8.4 %collective-permute-start.1 = (bf16[160,256]{1,0:T(8,128)(2,1)S(1)}, bf16[160,256]{1,0:T(8,128)(2,1)S(1)}, u32[]{:S(2)}, u32[]{:S(2)}) collective-permute-start(bf16[160,256]{1,0:T(8,128)(2,1)S(1)} %get-tuple-element.46), channel_id=1, source_target_pairs={{0,2},{1,3},{2,0},{3,1},{4,6},{5,7},{6,4},{7,5},{8,10},{9,11},{10,... | collective-permute-start | bytes 245768 | tf_op jit(solution)/shard_map/ppermute | solution.py:207
  34.0 8.5 %collective-permute-start.3 = (bf16[4,160,256]{2,1,0:T(8,128)(2,1)S(1)}, bf16[4,160,256]{2,1,0:T(8,128)(2,1)S(1)}, u32[]{:S(2)}, u32[]{:S(2)}) collective-permute-start(bf16[4,160,256]{2,1,0:T(8,128)(2,1)S(1)} %get-tuple-element.94), channel_id=1, source_target_pairs={{0,8},{4,12},{8,0},{12,4},{16,24},{20,28},{24,16},{28,20},{1,9},{5... | collective-permute-start | bytes 983048 | tf_op jit(solution)/shard_map/ppermute | solution.py:200
  34.1 8.4 %collective-permute-start.4 = (bf16[4,160,256]{2,1,0:T(8,128)(2,1)S(1)}, bf16[4,160,256]{2,1,0:T(8,128)(2,1)S(1)}, u32[]{:S(2)}, u32[]{:S(2)}) collective-permute-start(bf16[4,160,256]{2,1,0:T(8,128)(2,1)S(1)} %get-tuple-element.94), channel_id=1, source_target_pairs={{0,16},{4,20},{8,24},{12,28},{16,0},{20,4},{24,8},{28,12},{1,17},{... | collective-permute-start | bytes 983048 | tf_op jit(solution)/shard_map/ppermute | solution.py:200
  35.6 15.2 %collective-permute-start.5 = (bf16[4,160,256]{2,1,0:T(8,128)(2,1)S(1)}, bf16[4,160,256]{2,1,0:T(8,128)(2,1)S(1)}, u32[]{:S(2)}, u32[]{:S(2)}) collective-permute-start(bf16[4,160,256]{2,1,0:T(8,128)(2,1)S(1)} %get-tuple-element.94), channel_id=1, source_target_pairs={{0,24},{4,28},{8,16},{12,20},{16,8},{20,12},{24,0},{28,4},{1,25},{... | collective-permute-start | bytes 983048 | tf_op jit(solution)/shard_map/ppermute | solution.py:200
  50.9 18.0 %collective-permute-start.6 = (bf16[4,4,160,256]{3,2,1,0:T(8,128)(2,1)S(1)}, bf16[4,4,160,256]{3,2,1,0:T(8,128)(2,1)S(1)}, u32[]{:S(2)}, u32[]{:S(2)}) collective-permute-start(bf16[4,4,160,256]{3,2,1,0:T(8,128)(2,1)S(1)} %pad_maximum_fusion.1), channel_id=1, source_target_pairs={{0,4},{4,0},{8,12},{12,8},{16,20},{20,16},{24,28},{28,24},{1,5},{5... | collective-permute-start | bytes 3932168 | tf_op jit(solution)/shard_map/ppermute | solution.py:200
  52.6 16.3 %collective-permute-start.7 = (bf16[256,1280]{1,0:T(8,128)(2,1)S(1)}, bf16[256,1280]{1,0:T(8,128)(2,1)S(1)}, u32[]{:S(2)}, u32[]{:S(2)}) collective-permute-start(bf16[256,1280]{1,0:T(8,128)(2,1)S(1)} %bitcast.67), channel_id=1, source_target_pairs={{0,8},{4,12},{8,0},{12,4},{16,24},{20,28},{24,16},{28,20},{1,9},{5... | collective-permute-start | bytes 1966088 | tf_op jit(solution)/shard_map/ppermute | solution.py:200
  53.0 16.0 %collective-permute-start.8 = (bf16[256,1280]{1,0:T(8,128)(2,1)S(1)}, bf16[256,1280]{1,0:T(8,128)(2,1)S(1)}, u32[]{:S(2)}, u32[]{:S(2)}) collective-permute-start(bf16[256,1280]{1,0:T(8,128)(2,1)S(1)} %bitcast.68), channel_id=1, source_target_pairs={{0,16},{4,20},{8,24},{12,28},{16,0},{20,4},{24,8},{28,12},{1,17},{... | collective-permute-start | bytes 1966088 | tf_op jit(solution)/shard_map/ppermute | solution.py:200
  69.7 8.5 %collective-permute-start.9 = (bf16[128,1280]{1,0:T(8,128)(2,1)}, bf16[128,1280]{1,0:T(8,128)(2,1)S(1)}, u32[]{:S(2)}, u32[]{:S(2)}) collective-permute-start(bf16[128,1280]{1,0:T(8,128)(2,1)} %slice.56), channel_id=1, source_target_pairs={{0,16},{4,20},{8,24},{12,28},{16,0},{20,4},{24,8},{28,12},{1,17},{... | collective-permute-start | bytes 983048 | tf_op jit(solution)/shard_map/ppermute | solution.py:200
  81.5 20.1 %collective-permute-start.13 = (bf16[192,1280]{1,0:T(8,128)(2,1)}, bf16[192,1280]{1,0:T(8,128)(2,1)S(1)}, u32[]{:S(2)}, u32[]{:S(2)}) collective-permute-start(bf16[192,1280]{1,0:T(8,128)(2,1)} %pad_maximum_fusion.4), channel_id=1, source_target_pairs={{0,1},{4,5},{9,10},{13,14},{18,19},{22,23}} | collective-permute-start | bytes 1474568 | tf_op jit(solution)/shard_map/ppermute | solution.py:284
  82.2 19.4 %collective-permute-start.14 = (bf16[192,1280]{1,0:T(8,128)(2,1)}, bf16[192,1280]{1,0:T(8,128)(2,1)S(1)}, u32[]{:S(2)}, u32[]{:S(2)}) collective-permute-start(bf16[192,1280]{1,0:T(8,128)(2,1)} %pad_maximum_fusion.4), channel_id=1, source_target_pairs={{9,8},{13,12},{18,17},{22,21},{27,26},{31,30}} | collective-permute-start | bytes 1474568 | tf_op jit(solution)/shard_map/ppermute | solution.py:284
  85.9 15.7 %collective-permute-start.11 = (bf16[256,1280]{1,0:T(8,128)(2,1)S(1)}, bf16[256,1280]{1,0:T(8,128)(2,1)S(1)}, u32[]{:S(2)}, u32[]{:S(2)}) collective-permute-start(bf16[256,1280]{1,0:T(8,128)(2,1)S(1)} %get-tuple-element.59), channel_id=1, source_target_pairs={{0,8},{4,12},{8,0},{12,4},{16,24},{20,28},{24,16},{28,20},{1,9},{5... | collective-permute-start | bytes 1966088 | tf_op jit(solution)/shard_map/ppermute | solution.py:200
  86.5 15.9 %collective-permute-start.12 = (bf16[256,1280]{1,0:T(8,128)(2,1)S(1)}, bf16[256,1280]{1,0:T(8,128)(2,1)S(1)}, u32[]{:S(2)}, u32[]{:S(2)}) collective-permute-start(bf16[256,1280]{1,0:T(8,128)(2,1)S(1)} %get-tuple-element.60), channel_id=1, source_target_pairs={{0,16},{4,20},{8,24},{12,28},{16,0},{20,4},{24,8},{28,12},{1,17},{... | collective-permute-start | bytes 1966088 | tf_op jit(solution)/shard_map/ppermute | solution.py:200
  107.0 12.4 %collective-permute-start.15 = (bf16[256,1024]{1,0:T(8,128)(2,1)S(1)}, bf16[256,1024]{1,0:T(8,128)(2,1)S(1)}, u32[]{:S(2)}, u32[]{:S(2)}) collective-permute-start(bf16[256,1024]{1,0:T(8,128)(2,1)S(1)} %convert_element_type.35), channel_id=1, source_target_pairs={{0,8},{4,12},{8,0},{12,4},{16,24},{20,28},{24,16},{28,20},{1,9},{5... | collective-permute-start | bytes 1572872 | tf_op jit(solution)/shard_map/ppermute | solution.py:200
  107.3 12.1 %collective-permute-start.16 = (bf16[256,1024]{1,0:T(8,128)(2,1)S(1)}, bf16[256,1024]{1,0:T(8,128)(2,1)S(1)}, u32[]{:S(2)}, u32[]{:S(2)}) collective-permute-start(bf16[256,1024]{1,0:T(8,128)(2,1)S(1)} %convert_element_type.35), channel_id=1, source_target_pairs={{0,16},{4,20},{8,24},{12,28},{16,0},{20,4},{24,8},{28,12},{1,17},{... | collective-permute-start | bytes 1572872 | tf_op jit(solution)/shard_map/ppermute | solution.py:200
  108.2 11.2 %collective-permute-start.21 = (bf16[192,1280]{1,0:T(8,128)(2,1)S(1)}, bf16[192,1280]{1,0:T(8,128)(2,1)S(1)}, u32[]{:S(2)}, u32[]{:S(2)}) collective-permute-start(bf16[192,1280]{1,0:T(8,128)(2,1)S(1)} %broadcast_select_fusion), channel_id=1, source_target_pairs={{1,2},{5,6},{10,11},{14,15},{17,16},{21,20},{26,25},{30,29}} | collective-permute-start | bytes 1474568 | tf_op jit(solution)/shard_map/ppermute | solution.py:284
  110.7 8.7 %collective-permute-start.20 = (bf16[64,1280]{1,0:T(8,128)(2,1)S(1)}, bf16[64,1280]{1,0:T(8,128)(2,1)S(1)}, u32[]{:S(2)}, u32[]{:S(2)}) collective-permute-start(bf16[64,1280]{1,0:T(8,128)(2,1)S(1)} %constant_dynamic-slice_fusion.3), channel_id=1, source_target_pairs={{0,24},{4,28},{8,16},{12,20},{16,8},{20,12},{24,0},{28,4},{1,25},{... | collective-permute-start | bytes 491528 | tf_op jit(solution)/shard_map/ppermute | solution.py:200
  111.8 38.9 %collective-permute-start.23 = (bf16[256,1024]{1,0:T(8,128)(2,1)S(1)}, bf16[256,1024]{1,0:T(8,128)(2,1)S(1)}, u32[]{:S(2)}, u32[]{:S(2)}) collective-permute-start(bf16[256,1024]{1,0:T(8,128)(2,1)S(1)} %convert_element_type.35), channel_id=1, source_target_pairs={{0,24},{4,28},{8,16},{12,20},{16,8},{20,12},{24,0},{28,4},{1,25},{... | collective-permute-start | bytes 1572872 | tf_op jit(solution)/shard_map/ppermute | solution.py:200
  119.5 14.0 %collective-permute-start.25 = (bf16[256,256]{1,0:T(8,128)(2,1)S(1)}, bf16[256,256]{1,0:T(8,128)(2,1)S(1)}, u32[]{:S(2)}, u32[]{:S(2)}) collective-permute-start(bf16[256,256]{1,0:T(8,128)(2,1)S(1)} %get-tuple-element.92), channel_id=1, source_target_pairs={{0,8},{4,12},{8,0},{12,4},{16,24},{20,28},{24,16},{28,20},{1,9},{5... | collective-permute-start | bytes 393224 | tf_op jit(solution)/shard_map/ppermute | solution.py:200
  122.9 15.7 %collective-permute-start.26 = (bf16[256,256]{1,0:T(8,128)(2,1)S(1)}, bf16[256,256]{1,0:T(8,128)(2,1)S(1)}, u32[]{:S(2)}, u32[]{:S(2)}) collective-permute-start(bf16[256,256]{1,0:T(8,128)(2,1)S(1)} %get-tuple-element.91), channel_id=1, source_target_pairs={{0,16},{4,20},{8,24},{12,28},{16,0},{20,4},{24,8},{28,12},{1,17},{... | collective-permute-start | bytes 393224 | tf_op jit(solution)/shard_map/ppermute | solution.py:200
  122.9 15.7 %collective-permute-start.27 = (bf16[256,256]{1,0:T(8,128)(2,1)S(1)}, bf16[256,256]{1,0:T(8,128)(2,1)S(1)}, u32[]{:S(2)}, u32[]{:S(2)}) collective-permute-start(bf16[256,256]{1,0:T(8,128)(2,1)S(1)} %get-tuple-element.90), channel_id=1, source_target_pairs={{0,24},{4,28},{8,16},{12,20},{16,8},{20,12},{24,0},{28,4},{1,25},{... | collective-permute-start | bytes 393224 | tf_op jit(solution)/shard_map/ppermute | solution.py:200
  124.1 25.5 %collective-permute-start.22 = (bf16[192,1280]{1,0:T(8,128)(2,1)S(1)}, bf16[192,1280]{1,0:T(8,128)(2,1)S(1)}, u32[]{:S(2)}, u32[]{:S(2)}) collective-permute-start(bf16[192,1280]{1,0:T(8,128)(2,1)S(1)} %collective-permute-done.21), channel_id=1, source_target_pairs={{2,3},{6,7},{25,24},{29,28}} | collective-permute-start | bytes 1474568 | tf_op jit(solution)/shard_map/ppermute | solution.py:284
  141.3 15.6 %collective-permute-start.28 = (bf16[1280,128]{0,1:T(8,128)(2,1)S(1)}, bf16[1280,128]{0,1:T(8,128)(2,1)S(1)}, u32[]{:S(2)}, u32[]{:S(2)}) collective-permute-start(bf16[1280,128]{0,1:T(8,128)(2,1)S(1)} %select_convert_fusion), channel_id=1, source_target_pairs={{0,4},{4,0},{8,12},{12,8},{16,20},{20,16},{24,28},{28,24},{1,5},{5... | collective-permute-start | bytes 983048 | tf_op jit(solution)/shard_map/ppermute | solution.py:200
  (17 other events, 168.0 us)
Sparse Core Ops, SparseCore 0:
  24.3 55.9 all-gather.1

commit v12 on v10

--- a/solution.py
+++ b/solution.py
@@ -243,9 +243,9 @@
     pairs = jnp.stack(pairs)
     heads = [(mp + k) % n_mp * KV_HEADS // n_mp for k in range(n_mp)]
     shares = around([lax.dynamic_index_in_dim(pairs, h, 0, False) for h in heads])
-    arrived, *shares = together(arrived, *shares)
+    rows = pick(arrived, slot_source).reshape(tokens, width)
+    rows, *shares = together(rows, *shares)
     shares = jnp.stack(shares)
-    rows = pick(arrived, slot_source).reshape(tokens, width)
 
     x = lax.all_gather(rows, "mp", axis=1, tiled=True)
     shares = jnp.stack([shares] + other_chips([shares] * chips))

time: 166 us -> 164 us (0.988)
  waiting for transfers between devices: 57.1 us -> 55.2 us
    all_to_all x1, waiting for transfers between devices: 8.26 us -> 1.83 us  [local(): lax.all_to_all(outgoing, 'dp', split_axis=0, concat_axis=0, tiled=True)]
    all_gather x1, waiting for transfers between devices: 5.54 us -> 9.18 us  [local(): x = lax.all_gather(rows, 'mp', axis=1, tiled=True)]
    ppermute x6, waiting for transfers between devices: 4.98 us -> 6.76 us  [around(): lax.ppermute(blocks[k], 'mp', [(i, (i + k) % n_mp) for i in range(n_mp)])]
  transfers between devices with their start and end apart: 30 -> 30, of which waited for: 13 -> 15; matrix products, arithmetic and copies ran while one was open for 14% -> 16% of each run, Pallas kernels for 6% -> 6%
where the time goes in v12:
time: 164 us; the launch traced here: 163 us
  waiting for transfers between devices  55.2 us (34%)
  starting transfers between devices  52.4 us (32%)
  local copies, waits for them, and re-layouts  15.9 us (10%)
  between operations  14.4 us (9%)
  Pallas kernels  10.2 us (6%)
  matrix products  7.81 us (5%)
  other arithmetic  7.45 us (5%)
    ppermute x18, starting transfers between devices, flip(): return lax.ppermute(block, 'dp', [(i, i ^ bits) for i in range(n_dp)])  34.4 us
    ppermute x18, waiting for transfers between devices, flip(): return lax.ppermute(block, 'dp', [(i, i ^ bits) for i in range(n_dp)])  32.3 us
    pallas_call x1, Pallas kernels, attend(): pl.pallas_call(functools.partial(attend_kernel, length, device_cols), gri...  10.2 us
    ppermute x6, starting transfers between devices, around(): lax.ppermute(blocks[k], 'mp', [(i, (i + k) % n_mp) for i in range(n_mp)])  9.54 us
    all_gather x1, waiting for transfers between devices, local(): x = lax.all_gather(rows, 'mp', axis=1, tiled=True)  9.18 us
    ppermute x6, waiting for transfers between devices, around(): lax.ppermute(blocks[k], 'mp', [(i, (i + k) % n_mp) for i in range(n_mp)])  6.76 us
    gather x3, local copies, waits for them, and re-layouts, pick(): return array.at[index].get(mode='promise_in_bounds')  5.32 us
    dot_general x4, matrix products, product(): return jnp.einsum('td,tc->dc', mine, theirs, preferred_element_type=F32)  5.11 us
  transfers between devices with their start and end apart: 30, of which 15 were waited for; matrix products, arithmetic and copies ran while one was open for 16% of the time, Pallas kernels for 6%

profile of v12, /device:TPU:7, one launch (start us, length us, event | category | flops | bytes accessed | tf_op | source)
XLA Modules:
  0.0 163.5 jit_solution(8438282532851640934)
XLA Ops:
  9.7 4.6 %all-to-all-start = ((bf16[8,32,1280]{2,1,0:T(8,128)(2,1)}), bf16[8,32,1280]{2,1,0:T(8,128)(2,1)S(1)}, u32[]{:S(2)}, u32[]{:S(2)}) async-start(bf16[8,32,1280]{2,1,0:T(8,128)(2,1)} %gather_fusion), calls=%async_computation | async-start | bytes 1310720 | tf_op jit(solution)/shard_map/all_to_all | solution.py:234
  17.6 2.3 %collective-permute-start.1 = (bf16[160,256]{1,0:T(8,128)(2,1)S(1)}, bf16[160,256]{1,0:T(8,128)(2,1)S(1)}, u32[]{:S(2)}, u32[]{:S(2)}) collective-permute-start(bf16[160,256]{1,0:T(8,128)(2,1)S(1)} %get-tuple-element.92), channel_id=1, source_target_pairs={{0,2},{1,3},{2,0},{3,1},{4,6},{5,7},{6,4},{7,5},{8,10},{9,11},{10,... | collective-permute-start | bytes 245768 | tf_op jit(solution)/shard_map/ppermute | solution.py:207
  21.0 1.8 %all-to-all-done = bf16[8,32,1280]{2,1,0:T(8,128)(2,1)S(1)} async-done(((bf16[8,32,1280]{2,1,0:T(8,128)(2,1)}), bf16[8,32,1280]{2,1,0:T(8,128)(2,1)S(1)}, u32[]{:S(2)}, u32[]{:S(2)}) %all-to-all-start) | async-done | bytes 655392 | tf_op jit(solution)/shard_map/all_to_all | solution.py:234
  24.3 1.8 %collective-permute-done.1 = bf16[160,256]{1,0:T(8,128)(2,1)S(1)} collective-permute-done((bf16[160,256]{1,0:T(8,128)(2,1)S(1)}, bf16[160,256]{1,0:T(8,128)(2,1)S(1)}, u32[]{:S(2)}, u32[]{:S(2)}) %collective-permute-start.1) | collective-permute-done | bytes 81952 | tf_op jit(solution)/shard_map/ppermute | solution.py:207
  26.7 2.2 %collective-permute-start.5 = (bf16[4,160,256]{2,1,0:T(8,128)(2,1)S(1)}, bf16[4,160,256]{2,1,0:T(8,128)(2,1)S(1)}, u32[]{:S(2)}, u32[]{:S(2)}) collective-permute-start(bf16[4,160,256]{2,1,0:T(8,128)(2,1)S(1)} %get-tuple-element.90), channel_id=1, source_target_pairs={{0,24},{4,28},{8,16},{12,20},{16,8},{20,12},{24,0},{28,4},{1,25},{... | collective-permute-start | bytes 983048 | tf_op jit(solution)/shard_map/ppermute | solution.py:200
  28.9 5.8 %collective-permute-done.3 = bf16[4,160,256]{2,1,0:T(8,128)(2,1)S(1)} collective-permute-done((bf16[4,160,256]{2,1,0:T(8,128)(2,1)S(1)}, bf16[4,160,256]{2,1,0:T(8,128)(2,1)S(1)}, u32[]{:S(2)}, u32[]{:S(2)}) %collective-permute-start.3) | collective-permute-done | bytes 327712 | tf_op jit(solution)/shard_map/ppermute | solution.py:200
  34.7 7.2 %collective-permute-done.5 = bf16[4,160,256]{2,1,0:T(8,128)(2,1)S(1)} collective-permute-done((bf16[4,160,256]{2,1,0:T(8,128)(2,1)S(1)}, bf16[4,160,256]{2,1,0:T(8,128)(2,1)S(1)}, u32[]{:S(2)}, u32[]{:S(2)}) %collective-permute-start.5) | collective-permute-done | bytes 327712 | tf_op jit(solution)/shard_map/ppermute | solution.py:200
  42.0 1.9 %collective-permute-start.6 = (bf16[4,4,160,256]{3,2,1,0:T(8,128)(2,1)S(1)}, bf16[4,4,160,256]{3,2,1,0:T(8,128)(2,1)S(1)}, u32[]{:S(2)}, u32[]{:S(2)}) collective-permute-start(bf16[4,4,160,256]{3,2,1,0:T(8,128)(2,1)S(1)} %pad_maximum_fusion.1), channel_id=1, source_target_pairs={{0,4},{4,0},{8,12},{12,8},{16,20},{20,16},{24,28},{28,24},{1,5},{5... | collective-permute-start | bytes 3932168 | tf_op jit(solution)/shard_map/ppermute | solution.py:200
  48.7 11.6 %collective-permute-done.7 = bf16[256,1280]{1,0:T(8,128)(2,1)S(1)} collective-permute-done((bf16[256,1280]{1,0:T(8,128)(2,1)S(1)}, bf16[256,1280]{1,0:T(8,128)(2,1)S(1)}, u32[]{:S(2)}, u32[]{:S(2)}) %collective-permute-start.7) | collective-permute-done | bytes 655392 | tf_op jit(solution)/shard_map/ppermute | solution.py:200
  65.6 1.7 %pad_maximum_fusion = bf16[4,2,4,160,256]{4,3,2,1,0:T(8,128)(2,1)} fusion(bf16[4,1,4,160,256]{4,3,2,1,0:T(8,128)(2,1)S(1)} %bitcast.72, bf16[4,1,4,160,256]{4,3,2,1,0:T(8,128)(2,1)S(1)} %bitcast.70), kind=kLoop, calls=%fused_computation.3 | loop fusion | flops 1310720 | bytes 5242880 | tf_op jit(solution)/shard_map/stack | solution.py:259
  67.3 2.5 %gather_fusion.2 = bf16[32,160,256]{2,1,0:T(8,128)(2,1)S(1)} fusion(bf16[32,160,256]{2,1,0:T(8,128)(2,1)} %bitcast.65, s32[1024]{0:T(1024)S(1)} %get-tuple-element.95), kind=kCustom, calls=%fused_computation.2 | custom fusion | bytes 5243008 | tf_op jit(solution)/shard_map/gather | solution.py:169
  72.6 9.2 %all-gather.2.cloned.1.call-done.x_ref = bf16[256,5120]{1,0:T(8,128)(2,1)} async-done(((bf16[256,1280]{1,0:T(8,128)(2,1)}), bf16[256,5120]{1,0:T(8,128)(2,1)}) %all-gather.2.cloned.1.call-update) | async-done | bytes 2621456 | tf_op jit(solution)/shard_map/all_gather | solution.py:250
  86.4 10.2 %shard_map.138 = (f32[256,1024]{1,0:T(8,128)S(1)}, f32[256,1024]{1,0:T(8,128)S(1)}, f32[256,256]{1,0:T(8,128)S(1)}) custom-call(bf16[256,5120]{1,0:T(8,128)(2,1)S(1)} %copy-done.2, bf16[5120,1024]{1,0:T(8,128)(2,1)} %wq_ref.1, bf16[5120,256]{1,0:T(8,128)(2,1)S(1)} %bitcast.62, f32[256,1024]{1,0:T(8,128)S(1)} %copy-done.3, f32[1,128]{1,0:T(1,128)S(1)} %bitcast.63, ...), custom_call_target="tpu_custom_call" | custom-call | flops 16777216000 | bytes 41943040 | tf_op jit(solution)/shard_map/pallas_call | solution.py:137
  97.6 3.1 %collective-permute-done.11 = bf16[256,1280]{1,0:T(8,128)(2,1)S(1)} collective-permute-done((bf16[256,1280]{1,0:T(8,128)(2,1)S(1)}, bf16[256,1280]{1,0:T(8,128)(2,1)S(1)}, u32[]{:S(2)}, u32[]{:S(2)}) %collective-permute-start.11) | collective-permute-done | bytes 655392 | tf_op jit(solution)/shard_map/ppermute | solution.py:200
  100.8 1.9 %collective-permute-start.17 = (bf16[256,256]{1,0:T(8,128)(2,1)S(1)}, bf16[256,256]{1,0:T(8,128)(2,1)S(1)}, u32[]{:S(2)}, u32[]{:S(2)}) collective-permute-start(bf16[256,256]{1,0:T(8,128)(2,1)S(1)} %convert_element_type.36), channel_id=1, source_target_pairs={{0,1},{1,2},{2,3},{3,0},{4,5},{5,6},{6,7},{7,4},{8,9},{9,10},{10,1... | collective-permute-start | bytes 393224 | tf_op jit(solution)/shard_map/ppermute | solution.py:207
  108.1 4.8 %collective-permute-done.18 = bf16[256,256]{1,0:T(8,128)(2,1)S(1)} collective-permute-done((bf16[256,256]{1,0:T(8,128)(2,1)S(1)}, bf16[256,256]{1,0:T(8,128)(2,1)S(1)}, u32[]{:S(2)}, u32[]{:S(2)}) %collective-permute-start.18) | collective-permute-done | bytes 131104 | tf_op jit(solution)/shard_map/ppermute | solution.py:207
  112.9 2.5 %collective-permute-start.22 = (bf16[256,1024]{1,0:T(8,128)(2,1)S(1)}, bf16[256,1024]{1,0:T(8,128)(2,1)S(1)}, u32[]{:S(2)}, u32[]{:S(2)}) collective-permute-start(bf16[256,1024]{1,0:T(8,128)(2,1)S(1)} %convert_element_type.35), channel_id=1, source_target_pairs={{0,24},{4,28},{8,16},{12,20},{16,8},{20,12},{24,0},{28,4},{1,25},{... | collective-permute-start | bytes 1572872 | tf_op jit(solution)/shard_map/ppermute | solution.py:200
  115.6 13.4 %collective-permute-start.24 = (bf16[256,256]{1,0:T(8,128)(2,1)S(1)}, bf16[256,256]{1,0:T(8,128)(2,1)S(1)}, u32[]{:S(2)}, u32[]{:S(2)}) collective-permute-start(bf16[256,256]{1,0:T(8,128)(2,1)S(1)} %get-tuple-element.88), channel_id=1, source_target_pairs={{0,8},{4,12},{8,0},{12,4},{16,24},{20,28},{24,16},{28,20},{1,9},{5... | collective-permute-start | bytes 393224 | tf_op jit(solution)/shard_map/ppermute | solution.py:200
  131.8 2.8 %collective-permute-done.25 = bf16[256,256]{1,0:T(8,128)(2,1)S(1)} collective-permute-done((bf16[256,256]{1,0:T(8,128)(2,1)S(1)}, bf16[256,256]{1,0:T(8,128)(2,1)S(1)}, u32[]{:S(2)}, u32[]{:S(2)}) %collective-permute-start.25) | collective-permute-done | bytes 131104 | tf_op jit(solution)/shard_map/ppermute | solution.py:200
  134.7 2.7 %fusion.14 = f32[1280,256]{0,1:T(8,128)S(1)} fusion(bf16[1024,1280]{1,0:T(8,128)(2,1)} %constant_dynamic-update-slice_fusion, bf16[1024,256]{1,0:T(8,128)(2,1)S(1)} %bitcast.71), kind=kOutput, calls=%fused_computation.72 | convolution fusion | flops 671088640 | bytes 4456448 | tf_op jit(solution)/shard_map/td,tc->dc/dot_general | solution.py:350
  137.5 3.2 %collective-permute-start.27 = (bf16[1280,128]{0,1:T(8,128)(2,1)S(1)}, bf16[1280,128]{0,1:T(8,128)(2,1)S(1)}, u32[]{:S(2)}, u32[]{:S(2)}) collective-permute-start(bf16[1280,128]{0,1:T(8,128)(2,1)S(1)} %select_convert_fusion), channel_id=1, source_target_pairs={{0,4},{4,0},{8,12},{12,8},{16,20},{20,16},{24,28},{28,24},{1,5},{5... | collective-permute-start | bytes 983048 | tf_op jit(solution)/shard_map/ppermute | solution.py:200
  140.7 5.1 %collective-permute-done.21 = bf16[256,1280]{1,0:T(8,128)(2,1)S(1)} collective-permute-done((bf16[256,1280]{1,0:T(8,128)(2,1)S(1)}, bf16[256,1280]{1,0:T(8,128)(2,1)S(1)}, u32[]{:S(2)}, u32[]{:S(2)}) %collective-permute-start.21) | collective-permute-done | bytes 655392 | tf_op jit(solution)/shard_map/ppermute | solution.py:282
  147.7 4.2 %collective-permute-start.23 = (bf16[640,1024]{1,0:T(8,128)(2,1)S(1)}, bf16[640,1024]{1,0:T(8,128)(2,1)S(1)}, u32[]{:S(2)}, u32[]{:S(2)}) collective-permute-start(bf16[640,1024]{1,0:T(8,128)(2,1)S(1)} %add_convert_fusion), channel_id=1, source_target_pairs={{0,4},{4,0},{8,12},{12,8},{16,20},{20,16},{24,28},{28,24},{1,5},{5... | collective-permute-start | bytes 3932168 | tf_op jit(solution)/shard_map/ppermute | solution.py:200
  154.5 2.1 %add_add_fusion = f32[640,1024]{1,0:T(8,128)} fusion(f32[640,1024]{1,0:T(8,128)S(1)} %fusion.1, bf16[640,1024]{1,0:T(8,128)(2,1)S(1)} %collective-permute-done.23, bf16[256,1024]{1,0:T(8,128)(2,1)S(1)} %collective-permute-done.22, bf16[256,1280]{1,0:T(8,128)(2,1)S(1)} %select_select_fusion, s32[]{:T(128)S(6)} %select_n.193), kind=kOutput, calls=%fused_computation.4 | convolution fusion | flops 337510400 | bytes 7405572 | tf_op jit(solution)/shard_map/td,tc->dc/dot_general | solution.py:332
  (117 shorter events, 40.5 us)
Async XLA Ops:
  9.7 13.1 %all-to-all-start = ((bf16[8,32,1280]{2,1,0:T(8,128)(2,1)}), bf16[8,32,1280]{2,1,0:T(8,128)(2,1)S(1)}, u32[]{:S(2)}, u32[]{:S(2)}) async-start(bf16[8,32,1280]{2,1,0:T(8,128)(2,1)} %gather_fusion), calls=%async_computation | async-start | bytes 1310720 | tf_op jit(solution)/shard_map/all_to_all | solution.py:234
  14.3 67.5 %all-gather.2.cloned.1.call-start = ((), (), s32[]{:S(2)}) async-start(), calls=%async_computation.1 | async-start | bytes 3276800 | tf_op jit(solution)/shard_map/all_gather | solution.py:250
  17.6 8.4 %collective-permute-start.1 = (bf16[160,256]{1,0:T(8,128)(2,1)S(1)}, bf16[160,256]{1,0:T(8,128)(2,1)S(1)}, u32[]{:S(2)}, u32[]{:S(2)}) collective-permute-start(bf16[160,256]{1,0:T(8,128)(2,1)S(1)} %get-tuple-element.92), channel_id=1, source_target_pairs={{0,2},{1,3},{2,0},{3,1},{4,6},{5,7},{6,4},{7,5},{8,10},{9,11},{10,... | collective-permute-start | bytes 245768 | tf_op jit(solution)/shard_map/ppermute | solution.py:207
  26.2 8.5 %collective-permute-start.3 = (bf16[4,160,256]{2,1,0:T(8,128)(2,1)S(1)}, bf16[4,160,256]{2,1,0:T(8,128)(2,1)S(1)}, u32[]{:S(2)}, u32[]{:S(2)}) collective-permute-start(bf16[4,160,256]{2,1,0:T(8,128)(2,1)S(1)} %get-tuple-element.90), channel_id=1, source_target_pairs={{0,8},{4,12},{8,0},{12,4},{16,24},{20,28},{24,16},{28,20},{1,9},{5... | collective-permute-start | bytes 983048 | tf_op jit(solution)/shard_map/ppermute | solution.py:200
  26.5 8.1 %collective-permute-start.4 = (bf16[4,160,256]{2,1,0:T(8,128)(2,1)S(1)}, bf16[4,160,256]{2,1,0:T(8,128)(2,1)S(1)}, u32[]{:S(2)}, u32[]{:S(2)}) collective-permute-start(bf16[4,160,256]{2,1,0:T(8,128)(2,1)S(1)} %get-tuple-element.90), channel_id=1, source_target_pairs={{0,16},{4,20},{8,24},{12,28},{16,0},{20,4},{24,8},{28,12},{1,17},{... | collective-permute-start | bytes 983048 | tf_op jit(solution)/shard_map/ppermute | solution.py:200
  26.7 15.2 %collective-permute-start.5 = (bf16[4,160,256]{2,1,0:T(8,128)(2,1)S(1)}, bf16[4,160,256]{2,1,0:T(8,128)(2,1)S(1)}, u32[]{:S(2)}, u32[]{:S(2)}) collective-permute-start(bf16[4,160,256]{2,1,0:T(8,128)(2,1)S(1)} %get-tuple-element.90), channel_id=1, source_target_pairs={{0,24},{4,28},{8,16},{12,20},{16,8},{20,12},{24,0},{28,4},{1,25},{... | collective-permute-start | bytes 983048 | tf_op jit(solution)/shard_map/ppermute | solution.py:200
  42.0 19.1 %collective-permute-start.6 = (bf16[4,4,160,256]{3,2,1,0:T(8,128)(2,1)S(1)}, bf16[4,4,160,256]{3,2,1,0:T(8,128)(2,1)S(1)}, u32[]{:S(2)}, u32[]{:S(2)}) collective-permute-start(bf16[4,4,160,256]{3,2,1,0:T(8,128)(2,1)S(1)} %pad_maximum_fusion.1), channel_id=1, source_target_pairs={{0,4},{4,0},{8,12},{12,8},{16,20},{20,16},{24,28},{28,24},{1,5},{5... | collective-permute-start | bytes 3932168 | tf_op jit(solution)/shard_map/ppermute | solution.py:200
  43.9 16.3 %collective-permute-start.7 = (bf16[256,1280]{1,0:T(8,128)(2,1)S(1)}, bf16[256,1280]{1,0:T(8,128)(2,1)S(1)}, u32[]{:S(2)}, u32[]{:S(2)}) collective-permute-start(bf16[256,1280]{1,0:T(8,128)(2,1)S(1)} %bitcast.67), channel_id=1, source_target_pairs={{0,8},{4,12},{8,0},{12,4},{16,24},{20,28},{24,16},{28,20},{1,9},{5... | collective-permute-start | bytes 1966088 | tf_op jit(solution)/shard_map/ppermute | solution.py:200
  45.2 16.0 %collective-permute-start.8 = (bf16[256,1280]{1,0:T(8,128)(2,1)S(1)}, bf16[256,1280]{1,0:T(8,128)(2,1)S(1)}, u32[]{:S(2)}, u32[]{:S(2)}) collective-permute-start(bf16[256,1280]{1,0:T(8,128)(2,1)S(1)} %bitcast.68), channel_id=1, source_target_pairs={{0,16},{4,20},{8,24},{12,28},{16,0},{20,4},{24,8},{28,12},{1,17},{... | collective-permute-start | bytes 1966088 | tf_op jit(solution)/shard_map/ppermute | solution.py:200
  61.9 8.3 %collective-permute-start.9 = (bf16[128,1280]{1,0:T(8,128)(2,1)}, bf16[128,1280]{1,0:T(8,128)(2,1)S(1)}, u32[]{:S(2)}, u32[]{:S(2)}) collective-permute-start(bf16[128,1280]{1,0:T(8,128)(2,1)} %slice.50), channel_id=1, source_target_pairs={{0,16},{4,20},{8,24},{12,28},{16,0},{20,4},{24,8},{28,12},{1,17},{... | collective-permute-start | bytes 983048 | tf_op jit(solution)/shard_map/ppermute | solution.py:200
  62.9 8.1 %collective-permute-start.10 = (bf16[128,1280]{1,0:T(8,128)(2,1)}, bf16[128,1280]{1,0:T(8,128)(2,1)S(1)}, u32[]{:S(2)}, u32[]{:S(2)}) collective-permute-start(bf16[128,1280]{1,0:T(8,128)(2,1)} %slice.51), channel_id=1, source_target_pairs={{0,8},{4,12},{8,0},{12,4},{16,24},{20,28},{24,16},{28,20},{1,9},{5... | collective-permute-start | bytes 983048 | tf_op jit(solution)/shard_map/ppermute | solution.py:200
  81.8 19.0 %collective-permute-start.13 = (bf16[256,1280]{1,0:T(8,128)(2,1)}, bf16[256,1280]{1,0:T(8,128)(2,1)S(1)}, u32[]{:S(2)}, u32[]{:S(2)}) collective-permute-start(bf16[256,1280]{1,0:T(8,128)(2,1)} %pad_maximum_fusion.2), channel_id=1, source_target_pairs={{0,1},{4,5},{9,10},{13,14},{18,19},{22,23}} | collective-permute-start | bytes 1966088 | tf_op jit(solution)/shard_map/ppermute | solution.py:282
  82.6 18.1 %collective-permute-start.14 = (bf16[256,1280]{1,0:T(8,128)(2,1)}, bf16[256,1280]{1,0:T(8,128)(2,1)S(1)}, u32[]{:S(2)}, u32[]{:S(2)}) collective-permute-start(bf16[256,1280]{1,0:T(8,128)(2,1)} %pad_maximum_fusion.2), channel_id=1, source_target_pairs={{9,8},{13,12},{18,17},{22,21},{27,26},{31,30}} | collective-permute-start | bytes 1966088 | tf_op jit(solution)/shard_map/ppermute | solution.py:282
  85.1 15.7 %collective-permute-start.11 = (bf16[256,1280]{1,0:T(8,128)(2,1)S(1)}, bf16[256,1280]{1,0:T(8,128)(2,1)S(1)}, u32[]{:S(2)}, u32[]{:S(2)}) collective-permute-start(bf16[256,1280]{1,0:T(8,128)(2,1)S(1)} %get-tuple-element.57), channel_id=1, source_target_pairs={{0,8},{4,12},{8,0},{12,4},{16,24},{20,28},{24,16},{28,20},{1,9},{5... | collective-permute-start | bytes 1966088 | tf_op jit(solution)/shard_map/ppermute | solution.py:200
  85.4 15.3 %collective-permute-start.12 = (bf16[256,1280]{1,0:T(8,128)(2,1)S(1)}, bf16[256,1280]{1,0:T(8,128)(2,1)S(1)}, u32[]{:S(2)}, u32[]{:S(2)}) collective-permute-start(bf16[256,1280]{1,0:T(8,128)(2,1)S(1)} %get-tuple-element.58), channel_id=1, source_target_pairs={{0,16},{4,20},{8,24},{12,28},{16,0},{20,4},{24,8},{28,12},{1,17},{... | collective-permute-start | bytes 1966088 | tf_op jit(solution)/shard_map/ppermute | solution.py:200
  102.7 10.2 %collective-permute-start.18 = (bf16[256,256]{1,0:T(8,128)(2,1)S(1)}, bf16[256,256]{1,0:T(8,128)(2,1)S(1)}, u32[]{:S(2)}, u32[]{:S(2)}) collective-permute-start(bf16[256,256]{1,0:T(8,128)(2,1)S(1)} %convert_element_type.36), channel_id=1, source_target_pairs={{0,2},{1,3},{2,0},{3,1},{4,6},{5,7},{6,4},{7,5},{8,10},{9,11},{10,... | collective-permute-start | bytes 393224 | tf_op jit(solution)/shard_map/ppermute | solution.py:207
  104.1 11.3 %collective-permute-start.15 = (bf16[256,1024]{1,0:T(8,128)(2,1)S(1)}, bf16[256,1024]{1,0:T(8,128)(2,1)S(1)}, u32[]{:S(2)}, u32[]{:S(2)}) collective-permute-start(bf16[256,1024]{1,0:T(8,128)(2,1)S(1)} %convert_element_type.35), channel_id=1, source_target_pairs={{0,8},{4,12},{8,0},{12,4},{16,24},{20,28},{24,16},{28,20},{1,9},{5... | collective-permute-start | bytes 1572872 | tf_op jit(solution)/shard_map/ppermute | solution.py:200
  105.2 10.4 %collective-permute-start.16 = (bf16[256,1024]{1,0:T(8,128)(2,1)S(1)}, bf16[256,1024]{1,0:T(8,128)(2,1)S(1)}, u32[]{:S(2)}, u32[]{:S(2)}) collective-permute-start(bf16[256,1024]{1,0:T(8,128)(2,1)S(1)} %convert_element_type.35), channel_id=1, source_target_pairs={{0,16},{4,20},{8,24},{12,28},{16,0},{20,4},{24,8},{28,12},{1,17},{... | collective-permute-start | bytes 1572872 | tf_op jit(solution)/shard_map/ppermute | solution.py:200
  105.6 10.0 %collective-permute-start.20 = (bf16[256,1280]{1,0:T(8,128)(2,1)S(1)}, bf16[256,1280]{1,0:T(8,128)(2,1)S(1)}, u32[]{:S(2)}, u32[]{:S(2)}) collective-permute-start(bf16[256,1280]{1,0:T(8,128)(2,1)S(1)} %broadcast_select_fusion), channel_id=1, source_target_pairs={{1,2},{5,6},{10,11},{14,15},{17,16},{21,20},{26,25},{30,29}} | collective-permute-start | bytes 1966088 | tf_op jit(solution)/shard_map/ppermute | solution.py:282
  106.5 8.8 %collective-permute-start.19 = (bf16[256,256]{1,0:T(8,128)(2,1)S(1)}, bf16[256,256]{1,0:T(8,128)(2,1)S(1)}, u32[]{:S(2)}, u32[]{:S(2)}) collective-permute-start(bf16[256,256]{1,0:T(8,128)(2,1)S(1)} %convert_element_type.36), channel_id=1, source_target_pairs={{0,3},{1,0},{2,1},{3,2},{4,7},{5,4},{6,5},{7,6},{8,11},{9,8},{10,9... | collective-permute-start | bytes 393224 | tf_op jit(solution)/shard_map/ppermute | solution.py:207
  112.9 33.0 %collective-permute-start.22 = (bf16[256,1024]{1,0:T(8,128)(2,1)S(1)}, bf16[256,1024]{1,0:T(8,128)(2,1)S(1)}, u32[]{:S(2)}, u32[]{:S(2)}) collective-permute-start(bf16[256,1024]{1,0:T(8,128)(2,1)S(1)} %convert_element_type.35), channel_id=1, source_target_pairs={{0,24},{4,28},{8,16},{12,20},{16,8},{20,12},{24,0},{28,4},{1,25},{... | collective-permute-start | bytes 1572872 | tf_op jit(solution)/shard_map/ppermute | solution.py:200
  115.6 16.2 %collective-permute-start.24 = (bf16[256,256]{1,0:T(8,128)(2,1)S(1)}, bf16[256,256]{1,0:T(8,128)(2,1)S(1)}, u32[]{:S(2)}, u32[]{:S(2)}) collective-permute-start(bf16[256,256]{1,0:T(8,128)(2,1)S(1)} %get-tuple-element.88), channel_id=1, source_target_pairs={{0,8},{4,12},{8,0},{12,4},{16,24},{20,28},{24,16},{28,20},{1,9},{5... | collective-permute-start | bytes 393224 | tf_op jit(solution)/shard_map/ppermute | solution.py:200
  130.3 15.5 %collective-permute-start.21 = (bf16[256,1280]{1,0:T(8,128)(2,1)S(1)}, bf16[256,1280]{1,0:T(8,128)(2,1)S(1)}, u32[]{:S(2)}, u32[]{:S(2)}) collective-permute-start(bf16[256,1280]{1,0:T(8,128)(2,1)S(1)} %collective-permute-done.20), channel_id=1, source_target_pairs={{2,3},{6,7},{25,24},{29,28}} | collective-permute-start | bytes 1966088 | tf_op jit(solution)/shard_map/ppermute | solution.py:282
  137.5 15.7 %collective-permute-start.27 = (bf16[1280,128]{0,1:T(8,128)(2,1)S(1)}, bf16[1280,128]{0,1:T(8,128)(2,1)S(1)}, u32[]{:S(2)}, u32[]{:S(2)}) collective-permute-start(bf16[1280,128]{0,1:T(8,128)(2,1)S(1)} %select_convert_fusion), channel_id=1, source_target_pairs={{0,4},{4,0},{8,12},{12,8},{16,20},{20,16},{24,28},{28,24},{1,5},{5... | collective-permute-start | bytes 983048 | tf_op jit(solution)/shard_map/ppermute | solution.py:200
  (17 other events, 136.5 us)
Sparse Core Ops, SparseCore 0:
  26.2 55.5 all-gather.1

commit v13 on v12

--- a/solution.py
+++ b/solution.py
@@ -307,7 +307,7 @@
     d_all = [d_query] + other_chips([d_query] * chips)
     spread = jnp.stack(around([d_kv] * n_mp))
     d_near = [d_all[k] for k in near]
-    d_near, spread, last = lax.optimization_barrier((d_near, spread, hops[-1] if by_plane else x))
+    d_near, last = lax.optimization_barrier((d_near, hops[-1] if by_plane else x))
     for k, block in zip(near, d_near):
         d_all[k] = block
     for k, block in zip(near, near_rows):

time: 164 us -> 180 us (1.098)
  waiting for transfers between devices: 55.2 us -> 83.9 us
  starting transfers between devices: 52.4 us -> 39.3 us
    ppermute x18, waiting for transfers between devices: 32.3 us -> 53.2 us  [flip(): return lax.ppermute(block, 'dp', [(i, i ^ bits) for i in range(n_dp)])]
    ppermute x18, starting transfers between devices: 34.4 us -> 20.7 us  [flip(): return lax.ppermute(block, 'dp', [(i, i ^ bits) for i in range(n_dp)])]
    ppermute x4, waiting for transfers between devices: 5.1 us -> 13.6 us  [along(): return lax.ppermute(block, ('dp', 'mp'), pairs)]
  transfers between devices with their start and end apart: 30 -> 30, of which waited for: 15 -> 15; matrix products, arithmetic and copies ran while one was open for 16% -> 15% of each run, Pallas kernels for 6% -> 6%
where the time goes in v13:
time: 180 us; the launch traced here: 179 us
  waiting for transfers between devices  83.9 us (47%)
  starting transfers between devices  39.3 us (22%)
  local copies, waits for them, and re-layouts  15.9 us (9%)
  between operations  14.4 us (8%)
  Pallas kernels  10.2 us (6%)
  matrix products  7.74 us (4%)
  other arithmetic  7.45 us (4%)
    ppermute x18, waiting for transfers between devices, flip(): return lax.ppermute(block, 'dp', [(i, i ^ bits) for i in range(n_dp)])  53.2 us
    ppermute x18, starting transfers between devices, flip(): return lax.ppermute(block, 'dp', [(i, i ^ bits) for i in range(n_dp)])  20.7 us
    ppermute x4, waiting for transfers between devices, along(): return lax.ppermute(block, ('dp', 'mp'), pairs)  13.6 us
    pallas_call x1, Pallas kernels, attend(): pl.pallas_call(functools.partial(attend_kernel, length, device_cols), gri...  10.2 us
    ppermute x6, starting transfers between devices, around(): lax.ppermute(blocks[k], 'mp', [(i, (i + k) % n_mp) for i in range(n_mp)])  10.2 us
    all_gather x1, waiting for transfers between devices, local(): x = lax.all_gather(rows, 'mp', axis=1, tiled=True)  9.18 us
    ppermute x6, waiting for transfers between devices, around(): lax.ppermute(blocks[k], 'mp', [(i, (i + k) % n_mp) for i in range(n_mp)])  6.16 us
    gather x3, local copies, waits for them, and re-layouts, pick(): return array.at[index].get(mode='promise_in_bounds')  5.32 us
  transfers between devices with their start and end apart: 30, of which 15 were waited for; matrix products, arithmetic and copies ran while one was open for 15% of the time, Pallas kernels for 6%

profile of v13, /device:TPU:7, one launch (start us, length us, event | category | flops | bytes accessed | tf_op | source)
XLA Modules:
  0.0 179.0 jit_solution(14684715028842578242)
XLA Ops:
  9.7 4.6 %all-to-all-start = ((bf16[8,32,1280]{2,1,0:T(8,128)(2,1)}), bf16[8,32,1280]{2,1,0:T(8,128)(2,1)S(1)}, u32[]{:S(2)}, u32[]{:S(2)}) async-start(bf16[8,32,1280]{2,1,0:T(8,128)(2,1)} %gather_fusion), calls=%async_computation | async-start | bytes 1310720 | tf_op jit(solution)/shard_map/all_to_all | solution.py:234
  17.6 2.3 %collective-permute-start.1 = (bf16[160,256]{1,0:T(8,128)(2,1)S(1)}, bf16[160,256]{1,0:T(8,128)(2,1)S(1)}, u32[]{:S(2)}, u32[]{:S(2)}) collective-permute-start(bf16[160,256]{1,0:T(8,128)(2,1)S(1)} %get-tuple-element.90), channel_id=1, source_target_pairs={{0,2},{1,3},{2,0},{3,1},{4,6},{5,7},{6,4},{7,5},{8,10},{9,11},{10,... | collective-permute-start | bytes 245768 | tf_op jit(solution)/shard_map/ppermute | solution.py:207
  21.0 1.8 %all-to-all-done = bf16[8,32,1280]{2,1,0:T(8,128)(2,1)S(1)} async-done(((bf16[8,32,1280]{2,1,0:T(8,128)(2,1)}), bf16[8,32,1280]{2,1,0:T(8,128)(2,1)S(1)}, u32[]{:S(2)}, u32[]{:S(2)}) %all-to-all-start) | async-done | bytes 655392 | tf_op jit(solution)/shard_map/all_to_all | solution.py:234
  26.7 2.2 %collective-permute-start.5 = (bf16[4,160,256]{2,1,0:T(8,128)(2,1)S(1)}, bf16[4,160,256]{2,1,0:T(8,128)(2,1)S(1)}, u32[]{:S(2)}, u32[]{:S(2)}) collective-permute-start(bf16[4,160,256]{2,1,0:T(8,128)(2,1)S(1)} %get-tuple-element.88), channel_id=1, source_target_pairs={{0,24},{4,28},{8,16},{12,20},{16,8},{20,12},{24,0},{28,4},{1,25},{... | collective-permute-start | bytes 983048 | tf_op jit(solution)/shard_map/ppermute | solution.py:200
  28.9 5.8 %collective-permute-done.3 = bf16[4,160,256]{2,1,0:T(8,128)(2,1)S(1)} collective-permute-done((bf16[4,160,256]{2,1,0:T(8,128)(2,1)S(1)}, bf16[4,160,256]{2,1,0:T(8,128)(2,1)S(1)}, u32[]{:S(2)}, u32[]{:S(2)}) %collective-permute-start.3) | collective-permute-done | bytes 327712 | tf_op jit(solution)/shard_map/ppermute | solution.py:200
  34.7 7.2 %collective-permute-done.5 = bf16[4,160,256]{2,1,0:T(8,128)(2,1)S(1)} collective-permute-done((bf16[4,160,256]{2,1,0:T(8,128)(2,1)S(1)}, bf16[4,160,256]{2,1,0:T(8,128)(2,1)S(1)}, u32[]{:S(2)}, u32[]{:S(2)}) %collective-permute-start.5) | collective-permute-done | bytes 327712 | tf_op jit(solution)/shard_map/ppermute | solution.py:200
  42.0 1.9 %collective-permute-start.6 = (bf16[4,4,160,256]{3,2,1,0:T(8,128)(2,1)S(1)}, bf16[4,4,160,256]{3,2,1,0:T(8,128)(2,1)S(1)}, u32[]{:S(2)}, u32[]{:S(2)}) collective-permute-start(bf16[4,4,160,256]{3,2,1,0:T(8,128)(2,1)S(1)} %pad_maximum_fusion.1), channel_id=1, source_target_pairs={{0,4},{4,0},{8,12},{12,8},{16,20},{20,16},{24,28},{28,24},{1,5},{5... | collective-permute-start | bytes 3932168 | tf_op jit(solution)/shard_map/ppermute | solution.py:200
  48.7 11.6 %collective-permute-done.7 = bf16[256,1280]{1,0:T(8,128)(2,1)S(1)} collective-permute-done((bf16[256,1280]{1,0:T(8,128)(2,1)S(1)}, bf16[256,1280]{1,0:T(8,128)(2,1)S(1)}, u32[]{:S(2)}, u32[]{:S(2)}) %collective-permute-start.7) | collective-permute-done | bytes 655392 | tf_op jit(solution)/shard_map/ppermute | solution.py:200
  67.3 2.5 %gather_fusion.2 = bf16[32,160,256]{2,1,0:T(8,128)(2,1)S(1)} fusion(bf16[32,160,256]{2,1,0:T(8,128)(2,1)} %bitcast.65, s32[1024]{0:T(1024)S(1)} %get-tuple-element.93), kind=kCustom, calls=%fused_computation.2 | custom fusion | bytes 5243008 | tf_op jit(solution)/shard_map/gather | solution.py:169
  72.6 9.2 %all-gather.2.cloned.1.call-done.x_ref = bf16[256,5120]{1,0:T(8,128)(2,1)} async-done(((bf16[256,1280]{1,0:T(8,128)(2,1)}), bf16[256,5120]{1,0:T(8,128)(2,1)}) %all-gather.2.cloned.1.call-update) | async-done | bytes 2621456 | tf_op jit(solution)/shard_map/all_gather | solution.py:250
  86.4 10.2 %shard_map.138 = (f32[256,1024]{1,0:T(8,128)S(1)}, f32[256,1024]{1,0:T(8,128)S(1)}, f32[256,256]{1,0:T(8,128)S(1)}) custom-call(bf16[256,5120]{1,0:T(8,128)(2,1)S(1)} %copy-done.2, bf16[5120,1024]{1,0:T(8,128)(2,1)} %wq_ref.1, bf16[5120,256]{1,0:T(8,128)(2,1)S(1)} %bitcast.62, f32[256,1024]{1,0:T(8,128)S(1)} %copy-done.3, f32[1,128]{1,0:T(1,128)S(1)} %bitcast.63, ...), custom_call_target="tpu_custom_call" | custom-call | flops 16777216000 | bytes 41943040 | tf_op jit(solution)/shard_map/pallas_call | solution.py:137
  97.6 3.1 %collective-permute-done.11 = bf16[256,1280]{1,0:T(8,128)(2,1)S(1)} collective-permute-done((bf16[256,1280]{1,0:T(8,128)(2,1)S(1)}, bf16[256,1280]{1,0:T(8,128)(2,1)S(1)}, u32[]{:S(2)}, u32[]{:S(2)}) %collective-permute-start.11) | collective-permute-done | bytes 655392 | tf_op jit(solution)/shard_map/ppermute | solution.py:200
  100.8 1.9 %collective-permute-start.21 = (bf16[256,256]{1,0:T(8,128)(2,1)S(1)}, bf16[256,256]{1,0:T(8,128)(2,1)S(1)}, u32[]{:S(2)}, u32[]{:S(2)}) collective-permute-start(bf16[256,256]{1,0:T(8,128)(2,1)S(1)} %convert_element_type.36), channel_id=1, source_target_pairs={{0,1},{1,2},{2,3},{3,0},{4,5},{5,6},{6,7},{7,4},{8,9},{9,10},{10,1... | collective-permute-start | bytes 393224 | tf_op jit(solution)/shard_map/ppermute | solution.py:207
  104.1 2.1 %collective-permute-start.23 = (bf16[256,256]{1,0:T(8,128)(2,1)S(1)}, bf16[256,256]{1,0:T(8,128)(2,1)S(1)}, u32[]{:S(2)}, u32[]{:S(2)}) collective-permute-start(bf16[256,256]{1,0:T(8,128)(2,1)S(1)} %convert_element_type.36), channel_id=1, source_target_pairs={{0,3},{1,0},{2,1},{3,2},{4,7},{5,4},{6,5},{7,6},{8,11},{9,8},{10,9... | collective-permute-start | bytes 393224 | tf_op jit(solution)/shard_map/ppermute | solution.py:207
  108.1 4.4 %collective-permute-done.22 = bf16[256,256]{1,0:T(8,128)(2,1)S(1)} collective-permute-done((bf16[256,256]{1,0:T(8,128)(2,1)S(1)}, bf16[256,256]{1,0:T(8,128)(2,1)S(1)}, u32[]{:S(2)}, u32[]{:S(2)}) %collective-permute-start.22) | collective-permute-done | bytes 131104 | tf_op jit(solution)/shard_map/ppermute | solution.py:207
  112.6 2.3 %collective-permute-start.24 = (bf16[256,256]{1,0:T(8,128)(2,1)S(1)}, bf16[256,256]{1,0:T(8,128)(2,1)S(1)}, u32[]{:S(2)}, u32[]{:S(2)}) collective-permute-start(bf16[256,256]{1,0:T(8,128)(2,1)S(1)} %get-tuple-element.86), channel_id=1, source_target_pairs={{0,8},{4,12},{8,0},{12,4},{16,24},{20,28},{24,16},{28,20},{1,9},{5... | collective-permute-start | bytes 393224 | tf_op jit(solution)/shard_map/ppermute | solution.py:200
  116.3 4.3 %collective-permute-done.24 = bf16[256,256]{1,0:T(8,128)(2,1)S(1)} collective-permute-done((bf16[256,256]{1,0:T(8,128)(2,1)S(1)}, bf16[256,256]{1,0:T(8,128)(2,1)S(1)}, u32[]{:S(2)}, u32[]{:S(2)}) %collective-permute-start.24) | collective-permute-done | bytes 131104 | tf_op jit(solution)/shard_map/ppermute | solution.py:200
  121.2 1.9 %collective-permute-start.19 = (bf16[256,1024]{1,0:T(8,128)(2,1)S(1)}, bf16[256,1024]{1,0:T(8,128)(2,1)S(1)}, u32[]{:S(2)}, u32[]{:S(2)}) collective-permute-start(bf16[256,1024]{1,0:T(8,128)(2,1)S(1)} %convert_element_type.35), channel_id=1, source_target_pairs={{0,24},{4,28},{8,16},{12,20},{16,8},{20,12},{24,0},{28,4},{1,25},{... | collective-permute-start | bytes 1572872 | tf_op jit(solution)/shard_map/ppermute | solution.py:200
  123.5 2.6 %fusion.14 = f32[1280,256]{0,1:T(8,128)S(1)} fusion(bf16[1024,1280]{1,0:T(8,128)(2,1)} %constant_dynamic-update-slice_fusion, bf16[1024,256]{1,0:T(8,128)(2,1)S(1)} %bitcast.71), kind=kOutput, calls=%fused_computation.72 | convolution fusion | flops 671088640 | bytes 4456448 | tf_op jit(solution)/shard_map/td,tc->dc/dot_general | solution.py:350
  126.1 19.2 %collective-permute-done.16 = bf16[256,1024]{1,0:T(8,128)(2,1)S(1)} collective-permute-done((bf16[256,1024]{1,0:T(8,128)(2,1)S(1)}, bf16[256,1024]{1,0:T(8,128)(2,1)S(1)}, u32[]{:S(2)}, u32[]{:S(2)}) %collective-permute-start.16) | collective-permute-done | bytes 524320 | tf_op jit(solution)/shard_map/ppermute | solution.py:200
  146.9 2.4 %collective-permute-start.27 = (bf16[1280,128]{0,1:T(8,128)(2,1)S(1)}, bf16[1280,128]{0,1:T(8,128)(2,1)S(1)}, u32[]{:S(2)}, u32[]{:S(2)}) collective-permute-start(bf16[1280,128]{0,1:T(8,128)(2,1)S(1)} %select_convert_fusion), channel_id=1, source_target_pairs={{0,4},{4,0},{8,12},{12,8},{16,20},{20,16},{24,28},{28,24},{1,5},{5... | collective-permute-start | bytes 983048 | tf_op jit(solution)/shard_map/ppermute | solution.py:200
  149.4 13.6 %collective-permute-done.18 = bf16[256,1280]{1,0:T(8,128)(2,1)S(1)} collective-permute-done((bf16[256,1280]{1,0:T(8,128)(2,1)S(1)}, bf16[256,1280]{1,0:T(8,128)(2,1)S(1)}, u32[]{:S(2)}, u32[]{:S(2)}) %collective-permute-start.18) | collective-permute-done | bytes 655392 | tf_op jit(solution)/shard_map/ppermute | solution.py:282
  165.0 2.4 %collective-permute-start.20 = (bf16[640,1024]{1,0:T(8,128)(2,1)S(1)}, bf16[640,1024]{1,0:T(8,128)(2,1)S(1)}, u32[]{:S(2)}, u32[]{:S(2)}) collective-permute-start(bf16[640,1024]{1,0:T(8,128)(2,1)S(1)} %add_convert_fusion), channel_id=1, source_target_pairs={{0,4},{4,0},{8,12},{12,8},{16,20},{20,16},{24,28},{28,24},{1,5},{5... | collective-permute-start | bytes 3932168 | tf_op jit(solution)/shard_map/ppermute | solution.py:200
  170.1 2.1 %add_add_fusion = f32[640,1024]{1,0:T(8,128)} fusion(f32[640,1024]{1,0:T(8,128)S(1)} %fusion.1, bf16[640,1024]{1,0:T(8,128)(2,1)S(1)} %collective-permute-done.20, bf16[256,1024]{1,0:T(8,128)(2,1)S(1)} %collective-permute-done.19, bf16[256,1280]{1,0:T(8,128)(2,1)S(1)} %select_select_fusion, s32[]{:T(128)S(6)} %select_n.193), kind=kOutput, calls=%fused_computation.4 | convolution fusion | flops 337510400 | bytes 7405572 | tf_op jit(solution)/shard_map/td,tc->dc/dot_general | solution.py:332
  (117 shorter events, 42.8 us)
Async XLA Ops:
  9.7 13.1 %all-to-all-start = ((bf16[8,32,1280]{2,1,0:T(8,128)(2,1)}), bf16[8,32,1280]{2,1,0:T(8,128)(2,1)S(1)}, u32[]{:S(2)}, u32[]{:S(2)}) async-start(bf16[8,32,1280]{2,1,0:T(8,128)(2,1)} %gather_fusion), calls=%async_computation | async-start | bytes 1310720 | tf_op jit(solution)/shard_map/all_to_all | solution.py:234
  14.3 67.5 %all-gather.2.cloned.1.call-start = ((), (), s32[]{:S(2)}) async-start(), calls=%async_computation.1 | async-start | bytes 3276800 | tf_op jit(solution)/shard_map/all_gather | solution.py:250
  17.6 8.4 %collective-permute-start.1 = (bf16[160,256]{1,0:T(8,128)(2,1)S(1)}, bf16[160,256]{1,0:T(8,128)(2,1)S(1)}, u32[]{:S(2)}, u32[]{:S(2)}) collective-permute-start(bf16[160,256]{1,0:T(8,128)(2,1)S(1)} %get-tuple-element.90), channel_id=1, source_target_pairs={{0,2},{1,3},{2,0},{3,1},{4,6},{5,7},{6,4},{7,5},{8,10},{9,11},{10,... | collective-permute-start | bytes 245768 | tf_op jit(solution)/shard_map/ppermute | solution.py:207
  26.2 8.5 %collective-permute-start.3 = (bf16[4,160,256]{2,1,0:T(8,128)(2,1)S(1)}, bf16[4,160,256]{2,1,0:T(8,128)(2,1)S(1)}, u32[]{:S(2)}, u32[]{:S(2)}) collective-permute-start(bf16[4,160,256]{2,1,0:T(8,128)(2,1)S(1)} %get-tuple-element.88), channel_id=1, source_target_pairs={{0,8},{4,12},{8,0},{12,4},{16,24},{20,28},{24,16},{28,20},{1,9},{5... | collective-permute-start | bytes 983048 | tf_op jit(solution)/shard_map/ppermute | solution.py:200
  26.5 8.1 %collective-permute-start.4 = (bf16[4,160,256]{2,1,0:T(8,128)(2,1)S(1)}, bf16[4,160,256]{2,1,0:T(8,128)(2,1)S(1)}, u32[]{:S(2)}, u32[]{:S(2)}) collective-permute-start(bf16[4,160,256]{2,1,0:T(8,128)(2,1)S(1)} %get-tuple-element.88), channel_id=1, source_target_pairs={{0,16},{4,20},{8,24},{12,28},{16,0},{20,4},{24,8},{28,12},{1,17},{... | collective-permute-start | bytes 983048 | tf_op jit(solution)/shard_map/ppermute | solution.py:200
  26.7 15.2 %collective-permute-start.5 = (bf16[4,160,256]{2,1,0:T(8,128)(2,1)S(1)}, bf16[4,160,256]{2,1,0:T(8,128)(2,1)S(1)}, u32[]{:S(2)}, u32[]{:S(2)}) collective-permute-start(bf16[4,160,256]{2,1,0:T(8,128)(2,1)S(1)} %get-tuple-element.88), channel_id=1, source_target_pairs={{0,24},{4,28},{8,16},{12,20},{16,8},{20,12},{24,0},{28,4},{1,25},{... | collective-permute-start | bytes 983048 | tf_op jit(solution)/shard_map/ppermute | solution.py:200
  42.0 19.1 %collective-permute-start.6 = (bf16[4,4,160,256]{3,2,1,0:T(8,128)(2,1)S(1)}, bf16[4,4,160,256]{3,2,1,0:T(8,128)(2,1)S(1)}, u32[]{:S(2)}, u32[]{:S(2)}) collective-permute-start(bf16[4,4,160,256]{3,2,1,0:T(8,128)(2,1)S(1)} %pad_maximum_fusion.1), channel_id=1, source_target_pairs={{0,4},{4,0},{8,12},{12,8},{16,20},{20,16},{24,28},{28,24},{1,5},{5... | collective-permute-start | bytes 3932168 | tf_op jit(solution)/shard_map/ppermute | solution.py:200
  43.9 16.3 %collective-permute-start.7 = (bf16[256,1280]{1,0:T(8,128)(2,1)S(1)}, bf16[256,1280]{1,0:T(8,128)(2,1)S(1)}, u32[]{:S(2)}, u32[]{:S(2)}) collective-permute-start(bf16[256,1280]{1,0:T(8,128)(2,1)S(1)} %bitcast.67), channel_id=1, source_target_pairs={{0,8},{4,12},{8,0},{12,4},{16,24},{20,28},{24,16},{28,20},{1,9},{5... | collective-permute-start | bytes 1966088 | tf_op jit(solution)/shard_map/ppermute | solution.py:200
  45.2 16.0 %collective-permute-start.8 = (bf16[256,1280]{1,0:T(8,128)(2,1)S(1)}, bf16[256,1280]{1,0:T(8,128)(2,1)S(1)}, u32[]{:S(2)}, u32[]{:S(2)}) collective-permute-start(bf16[256,1280]{1,0:T(8,128)(2,1)S(1)} %bitcast.68), channel_id=1, source_target_pairs={{0,16},{4,20},{8,24},{12,28},{16,0},{20,4},{24,8},{28,12},{1,17},{... | collective-permute-start | bytes 1966088 | tf_op jit(solution)/shard_map/ppermute | solution.py:200
  61.9 8.3 %collective-permute-start.9 = (bf16[128,1280]{1,0:T(8,128)(2,1)}, bf16[128,1280]{1,0:T(8,128)(2,1)S(1)}, u32[]{:S(2)}, u32[]{:S(2)}) collective-permute-start(bf16[128,1280]{1,0:T(8,128)(2,1)} %slice.50), channel_id=1, source_target_pairs={{0,16},{4,20},{8,24},{12,28},{16,0},{20,4},{24,8},{28,12},{1,17},{... | collective-permute-start | bytes 983048 | tf_op jit(solution)/shard_map/ppermute | solution.py:200
  62.9 8.1 %collective-permute-start.10 = (bf16[128,1280]{1,0:T(8,128)(2,1)}, bf16[128,1280]{1,0:T(8,128)(2,1)S(1)}, u32[]{:S(2)}, u32[]{:S(2)}) collective-permute-start(bf16[128,1280]{1,0:T(8,128)(2,1)} %slice.51), channel_id=1, source_target_pairs={{0,8},{4,12},{8,0},{12,4},{16,24},{20,28},{24,16},{28,20},{1,9},{5... | collective-permute-start | bytes 983048 | tf_op jit(solution)/shard_map/ppermute | solution.py:200
  81.8 19.0 %collective-permute-start.13 = (bf16[256,1280]{1,0:T(8,128)(2,1)}, bf16[256,1280]{1,0:T(8,128)(2,1)S(1)}, u32[]{:S(2)}, u32[]{:S(2)}) collective-permute-start(bf16[256,1280]{1,0:T(8,128)(2,1)} %pad_maximum_fusion.2), channel_id=1, source_target_pairs={{0,1},{4,5},{9,10},{13,14},{18,19},{22,23}} | collective-permute-start | bytes 1966088 | tf_op jit(solution)/shard_map/ppermute | solution.py:282
  82.6 18.1 %collective-permute-start.14 = (bf16[256,1280]{1,0:T(8,128)(2,1)}, bf16[256,1280]{1,0:T(8,128)(2,1)S(1)}, u32[]{:S(2)}, u32[]{:S(2)}) collective-permute-start(bf16[256,1280]{1,0:T(8,128)(2,1)} %pad_maximum_fusion.2), channel_id=1, source_target_pairs={{9,8},{13,12},{18,17},{22,21},{27,26},{31,30}} | collective-permute-start | bytes 1966088 | tf_op jit(solution)/shard_map/ppermute | solution.py:282
  85.1 15.7 %collective-permute-start.11 = (bf16[256,1280]{1,0:T(8,128)(2,1)S(1)}, bf16[256,1280]{1,0:T(8,128)(2,1)S(1)}, u32[]{:S(2)}, u32[]{:S(2)}) collective-permute-start(bf16[256,1280]{1,0:T(8,128)(2,1)S(1)} %get-tuple-element.56), channel_id=1, source_target_pairs={{0,8},{4,12},{8,0},{12,4},{16,24},{20,28},{24,16},{28,20},{1,9},{5... | collective-permute-start | bytes 1966088 | tf_op jit(solution)/shard_map/ppermute | solution.py:200
  85.4 15.3 %collective-permute-start.12 = (bf16[256,1280]{1,0:T(8,128)(2,1)S(1)}, bf16[256,1280]{1,0:T(8,128)(2,1)S(1)}, u32[]{:S(2)}, u32[]{:S(2)}) collective-permute-start(bf16[256,1280]{1,0:T(8,128)(2,1)S(1)} %get-tuple-element.57), channel_id=1, source_target_pairs={{0,16},{4,20},{8,24},{12,28},{16,0},{20,4},{24,8},{28,12},{1,17},{... | collective-permute-start | bytes 1966088 | tf_op jit(solution)/shard_map/ppermute | solution.py:200
  102.7 9.8 %collective-permute-start.22 = (bf16[256,256]{1,0:T(8,128)(2,1)S(1)}, bf16[256,256]{1,0:T(8,128)(2,1)S(1)}, u32[]{:S(2)}, u32[]{:S(2)}) collective-permute-start(bf16[256,256]{1,0:T(8,128)(2,1)S(1)} %convert_element_type.36), channel_id=1, source_target_pairs={{0,2},{1,3},{2,0},{3,1},{4,6},{5,7},{6,4},{7,5},{8,10},{9,11},{10,... | collective-permute-start | bytes 393224 | tf_op jit(solution)/shard_map/ppermute | solution.py:207
  104.1 8.4 %collective-permute-start.23 = (bf16[256,256]{1,0:T(8,128)(2,1)S(1)}, bf16[256,256]{1,0:T(8,128)(2,1)S(1)}, u32[]{:S(2)}, u32[]{:S(2)}) collective-permute-start(bf16[256,256]{1,0:T(8,128)(2,1)S(1)} %convert_element_type.36), channel_id=1, source_target_pairs={{0,3},{1,0},{2,1},{3,2},{4,7},{5,4},{6,5},{7,6},{8,11},{9,8},{10,9... | collective-permute-start | bytes 393224 | tf_op jit(solution)/shard_map/ppermute | solution.py:207
  106.3 39.1 %collective-permute-start.17 = (bf16[256,1280]{1,0:T(8,128)(2,1)S(1)}, bf16[256,1280]{1,0:T(8,128)(2,1)S(1)}, u32[]{:S(2)}, u32[]{:S(2)}) collective-permute-start(bf16[256,1280]{1,0:T(8,128)(2,1)S(1)} %broadcast_select_fusion), channel_id=1, source_target_pairs={{1,2},{5,6},{10,11},{14,15},{17,16},{21,20},{26,25},{30,29}} | collective-permute-start | bytes 1966088 | tf_op jit(solution)/shard_map/ppermute | solution.py:282
  107.0 19.1 %collective-permute-start.15 = (bf16[256,1024]{1,0:T(8,128)(2,1)S(1)}, bf16[256,1024]{1,0:T(8,128)(2,1)S(1)}, u32[]{:S(2)}, u32[]{:S(2)}) collective-permute-start(bf16[256,1024]{1,0:T(8,128)(2,1)S(1)} %convert_element_type.35), channel_id=1, source_target_pairs={{0,8},{4,12},{8,0},{12,4},{16,24},{20,28},{24,16},{28,20},{1,9},{5... | collective-permute-start | bytes 1572872 | tf_op jit(solution)/shard_map/ppermute | solution.py:200
  115.4 8.1 %collective-permute-start.26 = (bf16[256,256]{1,0:T(8,128)(2,1)S(1)}, bf16[256,256]{1,0:T(8,128)(2,1)S(1)}, u32[]{:S(2)}, u32[]{:S(2)}) collective-permute-start(bf16[256,256]{1,0:T(8,128)(2,1)S(1)} %get-tuple-element.84), channel_id=1, source_target_pairs={{0,24},{4,28},{8,16},{12,20},{16,8},{20,12},{24,0},{28,4},{1,25},{... | collective-permute-start | bytes 393224 | tf_op jit(solution)/shard_map/ppermute | solution.py:200
  120.5 24.8 %collective-permute-start.16 = (bf16[256,1024]{1,0:T(8,128)(2,1)S(1)}, bf16[256,1024]{1,0:T(8,128)(2,1)S(1)}, u32[]{:S(2)}, u32[]{:S(2)}) collective-permute-start(bf16[256,1024]{1,0:T(8,128)(2,1)S(1)} %convert_element_type.35), channel_id=1, source_target_pairs={{0,16},{4,20},{8,24},{12,28},{16,0},{20,4},{24,8},{28,12},{1,17},{... | collective-permute-start | bytes 1572872 | tf_op jit(solution)/shard_map/ppermute | solution.py:200
  121.2 41.9 %collective-permute-start.19 = (bf16[256,1024]{1,0:T(8,128)(2,1)S(1)}, bf16[256,1024]{1,0:T(8,128)(2,1)S(1)}, u32[]{:S(2)}, u32[]{:S(2)}) collective-permute-start(bf16[256,1024]{1,0:T(8,128)(2,1)S(1)} %convert_element_type.35), channel_id=1, source_target_pairs={{0,24},{4,28},{8,16},{12,20},{16,8},{20,12},{24,0},{28,4},{1,25},{... | collective-permute-start | bytes 1572872 | tf_op jit(solution)/shard_map/ppermute | solution.py:200
  145.4 17.6 %collective-permute-start.18 = (bf16[256,1280]{1,0:T(8,128)(2,1)S(1)}, bf16[256,1280]{1,0:T(8,128)(2,1)S(1)}, u32[]{:S(2)}, u32[]{:S(2)}) collective-permute-start(bf16[256,1280]{1,0:T(8,128)(2,1)S(1)} %collective-permute-done.17), channel_id=1, source_target_pairs={{2,3},{6,7},{25,24},{29,28}} | collective-permute-start | bytes 1966088 | tf_op jit(solution)/shard_map/ppermute | solution.py:282
  146.9 20.5 %collective-permute-start.27 = (bf16[1280,128]{0,1:T(8,128)(2,1)S(1)}, bf16[1280,128]{0,1:T(8,128)(2,1)S(1)}, u32[]{:S(2)}, u32[]{:S(2)}) collective-permute-start(bf16[1280,128]{0,1:T(8,128)(2,1)S(1)} %select_convert_fusion), channel_id=1, source_target_pairs={{0,4},{4,0},{8,12},{12,8},{16,20},{20,16},{24,28},{28,24},{1,5},{5... | collective-permute-start | bytes 983048 | tf_op jit(solution)/shard_map/ppermute | solution.py:200
  (17 other events, 165.5 us)
Sparse Core Ops, SparseCore 0:
  26.2 55.5 all-gather.1
